TPU v7x, 128 devices: a whole 4x4x4 slice. The times are simulated.
128 devices in a mesh: section: 2 (over x_hi), dp: 16 (over z, y), tensor: 4 (over x_lo, core).
Axes of the slice: x: 4 (x_hi: 2, x_lo: 2; x = x_hi * 2 + x_lo), y: 4, z: 4, core: 2. Of those that a mesh axis runs over, the one named last changes fastest.
Arguments:
- hidden_in: bfloat16 [2, 4096, 8192], P('section', 'dp', 'tensor'), may hold values from -3.5 to 3.5
- preact: bfloat16 [2, 4096, 8192], P('section', 'dp', 'tensor'), may hold values from -6 to 6
- norm_gain: float32 [2, 8192], P('section', 'tensor'), may hold values from 0.5 to 1.5
- weight: bfloat16 [2, 8192, 8192], P('section', 'dp', 'tensor')
- bank: float32 [256, 256], replicated, may hold values from -0.18 to 0.18
- mix_index: int32 [2, 2, 128, 2], P('section'), may hold values from 0 to 255
- mix_weight: float32 [2, 2, 128, 2], P('section'), may hold values from 0.1 to 1
- grad_top: bfloat16 [4096, 8192], P('dp', 'tensor'), may hold values from -3.5 to 3.5
Outputs:
- grad_inputs: bfloat16 [2, 4096, 8192], P('section', 'dp', 'tensor')
- bank_grad: float32 [256, 256], replicated
All inputs are finite; a program needn't handle non-finite values.
Results may differ from a plain program's by a relative error of at most 0.014.
Values may be sent and summed in bfloat16 or wider, within the bound.
No kernel may reach another device: no remote copies, remote signals or barrier semaphores. Data moves between devices by JAX's collectives and lax.ppermute only.
A program may use at most 128 MiB of HBM per device.

v0:
```python
import math

import jax
import jax.numpy as jnp
from jax import lax
from jax.sharding import PartitionSpec as P

MODEL_WIDTH = 8192
RANK = 4
SUB = 256


epsilon = 1e-06


def passed_along(block, axis, distance):
    devices = range(lax.axis_size(axis))
    route = [(i - distance, i) for i in devices if i - distance in devices]
    return lax.ppermute(block, axis, route)


def compose(index_layer, weight_layer, bank):
    columns = lax.broadcasted_iota(jnp.int32, (1, 1, 1, bank.shape[0]), 3)
    onehot = (index_layer[..., None] == columns).astype(jnp.float32)
    return jnp.sum(onehot * weight_layer[..., None], axis=2)


def silu_slope(value):
    sig = jax.nn.sigmoid(value)
    return sig * (1.0 + value * (1.0 - sig))


def shards(hidden_in, preact, norm_gain, weight, bank, mix_index, mix_weight, grad_top):
    high = lax.Precision.HIGHEST
    tensor_idx = lax.axis_index("tensor")
    tensor_count = lax.axis_size("tensor")
    segment_idx = lax.axis_index("section")
    segments = lax.axis_size("section")
    replica_count = lax.axis_size("dp")
    local_width = MODEL_WIDTH // tensor_count
    seg_local = local_width // SUB
    seg_row = MODEL_WIDTH // SUB
    bank_rows_count = bank.shape[0]
    own_weight = weight[0]
    w_cols = lax.all_gather(own_weight, "dp", axis=0, tiled=True)
    hidden_state = hidden_in[0].astype(jnp.float32)
    gain_vector = norm_gain[0]
    squares = lax.psum(jnp.sum(hidden_state * hidden_state, axis=1), "tensor")
    inverse_norm_scale = lax.rsqrt(squares / MODEL_WIDTH + epsilon)[:, None]
    centered_input = hidden_state * inverse_norm_scale
    normalized_float = (centered_input * gain_vector).astype(jnp.bfloat16).astype(jnp.float32)
    mixing = compose(mix_index[0], mix_weight[0], bank)
    factors = jnp.einsum("fnb,bs->fns", mixing, bank, precision=high)
    a_full = factors[0].reshape(RANK, MODEL_WIDTH)
    b_full = factors[1].reshape(RANK, MODEL_WIDTH)
    offset = tensor_idx * local_width
    a_local = lax.dynamic_slice_in_dim(a_full, offset, local_width, 1)
    b_local = lax.dynamic_slice_in_dim(b_full, offset, local_width, 1)
    projected = lax.psum(jnp.dot(normalized_float, a_local.T, precision=high), "tensor")
    mix_first = lax.dynamic_slice_in_dim(
        mixing[0].reshape(RANK, seg_row, bank_rows_count), tensor_idx * seg_local, seg_local, 1
    ).reshape(RANK * seg_local, bank_rows_count)
    mix_second = lax.dynamic_slice_in_dim(
        mixing[1].reshape(RANK, seg_row, bank_rows_count), tensor_idx * seg_local, seg_local, 1
    ).reshape(RANK * seg_local, bank_rows_count)
    slope = silu_slope(preact[0].astype(jnp.float32))
    incoming = grad_top
    result = jnp.zeros_like(grad_top)
    bank_acc = jnp.zeros((bank_rows_count, SUB), jnp.float32)
    for step in range(segments):
        active = segments - 1 - step
        incoming_gradient = incoming.astype(jnp.float32)
        grad_z = (incoming_gradient * slope).astype(jnp.bfloat16)
        grad_zf = grad_z.astype(jnp.float32)
        mixed_part = jnp.dot(grad_zf, b_local.T, precision=high)
        partial_value = lax.dot_general(
            grad_z, w_cols, (((1,), (1,)), ((), ())), preferred_element_type=jnp.float32
        )
        partial_value = partial_value + jnp.dot(mixed_part, a_full, precision=high)
        residual_gradient = lax.psum_scatter(
            partial_value.astype(jnp.bfloat16), "tensor", scatter_dimension=1, tiled=True
        ).astype(jnp.float32)
        mixed = lax.psum(mixed_part, "tensor")
        row_inner_product = lax.psum(
            jnp.sum(gain_vector * residual_gradient * centered_input, axis=1), "tensor"
        )
        hidden_gradient = (
            incoming_gradient
            + inverse_norm_scale
            * (
                gain_vector * residual_gradient
                - centered_input * (row_inner_product / MODEL_WIDTH)[:, None]
            )
        ).astype(jnp.bfloat16)
        live = segment_idx == active
        result = jnp.where(live, hidden_gradient, result)
        grad_a = jnp.dot(mixed.T, normalized_float, precision=high).reshape(-1, SUB)
        grad_b = jnp.dot(projected.T, grad_zf, precision=high).reshape(-1, SUB)
        term = jnp.dot(mix_first.T, grad_a, precision=high) + jnp.dot(
            mix_second.T, grad_b, precision=high
        )
        bank_acc = bank_acc + jnp.where(live, term, jnp.zeros_like(term))
        if step + 1 < segments:
            incoming = passed_along(hidden_gradient, "section", -1)
    total = lax.psum(bank_acc, ("section", "dp", "tensor"))
    token_count = grad_top.shape[0] * replica_count
    return (result[None], total / math.sqrt(token_count))


def solution(mesh):
    return jax.shard_map(
        shards,
        mesh=mesh,
        in_specs=(
            P("section", "dp", "tensor"),
            P("section", "dp", "tensor"),
            P("section", "tensor"),
            P("section", "dp", "tensor"),
            P(),
            P("section", None, None, None),
            P("section", None, None, None),
            P("dp", "tensor"),
        ),
        out_specs=(P("section", "dp", "tensor"), P()),
        check_vma=False,
    )
```

profile of v0, /device:TPU:1, one launch (start us, length us, event | category | flops | bytes accessed | tf_op | source)
XLA Modules:
  0.0 568.5 jit_solution(12693782579958269176)
XLA Ops:
  7.2 0.0 all-gather.3.cloned.1.call-start
  7.3 0.7 all-gather.3.cloned.1.call-update
  8.0 0.0 reduce-scatter.3.cloned.1.call-start
  8.0 0.2 select_reduce_fusion
  8.2 0.7 copy-done.10
  8.9 0.4 fusion.38
  9.4 0.1 reshape_squeeze.13
  9.4 0.1 reshape_squeeze.12
  9.5 0.9 fusion.16
  10.4 0.9 fusion.54
  11.3 199.4 %all-gather.3.cloned.1.call-done = bf16[1,8192,2048]{2,1,0:T(8,128)(2,1)} async-done(((bf16[1,512,2048]{2,1,0:T(8,128)(2,1)}), bf16[1,8192,2048]{2,1,0:T(8,128)(2,1)}) %all-gather.3.cloned.1.call-update) | async-done | bytes 33554448 | tf_op jit(solution)/shard_map/all_gather | solution.py:45
  210.7 17.4 %fusion.2 = f32[256,8192]{1,0:T(8,128)} fusion(bf16[256,2048]{1,0:T(8,128)(2,1)S(1)} %fusion.16, bf16[1,8192,2048]{2,1,0:T(8,128)(2,1)} %all-gather.3.cloned.1.call-done), kind=kOutput, calls=%fused_computation.2 | convolution fusion | flops 8589934592 | bytes 42991616 | tf_op jit(solution)/shard_map/dot_general | solution.py:76
  228.0 10.6 %fusion.10 = bf16[256,8192]{1,0:T(8,128)(2,1)} fusion(f32[256,8192]{1,0:T(8,128)} %fusion.2, f32[256,4]{0,1:T(4,128)S(1)} %fusion.54, f32[4,8192]{1,0:T(4,128)S(1)} %reshape_squeeze.13), kind=kOutput, calls=%fused_computation.7 | convolution fusion | flops 104857600 | bytes 12718080 | tf_op jit(solution)/shard_map/dot_general | solution.py:79
  238.6 0.0 reduce-scatter.5.cloned.1.call-start
  238.7 1.1 copy-done.2
  239.8 0.3 fusion.32
  240.1 5.7 %psum.49 = f32[256]{0:T(256)S(1)} all-reduce(f32[256]{0:T(256)S(1)} %fusion.32), channel_id=1, replica_groups=mesh['section'=2,'dp'=16,'tensor'=4] {'tensor'}, use_global_device_ids=true, to_apply=%region_1.0 | all-reduce | flops 256 | bytes 2048 | tf_op jit(solution)/shard_map/psum | solution.py:48
  245.8 38.2 %reduce-scatter.3.cloned.1.call-done = bf16[256,2048]{1,0:T(8,128)(2,1)} async-done(((bf16[256,8192]{1,0:T(8,128)(2,1)}), bf16[256,2048]{1,0:T(8,128)(2,1)}) %reduce-scatter.3.cloned.1.call-update) | async-done | bytes 1048592 | tf_op jit(solution)/shard_map/reduce_scatter | solution.py:80
  284.0 1.8 fusion.31
  285.9 5.4 psum.50
  291.3 2.4 fusion.17
  293.7 1.5 collective-permute-start
  295.2 25.8 %collective-permute-done = bf16[256,2048]{1,0:T(8,128)(2,1)S(1)} collective-permute-done((bf16[256,2048]{1,0:T(8,128)(2,1)S(1)}, bf16[256,2048]{1,0:T(8,128)(2,1)S(1)}, u32[]{:S(2)}, u32[]{:S(2)}) %collective-permute-start) | collective-permute-done | bytes 1048608 | tf_op jit(solution)/shard_map/ppermute | solution.py:19
  321.0 0.9 fusion.18
  321.9 1.0 copy-done.3
  322.9 0.9 fusion.52
  323.8 8.9 %fusion.65 = f32[256,8192]{1,0:T(8,128)} fusion(f32[256,4]{0,1:T(4,128)S(1)} %fusion.52, f32[4,8192]{1,0:T(4,128)S(1)} %reshape_squeeze.13), kind=kOutput, calls=%fused_computation.80 | convolution fusion | flops 100663296 | bytes 8523776 | tf_op jit(solution)/shard_map/dot_general | solution.py:79
  332.7 18.5 %fusion.7 = bf16[256,8192]{1,0:T(8,128)(2,1)} fusion(f32[256,8192]{1,0:T(8,128)} %fusion.65, bf16[256,2048]{1,0:T(8,128)(2,1)} %copy-done.3, bf16[1,8192,2048]{2,1,0:T(8,128)(2,1)} %all-gather.3.cloned.1.call-done), kind=kOutput, calls=%fused_computation.6 | convolution fusion | flops 8594128896 | bytes 47185920 | tf_op jit(solution)/shard_map/dot_general | solution.py:76
  351.3 0.0 all-reduce.3.cloned.1.call-start
  351.3 0.9 copy-done.11
  352.2 0.7 fusion.63
  352.9 0.9 fusion.46
  353.8 43.0 %reduce-scatter.5.cloned.1.call-done = bf16[256,2048]{1,0:T(8,128)(2,1)} async-done(((bf16[256,8192]{1,0:T(8,128)(2,1)}), bf16[256,2048]{1,0:T(8,128)(2,1)}) %reduce-scatter.5.cloned.1.call-update) | async-done | bytes 1048592 | tf_op jit(solution)/shard_map/reduce_scatter | solution.py:80
  396.9 1.8 fusion.28
  398.6 9.4 %all-reduce = (f32[256]{0:T(256)S(1)}, f32[256,4]{0,1:T(4,128)S(1)}, f32[256,4]{0,1:T(4,128)S(1)}, f32[256,4]{0,1:T(4,128)S(1)}) all-reduce(f32[256]{0:T(256)S(1)} %fusion.28, f32[256,4]{0,1:T(4,128)S(1)} %fusion.54, f32[256,4]{0,1:T(4,128)S(1)} %fusion.46, ...), channel_id=1, replica_groups=mesh['section'=2,'dp'=16,'tensor'=4] {'tensor'}, use_global_device_ids=true, to_apply=%region_8.9 | all-reduce | flops 3328 | bytes 26624 | tf_op jit(solution)/shard_map/psum | solution.py:84
  408.1 1.8 fusion.69
  409.8 0.5 fusion.67
  410.3 0.6 reshape.34
  411.0 0.6 reshape.36
  411.6 0.5 fusion.66
  412.1 0.5 fusion.68
  412.7 0.4 fusion.44
  413.2 0.4 fusion.42
  413.6 1.2 fusion.35
  414.8 1.9 fusion.34
  416.8 3.2 fusion.37
  420.0 140.3 %all-reduce.3.cloned.1.call-done = f32[256,256]{1,0:T(8,128)} async-done(((f32[256,256]{1,0:T(8,128)}), f32[256,256]{1,0:T(8,128)}) %all-reduce.3.cloned.1.call-update) | async-done | bytes 262160 | tf_op jit(solution)/shard_map/psum | solution.py:105
  560.3 1.7 broadcast_multiply_fusion
  (41 shorter events, 0.2 us)
Async XLA Ops:
  7.2 1.8 copy-start
  7.2 0.8 copy-start.16
  7.2 0.8 copy-start.17
  7.2 2.3 copy-start.6
  7.2 2.3 copy-start.4
  7.2 203.4 %all-gather.3.cloned.1.call-start = ((), (), s32[]{:S(2)}) async-start(), calls=%async_computation.5 | async-start | bytes 35651584 | tf_op jit(solution)/shard_map/all_gather | solution.py:45
  8.0 276.0 %reduce-scatter.3.cloned.1.call-start = ((), (), s32[]{:S(2)}) async-start(), calls=%async_computation.2 | async-start | bytes 5242880 | tf_op jit(solution)/shard_map/reduce_scatter | solution.py:80
  8.2 0.7 copy-start.10
  238.6 1.2 copy-start.2
  238.6 45.4 %copy-start.13 = (f32[1,2048]{1,0:T(1,128)S(1)}, f32[1,2048]{1,0:T(1,128)}, u32[]{:S(2)}) copy-start(f32[1,2048]{1,0:T(1,128)} %param.10) | copy-start | bytes 24580
  238.6 158.2 %reduce-scatter.5.cloned.1.call-start = ((), (), s32[]{:S(2)}) async-start(), calls=%async_computation.3 | async-start | bytes 5242880 | tf_op jit(solution)/shard_map/reduce_scatter | solution.py:80
  245.8 47.9 %copy-start.14 = (f32[256]{0:T(256)}, f32[256]{0:T(256)S(1)}, u32[]{:S(2)}) copy-start(f32[256]{0:T(256)S(1)} %add_rsqrt_fusion) | copy-start | bytes 3076
  291.3 29.8 %copy-start.5 = (bf16[1,256,2048]{2,1,0:T(8,128)(2,1)S(1)}, bf16[1,256,2048]{2,1,0:T(8,128)(2,1)}, u32[]{:S(2)}) copy-start(bf16[1,256,2048]{2,1,0:T(8,128)(2,1)} %param.9) | copy-start | bytes 3145732
  293.7 30.1 %copy-start.9 = (bf16[256,2048]{1,0:T(8,128)(2,1)}, bf16[256,2048]{1,0:T(8,128)(2,1)S(1)}, u32[]{:S(2)}) copy-start(bf16[256,2048]{1,0:T(8,128)(2,1)S(1)} %fusion.17) | copy-start | bytes 3145732
  293.7 27.3 %collective-permute-start = (bf16[256,2048]{1,0:T(8,128)(2,1)S(1)}, bf16[256,2048]{1,0:T(8,128)(2,1)S(1)}, u32[]{:S(2)}, u32[]{:S(2)}) collective-permute-start(bf16[256,2048]{1,0:T(8,128)(2,1)S(1)} %fusion.17), channel_id=1, source_target_pairs={{64,0},{65,1},{66,2},{67,3},{68,4},{69,5},{70,6},{71,7},{72,8},{73... | collective-permute-start | bytes 3145736 | tf_op jit(solution)/shard_map/ppermute | solution.py:19
  321.0 2.8 copy-start.7
  321.9 1.0 copy-start.3
  351.2 0.9 copy-start.11
  351.3 209.0 %all-reduce.3.cloned.1.call-start = ((), (), s32[]{:S(2)}) async-start(), calls=%async_computation.4 | async-start | bytes 524288 | tf_op jit(solution)/shard_map/psum | solution.py:105
  408.0 4.7 copy-start.12
  411.6 5.1 copy-start.8
  411.6 5.1 copy-start.15
  416.8 145.2 %copy-start.1 = (f32[256,256]{1,0:T(8,128)S(1)}, f32[256,256]{1,0:T(8,128)}, u32[]{:S(2)}) copy-start(f32[256,256]{1,0:T(8,128)} %param.12) | copy-start | bytes 786436
Sparse Core Ops, SparseCore 0:
  10.2 200.4 all-gather.2
  238.8 45.1 reduce-scatter.2
  351.4 45.4 reduce-scatter.4
  416.9 143.3 all-reduce.2
where the time goes:
time: 569 us; the launch traced here: 568 us
  waiting for transfers between devices  447 us (79%)
  matrix products  65.8 us (12%)
  blocking collectives  20.5 us (4%)
  between operations  14 us (2%)
  other arithmetic  13.1 us (2%)
  local copies, waits for them, and re-layouts  5.94 us (1%)
    all_gather x1, waiting for transfers between devices, shards(): w_cols = lax.all_gather(own_weight, 'dp', axis=0, tiled=True)  199 us
    psum x1, waiting for transfers between devices, shards(): total = lax.psum(bank_acc, ('section', 'dp', 'tensor'))  140 us
    reduce_scatter x2, waiting for transfers between devices, shards(): lax.psum_scatter(partial_value.astype(jnp.bfloat16), 'tensor', scatter_di...  81.2 us
    dot_general x2, matrix products, shards(): lax.dot_general(grad_z, w_cols, (((1,), (1,)), ((), ())), preferred_eleme...  35.9 us
    ppermute x1, waiting for transfers between devices, passed_along(): return lax.ppermute(block, axis, route)  25.8 us
    dot_general x2, matrix products, shards(): partial_value = partial_value + jnp.dot(mixed_part, a_full, precision=high)  19.5 us
    psum x2, blocking collectives, shards(): lax.psum(jnp.sum(gain_vector * residual_gradient * centered_input, axis=1...  14.8 us
  transfers between devices with their start and end apart: 5, of which 5 were waited for; matrix products, arithmetic and copies ran while one was open for 1% of the time, Pallas kernels for 0%

commit v1 on v0

v1 whole, which is shorter than its diff:
```python
import math

import jax
import jax.numpy as jnp
from jax import lax
from jax.sharding import Mesh, PartitionSpec as P

MODEL_WIDTH = 8192
RANK = 4
SUB = 256
TOKENS = 4096
RING = 4
CHUNKS = 2

epsilon = 1e-06
HIGH = lax.Precision.HIGHEST


def ring_route(distance, sections=(0, 1)):
    return [(s * RING + i, s * RING + (i + distance) % RING) for s in sections for i in range(RING)]


def gather_ring(block, axis, sections=(0, 1)):
    axes = ("section", axis)
    half = block.shape[0] // 2
    after = lax.ppermute(block, axes, ring_route(-1, sections))
    before = lax.ppermute(block, axes, ring_route(1, sections))
    far_low = lax.ppermute(after[:half], axes, ring_route(-1, sections))
    far_high = lax.ppermute(before[half:], axes, ring_route(1, sections))
    return block, after, far_low, far_high, before


def swap(block, axis, sections=(0, 1)):
    pairs = [(s * 2 + i, s * 2 + 1 - i) for s in sections for i in range(2)]
    return lax.ppermute(block, ("section", axis), pairs)


def butterfly(value, axis, bit):
    size = lax.axis_size(axis)
    return value + lax.ppermute(value, axis, [(i, i ^ bit) for i in range(size)])


def compose(index_layer, weight_layer, rows):
    columns = lax.broadcasted_iota(jnp.int32, (1, 1, 1, 1, rows), 4)
    onehot = (index_layer[..., None] == columns).astype(jnp.float32)
    return jnp.sum(onehot * weight_layer[..., None], axis=3)


def silu_slope(value):
    sig = jax.nn.sigmoid(value)
    return sig * (1.0 + value * (1.0 - sig))


def after(value, earlier):
    return lax.optimization_barrier((value, earlier))[0]


def pick(stack, index):
    return lax.dynamic_index_in_dim(stack, index, 0, keepdims=False)


def shards(hidden_in, preact, norm_gain, weight, bank, mix_index, mix_weight, grad_top):
    section = lax.axis_index("section")
    z, y = lax.axis_index("z"), lax.axis_index("y")
    pair, core = lax.axis_index("pair"), lax.axis_index("core")
    place = pair * 2 + core
    tensor = ("pair", "core")
    bank_rows = bank.shape[0]
    top_layer = section == 1

    tokens, local_width = grad_top.shape
    chunk = tokens // CHUNKS
    seg_local = local_width // SUB
    seg_row = MODEL_WIDTH // SUB

    own_weight = weight[0]
    pieces_w = gather_ring(own_weight, "z")

    slope = silu_slope(preact[0].astype(jnp.float32))
    gain = norm_gain[0]
    hidden = hidden_in[0].astype(jnp.float32)

    def local_pieces(array):
        array = array.reshape(2, RANK, seg_row, 2)
        return lax.dynamic_slice_in_dim(array, place * seg_local, seg_local, 2)

    mixing = compose(local_pieces(mix_index[0]), local_pieces(mix_weight[0]), bank_rows)
    mixing = mixing.reshape(2, RANK * seg_local, bank_rows)
    factors = jnp.einsum("fnb,bs->fns", mixing, bank, precision=HIGH)
    a_local = factors[0].reshape(RANK, local_width)
    b_local = factors[1].reshape(RANK, local_width)

    def make_dz(incoming, c):
        rows = slice(c * chunk, (c + 1) * chunk)
        return (incoming.astype(jnp.float32) * slope[rows]).astype(jnp.bfloat16)

    top = [grad_top[c * chunk:(c + 1) * chunk] for c in range(CHUNKS)]
    dz_top = [make_dz(top[c], c) for c in range(CHUNKS)]
    dz_top_all = jnp.concatenate(dz_top, axis=0)

    sums = lax.psum(
        jnp.concatenate(
            [
                jnp.sum(hidden * hidden, axis=1, keepdims=True),
                jnp.dot(hidden * gain, a_local.T, precision=HIGH),
                jnp.dot(dz_top_all.astype(jnp.float32), b_local.T, precision=HIGH),
            ],
            axis=1,
        ),
        tensor,
    )
    scale = lax.rsqrt(sums[:, :1] / MODEL_WIDTH + epsilon)
    projected = sums[:, 1:1 + RANK] * scale
    mixed_top = sums[:, 1 + RANK:]
    xhat = hidden * scale
    x = (xhat * gain).astype(jnp.bfloat16)

    def projection_gradient(dz, sections):
        gathered = jnp.concatenate(gather_ring(dz, "y", sections), axis=0)

        def product(piece):
            return lax.dot_general(
                gathered, piece, (((1,), (1,)), ((), ())), preferred_element_type=jnp.float32
            ).astype(jnp.bfloat16)

        own, after, far_low, far_high, before = pieces_w
        parts = jnp.stack(
            [
                product(own),
                product(after),
                jnp.concatenate([product(far_low), product(far_high)], axis=1),
                product(before),
            ]
        )
        odd = (core - z) % 2
        parts = parts.reshape(2, 2, *parts.shape[1:])
        keep = lax.dynamic_index_in_dim(parts, odd, 1, keepdims=False)
        send = lax.dynamic_index_in_dim(parts, 1 - odd, 1, keepdims=False)
        got = swap(send, "core", sections)
        high_of = (place - z) % 4 // 2
        high_other = (place ^ 2) - z
        high_other = high_other % 4 // 2
        mine = pick(keep, high_of).astype(jnp.float32) + pick(got, high_of).astype(jnp.float32)
        theirs = pick(keep, high_other).astype(jnp.float32) + pick(got, high_other).astype(jnp.float32)
        other = swap(theirs.astype(jnp.bfloat16), "pair", sections)
        total = (mine + other.astype(jnp.float32)).astype(jnp.bfloat16)
        total = total.reshape(RING, chunk, total.shape[1])
        axes = ("section", "y")
        from_before = lax.ppermute(total[1], axes, ring_route(1, sections))
        from_far = lax.ppermute(total[2], axes, ring_route(2, sections))
        from_after = lax.ppermute(total[3], axes, ring_route(-1, sections))
        got = jnp.stack([total[0], from_after, from_far, from_before])
        return jnp.concatenate([pick(got, (j - y) % 4) for j in range(RING)], axis=1).astype(jnp.float32)

    def layer(incoming, dz, mixed, c, sections, earlier):
        rows = slice(c * chunk, (c + 1) * chunk)
        dx = projection_gradient(dz, sections) + jnp.dot(mixed, a_local, precision=HIGH)
        scaled = gain * dx
        inner = lax.psum(after(jnp.sum(scaled * xhat[rows], axis=1), earlier), tensor)
        return (
            incoming.astype(jnp.float32)
            + scale[rows] * (scaled - xhat[rows] * (inner / MODEL_WIDTH)[:, None])
        ).astype(jnp.bfloat16)

    top_grads = []
    earlier = mixed_top
    low_in = []
    for c in range(CHUNKS):
        rows = slice(c * chunk, (c + 1) * chunk)
        grad = layer(top[c], dz_top[c], mixed_top[rows], c, (1,), earlier)
        earlier = grad
        top_grads.append(grad)
        low_in.append(lax.ppermute(grad, "section", [(1, 0)]))
    low_grads, low_dz, low_mixed = [], [], []
    for c in range(CHUNKS):
        dz = make_dz(low_in[c], c)
        mixed = jnp.dot(dz.astype(jnp.float32), b_local.T, precision=HIGH)
        mixed = lax.psum(after(mixed, earlier), tensor)
        low_grads.append(layer(low_in[c], dz, mixed, c, (0,), mixed))
        earlier = low_grads[-1]
        low_dz.append(dz)
        low_mixed.append(mixed)

    result = jnp.where(top_layer, jnp.concatenate(top_grads, axis=0), jnp.concatenate(low_grads, axis=0))

    dz = jnp.where(top_layer, dz_top_all, jnp.concatenate(low_dz, axis=0))
    mixed = jnp.where(top_layer, mixed_top, jnp.concatenate(low_mixed, axis=0))
    grad_a = jnp.dot(mixed.T, x.astype(jnp.float32), precision=HIGH)
    grad_b = jnp.dot(projected.T, dz.astype(jnp.float32), precision=HIGH)
    grads = jnp.concatenate([grad_a, grad_b], axis=0)
    for axis, bit in (("y", 1), ("y", 2), ("z", 1), ("z", 2)):
        grads = butterfly(grads, axis, bit)
    grads = grads.reshape(2 * RANK * seg_local, SUB)
    bank_grad = jnp.dot(mixing.reshape(2 * RANK * seg_local, bank_rows).T, grads, precision=HIGH)
    bank_grad = bank_grad / math.sqrt(TOKENS)
    for axis in ("core", "pair", "section"):
        bank_grad = butterfly(bank_grad, axis, 1)
    return (result[None], bank_grad)


def solution(mesh):
    fine = Mesh(
        mesh.devices.reshape(2, RING, RING, 2, 2), ("section", "z", "y", "pair", "core")
    )
    rows, columns = ("z", "y"), ("pair", "core")
    return jax.shard_map(
        shards,
        mesh=fine,
        in_specs=(
            P("section", rows, columns),
            P("section", rows, columns),
            P("section", columns),
            P("section", rows, columns),
            P(),
            P("section", None, None, None),
            P("section", None, None, None),
            P(rows, columns),
        ),
        out_specs=(P("section", rows, columns), P()),
        check_vma=False,
    )
```

time: 569 us -> 445 us (0.78); the launches traced: 568 us -> 437 us
  waiting for transfers between devices: 447 us -> 133 us
  starting transfers between devices: 1.63 us -> 94.9 us
  blocking collectives: 20.5 us -> 65.4 us
  local copies, waits for them, and re-layouts: 5.94 us -> 47.8 us
  other arithmetic: 13.1 us -> 34.8 us
  between operations: 14 us -> 2.59 us
  matrix products: 65.8 us -> 58.4 us
    all_gather x1 -> x0, waiting for transfers between devices: 199 us -> none  [shards(): w_cols = lax.all_gather(own_weight, 'dp', axis=0, tiled=True)]
    psum x1 -> x0, waiting for transfers between devices: 140 us -> none  [shards(): total = lax.psum(bank_acc, ('section', 'dp', 'tensor'))]
    ppermute x1 -> x49, waiting for transfers between devices: 25.8 us -> 133 us  [the longest x2 56.2 us: shards(): low_in.append(lax.ppermute(grad, 'section', [(1, 0)]))]
    ppermute x1 -> x49, starting transfers between devices: 1.47 us -> 94.9 us  [the longest x8 20.1 us: swap(): return lax.ppermute(block, ('section', axis), pairs)]
    reduce_scatter x2 -> x0, waiting for transfers between devices: 81.2 us -> none  [shards(): lax.psum_scatter(partial_value.astype(jnp.bfloat16), 'tensor', scatter_di...]
    psum x3 -> x7, blocking collectives: 20.5 us -> 65.4 us  [the longest x4 28.1 us: layer(): lax.psum(after(jnp.sum(scaled * xhat[rows], axis=1), earlier), tensor)]
    dynamic_slice x0 -> x18, local copies, waits for them, and re-layouts: none -> 21.4 us  [the longest x8 11.2 us: pick(): return lax.dynamic_index_in_dim(stack, index, 0, keepdims=False)]
    unnamed x36 -> x146, local copies, waits for them, and re-layouts: 3.76 us -> 20.9 us
  transfers between devices with their start and end apart: 5 -> 49, of which waited for: 5 -> 14; matrix products, arithmetic and copies ran while one was open for 1% -> 21% of each run, Pallas kernels for 0% -> 0%
where the time goes in v1:
time: 445 us; the launch traced here: 437 us
  waiting for transfers between devices  133 us (30%)
  starting transfers between devices  94.9 us (21%)
  blocking collectives  65.4 us (15%)
  matrix products  58.4 us (13%)
  local copies, waits for them, and re-layouts  47.8 us (11%)
  other arithmetic  34.8 us (8%)
    ppermute x2, waiting for transfers between devices, shards(): low_in.append(lax.ppermute(grad, 'section', [(1, 0)]))  56.2 us
    dot_general x20, matrix products, product(): lax.dot_general(gathered, piece, (((1,), (1,)), ((), ())), preferred_elem...  38.4 us
    ppermute x5, waiting for transfers between devices, gather_ring(): after = lax.ppermute(block, axes, ring_route(-1, sections))  29 us
    psum x4, blocking collectives, layer(): lax.psum(after(jnp.sum(scaled * xhat[rows], axis=1), earlier), tensor)  28.1 us
    psum x2, blocking collectives, shards(): mixed = lax.psum(after(mixed, earlier), tensor)  25.5 us
    unnamed x146, local copies, waits for them, and re-layouts  20.9 us
    ppermute x8, starting transfers between devices, swap(): return lax.ppermute(block, ('section', axis), pairs)  20.1 us
    ppermute x7, waiting for transfers between devices, butterfly(): lax.ppermute(value, axis, [(i, i ^ bit) for i in range(size)])  16.1 us
  transfers between devices with their start and end apart: 49, of which 14 were waited for; matrix products, arithmetic and copies ran while one was open for 21% of the time, Pallas kernels for 0%

profile of v1, /device:TPU:1, one launch (start us, length us, event | category | flops | bytes accessed | tf_op | source)
XLA Modules:
  0.0 436.7 jit_solution(15830708953510467989)
XLA Ops:
  7.6 4.7 %collective-permute-start.4 = (bf16[512,2048]{1,0:T(8,128)(2,1)}, bf16[512,2048]{1,0:T(8,128)(2,1)}, u32[]{:S(2)}, u32[]{:S(2)}) collective-permute-start(bf16[512,2048]{1,0:T(8,128)(2,1)} %bitcast.9), channel_id=1, source_target_pairs={{0,48},{16,0},{32,16},{48,32},{64,112},{80,64},{96,80},{112,96},{1... | collective-permute-start | bytes 6291464 | tf_op jit(solution)/shard_map/ppermute | solution.py:26
  13.0 2.7 fusion.54
  22.0 3.0 fusion.15
  25.0 2.9 fusion.18
  27.9 29.0 %collective-permute-done.4 = bf16[512,2048]{1,0:T(8,128)(2,1)} collective-permute-done((bf16[512,2048]{1,0:T(8,128)(2,1)}, bf16[512,2048]{1,0:T(8,128)(2,1)}, u32[]{:S(2)}, u32[]{:S(2)}) %collective-permute-start.4) | collective-permute-done | bytes 2097184 | tf_op jit(solution)/shard_map/ppermute | solution.py:26
  58.2 3.5 collective-permute-start.5
  61.7 5.3 %collective-permute-done.6 = bf16[512,2048]{1,0:T(8,128)(2,1)S(1)} collective-permute-done((bf16[512,2048]{1,0:T(8,128)(2,1)}, bf16[512,2048]{1,0:T(8,128)(2,1)S(1)}, u32[]{:S(2)}, u32[]{:S(2)}) %collective-permute-start.6) | collective-permute-done | bytes 2097184 | tf_op jit(solution)/shard_map/ppermute | solution.py:27
  68.6 3.0 fusion.16
  73.0 2.9 fusion.19
  75.9 15.4 %collective-permute-done.7 = bf16[256,2048]{1,0:T(8,128)(2,1)S(1)} collective-permute-done((bf16[256,2048]{1,0:T(8,128)(2,1)S(1)}, bf16[256,2048]{1,0:T(8,128)(2,1)S(1)}, u32[]{:S(2)}, u32[]{:S(2)}) %collective-permute-start.7) | collective-permute-done | bytes 1048608 | tf_op jit(solution)/shard_map/ppermute | solution.py:29
  103.1 11.8 %psum.49 = f32[256,9]{0,1:T(8,128)S(1)} all-reduce(f32[256,9]{0,1:T(8,128)S(1)} %pad_maximum_fusion.12), channel_id=1, replica_groups=mesh['section'=2,'z'=4,'y'=4,'pair'=2,'core'=2] {'pair','core'}, use_global_device_ids=true, to_apply=%region_2.0 | all-reduce | flops 2304 | bytes 18432 | tf_op jit(solution)/shard_map/psum | solution.py:101
  115.1 2.3 fusion.48
  147.5 2.9 multiply_reduce_fusion.3
  150.4 6.2 %psum.50 = f32[128]{0:T(128)S(1)} all-reduce(f32[128]{0:T(128)} %get-tuple-element.8), channel_id=1, replica_groups=mesh['section'=2,'z'=4,'y'=4,'pair'=2,'core'=2] {'pair','core'}, use_global_device_ids=true, to_apply=%region_4.5 | all-reduce | flops 128 | bytes 1024 | tf_op jit(solution)/shard_map/psum | solution.py:159
  156.6 2.5 fusion.28
  159.1 5.7 %psum.51 = f32[128]{0:T(128)S(1)} all-reduce(f32[128]{0:T(128)S(1)} %copy-done.63), channel_id=1, replica_groups=mesh['section'=2,'z'=4,'y'=4,'pair'=2,'core'=2] {'pair','core'}, use_global_device_ids=true, to_apply=%region_6.7 | all-reduce | flops 128 | bytes 1024 | tf_op jit(solution)/shard_map/psum | solution.py:159
  169.3 45.0 %collective-permute-done.32 = bf16[128,2048]{1,0:T(8,128)(2,1)S(1)} collective-permute-done((bf16[128,2048]{1,0:T(8,128)(2,1)S(1)}, bf16[128,2048]{1,0:T(8,128)(2,1)S(1)}, u32[]{:S(2)}, u32[]{:S(2)}) %collective-permute-start.32) | collective-permute-done | bytes 524320 | tf_op jit(solution)/shard_map/ppermute | solution.py:173
  214.3 11.2 %collective-permute-done.22 = bf16[128,2048]{1,0:T(8,128)(2,1)S(1)} collective-permute-done((bf16[128,2048]{1,0:T(8,128)(2,1)S(1)}, bf16[128,2048]{1,0:T(8,128)(2,1)S(1)}, u32[]{:S(2)}, u32[]{:S(2)}) %collective-permute-start.22) | collective-permute-done | bytes 524320 | tf_op jit(solution)/shard_map/ppermute | solution.py:173
  228.3 4.5 %collective-permute-start.23 = (bf16[128,2048]{1,0:T(8,128)(2,1)S(1)}, bf16[128,2048]{1,0:T(8,128)(2,1)S(1)}, u32[]{:S(2)}, u32[]{:S(2)}) collective-permute-start(bf16[128,2048]{1,0:T(8,128)(2,1)S(1)} %get-tuple-element.19), channel_id=1, source_target_pairs={{0,12},{4,0},{8,4},{12,8},{1,13},{5,1},{9,5},{13,9},{2,14},{6,2},{... | collective-permute-start | bytes 1572872 | tf_op jit(solution)/shard_map/ppermute | solution.py:26
  234.7 4.6 %collective-permute-start.33 = (bf16[128,2048]{1,0:T(8,128)(2,1)S(1)}, bf16[128,2048]{1,0:T(8,128)(2,1)S(1)}, u32[]{:S(2)}, u32[]{:S(2)}) collective-permute-start(bf16[128,2048]{1,0:T(8,128)(2,1)S(1)} %get-tuple-element.31), channel_id=1, source_target_pairs={{0,12},{4,0},{8,4},{12,8},{1,13},{5,1},{9,5},{13,9},{2,14},{6,2},{... | collective-permute-start | bytes 1572872 | tf_op jit(solution)/shard_map/ppermute | solution.py:26
  243.0 4.6 %collective-permute-start.24 = (bf16[64,2048]{1,0:T(8,128)(2,1)S(1)}, bf16[64,2048]{1,0:T(8,128)(2,1)S(1)}, u32[]{:S(2)}, u32[]{:S(2)}) collective-permute-start(bf16[64,2048]{1,0:T(8,128)(2,1)S(1)} %slice.230), channel_id=1, source_target_pairs={{0,12},{4,0},{8,4},{12,8},{1,13},{5,1},{9,5},{13,9},{2,14},{6,2},{... | collective-permute-start | bytes 786440 | tf_op jit(solution)/shard_map/ppermute | solution.py:28
  247.6 4.7 %collective-permute-done.35 = bf16[128,2048]{1,0:T(8,128)(2,1)S(1)} collective-permute-done((bf16[128,2048]{1,0:T(8,128)(2,1)S(1)}, bf16[128,2048]{1,0:T(8,128)(2,1)S(1)}, u32[]{:S(2)}, u32[]{:S(2)}) %collective-permute-start.35) | collective-permute-done | bytes 524320 | tf_op jit(solution)/shard_map/ppermute | solution.py:27
  254.2 4.6 %collective-permute-start.34 = (bf16[64,2048]{1,0:T(8,128)(2,1)S(1)}, bf16[64,2048]{1,0:T(8,128)(2,1)S(1)}, u32[]{:S(2)}, u32[]{:S(2)}) collective-permute-start(bf16[64,2048]{1,0:T(8,128)(2,1)S(1)} %slice.236), channel_id=1, source_target_pairs={{0,12},{4,0},{8,4},{12,8},{1,13},{5,1},{9,5},{13,9},{2,14},{6,2},{... | collective-permute-start | bytes 786440 | tf_op jit(solution)/shard_map/ppermute | solution.py:28
  259.0 2.9 fusion.21
  261.9 2.3 collective-permute-done.34
  264.3 4.5 %fusion.24 = bf16[1,512,512]{1,2,0:T(8,128)(2,1)} fusion(bf16[512,2048]{1,0:T(8,128)(2,1)S(1)} %constant_dynamic-update-slice_fusion.15, bf16[1,512,2048]{2,1,0:T(8,128)(2,1)} %param.11), kind=kOutput, calls=%fused_computation.56 | convolution fusion | flops 1074003968 | bytes 4718592 | tf_op jit(solution)/shard_map/dot_general | solution.py:122
  273.0 2.9 fusion.22
  278.5 2.3 copy.35
  280.8 6.7 %collective-permute-start.27 = (bf16[2,512,512]{2,1,0:T(8,128)(2,1)}, bf16[2,512,512]{2,1,0:T(8,128)(2,1)}, u32[]{:S(2)}, u32[]{:S(2)}) collective-permute-start(bf16[2,512,512]{2,1,0:T(8,128)(2,1)} %bitcast.249), channel_id=1, source_target_pairs={{0,1},{1,0},{2,3},{3,2},{4,5},{5,4},{6,7},{7,6},{8,9},{9,8},{10,11... | collective-permute-start | bytes 3145736 | tf_op jit(solution)/shard_map/ppermute | solution.py:35
  287.5 2.6 convolution_convert_fusion.12
  293.0 3.0 fusion.25
  298.7 2.3 copy.38
  317.7 3.4 collective-permute-start.38
  322.6 19.8 %psum.52 = f32[128,4]{0,1:T(4,128)} all-reduce(f32[128,4]{0,1:T(4,128)S(1)} %fusion.82), channel_id=1, replica_groups=mesh['section'=2,'z'=4,'y'=4,'pair'=2,'core'=2] {'pair','core'}, use_global_device_ids=true, to_apply=%region_7.8 | all-reduce | flops 512 | bytes 4096 | tf_op jit(solution)/shard_map/psum | solution.py:178
  348.6 3.1 fusion.41
  353.8 6.5 %collective-permute-start.30 = (bf16[128,512]{1,0:T(8,128)(2,1)S(1)}, bf16[128,512]{1,0:T(8,128)(2,1)S(1)}, u32[]{:S(2)}, u32[]{:S(2)}) collective-permute-start(bf16[128,512]{1,0:T(8,128)(2,1)S(1)} %get-tuple-element.48), channel_id=1, source_target_pairs={{0,8},{4,12},{8,0},{12,4},{1,9},{5,13},{9,1},{13,5},{2,10},{6,14},... | collective-permute-start | bytes 393224 | tf_op jit(solution)/shard_map/ppermute | solution.py:150
  366.1 2.6 multiply_reduce_fusion.1
  368.8 7.8 %psum.53 = f32[128]{0:T(128)S(1)} all-reduce(f32[128]{0:T(128)} %get-tuple-element.11), channel_id=1, replica_groups=mesh['section'=2,'z'=4,'y'=4,'pair'=2,'core'=2] {'pair','core'}, use_global_device_ids=true, to_apply=%region_9.10 | all-reduce | flops 128 | bytes 1024 | tf_op jit(solution)/shard_map/psum | solution.py:159
  376.5 2.5 fusion.32
  379.0 5.7 %psum.54 = f32[128,4]{0,1:T(4,128)S(1)} all-reduce(f32[128,4]{0,1:T(4,128)S(1)} %copy-done.48), channel_id=1, replica_groups=mesh['section'=2,'z'=4,'y'=4,'pair'=2,'core'=2] {'pair','core'}, use_global_device_ids=true, to_apply=%region_10.11 | all-reduce | flops 512 | bytes 4096 | tf_op jit(solution)/shard_map/psum | solution.py:178
  386.2 3.1 collective-permute-done.42
  390.1 4.0 collective-permute-done.43
  394.1 3.4 collective-permute-done.44
  400.3 4.0 collective-permute-start.40
  404.3 2.6 collective-permute-start.39
  407.4 5.5 %collective-permute-start.46 = (f32[256,256]{1,0:T(8,128)S(1)}, f32[256,256]{1,0:T(8,128)S(1)}, u32[]{:S(2)}, u32[]{:S(2)}) collective-permute-start(f32[256,256]{1,0:T(8,128)S(1)} %convolution_multiply_fusion), channel_id=1, source_target_pairs={{0,1},{1,0},{2,3},{3,2},{4,5},{5,4},{6,7},{7,6},{8,9},{9,8},{10,11... | collective-permute-start | bytes 786440 | tf_op jit(solution)/shard_map/ppermute | solution.py:40
  417.5 8.4 %psum.55 = f32[128]{0:T(128)S(1)} all-reduce(f32[128]{0:T(128)S(1)} %get-tuple-element.13), channel_id=1, replica_groups=mesh['section'=2,'z'=4,'y'=4,'pair'=2,'core'=2] {'pair','core'}, use_global_device_ids=true, to_apply=%region_12.13 | all-reduce | flops 128 | bytes 1024 | tf_op jit(solution)/shard_map/psum | solution.py:159
  430.1 5.7 %collective-permute-done.48 = f32[256,256]{1,0:T(8,128)S(1)} collective-permute-done((f32[256,256]{1,0:T(8,128)S(1)}, f32[256,256]{1,0:T(8,128)S(1)}, u32[]{:S(2)}, u32[]{:S(2)}) %collective-permute-start.48) | collective-permute-done | bytes 262176 | tf_op jit(solution)/shard_map/ppermute | solution.py:40
  (326 shorter events, 133.8 us)
Async XLA Ops:
  4.7 14.7 %collective-permute-start.2 = (bf16[128,2048]{1,0:T(8,128)(2,1)}, bf16[128,2048]{1,0:T(8,128)(2,1)S(1)}, u32[]{:S(2)}, u32[]{:S(2)}) collective-permute-start(bf16[128,2048]{1,0:T(8,128)(2,1)} %get-tuple-element.21), channel_id=1, source_target_pairs={{64,68},{68,72},{72,76},{76,64},{65,69},{69,73},{73,77},{77,65},{6... | collective-permute-start | bytes 1572872 | tf_op jit(solution)/shard_map/ppermute | solution.py:27
  5.5 12.3 %collective-permute-start = (bf16[128,2048]{1,0:T(8,128)(2,1)}, bf16[128,2048]{1,0:T(8,128)(2,1)S(1)}, u32[]{:S(2)}, u32[]{:S(2)}) collective-permute-start(bf16[128,2048]{1,0:T(8,128)(2,1)} %get-tuple-element.21), channel_id=1, source_target_pairs={{64,76},{68,64},{72,68},{76,72},{65,77},{69,65},{73,69},{77,73},{6... | collective-permute-start | bytes 1572872 | tf_op jit(solution)/shard_map/ppermute | solution.py:26
  6.2 13.2 %collective-permute-start.15 = (bf16[128,2048]{1,0:T(8,128)(2,1)}, bf16[128,2048]{1,0:T(8,128)(2,1)S(1)}, u32[]{:S(2)}, u32[]{:S(2)}) collective-permute-start(bf16[128,2048]{1,0:T(8,128)(2,1)} %get-tuple-element.25), channel_id=1, source_target_pairs={{64,68},{68,72},{72,76},{76,64},{65,69},{69,73},{73,77},{77,65},{6... | collective-permute-start | bytes 1572872 | tf_op jit(solution)/shard_map/ppermute | solution.py:27
  6.9 13.4 %collective-permute-start.13 = (bf16[128,2048]{1,0:T(8,128)(2,1)}, bf16[128,2048]{1,0:T(8,128)(2,1)S(1)}, u32[]{:S(2)}, u32[]{:S(2)}) collective-permute-start(bf16[128,2048]{1,0:T(8,128)(2,1)} %get-tuple-element.25), channel_id=1, source_target_pairs={{64,76},{68,64},{72,68},{76,72},{65,77},{69,65},{73,69},{77,73},{6... | collective-permute-start | bytes 1572872 | tf_op jit(solution)/shard_map/ppermute | solution.py:26
  7.6 49.3 %collective-permute-start.4 = (bf16[512,2048]{1,0:T(8,128)(2,1)}, bf16[512,2048]{1,0:T(8,128)(2,1)}, u32[]{:S(2)}, u32[]{:S(2)}) collective-permute-start(bf16[512,2048]{1,0:T(8,128)(2,1)} %bitcast.9), channel_id=1, source_target_pairs={{0,48},{16,0},{32,16},{48,32},{64,112},{80,64},{96,80},{112,96},{1... | collective-permute-start | bytes 6291464 | tf_op jit(solution)/shard_map/ppermute | solution.py:26
  17.9 3.2 collective-permute-start.1
  19.4 47.6 %collective-permute-start.6 = (bf16[512,2048]{1,0:T(8,128)(2,1)}, bf16[512,2048]{1,0:T(8,128)(2,1)S(1)}, u32[]{:S(2)}, u32[]{:S(2)}) collective-permute-start(bf16[512,2048]{1,0:T(8,128)(2,1)} %bitcast.9), channel_id=1, source_target_pairs={{0,16},{16,32},{32,48},{48,0},{64,80},{80,96},{96,112},{112,64},{1... | collective-permute-start | bytes 6291464 | tf_op jit(solution)/shard_map/ppermute | solution.py:27
  19.4 2.4 collective-permute-start.3
  20.3 1.6 collective-permute-start.16
  58.2 33.9 %collective-permute-start.5 = (bf16[256,2048]{1,0:T(8,128)(2,1)S(1)}, bf16[256,2048]{1,0:T(8,128)(2,1)S(1)}, u32[]{:S(2)}, u32[]{:S(2)}) collective-permute-start(bf16[256,2048]{1,0:T(8,128)(2,1)S(1)} %slice.212), channel_id=1, source_target_pairs={{0,48},{16,0},{32,16},{48,32},{64,112},{80,64},{96,80},{112,96},{1... | collective-permute-start | bytes 3145736 | tf_op jit(solution)/shard_map/ppermute | solution.py:28
  67.1 24.2 %collective-permute-start.7 = (bf16[256,2048]{1,0:T(8,128)(2,1)S(1)}, bf16[256,2048]{1,0:T(8,128)(2,1)S(1)}, u32[]{:S(2)}, u32[]{:S(2)}) collective-permute-start(bf16[256,2048]{1,0:T(8,128)(2,1)S(1)} %slice.213), channel_id=1, source_target_pairs={{0,16},{16,32},{32,48},{48,0},{64,80},{80,96},{96,112},{112,64},{1... | collective-permute-start | bytes 3145736 | tf_op jit(solution)/shard_map/ppermute | solution.py:29
  94.4 20.7 %collective-permute-start.8 = (bf16[2,512,512]{1,2,0:T(8,128)(2,1)}, bf16[2,512,512]{1,2,0:T(8,128)(2,1)}, u32[]{:S(2)}, u32[]{:S(2)}) collective-permute-start(bf16[2,512,512]{1,2,0:T(8,128)(2,1)} %dynamic-slice_bitcast_fusion), channel_id=1, source_target_pairs={{64,65},{65,64},{66,67},{67,66},{68,69},{69,68},{70,71},{71,70},{7... | collective-permute-start | bytes 3145736 | tf_op jit(solution)/shard_map/ppermute | solution.py:35
  101.3 20.7 %collective-permute-start.17 = (bf16[2,512,512]{2,1,0:T(8,128)(2,1)}, bf16[2,512,512]{2,1,0:T(8,128)(2,1)}, u32[]{:S(2)}, u32[]{:S(2)}) collective-permute-start(bf16[2,512,512]{2,1,0:T(8,128)(2,1)} %bitcast.248), channel_id=1, source_target_pairs={{64,65},{65,64},{66,67},{67,66},{68,69},{69,68},{70,71},{71,70},{7... | collective-permute-start | bytes 3145736 | tf_op jit(solution)/shard_map/ppermute | solution.py:35
  117.4 10.8 %collective-permute-start.9 = (bf16[512,512]{0,1:T(8,128)(2,1)}, bf16[512,512]{0,1:T(8,128)(2,1)}, u32[]{:S(2)}, u32[]{:S(2)}) collective-permute-start(bf16[512,512]{0,1:T(8,128)(2,1)} %fusion.48), channel_id=1, source_target_pairs={{64,66},{66,64},{65,67},{67,65},{68,70},{70,68},{69,71},{71,69},{7... | collective-permute-start | bytes 1572872 | tf_op jit(solution)/shard_map/ppermute | solution.py:35
  124.1 7.9 %collective-permute-start.18 = (bf16[512,512]{1,0:T(8,128)(2,1)}, bf16[512,512]{1,0:T(8,128)(2,1)}, u32[]{:S(2)}, u32[]{:S(2)}) collective-permute-start(bf16[512,512]{1,0:T(8,128)(2,1)} %fusion.45), channel_id=1, source_target_pairs={{64,66},{66,64},{65,67},{67,65},{68,70},{70,68},{69,71},{71,69},{7... | collective-permute-start | bytes 1572872 | tf_op jit(solution)/shard_map/ppermute | solution.py:35
  129.9 6.9 %collective-permute-start.12 = (bf16[128,512]{0,1:T(8,128)(2,1)S(1)}, bf16[128,512]{0,1:T(8,128)(2,1)S(1)}, u32[]{:S(2)}, u32[]{:S(2)}) collective-permute-start(bf16[128,512]{0,1:T(8,128)(2,1)S(1)} %get-tuple-element.55), channel_id=1, source_target_pairs={{64,68},{68,72},{72,76},{76,64},{65,69},{69,73},{73,77},{77,65},{6... | collective-permute-start | bytes 393224 | tf_op jit(solution)/shard_map/ppermute | solution.py:149
  130.6 7.7 %collective-permute-start.11 = (bf16[128,512]{0,1:T(8,128)(2,1)S(1)}, bf16[128,512]{0,1:T(8,128)(2,1)S(1)}, u32[]{:S(2)}, u32[]{:S(2)}) collective-permute-start(bf16[128,512]{0,1:T(8,128)(2,1)S(1)} %get-tuple-element.56), channel_id=1, source_target_pairs={{64,72},{68,76},{72,64},{76,68},{65,73},{69,77},{73,65},{77,69},{6... | collective-permute-start | bytes 393224 | tf_op jit(solution)/shard_map/ppermute | solution.py:150
  131.3 7.1 %collective-permute-start.10 = (bf16[128,512]{0,1:T(8,128)(2,1)S(1)}, bf16[128,512]{0,1:T(8,128)(2,1)S(1)}, u32[]{:S(2)}, u32[]{:S(2)}) collective-permute-start(bf16[128,512]{0,1:T(8,128)(2,1)S(1)} %get-tuple-element.57), channel_id=1, source_target_pairs={{64,76},{68,64},{72,68},{76,72},{65,77},{69,65},{73,69},{77,73},{6... | collective-permute-start | bytes 393224 | tf_op jit(solution)/shard_map/ppermute | solution.py:151
  134.2 9.9 %collective-permute-start.21 = (bf16[128,512]{1,0:T(8,128)(2,1)}, bf16[128,512]{1,0:T(8,128)(2,1)}, u32[]{:S(2)}, u32[]{:S(2)}) collective-permute-start(bf16[128,512]{1,0:T(8,128)(2,1)} %get-tuple-element.63), channel_id=1, source_target_pairs={{64,68},{68,72},{72,76},{76,64},{65,69},{69,73},{73,77},{77,65},{6... | collective-permute-start | bytes 393224 | tf_op jit(solution)/shard_map/ppermute | solution.py:149
  135.5 8.6 %collective-permute-start.20 = (bf16[128,512]{1,0:T(8,128)(2,1)}, bf16[128,512]{1,0:T(8,128)(2,1)}, u32[]{:S(2)}, u32[]{:S(2)}) collective-permute-start(bf16[128,512]{1,0:T(8,128)(2,1)} %get-tuple-element.64), channel_id=1, source_target_pairs={{64,72},{68,76},{72,64},{76,68},{65,73},{69,77},{73,65},{77,69},{6... | collective-permute-start | bytes 393224 | tf_op jit(solution)/shard_map/ppermute | solution.py:150
  136.8 7.3 %collective-permute-start.19 = (bf16[128,512]{1,0:T(8,128)(2,1)}, bf16[128,512]{1,0:T(8,128)(2,1)}, u32[]{:S(2)}, u32[]{:S(2)}) collective-permute-start(bf16[128,512]{1,0:T(8,128)(2,1)} %get-tuple-element.65), channel_id=1, source_target_pairs={{64,76},{68,64},{72,68},{76,72},{65,77},{69,65},{73,69},{77,73},{6... | collective-permute-start | bytes 393224 | tf_op jit(solution)/shard_map/ppermute | solution.py:151
  166.7 47.6 %collective-permute-start.32 = (bf16[128,2048]{1,0:T(8,128)(2,1)S(1)}, bf16[128,2048]{1,0:T(8,128)(2,1)S(1)}, u32[]{:S(2)}, u32[]{:S(2)}) collective-permute-start(bf16[128,2048]{1,0:T(8,128)(2,1)S(1)} %fusion.30), channel_id=1, source_target_pairs={{64,0},{65,1},{66,2},{67,3},{68,4},{69,5},{70,6},{71,7},{72,8},{73... | collective-permute-start | bytes 1572872 | tf_op jit(solution)/shard_map/ppermute | solution.py:173
  168.0 57.5 %collective-permute-start.22 = (bf16[128,2048]{1,0:T(8,128)(2,1)S(1)}, bf16[128,2048]{1,0:T(8,128)(2,1)S(1)}, u32[]{:S(2)}, u32[]{:S(2)}) collective-permute-start(bf16[128,2048]{1,0:T(8,128)(2,1)S(1)} %copy-done.20), channel_id=1, source_target_pairs={{64,0},{65,1},{66,2},{67,3},{68,4},{69,5},{70,6},{71,7},{72,8},{73... | collective-permute-start | bytes 1572872 | tf_op jit(solution)/shard_map/ppermute | solution.py:173
  226.3 14.7 %collective-permute-start.25 = (bf16[128,2048]{1,0:T(8,128)(2,1)S(1)}, bf16[128,2048]{1,0:T(8,128)(2,1)S(1)}, u32[]{:S(2)}, u32[]{:S(2)}) collective-permute-start(bf16[128,2048]{1,0:T(8,128)(2,1)S(1)} %get-tuple-element.19), channel_id=1, source_target_pairs={{0,4},{4,8},{8,12},{12,0},{1,5},{5,9},{9,13},{13,1},{2,6},{6,10},{... | collective-permute-start | bytes 1572872 | tf_op jit(solution)/shard_map/ppermute | solution.py:27
  228.3 14.6 %collective-permute-start.23 = (bf16[128,2048]{1,0:T(8,128)(2,1)S(1)}, bf16[128,2048]{1,0:T(8,128)(2,1)S(1)}, u32[]{:S(2)}, u32[]{:S(2)}) collective-permute-start(bf16[128,2048]{1,0:T(8,128)(2,1)S(1)} %get-tuple-element.19), channel_id=1, source_target_pairs={{0,12},{4,0},{8,4},{12,8},{1,13},{5,1},{9,5},{13,9},{2,14},{6,2},{... | collective-permute-start | bytes 1572872 | tf_op jit(solution)/shard_map/ppermute | solution.py:26
  232.8 19.4 %collective-permute-start.35 = (bf16[128,2048]{1,0:T(8,128)(2,1)S(1)}, bf16[128,2048]{1,0:T(8,128)(2,1)S(1)}, u32[]{:S(2)}, u32[]{:S(2)}) collective-permute-start(bf16[128,2048]{1,0:T(8,128)(2,1)S(1)} %get-tuple-element.31), channel_id=1, source_target_pairs={{0,4},{4,8},{8,12},{12,0},{1,5},{5,9},{9,13},{13,1},{2,6},{6,10},{... | collective-permute-start | bytes 1572872 | tf_op jit(solution)/shard_map/ppermute | solution.py:27
  234.7 19.4 %collective-permute-start.33 = (bf16[128,2048]{1,0:T(8,128)(2,1)S(1)}, bf16[128,2048]{1,0:T(8,128)(2,1)S(1)}, u32[]{:S(2)}, u32[]{:S(2)}) collective-permute-start(bf16[128,2048]{1,0:T(8,128)(2,1)S(1)} %get-tuple-element.31), channel_id=1, source_target_pairs={{0,12},{4,0},{8,4},{12,8},{1,13},{5,1},{9,5},{13,9},{2,14},{6,2},{... | collective-permute-start | bytes 1572872 | tf_op jit(solution)/shard_map/ppermute | solution.py:26
  241.0 17.9 %collective-permute-start.26 = (bf16[64,2048]{1,0:T(8,128)(2,1)S(1)}, bf16[64,2048]{1,0:T(8,128)(2,1)S(1)}, u32[]{:S(2)}, u32[]{:S(2)}) collective-permute-start(bf16[64,2048]{1,0:T(8,128)(2,1)S(1)} %slice.231), channel_id=1, source_target_pairs={{0,4},{4,8},{8,12},{12,0},{1,5},{5,9},{9,13},{13,1},{2,6},{6,10},{... | collective-permute-start | bytes 786440 | tf_op jit(solution)/shard_map/ppermute | solution.py:29
  243.0 15.9 %collective-permute-start.24 = (bf16[64,2048]{1,0:T(8,128)(2,1)S(1)}, bf16[64,2048]{1,0:T(8,128)(2,1)S(1)}, u32[]{:S(2)}, u32[]{:S(2)}) collective-permute-start(bf16[64,2048]{1,0:T(8,128)(2,1)S(1)} %slice.230), channel_id=1, source_target_pairs={{0,12},{4,0},{8,4},{12,8},{1,13},{5,1},{9,5},{13,9},{2,14},{6,2},{... | collective-permute-start | bytes 786440 | tf_op jit(solution)/shard_map/ppermute | solution.py:28
  252.3 12.0 %collective-permute-start.36 = (bf16[64,2048]{1,0:T(8,128)(2,1)S(1)}, bf16[64,2048]{1,0:T(8,128)(2,1)S(1)}, u32[]{:S(2)}, u32[]{:S(2)}) collective-permute-start(bf16[64,2048]{1,0:T(8,128)(2,1)S(1)} %slice.237), channel_id=1, source_target_pairs={{0,4},{4,8},{8,12},{12,0},{1,5},{5,9},{9,13},{13,1},{2,6},{6,10},{... | collective-permute-start | bytes 786440 | tf_op jit(solution)/shard_map/ppermute | solution.py:29
  254.2 10.0 %collective-permute-start.34 = (bf16[64,2048]{1,0:T(8,128)(2,1)S(1)}, bf16[64,2048]{1,0:T(8,128)(2,1)S(1)}, u32[]{:S(2)}, u32[]{:S(2)}) collective-permute-start(bf16[64,2048]{1,0:T(8,128)(2,1)S(1)} %slice.236), channel_id=1, source_target_pairs={{0,12},{4,0},{8,4},{12,8},{1,13},{5,1},{9,5},{13,9},{2,14},{6,2},{... | collective-permute-start | bytes 786440 | tf_op jit(solution)/shard_map/ppermute | solution.py:28
  280.8 30.7 %collective-permute-start.27 = (bf16[2,512,512]{2,1,0:T(8,128)(2,1)}, bf16[2,512,512]{2,1,0:T(8,128)(2,1)}, u32[]{:S(2)}, u32[]{:S(2)}) collective-permute-start(bf16[2,512,512]{2,1,0:T(8,128)(2,1)} %bitcast.249), channel_id=1, source_target_pairs={{0,1},{1,0},{2,3},{3,2},{4,5},{5,4},{6,7},{7,6},{8,9},{9,8},{10,11... | collective-permute-start | bytes 3145736 | tf_op jit(solution)/shard_map/ppermute | solution.py:35
  301.0 14.6 %collective-permute-start.37 = (bf16[2,512,512]{2,1,0:T(8,128)(2,1)}, bf16[2,512,512]{2,1,0:T(8,128)(2,1)}, u32[]{:S(2)}, u32[]{:S(2)}) collective-permute-start(bf16[2,512,512]{2,1,0:T(8,128)(2,1)} %bitcast.250), channel_id=1, source_target_pairs={{0,1},{1,0},{2,3},{3,2},{4,5},{5,4},{6,7},{7,6},{8,9},{9,8},{10,11... | collective-permute-start | bytes 3145736 | tf_op jit(solution)/shard_map/ppermute | solution.py:35
  313.6 35.0 %collective-permute-start.28 = (bf16[512,512]{1,0:T(8,128)(2,1)}, bf16[512,512]{1,0:T(8,128)(2,1)}, u32[]{:S(2)}, u32[]{:S(2)}) collective-permute-start(bf16[512,512]{1,0:T(8,128)(2,1)} %fusion.42), channel_id=1, source_target_pairs={{0,2},{2,0},{1,3},{3,1},{4,6},{6,4},{5,7},{7,5},{8,10},{10,8},{9,1... | collective-permute-start | bytes 1572872 | tf_op jit(solution)/shard_map/ppermute | solution.py:35
  317.7 30.9 %collective-permute-start.38 = (bf16[512,512]{1,0:T(8,128)(2,1)}, bf16[512,512]{1,0:T(8,128)(2,1)}, u32[]{:S(2)}, u32[]{:S(2)}) collective-permute-start(bf16[512,512]{1,0:T(8,128)(2,1)} %fusion.39), channel_id=1, source_target_pairs={{0,2},{2,0},{1,3},{3,1},{4,6},{6,4},{5,7},{7,5},{8,10},{10,8},{9,1... | collective-permute-start | bytes 1572872 | tf_op jit(solution)/shard_map/ppermute | solution.py:35
  351.8 12.3 %collective-permute-start.31 = (bf16[128,512]{1,0:T(8,128)(2,1)S(1)}, bf16[128,512]{1,0:T(8,128)(2,1)S(1)}, u32[]{:S(2)}, u32[]{:S(2)}) collective-permute-start(bf16[128,512]{1,0:T(8,128)(2,1)S(1)} %get-tuple-element.47), channel_id=1, source_target_pairs={{0,4},{4,8},{8,12},{12,0},{1,5},{5,9},{9,13},{13,1},{2,6},{6,10},{... | collective-permute-start | bytes 393224 | tf_op jit(solution)/shard_map/ppermute | solution.py:149
  353.8 10.5 %collective-permute-start.30 = (bf16[128,512]{1,0:T(8,128)(2,1)S(1)}, bf16[128,512]{1,0:T(8,128)(2,1)S(1)}, u32[]{:S(2)}, u32[]{:S(2)}) collective-permute-start(bf16[128,512]{1,0:T(8,128)(2,1)S(1)} %get-tuple-element.48), channel_id=1, source_target_pairs={{0,8},{4,12},{8,0},{12,4},{1,9},{5,13},{9,1},{13,5},{2,10},{6,14},... | collective-permute-start | bytes 393224 | tf_op jit(solution)/shard_map/ppermute | solution.py:150
  360.3 5.7 %collective-permute-start.29 = (bf16[128,512]{1,0:T(8,128)(2,1)S(1)}, bf16[128,512]{1,0:T(8,128)(2,1)S(1)}, u32[]{:S(2)}, u32[]{:S(2)}) collective-permute-start(bf16[128,512]{1,0:T(8,128)(2,1)S(1)} %get-tuple-element.49), channel_id=1, source_target_pairs={{0,12},{4,0},{8,4},{12,8},{1,13},{5,1},{9,5},{13,9},{2,14},{6,2},{... | collective-permute-start | bytes 393224 | tf_op jit(solution)/shard_map/ppermute | solution.py:151
  386.1 3.2 collective-permute-start.42
  389.3 4.7 %collective-permute-start.43 = (f32[8,2048]{1,0:T(8,128)S(1)}, f32[8,2048]{1,0:T(8,128)S(1)}, u32[]{:S(2)}, u32[]{:S(2)}) collective-permute-start(f32[8,2048]{1,0:T(8,128)S(1)} %fusion.75), channel_id=1, source_target_pairs={{0,8},{4,12},{8,0},{12,4},{1,9},{5,13},{9,1},{13,5},{2,10},{6,14},... | collective-permute-start | bytes 196616 | tf_op jit(solution)/shard_map/ppermute | solution.py:40
  394.0 3.5 collective-permute-start.44
  397.5 9.4 %collective-permute-start.45 = (f32[8,2048]{1,0:T(8,128)S(1)}, f32[8,2048]{1,0:T(8,128)S(1)}, u32[]{:S(2)}, u32[]{:S(2)}) collective-permute-start(f32[8,2048]{1,0:T(8,128)S(1)} %add.294), channel_id=1, source_target_pairs={{0,32},{16,48},{32,0},{48,16},{1,33},{17,49},{33,1},{49,17},{2,34}... | collective-permute-start | bytes 196616 | tf_op jit(solution)/shard_map/ppermute | solution.py:40
  398.3 14.6 %collective-permute-start.41 = (bf16[128,512]{1,0:T(8,128)(2,1)}, bf16[128,512]{1,0:T(8,128)(2,1)S(1)}, u32[]{:S(2)}, u32[]{:S(2)}) collective-permute-start(bf16[128,512]{1,0:T(8,128)(2,1)} %get-tuple-element.39), channel_id=1, source_target_pairs={{0,4},{4,8},{8,12},{12,0},{1,5},{5,9},{9,13},{13,1},{2,6},{6,10},{... | collective-permute-start | bytes 393224 | tf_op jit(solution)/shard_map/ppermute | solution.py:149
  400.3 12.6 %collective-permute-start.40 = (bf16[128,512]{1,0:T(8,128)(2,1)S(1)}, bf16[128,512]{1,0:T(8,128)(2,1)S(1)}, u32[]{:S(2)}, u32[]{:S(2)}) collective-permute-start(bf16[128,512]{1,0:T(8,128)(2,1)S(1)} %get-tuple-element.40), channel_id=1, source_target_pairs={{0,8},{4,12},{8,0},{12,4},{1,9},{5,13},{9,1},{13,5},{2,10},{6,14},... | collective-permute-start | bytes 393224 | tf_op jit(solution)/shard_map/ppermute | solution.py:150
  404.3 8.6 %collective-permute-start.39 = (bf16[128,512]{1,0:T(8,128)(2,1)S(1)}, bf16[128,512]{1,0:T(8,128)(2,1)}, u32[]{:S(2)}, u32[]{:S(2)}) collective-permute-start(bf16[128,512]{1,0:T(8,128)(2,1)S(1)} %get-tuple-element.41), channel_id=1, source_target_pairs={{0,12},{4,0},{8,4},{12,8},{1,13},{5,1},{9,5},{13,9},{2,14},{6,2},{... | collective-permute-start | bytes 393224 | tf_op jit(solution)/shard_map/ppermute | solution.py:151
  407.4 7.4 %collective-permute-start.46 = (f32[256,256]{1,0:T(8,128)S(1)}, f32[256,256]{1,0:T(8,128)S(1)}, u32[]{:S(2)}, u32[]{:S(2)}) collective-permute-start(f32[256,256]{1,0:T(8,128)S(1)} %convolution_multiply_fusion), channel_id=1, source_target_pairs={{0,1},{1,0},{2,3},{3,2},{4,5},{5,4},{6,7},{7,6},{8,9},{9,8},{10,11... | collective-permute-start | bytes 786440 | tf_op jit(solution)/shard_map/ppermute | solution.py:40
  414.8 11.1 %collective-permute-start.47 = (f32[256,256]{1,0:T(8,128)S(1)}, f32[256,256]{1,0:T(8,128)}, u32[]{:S(2)}, u32[]{:S(2)}) collective-permute-start(f32[256,256]{1,0:T(8,128)S(1)} %add.296), channel_id=1, source_target_pairs={{0,2},{2,0},{1,3},{3,1},{4,6},{6,4},{5,7},{7,5},{8,10},{10,8},{9,1... | collective-permute-start | bytes 786440 | tf_op jit(solution)/shard_map/ppermute | solution.py:40
  427.0 8.8 %collective-permute-start.48 = (f32[256,256]{1,0:T(8,128)S(1)}, f32[256,256]{1,0:T(8,128)S(1)}, u32[]{:S(2)}, u32[]{:S(2)}) collective-permute-start(f32[256,256]{1,0:T(8,128)S(1)} %add.297), channel_id=1, source_target_pairs={{0,64},{64,0},{1,65},{65,1},{2,66},{66,2},{3,67},{67,3},{4,68},{68... | collective-permute-start | bytes 786440 | tf_op jit(solution)/shard_map/ppermute | solution.py:40
  (65 other events, 589.4 us)

commit v2 on v1

v2 whole, which is shorter than its diff:
```python
import functools
import math

import jax
import jax.numpy as jnp
from jax import lax
from jax.experimental import pallas as pl
from jax.experimental.pallas import tpu as pltpu
from jax.sharding import Mesh, PartitionSpec as P

MODEL_WIDTH = 8192
RANK = 4
SUB = 256
TOKENS = 4096
RING = 4
LANES = 128

epsilon = 1e-06
HIGH = lax.Precision.HIGHEST
F32 = jnp.float32
BF16 = jnp.bfloat16
ANY = pl.BlockSpec(memory_space=pl.ANY)
SMEM = pl.BlockSpec(memory_space=pltpu.SMEM)
VMEM = pl.BlockSpec(memory_space=pltpu.VMEM)
HBM = pl.BlockSpec(memory_space=pltpu.HBM)
BIG = 48 * 1024 * 1024
LIGHT = pl.CostEstimate(flops=0, bytes_accessed=2 ** 20, transcendentals=0)


def ring_route(distance, sections=(0, 1)):
    return [(s * RING + i, s * RING + (i + distance) % RING) for s in sections for i in range(RING)]


def ring_move(block, axis, distance, sections=(0, 1)):
    return lax.ppermute(block, ("section", axis), ring_route(distance, sections))


def swap(block, axis, sections=(0, 1)):
    pairs = [(s * 2 + i, s * 2 + 1 - i) for s in sections for i in range(2)]
    return lax.ppermute(block, ("section", axis), pairs)


def after(value, earlier):
    return lax.optimization_barrier((value, earlier))[0]


def in_order(kernel, operands, extra):
    return lambda *refs: kernel(*refs[:operands], *refs[operands + extra:])


def compose(index_layer, weight_layer, rows):
    columns = lax.broadcasted_iota(jnp.int32, (1, 1, 1, 1, rows), 4)
    onehot = (index_layer[..., None] == columns).astype(F32)
    return jnp.sum(onehot * weight_layer[..., None], axis=3)


def two_halves(value):
    high = value.astype(BF16)
    return jnp.concatenate([high, (value - high.astype(F32)).astype(BF16)], axis=0)


def activation_gradient(incoming_ref, preact_ref):
    value = preact_ref[...].astype(F32)
    sig = jax.nn.sigmoid(value)
    slope = sig * (1.0 + value * (1.0 - sig))
    return (incoming_ref[...].astype(F32) * slope).astype(BF16)


def dz_kernel(incoming_ref, preact_ref, b_ref, dz_ref, mixed_ref):
    dz = activation_gradient(incoming_ref, preact_ref)
    dz_ref[...] = dz
    both = lax.dot_general(b_ref[...], dz, (((1,), (1,)), ((), ())), preferred_element_type=F32)
    mixed_ref[...] = both[:RANK] + both[RANK:]


def first_kernel(where_ref, incoming_ref, preact_ref, weight_ref, out_ref):
    @pl.when(where_ref[3] == 1)
    def _():
        out_ref[:incoming_ref.shape[0]] = activation_gradient(incoming_ref, preact_ref)

    @pl.when(where_ref[3] == 0)
    def _():
        out_ref[...] = weight_ref[...]


def make_first(where, incoming, preact, weight):
    return pl.pallas_call(
        first_kernel,
        in_specs=[SMEM, VMEM, VMEM, VMEM],
        out_specs=VMEM,
        out_shape=jax.ShapeDtypeStruct(weight.shape, BF16),
        compiler_params=pltpu.CompilerParams(vmem_limit_bytes=BIG),
        cost_estimate=LIGHT,
    )(where, incoming, preact, weight)


def join_kernel(wanted, parts, where_ref, *refs):
    sources, out_ref, sem = refs[:len(parts)], refs[-2], refs[-1]

    def run():
        start = 0
        copies = []
        for i, (first, rows) in enumerate(parts):
            source = sources[i].at[pl.ds(first, rows)]
            copies.append(pltpu.make_async_copy(source, out_ref.at[pl.ds(start, rows)], sem.at[i]))
            start += rows
        for copy in copies:
            copy.start()
        for copy in copies:
            copy.wait()

    if wanted is None:
        run()
    else:
        pl.when(where_ref[3] == wanted)(run)


def join(where, wanted, arrays, parts, *earlier):
    rows = sum(count for _, count in parts)
    return pl.pallas_call(
        in_order(functools.partial(join_kernel, wanted, parts), 1 + len(arrays), len(earlier)),
        in_specs=[SMEM] + [ANY] * (len(arrays) + len(earlier)),
        out_specs=VMEM,
        out_shape=jax.ShapeDtypeStruct((rows, arrays[0].shape[1]), BF16),
        scratch_shapes=[pltpu.SemaphoreType.DMA((len(arrays),))],
        compiler_params=pltpu.CompilerParams(vmem_limit_bytes=BIG),
        cost_estimate=LIGHT,
    )(where, *arrays, *earlier)


def gather_ring(where, block, axis, sections=(0, 1), earlier=()):
    half = block.shape[0] // 2
    wanted = None if len(sections) == 2 else sections[0]
    after = ring_move(block, axis, -1, sections)
    before = ring_move(block, axis, 1, sections)
    far_low = ring_move(join(where, wanted, (after,), ((0, half),), *earlier), axis, -1, sections)
    far_high = ring_move(join(where, wanted, (before,), ((half, half),), *earlier), axis, 1, sections)
    return block, after, far_low, far_high, before


def make_dz(incoming, preact, b_both, c, *earlier):
    rows, width = incoming.shape
    return pl.pallas_call(
        in_order(dz_kernel, 3, len(earlier)),
        grid=(1,),
        in_specs=[
            pl.BlockSpec((rows, width), lambda i: (0, 0)),
            pl.BlockSpec((rows, width), lambda i: (c, 0)),
            pl.BlockSpec((2 * RANK, width), lambda i: (0, 0)),
        ]
        + [ANY] * len(earlier),
        out_specs=[
            pl.BlockSpec((rows, width), lambda i: (0, 0)),
            pl.BlockSpec((RANK, rows), lambda i: (0, 0)),
        ],
        out_shape=[
            jax.ShapeDtypeStruct((rows, width), BF16),
            jax.ShapeDtypeStruct((RANK, rows), F32),
        ],
        compiler_params=pltpu.CompilerParams(vmem_limit_bytes=BIG),
        cost_estimate=LIGHT,
    )(incoming, preact, b_both, *earlier)


def top_product_kernel(rows, where_ref, *refs):
    dz_refs, w_refs = refs[:4], refs[4:9]
    keep_ref, send_ref, dz_all, w_all, dz_sem, w_sem = refs[9:]

    @pl.when(where_ref[3] == 1)
    def _():
        copies = [
            pltpu.make_async_copy(ref.at[pl.ds(0, rows)], dz_all.at[pl.ds(i * rows, rows)], dz_sem.at[i])
            for i, ref in enumerate(dz_refs)
        ]
        for copy in copies:
            copy.start()
        own, after, far_low, far_high, before = w_refs
        half = far_low.shape[0]
        pltpu.make_async_copy(own, w_all.at[0], w_sem.at[0]).start()
        pltpu.make_async_copy(after, w_all.at[1], w_sem.at[1]).start()
        pltpu.make_async_copy(far_low, w_all.at[2, pl.ds(0, half)], w_sem.at[2]).start()
        pltpu.make_async_copy(far_high, w_all.at[2, pl.ds(half, half)], w_sem.at[2]).start()
        pltpu.make_async_copy(before, w_all.at[3], w_sem.at[3]).start()
        for copy in copies:
            copy.wait()
        z, place = where_ref[0], where_ref[1]

        @pl.loop(0, RING)
        def _(i):
            pltpu.make_async_copy(own, w_all.at[i], w_sem.at[i]).wait()
            value = lax.dot_general(
                dz_all[...], w_all[i], (((1,), (1,)), ((), ())), preferred_element_type=F32
            ).astype(BF16)
            target = lax.rem(z + i, RING)
            own_core = lax.rem(target, 2) == lax.rem(place, 2)
            far = jnp.where(target // 2 == place // 2, 0, 1)

            @pl.when(own_core)
            def _():
                keep_ref[far] = value

            @pl.when(jnp.logical_not(own_core))
            def _():
                send_ref[far] = value


def top_product(where, rows, dz_pieces, w_pieces, *earlier):
    wide, width = w_pieces[0].shape
    return pl.pallas_call(
        in_order(functools.partial(top_product_kernel, rows), 10, len(earlier)),
        in_specs=[SMEM] + [HBM] * 9 + [ANY] * len(earlier),
        out_specs=[VMEM, VMEM],
        out_shape=[jax.ShapeDtypeStruct((2, RING * rows, wide), BF16)] * 2,
        scratch_shapes=[
            pltpu.VMEM((RING * rows, width), BF16),
            pltpu.VMEM((RING, wide, width), BF16),
            pltpu.SemaphoreType.DMA((4,)),
            pltpu.SemaphoreType.DMA((RING,)),
        ],
        compiler_params=pltpu.CompilerParams(vmem_limit_bytes=BIG),
        cost_estimate=pl.CostEstimate(
            flops=2 * RING * RING * rows * wide * width, bytes_accessed=2 ** 24, transcendentals=0
        ),
    )(where, *dz_pieces, *w_pieces, *earlier)


def low_plan(shard, wide):
    copies, blocks = [], []

    def take(array, row, rows, *names):
        at = sum(rows for *_, rows in copies)
        copies.append((array, row, at, rows))
        blocks.extend(names)

    for base, step in ((0, lambda d, h: (d, 0, h)), (4, lambda d, h: (0, d, h))):
        if base == 0:
            take(0, 0, shard, step(0, 0), step(0, 1))
        take(base + 1, 0, shard, step(1, 0), step(1, 1))
        take(base + 2, 0, wide, step(2, 0))
        take(base + 3, 0, wide, step(2, 1))
        take(base + 4, 0, shard, step(3, 0), step(3, 1))
    corner, y_pair, z_pair = 9, {1: 10, 3: 11}, {1: 12, 3: 13}
    take(corner, 0, shard, (2, 2, 0), (2, 2, 1))
    for d in (1, 3):
        take(y_pair[d], 0, shard, (2, d, 0), (2, d, 1))
        take(z_pair[d], 0, shard, (d, 2, 0), (d, 2, 1))
    slim, rest = wide // 2, shard - wide // 2
    for i, d in enumerate((1, 3)):
        for j, e in enumerate((1, 3)):
            take(y_pair[e], shard + i * slim, slim)
            take(z_pair[d], shard + j * rest, rest, (d, e, 0), (d, e, 1))
    return copies, blocks


def low_product_kernel(plan, where_ref, table_ref, dz_ref, *refs):
    count = len(refs) - 4
    w_refs = refs[:count]
    keep_ref, send_ref, w_all, sem = refs[count:]
    steps, deep = w_all.shape[0], w_all.shape[1]
    wide = deep // 2

    @pl.when(where_ref[3] == 0)
    def _():
        for array, row, at, rows in plan:
            while rows:
                part = min(rows, deep - at % deep)
                pltpu.make_async_copy(
                    w_refs[array].at[pl.ds(row, part)],
                    w_all.at[at // deep, pl.ds(at % deep, part)],
                    sem.at[at // deep],
                ).start()
                row, at, rows = row + part, at + part, rows - part

        @pl.loop(0, steps)
        def _(step):
            pltpu.make_async_copy(w_refs[0], w_all.at[step], sem.at[step]).wait()
            value = lax.dot_general(
                dz_ref[...], w_all[step], (((1,), (1,)), ((), ())), preferred_element_type=F32
            ).astype(BF16)
            for k in range(2):
                entry = table_ref[2 * step + k]
                columns = pl.ds(pl.multiple_of(lax.rem(entry, 2 * RING) * wide, wide), wide)
                far = lax.rem(entry // (2 * RING), 2)
                block = value[:, k * wide:(k + 1) * wide]

                @pl.when(entry < 4 * RING)
                def _():
                    keep_ref[far, :, columns] = block

                @pl.when(entry >= 4 * RING)
                def _():
                    send_ref[far, :, columns] = block


def low_product(where, z, y, place, dz, w_pieces, *earlier):
    rows, width = dz.shape
    shard = w_pieces[0].shape[0]
    wide = shard // 2
    copies, blocks = low_plan(shard, wide)
    steps = [jnp.array(column, jnp.int32) for column in zip(*blocks)]
    target = (z + steps[0]) % RING
    column = (y + steps[1]) % RING * 2 + steps[2]
    other_core = (target % 2 != place % 2).astype(jnp.int32)
    other_pair = (target // 2 != place // 2).astype(jnp.int32)
    table = (other_core * 2 + other_pair) * 2 * RING + column
    return pl.pallas_call(
        in_order(functools.partial(low_product_kernel, copies), 3 + len(w_pieces), len(earlier)),
        in_specs=[SMEM, SMEM, VMEM] + [HBM] * len(w_pieces) + [ANY] * len(earlier),
        out_specs=[VMEM, VMEM],
        out_shape=[jax.ShapeDtypeStruct((2, rows, 2 * RING * wide), BF16)] * 2,
        scratch_shapes=[
            pltpu.VMEM((RING * RING, shard, width), BF16),
            pltpu.SemaphoreType.DMA((RING * RING,)),
        ],
        compiler_params=pltpu.CompilerParams(vmem_limit_bytes=BIG),
        cost_estimate=pl.CostEstimate(
            flops=16 * RING * rows * wide * width, bytes_accessed=2 ** 25, transcendentals=0
        ),
    )(where, table, dz, *w_pieces, *earlier)


def add_kernel(keep_ref, got_ref, out_ref):
    out_ref[...] = (keep_ref[0].astype(F32) + got_ref[0].astype(F32)).astype(BF16)


def add_theirs(keep, got):
    _, rows, wide = keep.shape
    spec = pl.BlockSpec((1, rows, wide), lambda i: (1, 0, 0))
    return pl.pallas_call(
        add_kernel,
        grid=(1,),
        in_specs=[spec, spec],
        out_specs=pl.BlockSpec((rows, wide), lambda i: (0, 0)),
        out_shape=jax.ShapeDtypeStruct((rows, wide), BF16),
        compiler_params=pltpu.CompilerParams(vmem_limit_bytes=BIG),
        cost_estimate=LIGHT,
    )(keep, got)


def total_kernel(keep_ref, got_ref, other_ref, *out_refs):
    rows = out_refs[0].shape[0]
    for i, ref in enumerate(out_refs):
        part = pl.ds(i * rows, rows)
        ref[...] = (
            keep_ref[0, part].astype(F32) + got_ref[0, part].astype(F32) + other_ref[part].astype(F32)
        ).astype(BF16)


def add_mine(keep, got, other):
    _, rows, wide = keep.shape
    spec = pl.BlockSpec((1, rows, wide), lambda i: (0, 0, 0))
    return pl.pallas_call(
        total_kernel,
        grid=(1,),
        in_specs=[spec, spec, pl.BlockSpec((rows, wide), lambda i: (0, 0))],
        out_specs=[pl.BlockSpec((rows // RING, wide), lambda i: (0, 0))] * RING,
        out_shape=[jax.ShapeDtypeStruct((rows // RING, wide), BF16)] * RING,
        compiler_params=pltpu.CompilerParams(vmem_limit_bytes=BIG),
        cost_estimate=LIGHT,
    )(keep, got, other)


def as_row(column):
    square = jnp.broadcast_to(column, (column.shape[0], LANES))
    return jnp.transpose(square)[:8]


def as_column(row):
    square = jnp.concatenate([row] * (LANES // 8), axis=0)
    return jnp.transpose(square)[:, :1]


def scaled_kernel(where_ref, own, after, far, before, mixed_ref, a_ref, gain_ref, hidden_ref, scale_ref, scaled_ref, inner_ref):
    wide = own.shape[1]
    mixed = mixed_ref[...]
    inner = jnp.zeros((own.shape[0], 1), F32)
    for r, piece in enumerate((own, after, far, before)):
        at = pl.ds(pl.multiple_of(lax.rem(where_ref[2] + r, RING) * wide, wide), wide)
        low_rank = lax.dot_general(
            mixed, a_ref[:, at], (((0,), (0,)), ((), ())), precision=HIGH, preferred_element_type=F32
        )
        scaled = gain_ref[:, at] * (piece[...].astype(F32) + low_rank)
        scaled_ref[:, at] = scaled
        inner = inner + jnp.sum(scaled * hidden_ref[:, at].astype(F32), axis=1, keepdims=True)
    inner_ref[...] = as_row(inner * scale_ref[...])


def make_scaled(where, pieces, mixed, a_local, gain, hidden, scale):
    rows, width = hidden.shape
    return pl.pallas_call(
        scaled_kernel,
        in_specs=[SMEM] + [VMEM] * 9,
        out_specs=[VMEM, VMEM],
        out_shape=[jax.ShapeDtypeStruct((rows, width), F32), jax.ShapeDtypeStruct((8, rows), F32)],
        compiler_params=pltpu.CompilerParams(vmem_limit_bytes=BIG),
        cost_estimate=LIGHT,
    )(where, *pieces, mixed, a_local, gain, hidden, scale)


def low_scaled_kernel(keep_ref, got_ref, other_ref, mixed_ref, a_ref, gain_ref, hidden_ref, scale_ref, scaled_ref, inner_ref):
    low_rank = lax.dot_general(
        mixed_ref[...], a_ref[...], (((0,), (0,)), ((), ())), precision=HIGH, preferred_element_type=F32
    )
    total = keep_ref[0].astype(F32) + got_ref[0].astype(F32) + other_ref[...].astype(F32)
    scaled = gain_ref[...] * (total + low_rank)
    scaled_ref[...] = scaled
    inner = jnp.sum(scaled * hidden_ref[...].astype(F32), axis=1, keepdims=True)
    inner_ref[...] = as_row(inner * scale_ref[...])


def low_scaled(keep, got, other, mixed, a_local, gain, hidden, scale):
    rows, width = hidden.shape
    whole = lambda shape: pl.BlockSpec(shape, lambda i: (0, 0))
    mine = pl.BlockSpec((1, rows, width), lambda i: (0, 0, 0))
    return pl.pallas_call(
        low_scaled_kernel,
        grid=(1,),
        in_specs=[
            mine, mine, whole((rows, width)), whole((RANK, rows)), whole((RANK, width)),
            whole((1, width)), whole((rows, width)), whole((rows, 1)),
        ],
        out_specs=[whole((rows, width)), whole((8, rows))],
        out_shape=[jax.ShapeDtypeStruct((rows, width), F32), jax.ShapeDtypeStruct((8, rows), F32)],
        compiler_params=pltpu.CompilerParams(vmem_limit_bytes=BIG),
        cost_estimate=LIGHT,
    )(keep, got, other, mixed, a_local, gain, hidden, scale)


def hidden_gradient(scaled_ref, inner_ref, hidden_ref, scale_ref, incoming_ref):
    scale = scale_ref[...]
    pull = as_column(inner_ref[...]) * scale / MODEL_WIDTH
    return (
        incoming_ref[...].astype(F32)
        + scale * (scaled_ref[...] - hidden_ref[...].astype(F32) * pull)
    ).astype(BF16)


def top_kernel(scaled_ref, inner_ref, hidden_ref, scale_ref, incoming_ref, out_ref):
    out_ref[...] = hidden_gradient(scaled_ref, inner_ref, hidden_ref, scale_ref, incoming_ref)


def low_kernel(where_ref, scaled_ref, inner_ref, hidden_ref, scale_ref, incoming_ref, top_ref, *rest):
    grad = hidden_gradient(scaled_ref, inner_ref, hidden_ref, scale_ref, incoming_ref)
    rest[-1][...] = jnp.where(where_ref[3] == 1, top_ref[...], grad)


def finish_specs(rows, width, c):
    whole = lambda shape: pl.BlockSpec(shape, lambda i: (0, 0))
    return [
        whole((rows, width)),
        whole((8, rows)),
        pl.BlockSpec((rows, width), lambda i: (c, 0)),
        pl.BlockSpec((rows, 1), lambda i: (c, 0)),
    ]


def finish_top(scaled, inner, hidden, scale, grad_top, c):
    rows, width = scaled.shape
    return pl.pallas_call(
        top_kernel,
        grid=(1,),
        in_specs=finish_specs(rows, width, c) + [pl.BlockSpec((rows, width), lambda i: (c, 0))],
        out_specs=pl.BlockSpec((rows, width), lambda i: (0, 0)),
        out_shape=jax.ShapeDtypeStruct((rows, width), BF16),
        compiler_params=pltpu.CompilerParams(vmem_limit_bytes=BIG),
        cost_estimate=LIGHT,
    )(scaled, inner, hidden, scale, grad_top)


def finish_low(where, scaled, inner, hidden, scale, incoming, top):
    rows, width = scaled.shape
    block = pl.BlockSpec((rows, width), lambda i: (0, 0))
    return pl.pallas_call(
        low_kernel,
        grid=(1,),
        in_specs=[SMEM] + finish_specs(rows, width, 0) + [block, block],
        out_specs=block,
        out_shape=jax.ShapeDtypeStruct((rows, width), BF16),
        compiler_params=pltpu.CompilerParams(vmem_limit_bytes=BIG),
        cost_estimate=LIGHT,
    )(where, scaled, inner, hidden, scale, incoming, top)


def grads_kernel(where_ref, hidden_ref, scale_ref, gain_ref, projected_ref, *refs):
    out_ref = refs[-1]
    top = where_ref[3] == 1
    count = (len(refs) - 2) // 3
    total_a, total_b = 0.0, 0.0
    for c in range(count):
        low_dz, top_mixed, low_mixed = [refs[1 + k * count + c] for k in range(3)]
        rows = pl.ds(c * low_dz.shape[0], low_dz.shape[0])
        dz = jnp.where(top, refs[0][rows], low_dz[...])
        mixed = jnp.where(top, top_mixed[...], low_mixed[...])
        x = (hidden_ref[rows].astype(F32) * scale_ref[rows] * gain_ref[...]).astype(BF16)
        projected = projected_ref[:, rows]

        def both(left, right):
            value = lax.dot_general(
                two_halves(left), right, (((1,), (0,)), ((), ())), preferred_element_type=F32
            )
            return value[:RANK] + value[RANK:]

        total_a = total_a + both(mixed, x)
        total_b = total_b + both(projected, dz)
    out_ref[...] = jnp.concatenate([total_a, total_b], axis=0)


def make_grads(where, hidden, scale, gain, projected, lists, *earlier):
    arrays = [array for arrays in lists for array in arrays]
    return pl.pallas_call(
        in_order(grads_kernel, 5 + len(arrays), len(earlier)),
        in_specs=[SMEM] + [VMEM] * (4 + len(arrays)) + [ANY] * len(earlier),
        out_specs=VMEM,
        out_shape=jax.ShapeDtypeStruct((2 * RANK, hidden.shape[1]), F32),
        compiler_params=pltpu.CompilerParams(vmem_limit_bytes=BIG),
        cost_estimate=LIGHT,
    )(where, hidden, scale, gain, projected, *arrays, *earlier)


def ring_total(value, moved):
    after, far, before = moved
    return (value[...] + far[...]) + (after[...] + before[...])


def ring_kernel(value, after, far, before, out_ref):
    out_ref[...] = ring_total(value, (after, far, before))


def bank_kernel(mixing_ref, value, after, far, before, out_ref):
    total = ring_total(value, (after, far, before))
    count = total.shape[1] // SUB
    pieces = jnp.concatenate([total[:, j * SUB:(j + 1) * SUB] for j in range(count)], axis=0)
    out_ref[...] = lax.dot_general(
        mixing_ref[...], pieces, (((0,), (0,)), ((), ())), precision=HIGH, preferred_element_type=F32
    )


def round_kernel(factor, left, right, out_ref):
    out_ref[...] = ((left[...].astype(F32) + right[...].astype(F32)) * factor).astype(out_ref.dtype)


def small_call(kernel, out, operands, *earlier):
    return pl.pallas_call(
        in_order(kernel, len(operands), len(earlier)),
        in_specs=[VMEM] * len(operands) + [ANY] * len(earlier),
        out_specs=VMEM,
        out_shape=out,
        compiler_params=pltpu.CompilerParams(vmem_limit_bytes=BIG),
        cost_estimate=LIGHT,
    )(*operands, *earlier)


def ring_moves(value, axis):
    return [ring_move(value, axis, d) for d in (-1, 2, 1)]


def shards(hidden_in, preact, norm_gain, weight, bank, mix_index, mix_weight, grad_top):
    section = lax.axis_index("section")
    z, y = lax.axis_index("z"), lax.axis_index("y")
    place = lax.axis_index("pair") * 2 + lax.axis_index("core")
    where = jnp.stack([z, place, y, section]).astype(jnp.int32)
    tensor = ("pair", "core")
    bank_rows = bank.shape[0]

    tokens, local_width = grad_top.shape
    seg_local = local_width // SUB
    seg_row = MODEL_WIDTH // SUB
    own_weight = weight[0]
    shard = own_weight.shape[0]
    half = shard // 2

    first = make_first(where, grad_top, preact[0], own_weight)
    hidden, preact = hidden_in[0], preact[0]

    def local_pieces(array):
        array = array.reshape(2, RANK, seg_row, 2)
        return lax.dynamic_slice_in_dim(array, place * seg_local, seg_local, 2)

    mixing = compose(local_pieces(mix_index[0]), local_pieces(mix_weight[0]), bank_rows)
    mixing = mixing.reshape(2, RANK * seg_local, bank_rows)
    factors = jnp.einsum("fnb,bs->fns", mixing, bank, precision=HIGH)
    a_local = factors[0].reshape(RANK, local_width)
    b_both = two_halves(factors[1].reshape(RANK, local_width))

    hidden_f = hidden.astype(F32)
    sums = lax.psum(
        jnp.concatenate(
            [
                jnp.sum(hidden_f * hidden_f, axis=1)[None],
                jnp.dot(a_local, (hidden_f * norm_gain).T, precision=HIGH),
                jnp.dot(factors[1].reshape(RANK, local_width), first[:tokens].astype(F32).T, precision=HIGH),
            ],
            axis=0,
        ),
        tensor,
    )
    scale_row = lax.rsqrt(sums[:1] / MODEL_WIDTH + epsilon)
    projected = sums[1:1 + RANK] * scale_row
    scale = scale_row.reshape(tokens, 1)
    top_mixed = sums[1 + RANK:]

    z_ring = gather_ring(where, own_weight, "z", earlier=(scale,))
    y_ring = gather_ring(where, first, "y", earlier=(scale,))

    dz_pieces = (y_ring[0], y_ring[1], y_ring[2], y_ring[4])
    keep, send = top_product(where, tokens, dz_pieces, z_ring, y_ring[3])
    got = swap(send, "core", (1,))
    theirs = add_theirs(keep, got)
    other = swap(theirs, "pair", (1,))

    own, to_after, to_far, to_before = add_mine(keep, got, other)
    from_before = ring_move(to_after, "y", 1, (1,))
    from_far = ring_move(to_far, "y", 2, (1,))
    from_after = ring_move(to_before, "y", -1, (1,))

    _, z_after, z_far_low, z_far_high, z_before = z_ring
    _, y_after, y_far_low, y_far_high, y_before = y_ring
    slim, rest = half // 2, shard - half // 2
    corner = join(where, 0, (z_far_low, z_far_high), ((0, half), (0, half)), own)
    corner = ring_move(corner, "y", 2, (0,))
    along_z = join(
        where, None, (y_far_low, y_far_high, y_after, y_before),
        ((0, half), (0, half), (slim, rest), (slim, rest)), own,
    )
    z_pair = (ring_move(along_z, "z", -1), ring_move(along_z, "z", 1))
    along_y = join(
        where, 0, (z_far_low, z_far_high, z_after, z_before),
        ((0, half), (0, half), (0, slim), (0, slim)), corner,
    )
    y_pair = (ring_move(along_y, "y", -1, (0,)), ring_move(along_y, "y", 1, (0,)))
    w_pieces = (*z_ring, *y_ring[1:], corner, *y_pair, *z_pair)

    pieces = (own, from_after, from_far, from_before)
    scaled, inner = make_scaled(where, pieces, top_mixed, a_local, norm_gain, hidden, scale)
    top_grad = finish_top(scaled, lax.psum(inner, tensor), hidden, scale, grad_top, 0)
    low_in = lax.ppermute(top_grad, "section", [(1, 0)])

    low_dz, part = make_dz(low_in, preact, b_both, 0)
    low_mixed = lax.psum(part, tensor)
    keep, send = low_product(where, z, y, place, low_dz, w_pieces, low_mixed)
    got = swap(send, "core", (0,))
    theirs = add_theirs(keep, got)
    other = swap(theirs, "pair", (0,))
    scaled, inner = low_scaled(keep, got, other, low_mixed, a_local, norm_gain, hidden, scale)
    result = finish_low(where, scaled, lax.psum(inner, tensor), hidden, scale, low_in, top_grad)

    grads = make_grads(
        where, hidden, scale, norm_gain, projected, ([first], [low_dz], [top_mixed], [low_mixed])
    )
    over_y = ring_moves(grads, "y")
    grads = small_call(ring_kernel, jax.ShapeDtypeStruct(grads.shape, F32), (grads, *over_y), send)
    over_z = ring_moves(grads, "z")
    flat = mixing.reshape(2, RANK, seg_local, bank_rows).transpose(2, 0, 1, 3)
    flat = flat.reshape(2 * RANK * seg_local, bank_rows)
    bank_shape = (bank_rows, SUB)
    share = small_call(bank_kernel, jax.ShapeDtypeStruct(bank_shape, F32), (flat, grads, *over_z), theirs)
    core_share = swap(share, "core")
    half_shape = jax.ShapeDtypeStruct(bank_shape, BF16)
    add_up = functools.partial(round_kernel, 1.0 / math.sqrt(TOKENS))
    share = small_call(add_up, half_shape, (share, core_share))
    pair_share = swap(share, "pair")
    add_up = functools.partial(round_kernel, 1.0)
    share = small_call(add_up, half_shape, (share, pair_share))
    other_share = lax.ppermute(share, "section", [(0, 1), (1, 0)])
    bank_grad = small_call(add_up, jax.ShapeDtypeStruct(bank_shape, F32), (share, other_share), result)
    return (result[None], bank_grad)


def solution(mesh):
    fine = Mesh(
        mesh.devices.reshape(2, RING, RING, 2, 2), ("section", "z", "y", "pair", "core")
    )
    rows, columns = ("z", "y"), ("pair", "core")
    return jax.shard_map(
        shards,
        mesh=fine,
        in_specs=(
            P("section", rows, columns),
            P("section", rows, columns),
            P("section", columns),
            P("section", rows, columns),
            P(),
            P("section", None, None, None),
            P("section", None, None, None),
            P(rows, columns),
        ),
        out_specs=(P("section", rows, columns), P()),
        check_vma=False,
    )
```

time: 445 us -> 329 us (0.74); the launches traced: 437 us -> 328 us
  Pallas kernels: 0 us -> 59.7 us
  matrix products: 58.4 us -> 4.13 us
  starting transfers between devices: 94.9 us -> 55.4 us
  other arithmetic: 34.8 us -> 0.57 us
  blocking collectives: 65.4 us -> 33.5 us
  local copies, waits for them, and re-layouts: 47.8 us -> 19.2 us
  waiting for transfers between devices: 133 us -> 154 us
    pallas_call x0 -> x24, Pallas kernels: none -> 59.7 us  [the longest x1 16.9 us: low_product(): pl.pallas_call(in_order(functools.partial(low_product_kernel, copies), 3...]
    dot_general x31 -> x2, matrix products: 58.2 us -> 3.88 us  [the longest x1 2.14 us: shards(): jnp.dot(factors[1].reshape(RANK, local_width), first[:tokens].astype(F32)...]
    psum x7 -> x4, blocking collectives: 65.4 us -> 33.5 us  [the longest x2 15.7 us: shards(): lax.psum(inner, tensor)]
    ppermute x41 -> x24, starting transfers between devices: 74.8 us -> 44 us  [the longest x22 35.4 us: ring_move(): lax.ppermute(block, ('section', axis), ring_route(distance, sections))]
    convert_element_type x10 -> x1, other arithmetic: 21.6 us -> 0.01 us  [two_halves(): (value - high.astype(F32)).astype(BF16)]
    dynamic_slice x14 -> x0, local copies, waits for them, and re-layouts: 21.2 us -> none  [the longest x8 11.2 us: pick(): return lax.dynamic_index_in_dim(stack, index, 0, keepdims=False)]
    ppermute x41 -> x24, waiting for transfers between devices: 133 us -> 145 us  [the longest x22 91.3 us: ring_move(): lax.ppermute(block, ('section', axis), ring_route(distance, sections))]
    ppermute x8 -> x6, waiting for transfers between devices: 0.02 us -> 9.18 us  [swap(): return lax.ppermute(block, ('section', axis), pairs)]
  transfers between devices with their start and end apart: 49 -> 30, of which waited for: 14 -> 17; matrix products, arithmetic and copies ran while one was open for 21% -> 2% of each run, Pallas kernels for 0% -> 10%
where the time goes in v2:
time: 329 us; the launch traced here: 328 us
  waiting for transfers between devices  154 us (47%)
  Pallas kernels  59.7 us (18%)
  starting transfers between devices  55.4 us (17%)
  blocking collectives  33.5 us (10%)
  local copies, waits for them, and re-layouts  19.2 us (6%)
  matrix products  4.13 us (1%)
    ppermute x22, waiting for transfers between devices, ring_move(): lax.ppermute(block, ('section', axis), ring_route(distance, sections))  91.3 us
    ppermute x1, waiting for transfers between devices, shards(): low_in = lax.ppermute(top_grad, 'section', [(1, 0)])  53.6 us
    ppermute x22, starting transfers between devices, ring_move(): lax.ppermute(block, ('section', axis), ring_route(distance, sections))  35.4 us
    unnamed x68, local copies, waits for them, and re-layouts  18.6 us
    pallas_call x1, Pallas kernels, low_product(): pl.pallas_call(in_order(functools.partial(low_product_kernel, copies), 3...  16.9 us
    psum x2, blocking collectives, shards(): lax.psum(inner, tensor)  15.7 us
    pallas_call x7, Pallas kernels, join(): pl.pallas_call(in_order(functools.partial(join_kernel, wanted, parts), 1...  15.1 us
    ppermute x6, starting transfers between devices, swap(): return lax.ppermute(block, ('section', axis), pairs)  11.5 us
  transfers between devices with their start and end apart: 30, of which 17 were waited for; matrix products, arithmetic and copies ran while one was open for 2% of the time, Pallas kernels for 10%

profile of v2, /device:TPU:1, one launch (start us, length us, event | category | flops | bytes accessed | tf_op | source)
XLA Modules:
  0.0 327.9 jit_solution(15510834535373566259)
XLA Ops:
  3.2 3.2 shard_map.122.refs_1_.refs_5_
  6.3 2.1 collective-permute-start.2
  8.5 3.8 %collective-permute-start.3 = (bf16[512,2048]{1,0:T(8,128)(2,1)}, bf16[512,2048]{1,0:T(8,128)(2,1)}, u32[]{:S(2)}, u32[]{:S(2)}) collective-permute-start(bf16[512,2048]{1,0:T(8,128)(2,1)} %bitcast.5.weight_ref.refs_5_.refs_3_), channel_id=1, source_target_pairs={{0,48},{16,0},{32,16},{48,32},{64,112},{80,64},{96,80},{112,96},{1... | collective-permute-start | bytes 6291464 | tf_op jit(solution)/shard_map/ppermute | solution.py:35
  14.8 2.1 fusion.4
  16.9 1.7 fusion
  18.7 11.2 %psum.28 = f32[9,256]{1,0:T(8,128)S(1)} all-reduce(f32[9,256]{1,0:T(8,128)S(1)} %pad_maximum_fusion.1), channel_id=1, replica_groups=mesh['section'=2,'z'=4,'y'=4,'pair'=2,'core'=2] {'pair','core'}, use_global_device_ids=true, to_apply=%region_2.0 | all-reduce | flops 2304 | bytes 18432 | tf_op jit(solution)/shard_map/psum | solution.py:586
  30.0 25.4 %collective-permute-done.2.refs_1_.refs_4_.refs_11_ = bf16[512,2048]{1,0:T(8,128)(2,1)S(1)} collective-permute-done((bf16[512,2048]{1,0:T(8,128)(2,1)}, bf16[512,2048]{1,0:T(8,128)(2,1)S(1)}, u32[]{:S(2)}, u32[]{:S(2)}) %collective-permute-start.2) | collective-permute-done | bytes 2097184 | tf_op jit(solution)/shard_map/ppermute | solution.py:35
  56.5 1.8 shard_map.124
  58.3 3.5 %collective-permute-start.4 = (bf16[256,2048]{1,0:T(8,128)(2,1)S(1)}, bf16[256,2048]{1,0:T(8,128)(2,1)S(1)}, u32[]{:S(2)}, u32[]{:S(2)}) collective-permute-start(bf16[256,2048]{1,0:T(8,128)(2,1)S(1)} %shard_map.124), channel_id=1, source_target_pairs={{0,48},{16,0},{32,16},{48,32},{64,112},{80,64},{96,80},{112,96},{1... | collective-permute-start | bytes 3145736 | tf_op jit(solution)/shard_map/ppermute | solution.py:35
  61.8 1.8 shard_map.125
  63.7 1.8 shard_map.123
  65.5 2.6 collective-permute-start.1
  68.1 12.7 %collective-permute-done.7.refs_10_.refs_2_ = bf16[256,2048]{1,0:T(8,128)(2,1)S(1)} collective-permute-done((bf16[256,2048]{1,0:T(8,128)(2,1)S(1)}, bf16[256,2048]{1,0:T(8,128)(2,1)S(1)}, u32[]{:S(2)}, u32[]{:S(2)}) %collective-permute-start.7) | collective-permute-done | bytes 1048608 | tf_op jit(solution)/shard_map/ppermute | solution.py:35
  80.7 1.7 collective-permute-done.4.refs_7_.refs_1_.refs_5_
  82.4 5.0 %collective-permute-done.6.refs_8_.refs_2_.refs_6_ = bf16[256,2048]{1,0:T(8,128)(2,1)S(1)} collective-permute-done((bf16[256,2048]{1,0:T(8,128)(2,1)S(1)}, bf16[256,2048]{1,0:T(8,128)(2,1)S(1)}, u32[]{:S(2)}, u32[]{:S(2)}) %collective-permute-start.6) | collective-permute-done | bytes 1048608 | tf_op jit(solution)/shard_map/ppermute | solution.py:35
  88.6 2.6 shard_map.127
  92.0 2.3 copy-done.8
  95.4 1.7 shard_map.129
  97.8 4.0 %collective-permute-start.14 = (bf16[512,2048]{1,0:T(8,128)(2,1)S(1)}, bf16[512,2048]{1,0:T(8,128)(2,1)S(1)}, u32[]{:S(2)}, u32[]{:S(2)}) collective-permute-start(bf16[512,2048]{1,0:T(8,128)(2,1)S(1)} %shard_map.133), channel_id=1, source_target_pairs={{0,8},{4,12},{8,0},{12,4},{1,9},{5,13},{9,1},{13,5},{2,10},{6,14},... | collective-permute-start | bytes 6291464 | tf_op jit(solution)/shard_map/ppermute | solution.py:35
  101.8 4.9 %shard_map.135 = bf16[1280,2048]{1,0:T(8,128)(2,1)} custom-call(s32[4]{0:T(128)S(1)} %pad_add_fusion.where_ref.refs_0_, bf16[256,2048]{1,0:T(8,128)(2,1)S(1)} %collective-permute-done.1.refs_3_.refs_1_.refs_9_, bf16[256,2048]{1,0:T(8,128)(2,1)S(1)} %collective-permute-done.7.refs_10_.refs_2_, ...), custom_call_target="tpu_custom_call" | custom-call | bytes 1048576 | tf_op jit(solution)/shard_map/pallas_call | solution.py:120
  106.6 2.4 collective-permute-start.17
  109.1 36.3 %collective-permute-done.14.refs_5_.refs_12_ = bf16[512,2048]{1,0:T(8,128)(2,1)S(1)} collective-permute-done((bf16[512,2048]{1,0:T(8,128)(2,1)S(1)}, bf16[512,2048]{1,0:T(8,128)(2,1)S(1)}, u32[]{:S(2)}, u32[]{:S(2)}) %collective-permute-start.14) | collective-permute-done | bytes 2097184 | tf_op jit(solution)/shard_map/ppermute | solution.py:35
  146.8 3.6 %shard_map.134 = bf16[768,2048]{1,0:T(8,128)(2,1)} custom-call(s32[4]{0:T(128)S(1)} %pad_add_fusion.where_ref.refs_0_, bf16[256,2048]{1,0:T(8,128)(2,1)S(1)} %collective-permute-done.4.refs_7_.refs_1_.refs_5_, bf16[256,2048]{1,0:T(8,128)(2,1)S(1)} %collective-permute-done.6.refs_8_.refs_2_.refs_6_, ...), custom_call_target="tpu_custom_call" | custom-call | bytes 1048576 | tf_op jit(solution)/shard_map/pallas_call | solution.py:120
  150.5 5.5 %collective-permute-start.15 = (bf16[768,2048]{1,0:T(8,128)(2,1)}, bf16[768,2048]{1,0:T(8,128)(2,1)}, u32[]{:S(2)}, u32[]{:S(2)}) collective-permute-start(bf16[768,2048]{1,0:T(8,128)(2,1)} %shard_map.134), channel_id=1, source_target_pairs={{0,12},{4,0},{8,4},{12,8},{1,13},{5,1},{9,5},{13,9},{2,14},{6,2},{... | collective-permute-start | bytes 9437192 | tf_op jit(solution)/shard_map/ppermute | solution.py:35
  155.9 1.9 collective-permute-start.16
  160.1 2.7 shard_map.130
  164.2 9.1 %psum.29.inner_ref = f32[8,256]{1,0:T(8,128)S(1)} all-reduce(f32[8,256]{1,0:T(8,128)S(1)} %get-tuple-element.23), channel_id=1, replica_groups=mesh['section'=2,'z'=4,'y'=4,'pair'=2,'core'=2] {'pair','core'}, use_global_device_ids=true, to_apply=%region_3.0 | all-reduce | flops 2048 | bytes 16384 | tf_op jit(solution)/shard_map/psum | solution.py:635
  173.3 1.6 copy-done.24
  178.0 53.6 %collective-permute-done.13.refs_0_.incoming_ref = bf16[256,2048]{1,0:T(8,128)(2,1)} collective-permute-done((bf16[256,2048]{1,0:T(8,128)(2,1)}, bf16[256,2048]{1,0:T(8,128)(2,1)}, u32[]{:S(2)}, u32[]{:S(2)}) %collective-permute-start.13) | collective-permute-done | bytes 1048608 | tf_op jit(solution)/shard_map/ppermute | solution.py:636
  232.8 2.1 shard_map.132
  235.9 6.7 %psum.30.refs_17_.mixed_ref.refs_8_ = f32[4,256]{1,0:T(4,128)S(1)} all-reduce(f32[4,256]{1,0:T(4,128)S(1)} %get-tuple-element.25), channel_id=1, replica_groups=mesh['section'=2,'z'=4,'y'=4,'pair'=2,'core'=2] {'pair','core'}, use_global_device_ids=true, to_apply=%region_4.0 | all-reduce | flops 1024 | bytes 8192 | tf_op jit(solution)/shard_map/psum | solution.py:639
  246.3 16.9 %shard_map.136 = (bf16[2,256,2048]{2,1,0:T(8,128)(2,1)}, bf16[2,256,2048]{2,1,0:T(8,128)(2,1)}) custom-call(s32[4]{0:T(128)S(1)} %pad_add_fusion.where_ref.refs_0_, s32[32]{0:T(128)S(1)} %fusion.16.refs_1_, bf16[256,2048]{1,0:T(8,128)(2,1)S(1)} %copy-done.20, bf16[512,2048]{1,0:T(8,128)(2,1)} %bitcast.5.weight_ref.refs_5_.refs_3_, ...), custom_call_target="tpu_custom_call" | custom-call | flops 8589934592 | bytes 33554432 | tf_op jit(solution)/shard_map/pallas_call | solution.py:306
  263.3 2.9 collective-permute-start.19
  266.1 4.0 %collective-permute-done.19.got_ref = bf16[2,256,2048]{2,1,0:T(8,128)(2,1)S(1)} collective-permute-done((bf16[2,256,2048]{2,1,0:T(8,128)(2,1)}, bf16[2,256,2048]{2,1,0:T(8,128)(2,1)S(1)}, u32[]{:S(2)}, u32[]{:S(2)}) %collective-permute-start.19) | collective-permute-done | bytes 2097184 | tf_op jit(solution)/shard_map/ppermute | solution.py:40
  270.1 2.3 copy-done.6
  273.7 1.9 collective-permute-start.20
  275.6 2.4 shard_map.140.refs_0_
  278.0 1.8 collective-permute-start.21
  281.6 2.9 collective-permute-done.22.refs_2_
  284.9 2.7 collective-permute-start.24
  289.5 2.8 collective-permute-done.25.refs_3_
  293.0 3.6 %collective-permute-start.27 = (f32[256,256]{1,0:T(8,128)S(1)}, f32[256,256]{1,0:T(8,128)S(1)}, u32[]{:S(2)}, u32[]{:S(2)}) collective-permute-start(f32[256,256]{1,0:T(8,128)S(1)} %shard_map.142.refs_0_), channel_id=1, source_target_pairs={{0,1},{1,0},{64,65},{65,64},{2,3},{3,2},{66,67},{67,66},{4,5},{5,4... | collective-permute-start | bytes 786440 | tf_op jit(solution)/shard_map/ppermute | solution.py:40
  299.3 4.0 %collective-permute-done.28.refs_1_ = bf16[256,256]{1,0:T(8,128)(2,1)S(1)} collective-permute-done((bf16[256,256]{1,0:T(8,128)(2,1)S(1)}, bf16[256,256]{1,0:T(8,128)(2,1)S(1)}, u32[]{:S(2)}, u32[]{:S(2)}) %collective-permute-start.28) | collective-permute-done | bytes 131104 | tf_op jit(solution)/shard_map/ppermute | solution.py:40
  304.1 7.2 %collective-permute-start.29 = (bf16[256,256]{1,0:T(8,128)(2,1)}, bf16[256,256]{1,0:T(8,128)(2,1)}, u32[]{:S(2)}, u32[]{:S(2)}) collective-permute-start(bf16[256,256]{1,0:T(8,128)(2,1)} %shard_map.144.refs_0_), channel_id=1, source_target_pairs={{0,64},{64,0},{1,65},{65,1},{2,66},{66,2},{3,67},{67,3},{4,68},{68... | collective-permute-start | bytes 393224 | tf_op jit(solution)/shard_map/ppermute | solution.py:664
  311.2 4.0 %shard_map.138 = (f32[256,2048]{1,0:T(8,128)S(1)}, f32[8,256]{1,0:T(8,128)S(1)}) custom-call(bf16[2,256,2048]{2,1,0:T(8,128)(2,1)} %get-tuple-element.26.keep_ref, bf16[2,256,2048]{2,1,0:T(8,128)(2,1)} %copy-done.7, bf16[256,2048]{1,0:T(8,128)(2,1)} %collective-permute-done.20.other_ref, f32[4,256]{1,0:T(4,128)S(1)} %psum.30.refs_17_.mixed_ref.refs_8_, ...), custom_call_target="tpu_custom_call" | custom-call | bytes 1048576 | tf_op jit(solution)/shard_map/pallas_call | solution.py:415
  315.2 6.5 %psum.31.inner_ref = f32[8,256]{1,0:T(8,128)S(1)} all-reduce(f32[8,256]{1,0:T(8,128)S(1)} %get-tuple-element.29), channel_id=1, replica_groups=mesh['section'=2,'z'=4,'y'=4,'pair'=2,'core'=2] {'pair','core'}, use_global_device_ids=true, to_apply=%region_5.6 | all-reduce | flops 2048 | bytes 16384 | tf_op jit(solution)/shard_map/psum | solution.py:645
  321.8 3.2 shard_map.139.refs_2_
  326.2 1.7 shard_map.145
  (133 shorter events, 34.6 us)
Async XLA Ops:
  0.6 13.5 %copy-start = (f32[256,256]{1,0:T(8,128)S(1)}, f32[256,256]{1,0:T(8,128)}, u32[]{:S(2)}) copy-start(f32[256,256]{1,0:T(8,128)} %param.15) | copy-start | bytes 786436
  3.2 10.5 %copy-start.29 = (s32[1,2,128,2]{2,3,1,0:T(2,128)S(1)}, s32[1,2,128,2]{2,3,1,0:T(2,128)}, u32[]{:S(2)}) copy-start(s32[1,2,128,2]{2,3,1,0:T(2,128)} %param.16) | copy-start | bytes 6148
  3.2 10.7 %copy-start.30 = (f32[1,2,128,2]{2,3,1,0:T(2,128)S(1)}, f32[1,2,128,2]{2,3,1,0:T(2,128)}, u32[]{:S(2)}) copy-start(f32[1,2,128,2]{2,3,1,0:T(2,128)} %param.17) | copy-start | bytes 6148
  3.2 11.3 %copy-start.2 = (bf16[1,256,2048]{2,1,0:T(8,128)(2,1)S(1)}, bf16[1,256,2048]{2,1,0:T(8,128)(2,1)}, u32[]{:S(2)}) copy-start(bf16[1,256,2048]{2,1,0:T(8,128)(2,1)} %param.11) | copy-start | bytes 3145732
  6.3 10.6 %copy-start.25 = (f32[1,2048]{1,0:T(1,128)S(1)}, f32[1,2048]{1,0:T(1,128)}, u32[]{:S(2)}) copy-start(f32[1,2048]{1,0:T(1,128)} %refs_3_.1) | copy-start | bytes 24580
  6.3 49.1 %collective-permute-start.2 = (bf16[512,2048]{1,0:T(8,128)(2,1)}, bf16[512,2048]{1,0:T(8,128)(2,1)S(1)}, u32[]{:S(2)}, u32[]{:S(2)}) collective-permute-start(bf16[512,2048]{1,0:T(8,128)(2,1)} %shard_map.122.refs_1_.refs_5_), channel_id=1, source_target_pairs={{0,4},{4,8},{8,12},{12,0},{64,68},{68,72},{72,76},{76,64},{1,5},{5... | collective-permute-start | bytes 6291464 | tf_op jit(solution)/shard_map/ppermute | solution.py:35
  8.5 48.1 %collective-permute-start.3 = (bf16[512,2048]{1,0:T(8,128)(2,1)}, bf16[512,2048]{1,0:T(8,128)(2,1)}, u32[]{:S(2)}, u32[]{:S(2)}) collective-permute-start(bf16[512,2048]{1,0:T(8,128)(2,1)} %bitcast.5.weight_ref.refs_5_.refs_3_), channel_id=1, source_target_pairs={{0,48},{16,0},{32,16},{48,32},{64,112},{80,64},{96,80},{112,96},{1... | collective-permute-start | bytes 6291464 | tf_op jit(solution)/shard_map/ppermute | solution.py:35
  12.2 49.6 %collective-permute-start.5 = (bf16[512,2048]{1,0:T(8,128)(2,1)}, bf16[512,2048]{1,0:T(8,128)(2,1)}, u32[]{:S(2)}, u32[]{:S(2)}) collective-permute-start(bf16[512,2048]{1,0:T(8,128)(2,1)} %bitcast.5.weight_ref.refs_5_.refs_3_), channel_id=1, source_target_pairs={{0,16},{16,32},{32,48},{48,0},{64,80},{80,96},{96,112},{112,64},{1... | collective-permute-start | bytes 6291464 | tf_op jit(solution)/shard_map/ppermute | solution.py:35
  12.2 51.4 %collective-permute-start = (bf16[512,2048]{1,0:T(8,128)(2,1)}, bf16[512,2048]{1,0:T(8,128)(2,1)}, u32[]{:S(2)}, u32[]{:S(2)}) collective-permute-start(bf16[512,2048]{1,0:T(8,128)(2,1)} %shard_map.122.refs_1_.refs_5_), channel_id=1, source_target_pairs={{0,12},{4,0},{8,4},{12,8},{64,76},{68,64},{72,68},{76,72},{1,13},{... | collective-permute-start | bytes 6291464 | tf_op jit(solution)/shard_map/ppermute | solution.py:35
  14.1 15.7 %copy-start.27 = (f32[2,4,8,256]{3,2,1,0:T(8,128)}, f32[2,4,8,256]{3,2,1,0:T(8,128)S(1)}, u32[]{:S(2)}) copy-start(f32[2,4,8,256]{3,2,1,0:T(8,128)S(1)} %select_reduce_fusion) | copy-start | bytes 196612
  56.1 24.7 %collective-permute-start.7 = (bf16[256,2048]{1,0:T(8,128)(2,1)S(1)}, bf16[256,2048]{1,0:T(8,128)(2,1)S(1)}, u32[]{:S(2)}, u32[]{:S(2)}) collective-permute-start(bf16[256,2048]{1,0:T(8,128)(2,1)S(1)} %shard_map.126), channel_id=1, source_target_pairs={{0,4},{4,8},{8,12},{12,0},{64,68},{68,72},{72,76},{76,64},{1,5},{5... | collective-permute-start | bytes 3145736 | tf_op jit(solution)/shard_map/ppermute | solution.py:35
  58.3 24.1 %collective-permute-start.4 = (bf16[256,2048]{1,0:T(8,128)(2,1)S(1)}, bf16[256,2048]{1,0:T(8,128)(2,1)S(1)}, u32[]{:S(2)}, u32[]{:S(2)}) collective-permute-start(bf16[256,2048]{1,0:T(8,128)(2,1)S(1)} %shard_map.124), channel_id=1, source_target_pairs={{0,48},{16,0},{32,16},{48,32},{64,112},{80,64},{96,80},{112,96},{1... | collective-permute-start | bytes 3145736 | tf_op jit(solution)/shard_map/ppermute | solution.py:35
  63.6 23.8 %collective-permute-start.6 = (bf16[256,2048]{1,0:T(8,128)(2,1)S(1)}, bf16[256,2048]{1,0:T(8,128)(2,1)S(1)}, u32[]{:S(2)}, u32[]{:S(2)}) collective-permute-start(bf16[256,2048]{1,0:T(8,128)(2,1)S(1)} %shard_map.125), channel_id=1, source_target_pairs={{0,16},{16,32},{32,48},{48,0},{64,80},{80,96},{96,112},{112,64},{1... | collective-permute-start | bytes 3145736 | tf_op jit(solution)/shard_map/ppermute | solution.py:35
  65.5 23.1 %collective-permute-start.1 = (bf16[256,2048]{1,0:T(8,128)(2,1)S(1)}, bf16[256,2048]{1,0:T(8,128)(2,1)S(1)}, u32[]{:S(2)}, u32[]{:S(2)}) collective-permute-start(bf16[256,2048]{1,0:T(8,128)(2,1)S(1)} %shard_map.123), channel_id=1, source_target_pairs={{0,12},{4,0},{8,4},{12,8},{64,76},{68,64},{72,68},{76,72},{1,13},{... | collective-permute-start | bytes 3145736 | tf_op jit(solution)/shard_map/ppermute | solution.py:35
  80.7 21.0 %copy-start.10 = (bf16[256,2048]{1,0:T(8,128)(2,1)}, bf16[256,2048]{1,0:T(8,128)(2,1)S(1)}, u32[]{:S(2)}) copy-start(bf16[256,2048]{1,0:T(8,128)(2,1)S(1)} %collective-permute-done.7.refs_10_.refs_2_) | copy-start | bytes 3145732
  82.4 63.0 %copy-start.4 = (bf16[256,2048]{1,0:T(8,128)(2,1)}, bf16[256,2048]{1,0:T(8,128)(2,1)S(1)}, u32[]{:S(2)}) copy-start(bf16[256,2048]{1,0:T(8,128)(2,1)S(1)} %collective-permute-done.4.refs_7_.refs_1_.refs_5_) | copy-start | bytes 3145732
  88.6 13.2 %copy-start.12 = (bf16[256,2048]{1,0:T(8,128)(2,1)}, bf16[256,2048]{1,0:T(8,128)(2,1)S(1)}, u32[]{:S(2)}) copy-start(bf16[256,2048]{1,0:T(8,128)(2,1)S(1)} %collective-permute-done.1.refs_3_.refs_1_.refs_9_) | copy-start | bytes 3145732
  91.2 0.8 collective-permute-start.8
  94.6 0.7 collective-permute-start.9
  97.8 47.7 %collective-permute-start.14 = (bf16[512,2048]{1,0:T(8,128)(2,1)S(1)}, bf16[512,2048]{1,0:T(8,128)(2,1)S(1)}, u32[]{:S(2)}, u32[]{:S(2)}) collective-permute-start(bf16[512,2048]{1,0:T(8,128)(2,1)S(1)} %shard_map.133), channel_id=1, source_target_pairs={{0,8},{4,12},{8,0},{12,4},{1,9},{5,13},{9,1},{13,5},{2,10},{6,14},... | collective-permute-start | bytes 6291464 | tf_op jit(solution)/shard_map/ppermute | solution.py:35
  106.6 136.0 %collective-permute-start.17 = (bf16[1280,2048]{1,0:T(8,128)(2,1)}, bf16[1280,2048]{1,0:T(8,128)(2,1)}, u32[]{:S(2)}, u32[]{:S(2)}) collective-permute-start(bf16[1280,2048]{1,0:T(8,128)(2,1)} %shard_map.135), channel_id=1, source_target_pairs={{0,48},{16,0},{32,16},{48,32},{64,112},{80,64},{96,80},{112,96},{1... | collective-permute-start | bytes 15728648 | tf_op jit(solution)/shard_map/ppermute | solution.py:35
  109.1 133.5 %collective-permute-start.18 = (bf16[1280,2048]{1,0:T(8,128)(2,1)}, bf16[1280,2048]{1,0:T(8,128)(2,1)}, u32[]{:S(2)}, u32[]{:S(2)}) collective-permute-start(bf16[1280,2048]{1,0:T(8,128)(2,1)} %shard_map.135), channel_id=1, source_target_pairs={{0,16},{16,32},{32,48},{48,0},{64,80},{80,96},{96,112},{112,64},{1... | collective-permute-start | bytes 15728648 | tf_op jit(solution)/shard_map/ppermute | solution.py:35
  150.4 22.9 %copy-start.18 = (bf16[256,2048]{1,0:T(8,128)(2,1)S(1)}, bf16[256,2048]{1,0:T(8,128)(2,1)}, u32[]{:S(2)}) copy-start(bf16[256,2048]{1,0:T(8,128)(2,1)} %incoming_ref.3) | copy-start | bytes 3145732
  150.5 92.1 %collective-permute-start.15 = (bf16[768,2048]{1,0:T(8,128)(2,1)}, bf16[768,2048]{1,0:T(8,128)(2,1)}, u32[]{:S(2)}, u32[]{:S(2)}) collective-permute-start(bf16[768,2048]{1,0:T(8,128)(2,1)} %shard_map.134), channel_id=1, source_target_pairs={{0,12},{4,0},{8,4},{12,8},{1,13},{5,1},{9,5},{13,9},{2,14},{6,2},{... | collective-permute-start | bytes 9437192 | tf_op jit(solution)/shard_map/ppermute | solution.py:35
  155.9 86.7 %collective-permute-start.16 = (bf16[768,2048]{1,0:T(8,128)(2,1)}, bf16[768,2048]{1,0:T(8,128)(2,1)}, u32[]{:S(2)}, u32[]{:S(2)}) collective-permute-start(bf16[768,2048]{1,0:T(8,128)(2,1)} %shard_map.134), channel_id=1, source_target_pairs={{0,4},{4,8},{8,12},{12,0},{1,5},{5,9},{9,13},{13,1},{2,6},{6,10},{... | collective-permute-start | bytes 9437192 | tf_op jit(solution)/shard_map/ppermute | solution.py:35
  157.8 0.7 collective-permute-start.10
  158.5 0.9 collective-permute-start.11
  159.4 0.7 collective-permute-start.12
  174.9 3.0 copy-start.32
  174.9 3.0 copy-start.33
  176.5 66.1 %copy-start.5 = (bf16[256,2048]{1,0:T(8,128)(2,1)S(1)}, bf16[256,2048]{1,0:T(8,128)(2,1)}, u32[]{:S(2)}) copy-start(bf16[256,2048]{1,0:T(8,128)(2,1)} %copy-done.4) | copy-start | bytes 3145732
  176.5 55.1 %collective-permute-start.13 = (bf16[256,2048]{1,0:T(8,128)(2,1)}, bf16[256,2048]{1,0:T(8,128)(2,1)}, u32[]{:S(2)}, u32[]{:S(2)}) collective-permute-start(bf16[256,2048]{1,0:T(8,128)(2,1)} %shard_map.131.top_ref), channel_id=1, source_target_pairs={{64,0},{65,1},{66,2},{67,3},{68,4},{69,5},{70,6},{71,7},{72,8},{73... | collective-permute-start | bytes 3145736 | tf_op jit(solution)/shard_map/ppermute | solution.py:636
  263.3 6.9 %collective-permute-start.19 = (bf16[2,256,2048]{2,1,0:T(8,128)(2,1)}, bf16[2,256,2048]{2,1,0:T(8,128)(2,1)S(1)}, u32[]{:S(2)}, u32[]{:S(2)}) collective-permute-start(bf16[2,256,2048]{2,1,0:T(8,128)(2,1)} %get-tuple-element.27.refs_4_), channel_id=1, source_target_pairs={{0,1},{1,0},{2,3},{3,2},{4,5},{5,4},{6,7},{7,6},{8,9},{9,8},{10,11... | collective-permute-start | bytes 6291464 | tf_op jit(solution)/shard_map/ppermute | solution.py:40
  270.1 3.6 %copy-start.7 = (bf16[2,256,2048]{2,1,0:T(8,128)(2,1)}, bf16[2,256,2048]{2,1,0:T(8,128)(2,1)S(1)}, u32[]{:S(2)}) copy-start(bf16[2,256,2048]{2,1,0:T(8,128)(2,1)S(1)} %collective-permute-done.19.got_ref) | copy-start | bytes 6291460
  272.5 3.2 copy-start.21
  273.7 37.5 %collective-permute-start.20 = (bf16[256,2048]{1,0:T(8,128)(2,1)}, bf16[256,2048]{1,0:T(8,128)(2,1)}, u32[]{:S(2)}, u32[]{:S(2)}) collective-permute-start(bf16[256,2048]{1,0:T(8,128)(2,1)} %shard_map.137.refs_5_), channel_id=1, source_target_pairs={{0,2},{2,0},{1,3},{3,1},{4,6},{6,4},{5,7},{7,5},{8,10},{10,8},{9,1... | collective-permute-start | bytes 3145736 | tf_op jit(solution)/shard_map/ppermute | solution.py:40
  275.6 9.2 %copy-start.22 = (bf16[2,256,2048]{2,1,0:T(8,128)(2,1)S(1)}, bf16[2,256,2048]{2,1,0:T(8,128)(2,1)}, u32[]{:S(2)}) copy-start(bf16[2,256,2048]{2,1,0:T(8,128)(2,1)} %get-tuple-element.27.refs_4_) | copy-start | bytes 6291460
  278.0 10.2 %copy-start.28 = (f32[2,4,8,256]{3,2,1,0:T(8,128)S(1)}, f32[2,4,8,256]{3,2,1,0:T(8,128)}, u32[]{:S(2)}) copy-start(f32[2,4,8,256]{3,2,1,0:T(8,128)} %copy-done.27) | copy-start | bytes 196612
  278.0 3.6 %collective-permute-start.21 = (f32[8,2048]{1,0:T(8,128)S(1)}, f32[8,2048]{1,0:T(8,128)S(1)}, u32[]{:S(2)}, u32[]{:S(2)}) collective-permute-start(f32[8,2048]{1,0:T(8,128)S(1)} %shard_map.140.refs_0_), channel_id=1, source_target_pairs={{0,12},{4,0},{8,4},{12,8},{64,76},{68,64},{72,68},{76,72},{1,13},{... | collective-permute-start | bytes 196616 | tf_op jit(solution)/shard_map/ppermute | solution.py:35
  279.8 4.7 %collective-permute-start.22 = (f32[8,2048]{1,0:T(8,128)S(1)}, f32[8,2048]{1,0:T(8,128)S(1)}, u32[]{:S(2)}, u32[]{:S(2)}) collective-permute-start(f32[8,2048]{1,0:T(8,128)S(1)} %shard_map.140.refs_0_), channel_id=1, source_target_pairs={{0,8},{4,12},{8,0},{12,4},{64,72},{68,76},{72,64},{76,68},{1,9},{5... | collective-permute-start | bytes 196616 | tf_op jit(solution)/shard_map/ppermute | solution.py:35
  279.8 5.0 %collective-permute-start.23 = (f32[8,2048]{1,0:T(8,128)S(1)}, f32[8,2048]{1,0:T(8,128)S(1)}, u32[]{:S(2)}, u32[]{:S(2)}) collective-permute-start(f32[8,2048]{1,0:T(8,128)S(1)} %shard_map.140.refs_0_), channel_id=1, source_target_pairs={{0,4},{4,8},{8,12},{12,0},{64,68},{68,72},{72,76},{76,64},{1,5},{5... | collective-permute-start | bytes 196616 | tf_op jit(solution)/shard_map/ppermute | solution.py:35
  284.9 4.6 %collective-permute-start.24 = (f32[8,2048]{1,0:T(8,128)S(1)}, f32[8,2048]{1,0:T(8,128)S(1)}, u32[]{:S(2)}, u32[]{:S(2)}) collective-permute-start(f32[8,2048]{1,0:T(8,128)S(1)} %shard_map.141.refs_1_), channel_id=1, source_target_pairs={{0,48},{16,0},{32,16},{48,32},{64,112},{80,64},{96,80},{112,96},{1... | collective-permute-start | bytes 196616 | tf_op jit(solution)/shard_map/ppermute | solution.py:35
  287.6 4.7 %collective-permute-start.25 = (f32[8,2048]{1,0:T(8,128)S(1)}, f32[8,2048]{1,0:T(8,128)S(1)}, u32[]{:S(2)}, u32[]{:S(2)}) collective-permute-start(f32[8,2048]{1,0:T(8,128)S(1)} %shard_map.141.refs_1_), channel_id=1, source_target_pairs={{0,32},{16,48},{32,0},{48,16},{64,96},{80,112},{96,64},{112,80},{1... | collective-permute-start | bytes 196616 | tf_op jit(solution)/shard_map/ppermute | solution.py:35
  287.6 5.0 %collective-permute-start.26 = (f32[8,2048]{1,0:T(8,128)S(1)}, f32[8,2048]{1,0:T(8,128)S(1)}, u32[]{:S(2)}, u32[]{:S(2)}) collective-permute-start(f32[8,2048]{1,0:T(8,128)S(1)} %shard_map.141.refs_1_), channel_id=1, source_target_pairs={{0,16},{16,32},{32,48},{48,0},{64,80},{80,96},{96,112},{112,64},{1... | collective-permute-start | bytes 196616 | tf_op jit(solution)/shard_map/ppermute | solution.py:35
  293.0 4.8 %collective-permute-start.27 = (f32[256,256]{1,0:T(8,128)S(1)}, f32[256,256]{1,0:T(8,128)S(1)}, u32[]{:S(2)}, u32[]{:S(2)}) collective-permute-start(f32[256,256]{1,0:T(8,128)S(1)} %shard_map.142.refs_0_), channel_id=1, source_target_pairs={{0,1},{1,0},{64,65},{65,64},{2,3},{3,2},{66,67},{67,66},{4,5},{5,4... | collective-permute-start | bytes 786440 | tf_op jit(solution)/shard_map/ppermute | solution.py:40
  297.8 5.6 %collective-permute-start.28 = (bf16[256,256]{1,0:T(8,128)(2,1)S(1)}, bf16[256,256]{1,0:T(8,128)(2,1)S(1)}, u32[]{:S(2)}, u32[]{:S(2)}) collective-permute-start(bf16[256,256]{1,0:T(8,128)(2,1)S(1)} %shard_map.143.refs_0_), channel_id=1, source_target_pairs={{0,2},{2,0},{64,66},{66,64},{1,3},{3,1},{65,67},{67,65},{4,6},{6,4... | collective-permute-start | bytes 393224 | tf_op jit(solution)/shard_map/ppermute | solution.py:40
  304.1 21.0 %collective-permute-start.29 = (bf16[256,256]{1,0:T(8,128)(2,1)}, bf16[256,256]{1,0:T(8,128)(2,1)}, u32[]{:S(2)}, u32[]{:S(2)}) collective-permute-start(bf16[256,256]{1,0:T(8,128)(2,1)} %shard_map.144.refs_0_), channel_id=1, source_target_pairs={{0,64},{64,0},{1,65},{65,1},{2,66},{66,2},{3,67},{67,3},{4,68},{68... | collective-permute-start | bytes 393224 | tf_op jit(solution)/shard_map/ppermute | solution.py:664
  321.8 6.1 %copy-start.1 = (f32[256,256]{1,0:T(8,128)S(1)}, f32[256,256]{1,0:T(8,128)}, u32[]{:S(2)}) copy-start(f32[256,256]{1,0:T(8,128)} %param.15) | copy-start | bytes 786436
  (16 other events, 27.1 us)

commit v3 on v2

--- a/solution.py
+++ b/solution.py
@@ -73,22 +73,35 @@
     mixed_ref[...] = both[:RANK] + both[RANK:]
 
 
-def first_kernel(where_ref, incoming_ref, preact_ref, weight_ref, out_ref):
+def first_kernel(where_ref, incoming_ref, preact_ref, weight_ref, out_ref, incoming, preact, sem):
+    def fetch(*pairs):
+        copies = [pltpu.make_async_copy(*pair, sem.at[i]) for i, pair in enumerate(pairs)]
+        for copy in copies:
+            copy.start()
+        for copy in copies:
+            copy.wait()
+
     @pl.when(where_ref[3] == 1)
     def _():
-        out_ref[:incoming_ref.shape[0]] = activation_gradient(incoming_ref, preact_ref)
+        fetch((incoming_ref, incoming), (preact_ref, preact))
+        out_ref[:incoming.shape[0]] = activation_gradient(incoming, preact)
 
     @pl.when(where_ref[3] == 0)
     def _():
-        out_ref[...] = weight_ref[...]
+        fetch((weight_ref, out_ref))
 
 
 def make_first(where, incoming, preact, weight):
     return pl.pallas_call(
         first_kernel,
-        in_specs=[SMEM, VMEM, VMEM, VMEM],
+        in_specs=[SMEM, HBM, HBM, HBM],
         out_specs=VMEM,
         out_shape=jax.ShapeDtypeStruct(weight.shape, BF16),
+        scratch_shapes=[
+            pltpu.VMEM(incoming.shape, BF16),
+            pltpu.VMEM(incoming.shape, BF16),
+            pltpu.SemaphoreType.DMA((2,)),
+        ],
         compiler_params=pltpu.CompilerParams(vmem_limit_bytes=BIG),
         cost_estimate=LIGHT,
     )(where, incoming, preact, weight)
@@ -128,14 +141,30 @@
     )(where, *arrays, *earlier)
 
 
-def gather_ring(where, block, axis, sections=(0, 1), earlier=()):
-    half = block.shape[0] // 2
-    wanted = None if len(sections) == 2 else sections[0]
-    after = ring_move(block, axis, -1, sections)
-    before = ring_move(block, axis, 1, sections)
-    far_low = ring_move(join(where, wanted, (after,), ((0, half),), *earlier), axis, -1, sections)
-    far_high = ring_move(join(where, wanted, (before,), ((half, half),), *earlier), axis, 1, sections)
-    return block, after, far_low, far_high, before
+def halves_kernel(after_ref, before_ref, low_ref, high_ref, sem):
+    half = low_ref.shape[0]
+    low = pltpu.make_async_copy(after_ref.at[pl.ds(0, half)], low_ref, sem.at[0])
+    high = pltpu.make_async_copy(before_ref.at[pl.ds(half, half)], high_ref, sem.at[1])
+    low.start()
+    high.start()
+    low.wait()
+    high.wait()
+
+
+def gather_ring(block, axis, *earlier):
+    rows, width = block.shape
+    after = ring_move(block, axis, -1)
+    before = ring_move(block, axis, 1)
+    low, high = pl.pallas_call(
+        in_order(halves_kernel, 2, len(earlier)),
+        in_specs=[ANY, ANY] + [ANY] * len(earlier),
+        out_specs=[VMEM, VMEM],
+        out_shape=[jax.ShapeDtypeStruct((rows // 2, width), BF16)] * 2,
+        scratch_shapes=[pltpu.SemaphoreType.DMA((2,))],
+        compiler_params=pltpu.CompilerParams(vmem_limit_bytes=BIG),
+        cost_estimate=LIGHT,
+    )(after, before, *earlier)
+    return block, after, ring_move(low, axis, -1), ring_move(high, axis, 1), before
 
 
 def make_dz(incoming, preact, b_both, c, *earlier):
@@ -164,7 +193,7 @@
 
 def top_product_kernel(rows, where_ref, *refs):
     dz_refs, w_refs = refs[:4], refs[4:9]
-    keep_ref, send_ref, dz_all, w_all, dz_sem, w_sem = refs[9:]
+    mine_ref, theirs_ref, send_ref, dz_all, w_all, dz_sem, w_sem = refs[9:]
 
     @pl.when(where_ref[3] == 1)
     def _():
@@ -195,9 +224,13 @@
             own_core = lax.rem(target, 2) == lax.rem(place, 2)
             far = jnp.where(target // 2 == place // 2, 0, 1)
 
-            @pl.when(own_core)
+            @pl.when(jnp.logical_and(own_core, far == 0))
             def _():
-                keep_ref[far] = value
+                mine_ref[...] = value
+
+            @pl.when(jnp.logical_and(own_core, far == 1))
+            def _():
+                theirs_ref[...] = value
 
             @pl.when(jnp.logical_not(own_core))
             def _():
@@ -209,8 +242,9 @@
     return pl.pallas_call(
         in_order(functools.partial(top_product_kernel, rows), 10, len(earlier)),
         in_specs=[SMEM] + [HBM] * 9 + [ANY] * len(earlier),
-        out_specs=[VMEM, VMEM],
-        out_shape=[jax.ShapeDtypeStruct((2, RING * rows, wide), BF16)] * 2,
+        out_specs=[VMEM, VMEM, VMEM],
+        out_shape=[jax.ShapeDtypeStruct((RING * rows, wide), BF16)] * 2
+        + [jax.ShapeDtypeStruct((2, RING * rows, wide), BF16)],
         scratch_shapes=[
             pltpu.VMEM((RING * rows, width), BF16),
             pltpu.VMEM((RING, wide, width), BF16),
@@ -253,14 +287,16 @@
 
 
 def low_product_kernel(plan, where_ref, table_ref, dz_ref, *refs):
-    count = len(refs) - 4
+    count = len(refs) - 7
     w_refs = refs[:count]
-    keep_ref, send_ref, w_all, sem = refs[count:]
+    mine_ref, theirs_ref, send_ref, dz_all, w_all, dz_sem, sem = refs[count:]
     steps, deep = w_all.shape[0], w_all.shape[1]
     wide = deep // 2
 
     @pl.when(where_ref[3] == 0)
     def _():
+        dz_copy = pltpu.make_async_copy(dz_ref, dz_all, dz_sem)
+        dz_copy.start()
         for array, row, at, rows in plan:
             while rows:
                 part = min(rows, deep - at % deep)
@@ -270,12 +306,13 @@
                     sem.at[at // deep],
                 ).start()
                 row, at, rows = row + part, at + part, rows - part
+        dz_copy.wait()
 
         @pl.loop(0, steps)
         def _(step):
             pltpu.make_async_copy(w_refs[0], w_all.at[step], sem.at[step]).wait()
             value = lax.dot_general(
-                dz_ref[...], w_all[step], (((1,), (1,)), ((), ())), preferred_element_type=F32
+                dz_all[...], w_all[step], (((1,), (1,)), ((), ())), preferred_element_type=F32
             ).astype(BF16)
             for k in range(2):
                 entry = table_ref[2 * step + k]
@@ -283,9 +320,13 @@
                 far = lax.rem(entry // (2 * RING), 2)
                 block = value[:, k * wide:(k + 1) * wide]
 
-                @pl.when(entry < 4 * RING)
+                @pl.when(entry < 2 * RING)
                 def _():
-                    keep_ref[far, :, columns] = block
+                    mine_ref[:, columns] = block
+
+                @pl.when(jnp.logical_and(entry >= 2 * RING, entry < 4 * RING))
+                def _():
+                    theirs_ref[:, columns] = block
 
                 @pl.when(entry >= 4 * RING)
                 def _():
@@ -305,11 +346,14 @@
     table = (other_core * 2 + other_pair) * 2 * RING + column
     return pl.pallas_call(
         in_order(functools.partial(low_product_kernel, copies), 3 + len(w_pieces), len(earlier)),
-        in_specs=[SMEM, SMEM, VMEM] + [HBM] * len(w_pieces) + [ANY] * len(earlier),
-        out_specs=[VMEM, VMEM],
-        out_shape=[jax.ShapeDtypeStruct((2, rows, 2 * RING * wide), BF16)] * 2,
+        in_specs=[SMEM, SMEM, HBM] + [HBM] * len(w_pieces) + [ANY] * len(earlier),
+        out_specs=[VMEM, VMEM, VMEM],
+        out_shape=[jax.ShapeDtypeStruct((rows, 2 * RING * wide), BF16)] * 2
+        + [jax.ShapeDtypeStruct((2, rows, 2 * RING * wide), BF16)],
         scratch_shapes=[
+            pltpu.VMEM((rows, width), BF16),
             pltpu.VMEM((RING * RING, shard, width), BF16),
+            pltpu.SemaphoreType.DMA,
             pltpu.SemaphoreType.DMA((RING * RING,)),
         ],
         compiler_params=pltpu.CompilerParams(vmem_limit_bytes=BIG),
@@ -320,17 +364,17 @@
 
 
 def add_kernel(keep_ref, got_ref, out_ref):
-    out_ref[...] = (keep_ref[0].astype(F32) + got_ref[0].astype(F32)).astype(BF16)
+    out_ref[...] = (keep_ref[...].astype(F32) + got_ref[0].astype(F32)).astype(BF16)
 
 
 def add_theirs(keep, got):
-    _, rows, wide = keep.shape
-    spec = pl.BlockSpec((1, rows, wide), lambda i: (1, 0, 0))
+    rows, wide = keep.shape
+    whole = pl.BlockSpec((rows, wide), lambda i: (0, 0))
     return pl.pallas_call(
         add_kernel,
         grid=(1,),
-        in_specs=[spec, spec],
-        out_specs=pl.BlockSpec((rows, wide), lambda i: (0, 0)),
+        in_specs=[whole, pl.BlockSpec((1, rows, wide), lambda i: (1, 0, 0))],
+        out_specs=whole,
         out_shape=jax.ShapeDtypeStruct((rows, wide), BF16),
         compiler_params=pltpu.CompilerParams(vmem_limit_bytes=BIG),
         cost_estimate=LIGHT,
@@ -342,22 +386,22 @@
     for i, ref in enumerate(out_refs):
         part = pl.ds(i * rows, rows)
         ref[...] = (
-            keep_ref[0, part].astype(F32) + got_ref[0, part].astype(F32) + other_ref[part].astype(F32)
+            keep_ref[part].astype(F32) + got_ref[0, part].astype(F32) + other_ref[part].astype(F32)
         ).astype(BF16)
 
 
-def add_mine(keep, got, other):
-    _, rows, wide = keep.shape
-    spec = pl.BlockSpec((1, rows, wide), lambda i: (0, 0, 0))
-    return pl.pallas_call(
-        total_kernel,
+def add_mine(keep, got, other, *earlier):
+    rows, wide = keep.shape
+    whole = pl.BlockSpec((rows, wide), lambda i: (0, 0))
+    return pl.pallas_call(
+        in_order(total_kernel, 3, len(earlier)),
         grid=(1,),
-        in_specs=[spec, spec, pl.BlockSpec((rows, wide), lambda i: (0, 0))],
+        in_specs=[whole, pl.BlockSpec((1, rows, wide), lambda i: (0, 0, 0)), whole] + [ANY] * len(earlier),
         out_specs=[pl.BlockSpec((rows // RING, wide), lambda i: (0, 0))] * RING,
         out_shape=[jax.ShapeDtypeStruct((rows // RING, wide), BF16)] * RING,
         compiler_params=pltpu.CompilerParams(vmem_limit_bytes=BIG),
         cost_estimate=LIGHT,
-    )(keep, got, other)
+    )(keep, got, other, *earlier)
 
 
 def as_row(column):
@@ -380,7 +424,7 @@
             mixed, a_ref[:, at], (((0,), (0,)), ((), ())), precision=HIGH, preferred_element_type=F32
         )
         scaled = gain_ref[:, at] * (piece[...].astype(F32) + low_rank)
-        scaled_ref[:, at] = scaled
+        scaled_ref[:, at] = scaled.astype(BF16)
         inner = inner + jnp.sum(scaled * hidden_ref[:, at].astype(F32), axis=1, keepdims=True)
     inner_ref[...] = as_row(inner * scale_ref[...])
 
@@ -391,7 +435,7 @@
         scaled_kernel,
         in_specs=[SMEM] + [VMEM] * 9,
         out_specs=[VMEM, VMEM],
-        out_shape=[jax.ShapeDtypeStruct((rows, width), F32), jax.ShapeDtypeStruct((8, rows), F32)],
+        out_shape=[jax.ShapeDtypeStruct((rows, width), BF16), jax.ShapeDtypeStruct((8, rows), F32)],
         compiler_params=pltpu.CompilerParams(vmem_limit_bytes=BIG),
         cost_estimate=LIGHT,
     )(where, *pieces, mixed, a_local, gain, hidden, scale)
@@ -401,9 +445,9 @@
     low_rank = lax.dot_general(
         mixed_ref[...], a_ref[...], (((0,), (0,)), ((), ())), precision=HIGH, preferred_element_type=F32
     )
-    total = keep_ref[0].astype(F32) + got_ref[0].astype(F32) + other_ref[...].astype(F32)
+    total = keep_ref[...].astype(F32) + got_ref[0].astype(F32) + other_ref[...].astype(F32)
     scaled = gain_ref[...] * (total + low_rank)
-    scaled_ref[...] = scaled
+    scaled_ref[...] = scaled.astype(BF16)
     inner = jnp.sum(scaled * hidden_ref[...].astype(F32), axis=1, keepdims=True)
     inner_ref[...] = as_row(inner * scale_ref[...])
 
@@ -416,11 +460,11 @@
         low_scaled_kernel,
         grid=(1,),
         in_specs=[
-            mine, mine, whole((rows, width)), whole((RANK, rows)), whole((RANK, width)),
+            whole((rows, width)), mine, whole((rows, width)), whole((RANK, rows)), whole((RANK, width)),
             whole((1, width)), whole((rows, width)), whole((rows, 1)),
         ],
         out_specs=[whole((rows, width)), whole((8, rows))],
-        out_shape=[jax.ShapeDtypeStruct((rows, width), F32), jax.ShapeDtypeStruct((8, rows), F32)],
+        out_shape=[jax.ShapeDtypeStruct((rows, width), BF16), jax.ShapeDtypeStruct((8, rows), F32)],
         compiler_params=pltpu.CompilerParams(vmem_limit_bytes=BIG),
         cost_estimate=LIGHT,
     )(keep, got, other, mixed, a_local, gain, hidden, scale)
@@ -431,7 +475,7 @@
     pull = as_column(inner_ref[...]) * scale / MODEL_WIDTH
     return (
         incoming_ref[...].astype(F32)
-        + scale * (scaled_ref[...] - hidden_ref[...].astype(F32) * pull)
+        + scale * (scaled_ref[...].astype(F32) - hidden_ref[...].astype(F32) * pull)
     ).astype(BF16)
 
 
@@ -599,33 +643,32 @@
     scale = scale_row.reshape(tokens, 1)
     top_mixed = sums[1 + RANK:]
 
-    z_ring = gather_ring(where, own_weight, "z", earlier=(scale,))
-    y_ring = gather_ring(where, first, "y", earlier=(scale,))
+    z_ring = gather_ring(own_weight, "z", scale)
+    y_ring = gather_ring(first, "y", scale)
+
+    _, z_after, z_far_low, z_far_high, z_before = z_ring
+    _, y_after, y_far_low, y_far_high, y_before = y_ring
+    slim, rest = half // 2, shard - half // 2
+    corner = join(where, 0, (z_far_low, z_far_high), ((0, half), (0, half)), y_far_high)
+    corner = ring_move(corner, "y", 2, (0,))
 
     dz_pieces = (y_ring[0], y_ring[1], y_ring[2], y_ring[4])
-    keep, send = top_product(where, tokens, dz_pieces, z_ring, y_ring[3])
+    mine, keep, send = top_product(where, tokens, dz_pieces, z_ring, y_far_high)
     got = swap(send, "core", (1,))
     theirs = add_theirs(keep, got)
     other = swap(theirs, "pair", (1,))
-
-    own, to_after, to_far, to_before = add_mine(keep, got, other)
+    along_z = join(
+        where, 0, (y_far_low, y_far_high, y_after, y_before),
+        ((0, half), (0, half), (slim, rest), (slim, rest)), theirs,
+    )
+    z_pair = (ring_move(along_z, "z", -1, (0,)), ring_move(along_z, "z", 1, (0,)))
+    own, to_after, to_far, to_before = add_mine(mine, got, other, corner)
     from_before = ring_move(to_after, "y", 1, (1,))
     from_far = ring_move(to_far, "y", 2, (1,))
     from_after = ring_move(to_before, "y", -1, (1,))
-
-    _, z_after, z_far_low, z_far_high, z_before = z_ring
-    _, y_after, y_far_low, y_far_high, y_before = y_ring
-    slim, rest = half // 2, shard - half // 2
-    corner = join(where, 0, (z_far_low, z_far_high), ((0, half), (0, half)), own)
-    corner = ring_move(corner, "y", 2, (0,))
-    along_z = join(
-        where, None, (y_far_low, y_far_high, y_after, y_before),
-        ((0, half), (0, half), (slim, rest), (slim, rest)), own,
-    )
-    z_pair = (ring_move(along_z, "z", -1), ring_move(along_z, "z", 1))
     along_y = join(
         where, 0, (z_far_low, z_far_high, z_after, z_before),
-        ((0, half), (0, half), (0, slim), (0, slim)), corner,
+        ((0, half), (0, half), (0, slim), (0, slim)), from_before, from_far, from_after,
     )
     y_pair = (ring_move(along_y, "y", -1, (0,)), ring_move(along_y, "y", 1, (0,)))
     w_pieces = (*z_ring, *y_ring[1:], corner, *y_pair, *z_pair)
@@ -637,11 +680,11 @@
 
     low_dz, part = make_dz(low_in, preact, b_both, 0)
     low_mixed = lax.psum(part, tensor)
-    keep, send = low_product(where, z, y, place, low_dz, w_pieces, low_mixed)
+    mine, keep, send = low_product(where, z, y, place, low_dz, w_pieces, low_mixed)
     got = swap(send, "core", (0,))
     theirs = add_theirs(keep, got)
     other = swap(theirs, "pair", (0,))
-    scaled, inner = low_scaled(keep, got, other, low_mixed, a_local, norm_gain, hidden, scale)
+    scaled, inner = low_scaled(mine, got, other, low_mixed, a_local, norm_gain, hidden, scale)
     result = finish_low(where, scaled, lax.psum(inner, tensor), hidden, scale, low_in, top_grad)
 
     grads = make_grads(

time: 329 us -> 300 us (0.912)
  starting transfers between devices: 55.4 us -> 44.6 us
  waiting for transfers between devices: 154 us -> 144 us
  Pallas kernels: 59.7 us -> 52.7 us
    ppermute x1, waiting for transfers between devices: 53.6 us -> 42.8 us  [shards(): low_in = lax.ppermute(top_grad, 'section', [(1, 0)])]
    ppermute x1, starting transfers between devices: 7.19 us -> 0.09 us  [shards(): other_share = lax.ppermute(share, 'section', [(0, 1), (1, 0)])]
    pallas_call x7 -> x3, Pallas kernels: 15.1 us -> 9.06 us  [join(): pl.pallas_call(in_order(functools.partial(join_kernel, wanted, parts), 1...]
    ppermute x22, starting transfers between devices: 35.4 us -> 31.4 us  [ring_move(): lax.ppermute(block, ('section', axis), ring_route(distance, sections))]
    unnamed x68 -> x72, local copies, waits for them, and re-layouts: 18.6 us -> 15.6 us
    pallas_call x5 -> x7, Pallas kernels: 10.3 us -> 11.9 us  [the longest x1 3.72 us: low_scaled(): pl.pallas_call(low_scaled_kernel, grid=(1,), in_specs=[whole((rows, width...]
  transfers between devices with their start and end apart: 30 -> 30, of which waited for: 17 -> 18; matrix products, arithmetic and copies ran while one was open for 2% -> 2% of each run, Pallas kernels for 10% -> 11%
where the time goes in v3:
time: 300 us; the launch traced here: 298 us
  waiting for transfers between devices  144 us (48%)
  Pallas kernels  52.7 us (18%)
  starting transfers between devices  44.6 us (15%)
  blocking collectives  34.1 us (11%)
  local copies, waits for them, and re-layouts  16.2 us (5%)
  matrix products  4.13 us (1%)
    ppermute x22, waiting for transfers between devices, ring_move(): lax.ppermute(block, ('section', axis), ring_route(distance, sections))  91.2 us
    ppermute x1, waiting for transfers between devices, shards(): low_in = lax.ppermute(top_grad, 'section', [(1, 0)])  42.8 us
    ppermute x22, starting transfers between devices, ring_move(): lax.ppermute(block, ('section', axis), ring_route(distance, sections))  31.4 us
    pallas_call x1, Pallas kernels, low_product(): pl.pallas_call(in_order(functools.partial(low_product_kernel, copies), 3...  16.4 us
    psum x2, blocking collectives, shards(): lax.psum(inner, tensor)  15.9 us
    unnamed x72, local copies, waits for them, and re-layouts  15.6 us
    ppermute x6, starting transfers between devices, swap(): return lax.ppermute(block, ('section', axis), pairs)  11.7 us
    psum x1, blocking collectives, shards(): lax.psum(jnp.concatenate([jnp.sum(hidden_f * hidden_f, axis=1)[None], jnp...  11 us
  transfers between devices with their start and end apart: 30, of which 18 were waited for; matrix products, arithmetic and copies ran while one was open for 2% of the time, Pallas kernels for 11%

profile of v3, /device:TPU:1, one launch (start us, length us, event | category | flops | bytes accessed | tf_op | source)
XLA Modules:
  0.0 298.0 jit_solution(6225854848726000008)
XLA Ops:
  0.6 4.7 %collective-permute-start.3 = (bf16[512,2048]{1,0:T(8,128)(2,1)}, bf16[512,2048]{1,0:T(8,128)(2,1)S(1)}, u32[]{:S(2)}, u32[]{:S(2)}) collective-permute-start(bf16[512,2048]{1,0:T(8,128)(2,1)} %bitcast.39), channel_id=1, source_target_pairs={{0,48},{16,0},{32,16},{48,32},{64,112},{80,64},{96,80},{112,96},{1... | collective-permute-start | bytes 6291464 | tf_op jit(solution)/shard_map/ppermute | solution.py:35
  7.8 3.5 %shard_map.122.refs_1_.refs_5_ = bf16[512,2048]{1,0:T(8,128)(2,1)} custom-call(s32[4]{0:T(128)S(1)} %pad_add_fusion.where_ref.refs_0_, bf16[256,2048]{1,0:T(8,128)(2,1)S(1)} %copy-done.16, bf16[256,2048]{1,0:T(8,128)(2,1)S(1)} %bitcast.35, bf16[512,2048]{1,0:T(8,128)(2,1)} %bitcast.41), custom_call_target="tpu_custom_call" | custom-call | bytes 1048576 | tf_op jit(solution)/shard_map/pallas_call | solution.py:95
  11.3 2.8 collective-permute-start
  15.2 2.1 fusion.4
  17.4 1.7 fusion
  19.2 11.0 %psum.28 = f32[9,256]{1,0:T(8,128)S(1)} all-reduce(f32[9,256]{1,0:T(8,128)S(1)} %pad_maximum_fusion.1), channel_id=1, replica_groups=mesh['section'=2,'z'=4,'y'=4,'pair'=2,'core'=2] {'pair','core'}, use_global_device_ids=true, to_apply=%region_2.0 | all-reduce | flops 2304 | bytes 18432 | tf_op jit(solution)/shard_map/psum | solution.py:630
  30.3 19.6 %collective-permute-done.3.refs_0_.refs_6_.refs_3_.refs_4_ = bf16[512,2048]{1,0:T(8,128)(2,1)S(1)} collective-permute-done((bf16[512,2048]{1,0:T(8,128)(2,1)}, bf16[512,2048]{1,0:T(8,128)(2,1)S(1)}, u32[]{:S(2)}, u32[]{:S(2)}) %collective-permute-start.3) | collective-permute-done | bytes 2097184 | tf_op jit(solution)/shard_map/ppermute | solution.py:35
  49.9 3.1 %collective-permute-done.4.refs_1_.refs_9_.refs_4_.refs_7_ = bf16[512,2048]{1,0:T(8,128)(2,1)} collective-permute-done((bf16[512,2048]{1,0:T(8,128)(2,1)}, bf16[512,2048]{1,0:T(8,128)(2,1)}, u32[]{:S(2)}, u32[]{:S(2)}) %collective-permute-start.4) | collective-permute-done | bytes 2097184 | tf_op jit(solution)/shard_map/ppermute | solution.py:35
  53.0 1.3 shard_map.124
  55.9 2.6 collective-permute-done.refs_0_.refs_2_.refs_3_.refs_8_
  58.4 3.1 %collective-permute-done.1.refs_1_.refs_4_.refs_11_ = bf16[512,2048]{1,0:T(8,128)(2,1)} collective-permute-done((bf16[512,2048]{1,0:T(8,128)(2,1)}, bf16[512,2048]{1,0:T(8,128)(2,1)}, u32[]{:S(2)}, u32[]{:S(2)}) %collective-permute-start.1) | collective-permute-done | bytes 2097184 | tf_op jit(solution)/shard_map/ppermute | solution.py:35
  61.6 1.6 shard_map.123
  63.2 2.7 collective-permute-start.2
  65.9 11.3 %collective-permute-done.5.refs_7_.refs_1_.refs_5_ = bf16[256,2048]{1,0:T(8,128)(2,1)S(1)} collective-permute-done((bf16[256,2048]{1,0:T(8,128)(2,1)S(1)}, bf16[256,2048]{1,0:T(8,128)(2,1)S(1)}, u32[]{:S(2)}, u32[]{:S(2)}) %collective-permute-start.5) | collective-permute-done | bytes 1048608 | tf_op jit(solution)/shard_map/ppermute | solution.py:35
  77.2 2.4 collective-permute-done.6.refs_8_.refs_2_.refs_6_
  79.6 7.3 %collective-permute-done.7.refs_10_.refs_3_.refs_2_ = bf16[256,2048]{1,0:T(8,128)(2,1)S(1)} collective-permute-done((bf16[256,2048]{1,0:T(8,128)(2,1)S(1)}, bf16[256,2048]{1,0:T(8,128)(2,1)S(1)}, u32[]{:S(2)}, u32[]{:S(2)}) %collective-permute-start.7) | collective-permute-done | bytes 1048608 | tf_op jit(solution)/shard_map/ppermute | solution.py:35
  87.9 2.0 shard_map.125
  92.6 2.1 collective-permute-start.10
  96.0 4.9 %shard_map.133 = bf16[1280,2048]{1,0:T(8,128)(2,1)} custom-call(s32[4]{0:T(128)S(1)} %pad_add_fusion.where_ref.refs_0_, bf16[256,2048]{1,0:T(8,128)(2,1)S(1)} %collective-permute-done.2.refs_3_.refs_1_.refs_9_, bf16[256,2048]{1,0:T(8,128)(2,1)S(1)} %copy-done.11, bf16[512,2048]{1,0:T(8,128)(2,1)} %collective-permute-done.refs_0_.refs_2_.refs_3_.refs_8_, ...), custom_call_target="tpu_custom_call" | custom-call | bytes 1048576 | tf_op jit(solution)/shard_map/pallas_call | solution.py:133
  100.9 4.0 %collective-permute-start.17 = (bf16[1280,2048]{1,0:T(8,128)(2,1)}, bf16[1280,2048]{1,0:T(8,128)(2,1)}, u32[]{:S(2)}, u32[]{:S(2)}) collective-permute-start(bf16[1280,2048]{1,0:T(8,128)(2,1)} %shard_map.133), channel_id=1, source_target_pairs={{0,48},{16,0},{32,16},{48,32},{1,49},{17,1},{33,17},{49,33},{2,50}... | collective-permute-start | bytes 15728648 | tf_op jit(solution)/shard_map/ppermute | solution.py:35
  104.9 1.9 collective-permute-start.18
  107.6 32.5 %collective-permute-done.10.refs_3_.refs_12_ = bf16[512,2048]{1,0:T(8,128)(2,1)S(1)} collective-permute-done((bf16[512,2048]{1,0:T(8,128)(2,1)S(1)}, bf16[512,2048]{1,0:T(8,128)(2,1)S(1)}, u32[]{:S(2)}, u32[]{:S(2)}) %collective-permute-start.10) | collective-permute-done | bytes 2097184 | tf_op jit(solution)/shard_map/ppermute | solution.py:35
  140.1 1.4 copy-done.28
  145.3 3.5 %shard_map.132 = bf16[768,2048]{1,0:T(8,128)(2,1)} custom-call(s32[4]{0:T(128)S(1)} %pad_add_fusion.where_ref.refs_0_, bf16[256,2048]{1,0:T(8,128)(2,1)S(1)} %collective-permute-done.5.refs_7_.refs_1_.refs_5_, bf16[256,2048]{1,0:T(8,128)(2,1)S(1)} %collective-permute-done.6.refs_8_.refs_2_.refs_6_, bf16[512,2048]{1,0:T(8,128)(2,1)S(1)} %copy-done.4, ...), custom_call_target="tpu_custom_call" | custom-call | bytes 1048576 | tf_op jit(solution)/shard_map/pallas_call | solution.py:133
  148.8 3.2 %collective-permute-start.15 = (bf16[768,2048]{1,0:T(8,128)(2,1)}, bf16[768,2048]{1,0:T(8,128)(2,1)}, u32[]{:S(2)}, u32[]{:S(2)}) collective-permute-start(bf16[768,2048]{1,0:T(8,128)(2,1)} %shard_map.132), channel_id=1, source_target_pairs={{0,12},{4,0},{8,4},{12,8},{1,13},{5,1},{9,5},{13,9},{2,14},{6,2},{... | collective-permute-start | bytes 9437192 | tf_op jit(solution)/shard_map/ppermute | solution.py:35
  152.0 2.4 collective-permute-start.16
  154.4 2.7 shard_map.129
  157.1 9.7 %psum.29.inner_ref = f32[8,256]{1,0:T(8,128)S(1)} all-reduce(f32[8,256]{1,0:T(8,128)S(1)} %get-tuple-element.34), channel_id=1, replica_groups=mesh['section'=2,'z'=4,'y'=4,'pair'=2,'core'=2] {'pair','core'}, use_global_device_ids=true, to_apply=%region_3.0 | all-reduce | flops 2048 | bytes 16384 | tf_op jit(solution)/shard_map/psum | solution.py:678
  166.9 1.6 shard_map.130.top_ref
  168.5 1.4 collective-permute-start.14
  170.0 42.8 %collective-permute-done.14.refs_0_.incoming_ref = bf16[256,2048]{1,0:T(8,128)(2,1)} collective-permute-done((bf16[256,2048]{1,0:T(8,128)(2,1)}, bf16[256,2048]{1,0:T(8,128)(2,1)}, u32[]{:S(2)}, u32[]{:S(2)}) %collective-permute-start.14) | collective-permute-done | bytes 1048608 | tf_op jit(solution)/shard_map/ppermute | solution.py:679
  214.1 2.1 shard_map.131
  217.2 7.2 %psum.30.refs_17_.mixed_ref.refs_8_ = f32[4,256]{1,0:T(4,128)S(1)} all-reduce(f32[4,256]{1,0:T(4,128)S(1)} %get-tuple-element.36), channel_id=1, replica_groups=mesh['section'=2,'z'=4,'y'=4,'pair'=2,'core'=2] {'pair','core'}, use_global_device_ids=true, to_apply=%region_4.0 | all-reduce | flops 1024 | bytes 8192 | tf_op jit(solution)/shard_map/psum | solution.py:682
  225.7 16.4 %shard_map.134 = (bf16[256,2048]{1,0:T(8,128)(2,1)S(1)}, bf16[256,2048]{1,0:T(8,128)(2,1)S(1)}, bf16[2,256,2048]{2,1,0:T(8,128)(2,1)}) custom-call(s32[4]{0:T(128)S(1)} %pad_add_fusion.where_ref.refs_0_, s32[32]{0:T(128)S(1)} %fusion.16.refs_1_, bf16[256,2048]{1,0:T(8,128)(2,1)S(1)} %copy-done.19, bf16[512,2048]{1,0:T(8,128)(2,1)} %bitcast.43, ...), custom_call_target="tpu_custom_call" | custom-call | flops 8589934592 | bytes 33554432 | tf_op jit(solution)/shard_map/pallas_call | solution.py:347
  243.1 3.4 %collective-permute-start.19 = (bf16[2,256,2048]{2,1,0:T(8,128)(2,1)}, bf16[2,256,2048]{2,1,0:T(8,128)(2,1)S(1)}, u32[]{:S(2)}, u32[]{:S(2)}) collective-permute-start(bf16[2,256,2048]{2,1,0:T(8,128)(2,1)} %get-tuple-element.38.refs_4_), channel_id=1, source_target_pairs={{0,1},{1,0},{2,3},{3,2},{4,5},{5,4},{6,7},{7,6},{8,9},{9,8},{10,11... | collective-permute-start | bytes 6291464 | tf_op jit(solution)/shard_map/ppermute | solution.py:40
  246.5 4.0 %collective-permute-done.19.got_ref = bf16[2,256,2048]{2,1,0:T(8,128)(2,1)S(1)} collective-permute-done((bf16[2,256,2048]{2,1,0:T(8,128)(2,1)}, bf16[2,256,2048]{2,1,0:T(8,128)(2,1)S(1)}, u32[]{:S(2)}, u32[]{:S(2)}) %collective-permute-start.19) | collective-permute-done | bytes 2097184 | tf_op jit(solution)/shard_map/ppermute | solution.py:40
  252.1 3.1 %collective-permute-start.20 = (bf16[256,2048]{1,0:T(8,128)(2,1)}, bf16[256,2048]{1,0:T(8,128)(2,1)}, u32[]{:S(2)}, u32[]{:S(2)}) collective-permute-start(bf16[256,2048]{1,0:T(8,128)(2,1)} %shard_map.135.refs_5_), channel_id=1, source_target_pairs={{0,2},{2,0},{1,3},{3,1},{4,6},{6,4},{5,7},{7,5},{8,10},{10,8},{9,1... | collective-permute-start | bytes 3145736 | tf_op jit(solution)/shard_map/ppermute | solution.py:40
  255.3 2.4 shard_map.138.refs_0_
  257.7 1.4 collective-permute-start.22
  259.2 2.0 collective-permute-done.21.refs_1_
  262.4 1.7 collective-permute-done.23.refs_3_
  264.2 1.7 collective-permute-start.24
  267.8 2.8 collective-permute-done.25.refs_3_
  271.3 2.9 collective-permute-start.27
  276.2 5.2 %collective-permute-done.28.refs_1_ = bf16[256,256]{1,0:T(8,128)(2,1)S(1)} collective-permute-done((bf16[256,256]{1,0:T(8,128)(2,1)S(1)}, bf16[256,256]{1,0:T(8,128)(2,1)S(1)}, u32[]{:S(2)}, u32[]{:S(2)}) %collective-permute-start.28) | collective-permute-done | bytes 131104 | tf_op jit(solution)/shard_map/ppermute | solution.py:40
  282.8 3.7 %shard_map.136 = (bf16[256,2048]{1,0:T(8,128)(2,1)S(1)}, f32[8,256]{1,0:T(8,128)S(1)}) custom-call(bf16[256,2048]{1,0:T(8,128)(2,1)S(1)} %copy-done.24, bf16[2,256,2048]{2,1,0:T(8,128)(2,1)} %copy-done.12, bf16[256,2048]{1,0:T(8,128)(2,1)} %collective-permute-done.20.other_ref, f32[4,256]{1,0:T(4,128)S(1)} %psum.30.refs_17_.mixed_ref.refs_8_, ...), custom_call_target="tpu_custom_call" | custom-call | bytes 1048576 | tf_op jit(solution)/shard_map/pallas_call | solution.py:459
  286.5 6.3 %psum.31.inner_ref = f32[8,256]{1,0:T(8,128)S(1)} all-reduce(f32[8,256]{1,0:T(8,128)S(1)} %get-tuple-element.41), channel_id=1, replica_groups=mesh['section'=2,'z'=4,'y'=4,'pair'=2,'core'=2] {'pair','core'}, use_global_device_ids=true, to_apply=%region_5.6 | all-reduce | flops 2048 | bytes 16384 | tf_op jit(solution)/shard_map/psum | solution.py:688
  292.8 3.3 %shard_map.137.refs_2_ = bf16[256,2048]{1,0:T(8,128)(2,1)} custom-call(s32[4]{0:T(128)S(1)} %pad_add_fusion.where_ref.refs_0_, bf16[256,2048]{1,0:T(8,128)(2,1)S(1)} %get-tuple-element.40.scaled_ref, f32[8,256]{1,0:T(8,128)S(1)} %psum.31.inner_ref, bf16[256,2048]{1,0:T(8,128)(2,1)S(1)} %bitcast.34, f32[256,1]{1,0:T(8,128)S(1)} %copy.28.refs_2_.scale_ref, ...), custom_call_target="tpu_custom_call" | custom-call | bytes 1048576 | tf_op jit(solution)/shard_map/pallas_call | solution.py:517
  (135 shorter events, 30.2 us)
Async XLA Ops:
  0.6 14.0 %copy-start = (f32[256,256]{1,0:T(8,128)S(1)}, f32[256,256]{1,0:T(8,128)}, u32[]{:S(2)}) copy-start(f32[256,256]{1,0:T(8,128)} %param.15) | copy-start | bytes 786436
  0.6 49.3 %collective-permute-start.3 = (bf16[512,2048]{1,0:T(8,128)(2,1)}, bf16[512,2048]{1,0:T(8,128)(2,1)S(1)}, u32[]{:S(2)}, u32[]{:S(2)}) collective-permute-start(bf16[512,2048]{1,0:T(8,128)(2,1)} %bitcast.39), channel_id=1, source_target_pairs={{0,48},{16,0},{32,16},{48,32},{64,112},{80,64},{96,80},{112,96},{1... | collective-permute-start | bytes 6291464 | tf_op jit(solution)/shard_map/ppermute | solution.py:35
  5.3 47.7 %collective-permute-start.4 = (bf16[512,2048]{1,0:T(8,128)(2,1)}, bf16[512,2048]{1,0:T(8,128)(2,1)}, u32[]{:S(2)}, u32[]{:S(2)}) collective-permute-start(bf16[512,2048]{1,0:T(8,128)(2,1)} %bitcast.40), channel_id=1, source_target_pairs={{0,16},{16,32},{32,48},{48,0},{64,80},{80,96},{96,112},{112,64},{1... | collective-permute-start | bytes 6291464 | tf_op jit(solution)/shard_map/ppermute | solution.py:35
  7.8 6.3 %copy-start.31 = (s32[1,2,128,2]{2,3,1,0:T(2,128)S(1)}, s32[1,2,128,2]{2,3,1,0:T(2,128)}, u32[]{:S(2)}) copy-start(s32[1,2,128,2]{2,3,1,0:T(2,128)} %param.16) | copy-start | bytes 6148
  7.8 6.5 %copy-start.32 = (f32[1,2,128,2]{2,3,1,0:T(2,128)S(1)}, f32[1,2,128,2]{2,3,1,0:T(2,128)}, u32[]{:S(2)}) copy-start(f32[1,2,128,2]{2,3,1,0:T(2,128)} %param.17) | copy-start | bytes 6148
  7.8 7.1 %copy-start.2 = (bf16[1,256,2048]{2,1,0:T(8,128)(2,1)S(1)}, bf16[1,256,2048]{2,1,0:T(8,128)(2,1)}, u32[]{:S(2)}) copy-start(bf16[1,256,2048]{2,1,0:T(8,128)(2,1)} %param.11) | copy-start | bytes 3145732
  11.3 6.0 %copy-start.27 = (f32[1,2048]{1,0:T(1,128)S(1)}, f32[1,2048]{1,0:T(1,128)}, u32[]{:S(2)}) copy-start(f32[1,2048]{1,0:T(1,128)} %refs_3_.1) | copy-start | bytes 24580
  11.3 47.1 %collective-permute-start = (bf16[512,2048]{1,0:T(8,128)(2,1)}, bf16[512,2048]{1,0:T(8,128)(2,1)}, u32[]{:S(2)}, u32[]{:S(2)}) collective-permute-start(bf16[512,2048]{1,0:T(8,128)(2,1)} %shard_map.122.refs_1_.refs_5_), channel_id=1, source_target_pairs={{0,12},{4,0},{8,4},{12,8},{64,76},{68,64},{72,68},{76,72},{1,13},{... | collective-permute-start | bytes 6291464 | tf_op jit(solution)/shard_map/ppermute | solution.py:35
  14.1 47.4 %collective-permute-start.1 = (bf16[512,2048]{1,0:T(8,128)(2,1)}, bf16[512,2048]{1,0:T(8,128)(2,1)}, u32[]{:S(2)}, u32[]{:S(2)}) collective-permute-start(bf16[512,2048]{1,0:T(8,128)(2,1)} %shard_map.122.refs_1_.refs_5_), channel_id=1, source_target_pairs={{0,4},{4,8},{8,12},{12,0},{64,68},{68,72},{72,76},{76,64},{1,5},{5... | collective-permute-start | bytes 6291464 | tf_op jit(solution)/shard_map/ppermute | solution.py:35
  14.6 15.5 %copy-start.29 = (f32[2,4,8,256]{3,2,1,0:T(8,128)}, f32[2,4,8,256]{3,2,1,0:T(8,128)S(1)}, u32[]{:S(2)}) copy-start(f32[2,4,8,256]{3,2,1,0:T(8,128)S(1)} %select_reduce_fusion) | copy-start | bytes 196612
  49.9 4.4 %copy-start.3 = (bf16[512,2048]{1,0:T(8,128)(2,1)}, bf16[512,2048]{1,0:T(8,128)(2,1)S(1)}, u32[]{:S(2)}) copy-start(bf16[512,2048]{1,0:T(8,128)(2,1)S(1)} %collective-permute-done.3.refs_0_.refs_6_.refs_3_.refs_4_) | copy-start | bytes 6291460
  54.3 22.9 %collective-permute-start.5 = (bf16[256,2048]{1,0:T(8,128)(2,1)S(1)}, bf16[256,2048]{1,0:T(8,128)(2,1)S(1)}, u32[]{:S(2)}, u32[]{:S(2)}) collective-permute-start(bf16[256,2048]{1,0:T(8,128)(2,1)S(1)} %get-tuple-element.23), channel_id=1, source_target_pairs={{0,48},{16,0},{32,16},{48,32},{64,112},{80,64},{96,80},{112,96},{1... | collective-permute-start | bytes 3145736 | tf_op jit(solution)/shard_map/ppermute | solution.py:35
  55.4 24.1 %collective-permute-start.6 = (bf16[256,2048]{1,0:T(8,128)(2,1)S(1)}, bf16[256,2048]{1,0:T(8,128)(2,1)S(1)}, u32[]{:S(2)}, u32[]{:S(2)}) collective-permute-start(bf16[256,2048]{1,0:T(8,128)(2,1)S(1)} %get-tuple-element.24), channel_id=1, source_target_pairs={{0,16},{16,32},{32,48},{48,0},{64,80},{80,96},{96,112},{112,64},{1... | collective-permute-start | bytes 3145736 | tf_op jit(solution)/shard_map/ppermute | solution.py:35
  63.1 23.8 %collective-permute-start.7 = (bf16[256,2048]{1,0:T(8,128)(2,1)S(1)}, bf16[256,2048]{1,0:T(8,128)(2,1)S(1)}, u32[]{:S(2)}, u32[]{:S(2)}) collective-permute-start(bf16[256,2048]{1,0:T(8,128)(2,1)S(1)} %get-tuple-element.25), channel_id=1, source_target_pairs={{0,4},{4,8},{8,12},{12,0},{64,68},{68,72},{72,76},{76,64},{1,5},{5... | collective-permute-start | bytes 3145736 | tf_op jit(solution)/shard_map/ppermute | solution.py:35
  63.2 23.7 %collective-permute-start.2 = (bf16[256,2048]{1,0:T(8,128)(2,1)S(1)}, bf16[256,2048]{1,0:T(8,128)(2,1)S(1)}, u32[]{:S(2)}, u32[]{:S(2)}) collective-permute-start(bf16[256,2048]{1,0:T(8,128)(2,1)S(1)} %get-tuple-element.22), channel_id=1, source_target_pairs={{0,12},{4,0},{8,4},{12,8},{64,76},{68,64},{72,68},{76,72},{1,13},{... | collective-permute-start | bytes 3145736 | tf_op jit(solution)/shard_map/ppermute | solution.py:35
  77.2 68.0 %copy-start.5 = (bf16[256,2048]{1,0:T(8,128)(2,1)}, bf16[256,2048]{1,0:T(8,128)(2,1)S(1)}, u32[]{:S(2)}) copy-start(bf16[256,2048]{1,0:T(8,128)(2,1)S(1)} %collective-permute-done.5.refs_7_.refs_1_.refs_5_) | copy-start | bytes 3145732
  79.6 65.7 %copy-start.7 = (bf16[256,2048]{1,0:T(8,128)(2,1)}, bf16[256,2048]{1,0:T(8,128)(2,1)S(1)}, u32[]{:S(2)}) copy-start(bf16[256,2048]{1,0:T(8,128)(2,1)S(1)} %collective-permute-done.6.refs_8_.refs_2_.refs_6_) | copy-start | bytes 3145732
  87.9 7.2 %copy-start.13 = (bf16[256,2048]{1,0:T(8,128)(2,1)}, bf16[256,2048]{1,0:T(8,128)(2,1)S(1)}, u32[]{:S(2)}) copy-start(bf16[256,2048]{1,0:T(8,128)(2,1)S(1)} %collective-permute-done.2.refs_3_.refs_1_.refs_9_) | copy-start | bytes 3145732
  89.9 4.9 %collective-permute-start.8 = (bf16[2,1024,512]{2,1,0:T(8,128)(2,1)}, bf16[2,1024,512]{2,1,0:T(8,128)(2,1)S(1)}, u32[]{:S(2)}, u32[]{:S(2)}) collective-permute-start(bf16[2,1024,512]{2,1,0:T(8,128)(2,1)} %get-tuple-element.27), channel_id=1, source_target_pairs={{64,65},{65,64},{66,67},{67,66},{68,69},{69,68},{70,71},{71,70},{7... | collective-permute-start | bytes 6291464 | tf_op jit(solution)/shard_map/ppermute | solution.py:40
  92.6 47.4 %collective-permute-start.10 = (bf16[512,2048]{1,0:T(8,128)(2,1)S(1)}, bf16[512,2048]{1,0:T(8,128)(2,1)S(1)}, u32[]{:S(2)}, u32[]{:S(2)}) collective-permute-start(bf16[512,2048]{1,0:T(8,128)(2,1)S(1)} %shard_map.127), channel_id=1, source_target_pairs={{0,8},{4,12},{8,0},{12,4},{1,9},{5,13},{9,1},{13,5},{2,10},{6,14},... | collective-permute-start | bytes 6291464 | tf_op jit(solution)/shard_map/ppermute | solution.py:35
  100.9 123.6 %collective-permute-start.17 = (bf16[1280,2048]{1,0:T(8,128)(2,1)}, bf16[1280,2048]{1,0:T(8,128)(2,1)}, u32[]{:S(2)}, u32[]{:S(2)}) collective-permute-start(bf16[1280,2048]{1,0:T(8,128)(2,1)} %shard_map.133), channel_id=1, source_target_pairs={{0,48},{16,0},{32,16},{48,32},{1,49},{17,1},{33,17},{49,33},{2,50}... | collective-permute-start | bytes 15728648 | tf_op jit(solution)/shard_map/ppermute | solution.py:35
  104.9 119.5 %collective-permute-start.18 = (bf16[1280,2048]{1,0:T(8,128)(2,1)}, bf16[1280,2048]{1,0:T(8,128)(2,1)}, u32[]{:S(2)}, u32[]{:S(2)}) collective-permute-start(bf16[1280,2048]{1,0:T(8,128)(2,1)} %shard_map.133), channel_id=1, source_target_pairs={{0,16},{16,32},{32,48},{48,0},{1,17},{17,33},{33,49},{49,1},{2,18}... | collective-permute-start | bytes 15728648 | tf_op jit(solution)/shard_map/ppermute | solution.py:35
  106.8 33.2 %collective-permute-start.9 = (bf16[1024,512]{1,0:T(8,128)(2,1)S(1)}, bf16[1024,512]{1,0:T(8,128)(2,1)S(1)}, u32[]{:S(2)}, u32[]{:S(2)}) collective-permute-start(bf16[1024,512]{1,0:T(8,128)(2,1)S(1)} %shard_map.126.refs_5_), channel_id=1, source_target_pairs={{64,66},{66,64},{65,67},{67,65},{68,70},{70,68},{69,71},{71,69},{7... | collective-permute-start | bytes 3145736 | tf_op jit(solution)/shard_map/ppermute | solution.py:40
  143.0 2.2 collective-permute-start.11
  143.8 1.4 collective-permute-start.12
  144.5 0.7 collective-permute-start.13
  148.8 18.1 %copy-start.17 = (bf16[256,2048]{1,0:T(8,128)(2,1)S(1)}, bf16[256,2048]{1,0:T(8,128)(2,1)}, u32[]{:S(2)}) copy-start(bf16[256,2048]{1,0:T(8,128)(2,1)} %incoming_ref.3) | copy-start | bytes 3145732
  148.8 75.7 %collective-permute-start.15 = (bf16[768,2048]{1,0:T(8,128)(2,1)}, bf16[768,2048]{1,0:T(8,128)(2,1)}, u32[]{:S(2)}, u32[]{:S(2)}) collective-permute-start(bf16[768,2048]{1,0:T(8,128)(2,1)} %shard_map.132), channel_id=1, source_target_pairs={{0,12},{4,0},{8,4},{12,8},{1,13},{5,1},{9,5},{13,9},{2,14},{6,2},{... | collective-permute-start | bytes 9437192 | tf_op jit(solution)/shard_map/ppermute | solution.py:35
  152.0 72.5 %collective-permute-start.16 = (bf16[768,2048]{1,0:T(8,128)(2,1)}, bf16[768,2048]{1,0:T(8,128)(2,1)}, u32[]{:S(2)}, u32[]{:S(2)}) collective-permute-start(bf16[768,2048]{1,0:T(8,128)(2,1)} %shard_map.132), channel_id=1, source_target_pairs={{0,4},{4,8},{8,12},{12,0},{1,5},{5,9},{9,13},{13,1},{2,6},{6,10},{... | collective-permute-start | bytes 9437192 | tf_op jit(solution)/shard_map/ppermute | solution.py:35
  166.8 3.1 %copy-start.33 = (s32[32]{0:T(128)S(1)}, s32[32]{0:T(128)}, u32[]{:S(2)}) copy-start(s32[32]{0:T(128)} %constant.100.clone) | copy-start | bytes 388
  168.5 56.0 %copy-start.6 = (bf16[256,2048]{1,0:T(8,128)(2,1)S(1)}, bf16[256,2048]{1,0:T(8,128)(2,1)}, u32[]{:S(2)}) copy-start(bf16[256,2048]{1,0:T(8,128)(2,1)} %copy-done.5) | copy-start | bytes 3145732
  168.5 56.0 %copy-start.8 = (bf16[256,2048]{1,0:T(8,128)(2,1)S(1)}, bf16[256,2048]{1,0:T(8,128)(2,1)}, u32[]{:S(2)}) copy-start(bf16[256,2048]{1,0:T(8,128)(2,1)} %copy-done.7) | copy-start | bytes 3145732
  168.5 44.4 %collective-permute-start.14 = (bf16[256,2048]{1,0:T(8,128)(2,1)}, bf16[256,2048]{1,0:T(8,128)(2,1)}, u32[]{:S(2)}, u32[]{:S(2)}) collective-permute-start(bf16[256,2048]{1,0:T(8,128)(2,1)} %shard_map.130.top_ref), channel_id=1, source_target_pairs={{64,0},{65,1},{66,2},{67,3},{68,4},{69,5},{70,6},{71,7},{72,8},{73... | collective-permute-start | bytes 3145736 | tf_op jit(solution)/shard_map/ppermute | solution.py:679
  243.1 7.3 %collective-permute-start.19 = (bf16[2,256,2048]{2,1,0:T(8,128)(2,1)}, bf16[2,256,2048]{2,1,0:T(8,128)(2,1)S(1)}, u32[]{:S(2)}, u32[]{:S(2)}) collective-permute-start(bf16[2,256,2048]{2,1,0:T(8,128)(2,1)} %get-tuple-element.38.refs_4_), channel_id=1, source_target_pairs={{0,1},{1,0},{2,3},{3,2},{4,5},{5,4},{6,7},{7,6},{8,9},{9,8},{10,11... | collective-permute-start | bytes 6291464 | tf_op jit(solution)/shard_map/ppermute | solution.py:40
  250.4 4.8 %copy-start.20 = (bf16[256,2048]{1,0:T(8,128)(2,1)S(1)}, bf16[256,2048]{1,0:T(8,128)(2,1)}, u32[]{:S(2)}) copy-start(bf16[256,2048]{1,0:T(8,128)(2,1)} %copy-done.18) | copy-start | bytes 3145732
  252.1 29.4 %collective-permute-start.20 = (bf16[256,2048]{1,0:T(8,128)(2,1)}, bf16[256,2048]{1,0:T(8,128)(2,1)}, u32[]{:S(2)}, u32[]{:S(2)}) collective-permute-start(bf16[256,2048]{1,0:T(8,128)(2,1)} %shard_map.135.refs_5_), channel_id=1, source_target_pairs={{0,2},{2,0},{1,3},{3,1},{4,6},{6,4},{5,7},{7,5},{8,10},{10,8},{9,1... | collective-permute-start | bytes 3145736 | tf_op jit(solution)/shard_map/ppermute | solution.py:40
  255.3 8.9 %copy-start.22 = (bf16[2,256,2048]{2,1,0:T(8,128)(2,1)S(1)}, bf16[2,256,2048]{2,1,0:T(8,128)(2,1)}, u32[]{:S(2)}) copy-start(bf16[2,256,2048]{2,1,0:T(8,128)(2,1)} %get-tuple-element.38.refs_4_) | copy-start | bytes 6291460
  257.7 8.9 %copy-start.30 = (f32[2,4,8,256]{3,2,1,0:T(8,128)S(1)}, f32[2,4,8,256]{3,2,1,0:T(8,128)}, u32[]{:S(2)}) copy-start(f32[2,4,8,256]{3,2,1,0:T(8,128)} %copy-done.29) | copy-start | bytes 196612
  257.7 3.6 %collective-permute-start.21 = (f32[8,2048]{1,0:T(8,128)S(1)}, f32[8,2048]{1,0:T(8,128)S(1)}, u32[]{:S(2)}, u32[]{:S(2)}) collective-permute-start(f32[8,2048]{1,0:T(8,128)S(1)} %shard_map.138.refs_0_), channel_id=1, source_target_pairs={{0,12},{4,0},{8,4},{12,8},{64,76},{68,64},{72,68},{76,72},{1,13},{... | collective-permute-start | bytes 196616 | tf_op jit(solution)/shard_map/ppermute | solution.py:35
  257.7 4.7 %collective-permute-start.22 = (f32[8,2048]{1,0:T(8,128)S(1)}, f32[8,2048]{1,0:T(8,128)S(1)}, u32[]{:S(2)}, u32[]{:S(2)}) collective-permute-start(f32[8,2048]{1,0:T(8,128)S(1)} %shard_map.138.refs_0_), channel_id=1, source_target_pairs={{0,8},{4,12},{8,0},{12,4},{64,72},{68,76},{72,64},{76,68},{1,9},{5... | collective-permute-start | bytes 196616 | tf_op jit(solution)/shard_map/ppermute | solution.py:35
  259.2 5.0 %collective-permute-start.23 = (f32[8,2048]{1,0:T(8,128)S(1)}, f32[8,2048]{1,0:T(8,128)S(1)}, u32[]{:S(2)}, u32[]{:S(2)}) collective-permute-start(f32[8,2048]{1,0:T(8,128)S(1)} %shard_map.138.refs_0_), channel_id=1, source_target_pairs={{0,4},{4,8},{8,12},{12,0},{64,68},{68,72},{72,76},{76,64},{1,5},{5... | collective-permute-start | bytes 196616 | tf_op jit(solution)/shard_map/ppermute | solution.py:35
  264.2 3.6 %collective-permute-start.24 = (f32[8,2048]{1,0:T(8,128)S(1)}, f32[8,2048]{1,0:T(8,128)S(1)}, u32[]{:S(2)}, u32[]{:S(2)}) collective-permute-start(f32[8,2048]{1,0:T(8,128)S(1)} %shard_map.139.refs_1_), channel_id=1, source_target_pairs={{0,48},{16,0},{32,16},{48,32},{64,112},{80,64},{96,80},{112,96},{1... | collective-permute-start | bytes 196616 | tf_op jit(solution)/shard_map/ppermute | solution.py:35
  265.9 4.7 %collective-permute-start.25 = (f32[8,2048]{1,0:T(8,128)S(1)}, f32[8,2048]{1,0:T(8,128)S(1)}, u32[]{:S(2)}, u32[]{:S(2)}) collective-permute-start(f32[8,2048]{1,0:T(8,128)S(1)} %shard_map.139.refs_1_), channel_id=1, source_target_pairs={{0,32},{16,48},{32,0},{48,16},{64,96},{80,112},{96,64},{112,80},{1... | collective-permute-start | bytes 196616 | tf_op jit(solution)/shard_map/ppermute | solution.py:35
  265.9 5.0 %collective-permute-start.26 = (f32[8,2048]{1,0:T(8,128)S(1)}, f32[8,2048]{1,0:T(8,128)S(1)}, u32[]{:S(2)}, u32[]{:S(2)}) collective-permute-start(f32[8,2048]{1,0:T(8,128)S(1)} %shard_map.139.refs_1_), channel_id=1, source_target_pairs={{0,16},{16,32},{32,48},{48,0},{64,80},{80,96},{96,112},{112,64},{1... | collective-permute-start | bytes 196616 | tf_op jit(solution)/shard_map/ppermute | solution.py:35
  271.3 4.1 %collective-permute-start.27 = (f32[256,256]{1,0:T(8,128)S(1)}, f32[256,256]{1,0:T(8,128)S(1)}, u32[]{:S(2)}, u32[]{:S(2)}) collective-permute-start(f32[256,256]{1,0:T(8,128)S(1)} %shard_map.140.refs_0_), channel_id=1, source_target_pairs={{0,1},{1,0},{64,65},{65,64},{2,3},{3,2},{66,67},{67,66},{4,5},{5,4... | collective-permute-start | bytes 786440 | tf_op jit(solution)/shard_map/ppermute | solution.py:40
  275.4 6.0 %collective-permute-start.28 = (bf16[256,256]{1,0:T(8,128)(2,1)S(1)}, bf16[256,256]{1,0:T(8,128)(2,1)S(1)}, u32[]{:S(2)}, u32[]{:S(2)}) collective-permute-start(bf16[256,256]{1,0:T(8,128)(2,1)S(1)} %shard_map.141.refs_0_), channel_id=1, source_target_pairs={{0,2},{2,0},{64,66},{66,64},{1,3},{3,1},{65,67},{67,65},{4,6},{6,4... | collective-permute-start | bytes 393224 | tf_op jit(solution)/shard_map/ppermute | solution.py:40
  281.5 14.6 %collective-permute-start.29 = (bf16[256,256]{1,0:T(8,128)(2,1)S(1)}, bf16[256,256]{1,0:T(8,128)(2,1)S(1)}, u32[]{:S(2)}, u32[]{:S(2)}) collective-permute-start(bf16[256,256]{1,0:T(8,128)(2,1)S(1)} %shard_map.142.refs_0_), channel_id=1, source_target_pairs={{0,64},{64,0},{1,65},{65,1},{2,66},{66,2},{3,67},{67,3},{4,68},{68... | collective-permute-start | bytes 393224 | tf_op jit(solution)/shard_map/ppermute | solution.py:707
  292.8 5.2 %copy-start.1 = (f32[256,256]{1,0:T(8,128)S(1)}, f32[256,256]{1,0:T(8,128)}, u32[]{:S(2)}) copy-start(f32[256,256]{1,0:T(8,128)} %param.15) | copy-start | bytes 786436
  (18 other events, 28.6 us)

commit v4 on v3

--- a/solution.py
+++ b/solution.py
@@ -24,6 +24,8 @@
 VMEM = pl.BlockSpec(memory_space=pltpu.VMEM)
 HBM = pl.BlockSpec(memory_space=pltpu.HBM)
 BIG = 48 * 1024 * 1024
+MEDIUM = 20 * 1024 * 1024
+SMALL = 12 * 1024 * 1024
 LIGHT = pl.CostEstimate(flops=0, bytes_accessed=2 ** 20, transcendentals=0)
 
 
@@ -102,41 +104,46 @@
             pltpu.VMEM(incoming.shape, BF16),
             pltpu.SemaphoreType.DMA((2,)),
         ],
-        compiler_params=pltpu.CompilerParams(vmem_limit_bytes=BIG),
+        compiler_params=pltpu.CompilerParams(vmem_limit_bytes=MEDIUM),
         cost_estimate=LIGHT,
     )(where, incoming, preact, weight)
 
 
 def join_kernel(wanted, parts, where_ref, *refs):
-    sources, out_ref, sem = refs[:len(parts)], refs[-2], refs[-1]
-
-    def run():
+    sources, out_ref, held, sem, out_sem = refs[:len(parts)], *refs[-4:]
+
+    @pl.when(where_ref[3] == wanted)
+    def _():
         start = 0
-        copies = []
+        steps = []
         for i, (first, rows) in enumerate(parts):
-            source = sources[i].at[pl.ds(first, rows)]
-            copies.append(pltpu.make_async_copy(source, out_ref.at[pl.ds(start, rows)], sem.at[i]))
+            here = held.at[pl.ds(start, rows)]
+            fetch = pltpu.make_async_copy(sources[i].at[pl.ds(first, rows)], here, sem.at[i])
+            store = pltpu.make_async_copy(here, out_ref.at[pl.ds(start, rows)], out_sem.at[i])
+            steps.append((fetch, store))
             start += rows
-        for copy in copies:
-            copy.start()
-        for copy in copies:
-            copy.wait()
-
-    if wanted is None:
-        run()
-    else:
-        pl.when(where_ref[3] == wanted)(run)
+        for fetch, _ in steps:
+            fetch.start()
+        for fetch, store in steps:
+            fetch.wait()
+            store.start()
+        for _, store in steps:
+            store.wait()
 
 
 def join(where, wanted, arrays, parts, *earlier):
-    rows = sum(count for _, count in parts)
+    rows, width = sum(count for _, count in parts), arrays[0].shape[1]
     return pl.pallas_call(
         in_order(functools.partial(join_kernel, wanted, parts), 1 + len(arrays), len(earlier)),
         in_specs=[SMEM] + [ANY] * (len(arrays) + len(earlier)),
-        out_specs=VMEM,
-        out_shape=jax.ShapeDtypeStruct((rows, arrays[0].shape[1]), BF16),
-        scratch_shapes=[pltpu.SemaphoreType.DMA((len(arrays),))],
-        compiler_params=pltpu.CompilerParams(vmem_limit_bytes=BIG),
+        out_specs=HBM,
+        out_shape=jax.ShapeDtypeStruct((rows, width), BF16),
+        scratch_shapes=[
+            pltpu.VMEM((rows, width), BF16),
+            pltpu.SemaphoreType.DMA((len(arrays),)),
+            pltpu.SemaphoreType.DMA((len(arrays),)),
+        ],
+        compiler_params=pltpu.CompilerParams(vmem_limit_bytes=SMALL),
         cost_estimate=LIGHT,
     )(where, *arrays, *earlier)
 
@@ -161,7 +168,7 @@
         out_specs=[VMEM, VMEM],
         out_shape=[jax.ShapeDtypeStruct((rows // 2, width), BF16)] * 2,
         scratch_shapes=[pltpu.SemaphoreType.DMA((2,))],
-        compiler_params=pltpu.CompilerParams(vmem_limit_bytes=BIG),
+        compiler_params=pltpu.CompilerParams(vmem_limit_bytes=SMALL),
         cost_estimate=LIGHT,
     )(after, before, *earlier)
     return block, after, ring_move(low, axis, -1), ring_move(high, axis, 1), before
@@ -186,7 +193,7 @@
             jax.ShapeDtypeStruct((rows, width), BF16),
             jax.ShapeDtypeStruct((RANK, rows), F32),
         ],
-        compiler_params=pltpu.CompilerParams(vmem_limit_bytes=BIG),
+        compiler_params=pltpu.CompilerParams(vmem_limit_bytes=MEDIUM),
         cost_estimate=LIGHT,
     )(incoming, preact, b_both, *earlier)
 
@@ -251,7 +258,7 @@
             pltpu.SemaphoreType.DMA((4,)),
             pltpu.SemaphoreType.DMA((RING,)),
         ],
-        compiler_params=pltpu.CompilerParams(vmem_limit_bytes=BIG),
+        compiler_params=pltpu.CompilerParams(vmem_limit_bytes=36 * 1024 * 1024),
         cost_estimate=pl.CostEstimate(
             flops=2 * RING * RING * rows * wide * width, bytes_accessed=2 ** 24, transcendentals=0
         ),
@@ -376,7 +383,7 @@
         in_specs=[whole, pl.BlockSpec((1, rows, wide), lambda i: (1, 0, 0))],
         out_specs=whole,
         out_shape=jax.ShapeDtypeStruct((rows, wide), BF16),
-        compiler_params=pltpu.CompilerParams(vmem_limit_bytes=BIG),
+        compiler_params=pltpu.CompilerParams(vmem_limit_bytes=SMALL),
         cost_estimate=LIGHT,
     )(keep, got)
 
@@ -399,7 +406,7 @@
         in_specs=[whole, pl.BlockSpec((1, rows, wide), lambda i: (0, 0, 0)), whole] + [ANY] * len(earlier),
         out_specs=[pl.BlockSpec((rows // RING, wide), lambda i: (0, 0))] * RING,
         out_shape=[jax.ShapeDtypeStruct((rows // RING, wide), BF16)] * RING,
-        compiler_params=pltpu.CompilerParams(vmem_limit_bytes=BIG),
+        compiler_params=pltpu.CompilerParams(vmem_limit_bytes=SMALL),
         cost_estimate=LIGHT,
     )(keep, got, other, *earlier)
 
@@ -436,7 +443,7 @@
         in_specs=[SMEM] + [VMEM] * 9,
         out_specs=[VMEM, VMEM],
         out_shape=[jax.ShapeDtypeStruct((rows, width), BF16), jax.ShapeDtypeStruct((8, rows), F32)],
-        compiler_params=pltpu.CompilerParams(vmem_limit_bytes=BIG),
+        compiler_params=pltpu.CompilerParams(vmem_limit_bytes=MEDIUM),
         cost_estimate=LIGHT,
     )(where, *pieces, mixed, a_local, gain, hidden, scale)
 
@@ -465,7 +472,7 @@
         ],
         out_specs=[whole((rows, width)), whole((8, rows))],
         out_shape=[jax.ShapeDtypeStruct((rows, width), BF16), jax.ShapeDtypeStruct((8, rows), F32)],
-        compiler_params=pltpu.CompilerParams(vmem_limit_bytes=BIG),
+        compiler_params=pltpu.CompilerParams(vmem_limit_bytes=MEDIUM),
         cost_estimate=LIGHT,
     )(keep, got, other, mixed, a_local, gain, hidden, scale)
 
@@ -506,7 +513,7 @@
         in_specs=finish_specs(rows, width, c) + [pl.BlockSpec((rows, width), lambda i: (c, 0))],
         out_specs=pl.BlockSpec((rows, width), lambda i: (0, 0)),
         out_shape=jax.ShapeDtypeStruct((rows, width), BF16),
-        compiler_params=pltpu.CompilerParams(vmem_limit_bytes=BIG),
+        compiler_params=pltpu.CompilerParams(vmem_limit_bytes=MEDIUM),
         cost_estimate=LIGHT,
     )(scaled, inner, hidden, scale, grad_top)
 
@@ -520,7 +527,7 @@
         in_specs=[SMEM] + finish_specs(rows, width, 0) + [block, block],
         out_specs=block,
         out_shape=jax.ShapeDtypeStruct((rows, width), BF16),
-        compiler_params=pltpu.CompilerParams(vmem_limit_bytes=BIG),
+        compiler_params=pltpu.CompilerParams(vmem_limit_bytes=MEDIUM),
         cost_estimate=LIGHT,
     )(where, scaled, inner, hidden, scale, incoming, top)
 
@@ -556,7 +563,7 @@
         in_specs=[SMEM] + [VMEM] * (4 + len(arrays)) + [ANY] * len(earlier),
         out_specs=VMEM,
         out_shape=jax.ShapeDtypeStruct((2 * RANK, hidden.shape[1]), F32),
-        compiler_params=pltpu.CompilerParams(vmem_limit_bytes=BIG),
+        compiler_params=pltpu.CompilerParams(vmem_limit_bytes=MEDIUM),
         cost_estimate=LIGHT,
     )(where, hidden, scale, gain, projected, *arrays, *earlier)
 
@@ -589,7 +596,7 @@
         in_specs=[VMEM] * len(operands) + [ANY] * len(earlier),
         out_specs=VMEM,
         out_shape=out,
-        compiler_params=pltpu.CompilerParams(vmem_limit_bytes=BIG),
+        compiler_params=pltpu.CompilerParams(vmem_limit_bytes=SMALL),
         cost_estimate=LIGHT,
     )(*operands, *earlier)
 
@@ -685,7 +692,8 @@
     theirs = add_theirs(keep, got)
     other = swap(theirs, "pair", (0,))
     scaled, inner = low_scaled(mine, got, other, low_mixed, a_local, norm_gain, hidden, scale)
-    result = finish_low(where, scaled, lax.psum(inner, tensor), hidden, scale, low_in, top_grad)
+    inner = lax.psum(inner, tensor)
+    result = finish_low(where, scaled, inner, hidden, scale, low_in, top_grad)
 
     grads = make_grads(
         where, hidden, scale, norm_gain, projected, ([first], [low_dz], [top_mixed], [low_mixed])
@@ -705,7 +713,7 @@
     add_up = functools.partial(round_kernel, 1.0)
     share = small_call(add_up, half_shape, (share, pair_share))
     other_share = lax.ppermute(share, "section", [(0, 1), (1, 0)])
-    bank_grad = small_call(add_up, jax.ShapeDtypeStruct(bank_shape, F32), (share, other_share), result)
+    bank_grad = small_call(add_up, jax.ShapeDtypeStruct(bank_shape, F32), (share, other_share), inner)
     return (result[None], bank_grad)
 
 

time: 300 us -> 295 us (0.983)
  starting transfers between devices: 44.6 us -> 48.9 us
  waiting for transfers between devices: 144 us -> 140 us
  local copies, waits for them, and re-layouts: 16.2 us -> 12.9 us
    psum x2 -> x1, blocking collectives: 15.9 us -> 9.65 us  [shards(): lax.psum(inner, tensor)]
    psum x0 -> x1, blocking collectives: none -> 6.27 us  [shards(): inner = lax.psum(inner, tensor)]
    unnamed x72 -> x66, local copies, waits for them, and re-layouts: 15.6 us -> 10.9 us
  transfers between devices with their start and end apart: 30 -> 30, of which waited for: 18 -> 17; matrix products, arithmetic and copies ran while one was open for 2% -> 2% of each run, Pallas kernels for 11% -> 10%
where the time goes in v4:
time: 295 us; the launch traced here: 293 us
  waiting for transfers between devices  140 us (47%)
  Pallas kernels  51.5 us (17%)
  starting transfers between devices  48.9 us (17%)
  blocking collectives  34.1 us (12%)
  local copies, waits for them, and re-layouts  12.9 us (4%)
  matrix products  4.13 us (1%)
    ppermute x22, waiting for transfers between devices, ring_move(): lax.ppermute(block, ('section', axis), ring_route(distance, sections))  89.6 us
    ppermute x1, waiting for transfers between devices, shards(): low_in = lax.ppermute(top_grad, 'section', [(1, 0)])  40.8 us
    ppermute x22, starting transfers between devices, ring_move(): lax.ppermute(block, ('section', axis), ring_route(distance, sections))  33.5 us
    pallas_call x1, Pallas kernels, low_product(): pl.pallas_call(in_order(functools.partial(low_product_kernel, copies), 3...  16.4 us
    ppermute x6, starting transfers between devices, swap(): return lax.ppermute(block, ('section', axis), pairs)  13.9 us
    psum x1, blocking collectives, shards(): lax.psum(jnp.concatenate([jnp.sum(hidden_f * hidden_f, axis=1)[None], jnp...  11 us
    unnamed x66, local copies, waits for them, and re-layouts  10.9 us
    psum x1, blocking collectives, shards(): lax.psum(inner, tensor)  9.65 us
  transfers between devices with their start and end apart: 30, of which 17 were waited for; matrix products, arithmetic and copies ran while one was open for 2% of the time, Pallas kernels for 10%

profile of v4, /device:TPU:1, one launch (start us, length us, event | category | flops | bytes accessed | tf_op | source)
XLA Modules:
  0.0 293.3 jit_solution(17310440334755601270)
XLA Ops:
  0.6 4.7 %collective-permute-start.3 = (bf16[512,2048]{1,0:T(8,128)(2,1)}, bf16[512,2048]{1,0:T(8,128)(2,1)S(1)}, u32[]{:S(2)}, u32[]{:S(2)}) collective-permute-start(bf16[512,2048]{1,0:T(8,128)(2,1)} %bitcast.35), channel_id=1, source_target_pairs={{0,48},{16,0},{32,16},{48,32},{64,112},{80,64},{96,80},{112,96},{1... | collective-permute-start | bytes 6291464 | tf_op jit(solution)/shard_map/ppermute | solution.py:37
  5.4 1.6 copy-done.10
  9.5 2.0 shard_map.122.refs_1_.refs_5_
  11.5 2.8 collective-permute-start
  15.4 2.1 fusion.4
  17.6 1.7 fusion
  19.3 11.0 %psum.28 = f32[9,256]{1,0:T(8,128)S(1)} all-reduce(f32[9,256]{1,0:T(8,128)S(1)} %pad_maximum_fusion.1), channel_id=1, replica_groups=mesh['section'=2,'z'=4,'y'=4,'pair'=2,'core'=2] {'pair','core'}, use_global_device_ids=true, to_apply=%region_2.0 | all-reduce | flops 2304 | bytes 18432 | tf_op jit(solution)/shard_map/psum | solution.py:637
  30.5 19.4 %collective-permute-done.3.refs_0_.refs_6_.refs_3_.refs_4_ = bf16[512,2048]{1,0:T(8,128)(2,1)S(1)} collective-permute-done((bf16[512,2048]{1,0:T(8,128)(2,1)}, bf16[512,2048]{1,0:T(8,128)(2,1)S(1)}, u32[]{:S(2)}, u32[]{:S(2)}) %collective-permute-start.3) | collective-permute-done | bytes 2097184 | tf_op jit(solution)/shard_map/ppermute | solution.py:37
  49.9 3.1 %collective-permute-done.4.refs_1_.refs_9_.refs_4_.refs_7_ = bf16[512,2048]{1,0:T(8,128)(2,1)} collective-permute-done((bf16[512,2048]{1,0:T(8,128)(2,1)}, bf16[512,2048]{1,0:T(8,128)(2,1)}, u32[]{:S(2)}, u32[]{:S(2)}) %collective-permute-start.4) | collective-permute-done | bytes 2097184 | tf_op jit(solution)/shard_map/ppermute | solution.py:37
  53.0 1.3 shard_map.124
  55.9 2.7 collective-permute-done.refs_0_.refs_2_.refs_3_.refs_8_
  58.6 3.1 %collective-permute-done.1.refs_1_.refs_4_.refs_11_ = bf16[512,2048]{1,0:T(8,128)(2,1)} collective-permute-done((bf16[512,2048]{1,0:T(8,128)(2,1)}, bf16[512,2048]{1,0:T(8,128)(2,1)}, u32[]{:S(2)}, u32[]{:S(2)}) %collective-permute-start.1) | collective-permute-done | bytes 2097184 | tf_op jit(solution)/shard_map/ppermute | solution.py:37
  61.7 1.6 shard_map.123
  63.4 2.7 collective-permute-start.2
  66.0 11.1 %collective-permute-done.5.refs_7_.refs_1_.refs_5_ = bf16[256,2048]{1,0:T(8,128)(2,1)S(1)} collective-permute-done((bf16[256,2048]{1,0:T(8,128)(2,1)S(1)}, bf16[256,2048]{1,0:T(8,128)(2,1)S(1)}, u32[]{:S(2)}, u32[]{:S(2)}) %collective-permute-start.5) | collective-permute-done | bytes 1048608 | tf_op jit(solution)/shard_map/ppermute | solution.py:37
  77.2 2.4 collective-permute-done.6.refs_8_.refs_2_.refs_6_
  79.6 7.5 %collective-permute-done.7.refs_10_.refs_3_.refs_2_ = bf16[256,2048]{1,0:T(8,128)(2,1)S(1)} collective-permute-done((bf16[256,2048]{1,0:T(8,128)(2,1)S(1)}, bf16[256,2048]{1,0:T(8,128)(2,1)S(1)}, u32[]{:S(2)}, u32[]{:S(2)}) %collective-permute-start.7) | collective-permute-done | bytes 1048608 | tf_op jit(solution)/shard_map/ppermute | solution.py:37
  89.4 3.1 %collective-permute-start.10 = (bf16[512,2048]{1,0:T(8,128)(2,1)S(1)}, bf16[512,2048]{1,0:T(8,128)(2,1)S(1)}, u32[]{:S(2)}, u32[]{:S(2)}) collective-permute-start(bf16[512,2048]{1,0:T(8,128)(2,1)S(1)} %shard_map.127), channel_id=1, source_target_pairs={{0,8},{4,12},{8,0},{12,4},{1,9},{5,13},{9,1},{13,5},{2,10},{6,14},... | collective-permute-start | bytes 6291464 | tf_op jit(solution)/shard_map/ppermute | solution.py:37
  92.8 4.6 %shard_map.133 = bf16[1280,2048]{1,0:T(8,128)(2,1)} custom-call(s32[4]{0:T(128)S(1)} %pad_add_fusion.where_ref.refs_0_, bf16[256,2048]{1,0:T(8,128)(2,1)S(1)} %collective-permute-done.2.refs_3_.refs_1_.refs_9_, bf16[256,2048]{1,0:T(8,128)(2,1)S(1)} %collective-permute-done.7.refs_10_.refs_3_.refs_2_, ...), custom_call_target="tpu_custom_call" | custom-call | bytes 1048576 | tf_op jit(solution)/shard_map/pallas_call | solution.py:136
  97.3 4.0 %collective-permute-start.17 = (bf16[1280,2048]{1,0:T(8,128)(2,1)}, bf16[1280,2048]{1,0:T(8,128)(2,1)}, u32[]{:S(2)}, u32[]{:S(2)}) collective-permute-start(bf16[1280,2048]{1,0:T(8,128)(2,1)} %shard_map.133), channel_id=1, source_target_pairs={{0,48},{16,0},{32,16},{48,32},{1,49},{17,1},{33,17},{49,33},{2,50}... | collective-permute-start | bytes 15728648 | tf_op jit(solution)/shard_map/ppermute | solution.py:37
  101.3 1.9 collective-permute-start.18
  104.0 32.8 %collective-permute-done.10.refs_3_.refs_12_ = bf16[512,2048]{1,0:T(8,128)(2,1)S(1)} collective-permute-done((bf16[512,2048]{1,0:T(8,128)(2,1)S(1)}, bf16[512,2048]{1,0:T(8,128)(2,1)S(1)}, u32[]{:S(2)}, u32[]{:S(2)}) %collective-permute-start.10) | collective-permute-done | bytes 2097184 | tf_op jit(solution)/shard_map/ppermute | solution.py:37
  140.5 3.1 %shard_map.132 = bf16[768,2048]{1,0:T(8,128)(2,1)} custom-call(s32[4]{0:T(128)S(1)} %pad_add_fusion.where_ref.refs_0_, bf16[256,2048]{1,0:T(8,128)(2,1)S(1)} %collective-permute-done.5.refs_7_.refs_1_.refs_5_, bf16[256,2048]{1,0:T(8,128)(2,1)S(1)} %collective-permute-done.6.refs_8_.refs_2_.refs_6_, bf16[512,2048]{1,0:T(8,128)(2,1)S(1)} %copy-done.4, ...), custom_call_target="tpu_custom_call" | custom-call | bytes 1048576 | tf_op jit(solution)/shard_map/pallas_call | solution.py:136
  143.6 4.1 %collective-permute-start.15 = (bf16[768,2048]{1,0:T(8,128)(2,1)}, bf16[768,2048]{1,0:T(8,128)(2,1)}, u32[]{:S(2)}, u32[]{:S(2)}) collective-permute-start(bf16[768,2048]{1,0:T(8,128)(2,1)} %shard_map.132), channel_id=1, source_target_pairs={{0,12},{4,0},{8,4},{12,8},{1,13},{5,1},{9,5},{13,9},{2,14},{6,2},{... | collective-permute-start | bytes 9437192 | tf_op jit(solution)/shard_map/ppermute | solution.py:37
  147.7 2.1 collective-permute-start.16
  149.8 2.7 shard_map.129
  152.6 9.7 %psum.29.inner_ref = f32[8,256]{1,0:T(8,128)S(1)} all-reduce(f32[8,256]{1,0:T(8,128)S(1)} %get-tuple-element.34), channel_id=1, replica_groups=mesh['section'=2,'z'=4,'y'=4,'pair'=2,'core'=2] {'pair','core'}, use_global_device_ids=true, to_apply=%region_3.0 | all-reduce | flops 2048 | bytes 16384 | tf_op jit(solution)/shard_map/psum | solution.py:685
  162.3 1.6 shard_map.130.top_ref
  163.9 1.4 collective-permute-start.14
  165.5 40.8 %collective-permute-done.14.refs_0_.incoming_ref = bf16[256,2048]{1,0:T(8,128)(2,1)} collective-permute-done((bf16[256,2048]{1,0:T(8,128)(2,1)}, bf16[256,2048]{1,0:T(8,128)(2,1)}, u32[]{:S(2)}, u32[]{:S(2)}) %collective-permute-start.14) | collective-permute-done | bytes 1048608 | tf_op jit(solution)/shard_map/ppermute | solution.py:686
  207.5 2.1 shard_map.131
  210.5 7.2 %psum.30.refs_17_.mixed_ref.refs_8_ = f32[4,256]{1,0:T(4,128)S(1)} all-reduce(f32[4,256]{1,0:T(4,128)S(1)} %get-tuple-element.36), channel_id=1, replica_groups=mesh['section'=2,'z'=4,'y'=4,'pair'=2,'core'=2] {'pair','core'}, use_global_device_ids=true, to_apply=%region_4.0 | all-reduce | flops 1024 | bytes 8192 | tf_op jit(solution)/shard_map/psum | solution.py:689
  219.0 16.4 %shard_map.134 = (bf16[256,2048]{1,0:T(8,128)(2,1)S(1)}, bf16[256,2048]{1,0:T(8,128)(2,1)S(1)}, bf16[2,256,2048]{2,1,0:T(8,128)(2,1)}) custom-call(s32[4]{0:T(128)S(1)} %pad_add_fusion.where_ref.refs_0_, s32[32]{0:T(128)S(1)} %fusion.16.refs_1_, bf16[256,2048]{1,0:T(8,128)(2,1)S(1)} %copy-done.19, bf16[512,2048]{1,0:T(8,128)(2,1)} %bitcast.37, ...), custom_call_target="tpu_custom_call" | custom-call | flops 8589934592 | bytes 33554432 | tf_op jit(solution)/shard_map/pallas_call | solution.py:354
  235.5 5.8 %collective-permute-start.19 = (bf16[2,256,2048]{2,1,0:T(8,128)(2,1)}, bf16[2,256,2048]{2,1,0:T(8,128)(2,1)S(1)}, u32[]{:S(2)}, u32[]{:S(2)}) collective-permute-start(bf16[2,256,2048]{2,1,0:T(8,128)(2,1)} %get-tuple-element.38.refs_4_), channel_id=1, source_target_pairs={{0,1},{1,0},{2,3},{3,2},{4,5},{5,4},{6,7},{7,6},{8,9},{9,8},{10,11... | collective-permute-start | bytes 6291464 | tf_op jit(solution)/shard_map/ppermute | solution.py:42
  241.2 4.0 %collective-permute-done.19.got_ref = bf16[2,256,2048]{2,1,0:T(8,128)(2,1)S(1)} collective-permute-done((bf16[2,256,2048]{2,1,0:T(8,128)(2,1)}, bf16[2,256,2048]{2,1,0:T(8,128)(2,1)S(1)}, u32[]{:S(2)}, u32[]{:S(2)}) %collective-permute-start.19) | collective-permute-done | bytes 2097184 | tf_op jit(solution)/shard_map/ppermute | solution.py:42
  246.5 3.1 %collective-permute-start.20 = (bf16[256,2048]{1,0:T(8,128)(2,1)}, bf16[256,2048]{1,0:T(8,128)(2,1)}, u32[]{:S(2)}, u32[]{:S(2)}) collective-permute-start(bf16[256,2048]{1,0:T(8,128)(2,1)} %shard_map.135.refs_5_), channel_id=1, source_target_pairs={{0,2},{2,0},{1,3},{3,1},{4,6},{6,4},{5,7},{7,5},{8,10},{10,8},{9,1... | collective-permute-start | bytes 3145736 | tf_op jit(solution)/shard_map/ppermute | solution.py:42
  249.6 2.4 shard_map.138.refs_0_
  252.1 2.1 collective-permute-start.22
  254.2 1.4 collective-permute-done.21.refs_1_
  256.8 1.8 collective-permute-done.23.refs_3_
  258.6 1.5 collective-permute-start.24
  262.4 2.6 collective-permute-done.25.refs_3_
  266.6 3.2 %collective-permute-start.27 = (f32[256,256]{1,0:T(8,128)S(1)}, f32[256,256]{1,0:T(8,128)S(1)}, u32[]{:S(2)}, u32[]{:S(2)}) collective-permute-start(f32[256,256]{1,0:T(8,128)S(1)} %shard_map.140.refs_0_), channel_id=1, source_target_pairs={{0,1},{1,0},{64,65},{65,64},{2,3},{3,2},{66,67},{67,66},{4,5},{5,4... | collective-permute-start | bytes 786440 | tf_op jit(solution)/shard_map/ppermute | solution.py:42
  271.3 4.5 %collective-permute-done.28.refs_1_ = bf16[256,256]{1,0:T(8,128)(2,1)S(1)} collective-permute-done((bf16[256,256]{1,0:T(8,128)(2,1)S(1)}, bf16[256,256]{1,0:T(8,128)(2,1)S(1)}, u32[]{:S(2)}, u32[]{:S(2)}) %collective-permute-start.28) | collective-permute-done | bytes 131104 | tf_op jit(solution)/shard_map/ppermute | solution.py:42
  276.5 3.4 %shard_map.136 = (bf16[256,2048]{1,0:T(8,128)(2,1)S(1)}, f32[8,256]{1,0:T(8,128)S(1)}) custom-call(bf16[256,2048]{1,0:T(8,128)(2,1)S(1)} %copy-done.22, bf16[2,256,2048]{2,1,0:T(8,128)(2,1)S(1)} %collective-permute-done.19.got_ref, bf16[256,2048]{1,0:T(8,128)(2,1)} %collective-permute-done.20.other_ref, f32[4,256]{1,0:T(4,128)S(1)} %psum.30.refs_17_.mixed_ref.refs_8_, ...), custom_call_target="tpu_custom_call" | custom-call | bytes 1048576 | tf_op jit(solution)/shard_map/pallas_call | solution.py:466
  280.9 6.3 %psum.31.inner_ref.refs_2_ = f32[8,256]{1,0:T(8,128)S(1)} all-reduce(f32[8,256]{1,0:T(8,128)S(1)} %get-tuple-element.41), channel_id=1, replica_groups=mesh['section'=2,'z'=4,'y'=4,'pair'=2,'core'=2] {'pair','core'}, use_global_device_ids=true, to_apply=%region_5.6 | all-reduce | flops 2048 | bytes 16384 | tf_op jit(solution)/shard_map/psum | solution.py:695
  287.2 1.6 shard_map.143
  290.1 3.2 %shard_map.137 = bf16[256,2048]{1,0:T(8,128)(2,1)} custom-call(s32[4]{0:T(128)S(1)} %pad_add_fusion.where_ref.refs_0_, bf16[256,2048]{1,0:T(8,128)(2,1)S(1)} %copy-done.24, f32[8,256]{1,0:T(8,128)S(1)} %psum.31.inner_ref.refs_2_, bf16[256,2048]{1,0:T(8,128)(2,1)S(1)} %bitcast.34, f32[256,1]{1,0:T(8,128)S(1)} %copy.28.refs_2_.scale_ref, ...), custom_call_target="tpu_custom_call" | custom-call | bytes 1048576 | tf_op jit(solution)/shard_map/pallas_call | solution.py:524
  (129 shorter events, 26.6 us)
Async XLA Ops:
  0.6 14.2 %copy-start = (f32[256,256]{1,0:T(8,128)S(1)}, f32[256,256]{1,0:T(8,128)}, u32[]{:S(2)}) copy-start(f32[256,256]{1,0:T(8,128)} %param.15) | copy-start | bytes 786436
  0.6 49.3 %collective-permute-start.3 = (bf16[512,2048]{1,0:T(8,128)(2,1)}, bf16[512,2048]{1,0:T(8,128)(2,1)S(1)}, u32[]{:S(2)}, u32[]{:S(2)}) collective-permute-start(bf16[512,2048]{1,0:T(8,128)(2,1)} %bitcast.35), channel_id=1, source_target_pairs={{0,48},{16,0},{32,16},{48,32},{64,112},{80,64},{96,80},{112,96},{1... | collective-permute-start | bytes 6291464 | tf_op jit(solution)/shard_map/ppermute | solution.py:37
  5.3 47.7 %collective-permute-start.4 = (bf16[512,2048]{1,0:T(8,128)(2,1)}, bf16[512,2048]{1,0:T(8,128)(2,1)}, u32[]{:S(2)}, u32[]{:S(2)}) collective-permute-start(bf16[512,2048]{1,0:T(8,128)(2,1)} %bitcast.36), channel_id=1, source_target_pairs={{0,16},{16,32},{32,48},{48,0},{64,80},{80,96},{96,112},{112,64},{1... | collective-permute-start | bytes 6291464 | tf_op jit(solution)/shard_map/ppermute | solution.py:37
  9.5 4.9 %copy-start.28 = (s32[1,2,128,2]{2,3,1,0:T(2,128)S(1)}, s32[1,2,128,2]{2,3,1,0:T(2,128)}, u32[]{:S(2)}) copy-start(s32[1,2,128,2]{2,3,1,0:T(2,128)} %param.16) | copy-start | bytes 6148
  9.5 5.0 %copy-start.29 = (f32[1,2,128,2]{2,3,1,0:T(2,128)S(1)}, f32[1,2,128,2]{2,3,1,0:T(2,128)}, u32[]{:S(2)}) copy-start(f32[1,2,128,2]{2,3,1,0:T(2,128)} %param.17) | copy-start | bytes 6148
  9.5 5.7 %copy-start.2 = (bf16[1,256,2048]{2,1,0:T(8,128)(2,1)S(1)}, bf16[1,256,2048]{2,1,0:T(8,128)(2,1)}, u32[]{:S(2)}) copy-start(bf16[1,256,2048]{2,1,0:T(8,128)(2,1)} %param.11) | copy-start | bytes 3145732
  11.5 6.0 %copy-start.25 = (f32[1,2048]{1,0:T(1,128)S(1)}, f32[1,2048]{1,0:T(1,128)}, u32[]{:S(2)}) copy-start(f32[1,2048]{1,0:T(1,128)} %refs_3_.1) | copy-start | bytes 24580
  11.5 47.1 %collective-permute-start = (bf16[512,2048]{1,0:T(8,128)(2,1)}, bf16[512,2048]{1,0:T(8,128)(2,1)}, u32[]{:S(2)}, u32[]{:S(2)}) collective-permute-start(bf16[512,2048]{1,0:T(8,128)(2,1)} %shard_map.122.refs_1_.refs_5_), channel_id=1, source_target_pairs={{0,12},{4,0},{8,4},{12,8},{64,76},{68,64},{72,68},{76,72},{1,13},{... | collective-permute-start | bytes 6291464 | tf_op jit(solution)/shard_map/ppermute | solution.py:37
  14.3 47.4 %collective-permute-start.1 = (bf16[512,2048]{1,0:T(8,128)(2,1)}, bf16[512,2048]{1,0:T(8,128)(2,1)}, u32[]{:S(2)}, u32[]{:S(2)}) collective-permute-start(bf16[512,2048]{1,0:T(8,128)(2,1)} %shard_map.122.refs_1_.refs_5_), channel_id=1, source_target_pairs={{0,4},{4,8},{8,12},{12,0},{64,68},{68,72},{72,76},{76,64},{1,5},{5... | collective-permute-start | bytes 6291464 | tf_op jit(solution)/shard_map/ppermute | solution.py:37
  14.8 15.5 %copy-start.26 = (f32[2,4,8,256]{3,2,1,0:T(8,128)}, f32[2,4,8,256]{3,2,1,0:T(8,128)S(1)}, u32[]{:S(2)}) copy-start(f32[2,4,8,256]{3,2,1,0:T(8,128)S(1)} %select_reduce_fusion) | copy-start | bytes 196612
  54.3 22.9 %collective-permute-start.5 = (bf16[256,2048]{1,0:T(8,128)(2,1)S(1)}, bf16[256,2048]{1,0:T(8,128)(2,1)S(1)}, u32[]{:S(2)}, u32[]{:S(2)}) collective-permute-start(bf16[256,2048]{1,0:T(8,128)(2,1)S(1)} %get-tuple-element.23), channel_id=1, source_target_pairs={{0,48},{16,0},{32,16},{48,32},{64,112},{80,64},{96,80},{112,96},{1... | collective-permute-start | bytes 3145736 | tf_op jit(solution)/shard_map/ppermute | solution.py:37
  55.4 31.7 %copy-start.11 = (bf16[1,512,2048]{2,1,0:T(8,128)(2,1)S(1)}, bf16[1,512,2048]{2,1,0:T(8,128)(2,1)}, u32[]{:S(2)}) copy-start(bf16[1,512,2048]{2,1,0:T(8,128)(2,1)} %param.14) | copy-start | bytes 6291460
  55.4 24.1 %collective-permute-start.6 = (bf16[256,2048]{1,0:T(8,128)(2,1)S(1)}, bf16[256,2048]{1,0:T(8,128)(2,1)S(1)}, u32[]{:S(2)}, u32[]{:S(2)}) collective-permute-start(bf16[256,2048]{1,0:T(8,128)(2,1)S(1)} %get-tuple-element.24), channel_id=1, source_target_pairs={{0,16},{16,32},{32,48},{48,0},{64,80},{80,96},{96,112},{112,64},{1... | collective-permute-start | bytes 3145736 | tf_op jit(solution)/shard_map/ppermute | solution.py:37
  63.3 23.8 %collective-permute-start.7 = (bf16[256,2048]{1,0:T(8,128)(2,1)S(1)}, bf16[256,2048]{1,0:T(8,128)(2,1)S(1)}, u32[]{:S(2)}, u32[]{:S(2)}) collective-permute-start(bf16[256,2048]{1,0:T(8,128)(2,1)S(1)} %get-tuple-element.25), channel_id=1, source_target_pairs={{0,4},{4,8},{8,12},{12,0},{64,68},{68,72},{72,76},{76,64},{1,5},{5... | collective-permute-start | bytes 3145736 | tf_op jit(solution)/shard_map/ppermute | solution.py:37
  63.4 23.7 %collective-permute-start.2 = (bf16[256,2048]{1,0:T(8,128)(2,1)S(1)}, bf16[256,2048]{1,0:T(8,128)(2,1)S(1)}, u32[]{:S(2)}, u32[]{:S(2)}) collective-permute-start(bf16[256,2048]{1,0:T(8,128)(2,1)S(1)} %get-tuple-element.22), channel_id=1, source_target_pairs={{0,12},{4,0},{8,4},{12,8},{64,76},{68,64},{72,68},{76,72},{1,13},{... | collective-permute-start | bytes 3145736 | tf_op jit(solution)/shard_map/ppermute | solution.py:37
  77.2 63.2 %copy-start.5 = (bf16[256,2048]{1,0:T(8,128)(2,1)}, bf16[256,2048]{1,0:T(8,128)(2,1)S(1)}, u32[]{:S(2)}) copy-start(bf16[256,2048]{1,0:T(8,128)(2,1)S(1)} %collective-permute-done.5.refs_7_.refs_1_.refs_5_) | copy-start | bytes 3145732
  79.6 60.9 %copy-start.7 = (bf16[256,2048]{1,0:T(8,128)(2,1)}, bf16[256,2048]{1,0:T(8,128)(2,1)S(1)}, u32[]{:S(2)}) copy-start(bf16[256,2048]{1,0:T(8,128)(2,1)S(1)} %collective-permute-done.6.refs_8_.refs_2_.refs_6_) | copy-start | bytes 3145732
  87.1 5.7 %copy-start.9 = (bf16[256,2048]{1,0:T(8,128)(2,1)}, bf16[256,2048]{1,0:T(8,128)(2,1)S(1)}, u32[]{:S(2)}) copy-start(bf16[256,2048]{1,0:T(8,128)(2,1)S(1)} %collective-permute-done.7.refs_10_.refs_3_.refs_2_) | copy-start | bytes 3145732
  87.1 5.7 %copy-start.13 = (bf16[256,2048]{1,0:T(8,128)(2,1)}, bf16[256,2048]{1,0:T(8,128)(2,1)S(1)}, u32[]{:S(2)}) copy-start(bf16[256,2048]{1,0:T(8,128)(2,1)S(1)} %collective-permute-done.2.refs_3_.refs_1_.refs_9_) | copy-start | bytes 3145732
  87.7 4.8 %collective-permute-start.8 = (bf16[2,1024,512]{2,1,0:T(8,128)(2,1)S(1)}, bf16[2,1024,512]{2,1,0:T(8,128)(2,1)S(1)}, u32[]{:S(2)}, u32[]{:S(2)}) collective-permute-start(bf16[2,1024,512]{2,1,0:T(8,128)(2,1)S(1)} %get-tuple-element.27), channel_id=1, source_target_pairs={{64,65},{65,64},{66,67},{67,66},{68,69},{69,68},{70,71},{71,70},{7... | collective-permute-start | bytes 6291464 | tf_op jit(solution)/shard_map/ppermute | solution.py:42
  89.4 47.4 %collective-permute-start.10 = (bf16[512,2048]{1,0:T(8,128)(2,1)S(1)}, bf16[512,2048]{1,0:T(8,128)(2,1)S(1)}, u32[]{:S(2)}, u32[]{:S(2)}) collective-permute-start(bf16[512,2048]{1,0:T(8,128)(2,1)S(1)} %shard_map.127), channel_id=1, source_target_pairs={{0,8},{4,12},{8,0},{12,4},{1,9},{5,13},{9,1},{13,5},{2,10},{6,14},... | collective-permute-start | bytes 6291464 | tf_op jit(solution)/shard_map/ppermute | solution.py:37
  97.3 120.4 %collective-permute-start.17 = (bf16[1280,2048]{1,0:T(8,128)(2,1)}, bf16[1280,2048]{1,0:T(8,128)(2,1)}, u32[]{:S(2)}, u32[]{:S(2)}) collective-permute-start(bf16[1280,2048]{1,0:T(8,128)(2,1)} %shard_map.133), channel_id=1, source_target_pairs={{0,48},{16,0},{32,16},{48,32},{1,49},{17,1},{33,17},{49,33},{2,50}... | collective-permute-start | bytes 15728648 | tf_op jit(solution)/shard_map/ppermute | solution.py:37
  101.3 116.4 %collective-permute-start.18 = (bf16[1280,2048]{1,0:T(8,128)(2,1)}, bf16[1280,2048]{1,0:T(8,128)(2,1)}, u32[]{:S(2)}, u32[]{:S(2)}) collective-permute-start(bf16[1280,2048]{1,0:T(8,128)(2,1)} %shard_map.133), channel_id=1, source_target_pairs={{0,16},{16,32},{32,48},{48,0},{1,17},{17,33},{33,49},{49,1},{2,18}... | collective-permute-start | bytes 15728648 | tf_op jit(solution)/shard_map/ppermute | solution.py:37
  103.3 33.6 %collective-permute-start.9 = (bf16[1024,512]{1,0:T(8,128)(2,1)S(1)}, bf16[1024,512]{1,0:T(8,128)(2,1)S(1)}, u32[]{:S(2)}, u32[]{:S(2)}) collective-permute-start(bf16[1024,512]{1,0:T(8,128)(2,1)S(1)} %shard_map.126.refs_5_), channel_id=1, source_target_pairs={{64,66},{66,64},{65,67},{67,65},{68,70},{70,68},{69,71},{71,69},{7... | collective-permute-start | bytes 3145736 | tf_op jit(solution)/shard_map/ppermute | solution.py:42
  138.2 2.2 collective-permute-start.11
  139.0 1.4 collective-permute-start.12
  139.7 0.7 collective-permute-start.13
  143.5 18.7 %copy-start.17 = (bf16[256,2048]{1,0:T(8,128)(2,1)S(1)}, bf16[256,2048]{1,0:T(8,128)(2,1)}, u32[]{:S(2)}) copy-start(bf16[256,2048]{1,0:T(8,128)(2,1)} %incoming_ref.3) | copy-start | bytes 3145732
  143.6 74.2 %collective-permute-start.15 = (bf16[768,2048]{1,0:T(8,128)(2,1)}, bf16[768,2048]{1,0:T(8,128)(2,1)}, u32[]{:S(2)}, u32[]{:S(2)}) collective-permute-start(bf16[768,2048]{1,0:T(8,128)(2,1)} %shard_map.132), channel_id=1, source_target_pairs={{0,12},{4,0},{8,4},{12,8},{1,13},{5,1},{9,5},{13,9},{2,14},{6,2},{... | collective-permute-start | bytes 9437192 | tf_op jit(solution)/shard_map/ppermute | solution.py:37
  147.7 70.1 %collective-permute-start.16 = (bf16[768,2048]{1,0:T(8,128)(2,1)}, bf16[768,2048]{1,0:T(8,128)(2,1)}, u32[]{:S(2)}, u32[]{:S(2)}) collective-permute-start(bf16[768,2048]{1,0:T(8,128)(2,1)} %shard_map.132), channel_id=1, source_target_pairs={{0,4},{4,8},{8,12},{12,0},{1,5},{5,9},{9,13},{13,1},{2,6},{6,10},{... | collective-permute-start | bytes 9437192 | tf_op jit(solution)/shard_map/ppermute | solution.py:37
  163.9 53.9 %copy-start.6 = (bf16[256,2048]{1,0:T(8,128)(2,1)S(1)}, bf16[256,2048]{1,0:T(8,128)(2,1)}, u32[]{:S(2)}) copy-start(bf16[256,2048]{1,0:T(8,128)(2,1)} %copy-done.5) | copy-start | bytes 3145732
  163.9 53.9 %copy-start.8 = (bf16[256,2048]{1,0:T(8,128)(2,1)S(1)}, bf16[256,2048]{1,0:T(8,128)(2,1)}, u32[]{:S(2)}) copy-start(bf16[256,2048]{1,0:T(8,128)(2,1)} %copy-done.7) | copy-start | bytes 3145732
  163.9 42.3 %collective-permute-start.14 = (bf16[256,2048]{1,0:T(8,128)(2,1)}, bf16[256,2048]{1,0:T(8,128)(2,1)}, u32[]{:S(2)}, u32[]{:S(2)}) collective-permute-start(bf16[256,2048]{1,0:T(8,128)(2,1)} %shard_map.130.top_ref), channel_id=1, source_target_pairs={{64,0},{65,1},{66,2},{67,3},{68,4},{69,5},{70,6},{71,7},{72,8},{73... | collective-permute-start | bytes 3145736 | tf_op jit(solution)/shard_map/ppermute | solution.py:686
  235.5 11.1 %copy-start.21 = (bf16[256,2048]{1,0:T(8,128)(2,1)}, bf16[256,2048]{1,0:T(8,128)(2,1)S(1)}, u32[]{:S(2)}) copy-start(bf16[256,2048]{1,0:T(8,128)(2,1)S(1)} %get-tuple-element.37.keep_ref) | copy-start | bytes 3145732
  235.5 9.8 %collective-permute-start.19 = (bf16[2,256,2048]{2,1,0:T(8,128)(2,1)}, bf16[2,256,2048]{2,1,0:T(8,128)(2,1)S(1)}, u32[]{:S(2)}, u32[]{:S(2)}) collective-permute-start(bf16[2,256,2048]{2,1,0:T(8,128)(2,1)} %get-tuple-element.38.refs_4_), channel_id=1, source_target_pairs={{0,1},{1,0},{2,3},{3,2},{4,5},{5,4},{6,7},{7,6},{8,9},{9,8},{10,11... | collective-permute-start | bytes 6291464 | tf_op jit(solution)/shard_map/ppermute | solution.py:42
  246.5 30.0 %collective-permute-start.20 = (bf16[256,2048]{1,0:T(8,128)(2,1)}, bf16[256,2048]{1,0:T(8,128)(2,1)}, u32[]{:S(2)}, u32[]{:S(2)}) collective-permute-start(bf16[256,2048]{1,0:T(8,128)(2,1)} %shard_map.135.refs_5_), channel_id=1, source_target_pairs={{0,2},{2,0},{1,3},{3,1},{4,6},{6,4},{5,7},{7,5},{8,10},{10,8},{9,1... | collective-permute-start | bytes 3145736 | tf_op jit(solution)/shard_map/ppermute | solution.py:42
  249.6 9.0 %copy-start.20 = (bf16[2,256,2048]{2,1,0:T(8,128)(2,1)S(1)}, bf16[2,256,2048]{2,1,0:T(8,128)(2,1)}, u32[]{:S(2)}) copy-start(bf16[2,256,2048]{2,1,0:T(8,128)(2,1)} %get-tuple-element.38.refs_4_) | copy-start | bytes 6291460
  252.0 8.8 %copy-start.27 = (f32[2,4,8,256]{3,2,1,0:T(8,128)S(1)}, f32[2,4,8,256]{3,2,1,0:T(8,128)}, u32[]{:S(2)}) copy-start(f32[2,4,8,256]{3,2,1,0:T(8,128)} %copy-done.26) | copy-start | bytes 196612
  252.0 3.6 %collective-permute-start.21 = (f32[8,2048]{1,0:T(8,128)S(1)}, f32[8,2048]{1,0:T(8,128)S(1)}, u32[]{:S(2)}, u32[]{:S(2)}) collective-permute-start(f32[8,2048]{1,0:T(8,128)S(1)} %shard_map.138.refs_0_), channel_id=1, source_target_pairs={{0,12},{4,0},{8,4},{12,8},{64,76},{68,64},{72,68},{76,72},{1,13},{... | collective-permute-start | bytes 196616 | tf_op jit(solution)/shard_map/ppermute | solution.py:37
  252.1 4.7 %collective-permute-start.22 = (f32[8,2048]{1,0:T(8,128)S(1)}, f32[8,2048]{1,0:T(8,128)S(1)}, u32[]{:S(2)}, u32[]{:S(2)}) collective-permute-start(f32[8,2048]{1,0:T(8,128)S(1)} %shard_map.138.refs_0_), channel_id=1, source_target_pairs={{0,8},{4,12},{8,0},{12,4},{64,72},{68,76},{72,64},{76,68},{1,9},{5... | collective-permute-start | bytes 196616 | tf_op jit(solution)/shard_map/ppermute | solution.py:37
  254.2 4.4 %collective-permute-start.23 = (f32[8,2048]{1,0:T(8,128)S(1)}, f32[8,2048]{1,0:T(8,128)S(1)}, u32[]{:S(2)}, u32[]{:S(2)}) collective-permute-start(f32[8,2048]{1,0:T(8,128)S(1)} %shard_map.138.refs_0_), channel_id=1, source_target_pairs={{0,4},{4,8},{8,12},{12,0},{64,68},{68,72},{72,76},{76,64},{1,5},{5... | collective-permute-start | bytes 196616 | tf_op jit(solution)/shard_map/ppermute | solution.py:37
  258.6 3.8 %collective-permute-start.24 = (f32[8,2048]{1,0:T(8,128)S(1)}, f32[8,2048]{1,0:T(8,128)S(1)}, u32[]{:S(2)}, u32[]{:S(2)}) collective-permute-start(f32[8,2048]{1,0:T(8,128)S(1)} %shard_map.139.refs_1_), channel_id=1, source_target_pairs={{0,48},{16,0},{32,16},{48,32},{64,112},{80,64},{96,80},{112,96},{1... | collective-permute-start | bytes 196616 | tf_op jit(solution)/shard_map/ppermute | solution.py:37
  260.2 4.8 %collective-permute-start.25 = (f32[8,2048]{1,0:T(8,128)S(1)}, f32[8,2048]{1,0:T(8,128)}, u32[]{:S(2)}, u32[]{:S(2)}) collective-permute-start(f32[8,2048]{1,0:T(8,128)S(1)} %shard_map.139.refs_1_), channel_id=1, source_target_pairs={{0,32},{16,48},{32,0},{48,16},{64,96},{80,112},{96,64},{112,80},{1... | collective-permute-start | bytes 196616 | tf_op jit(solution)/shard_map/ppermute | solution.py:37
  260.2 5.1 %collective-permute-start.26 = (f32[8,2048]{1,0:T(8,128)S(1)}, f32[8,2048]{1,0:T(8,128)}, u32[]{:S(2)}, u32[]{:S(2)}) collective-permute-start(f32[8,2048]{1,0:T(8,128)S(1)} %shard_map.139.refs_1_), channel_id=1, source_target_pairs={{0,16},{16,32},{32,48},{48,0},{64,80},{80,96},{96,112},{112,64},{1... | collective-permute-start | bytes 196616 | tf_op jit(solution)/shard_map/ppermute | solution.py:37
  262.4 14.1 %copy-start.22 = (bf16[256,2048]{1,0:T(8,128)(2,1)S(1)}, bf16[256,2048]{1,0:T(8,128)(2,1)}, u32[]{:S(2)}) copy-start(bf16[256,2048]{1,0:T(8,128)(2,1)} %copy-done.21) | copy-start | bytes 3145732
  266.6 4.4 %collective-permute-start.27 = (f32[256,256]{1,0:T(8,128)S(1)}, f32[256,256]{1,0:T(8,128)S(1)}, u32[]{:S(2)}, u32[]{:S(2)}) collective-permute-start(f32[256,256]{1,0:T(8,128)S(1)} %shard_map.140.refs_0_), channel_id=1, source_target_pairs={{0,1},{1,0},{64,65},{65,64},{2,3},{3,2},{66,67},{67,66},{4,5},{5,4... | collective-permute-start | bytes 786440 | tf_op jit(solution)/shard_map/ppermute | solution.py:42
  271.0 4.8 %collective-permute-start.28 = (bf16[256,256]{1,0:T(8,128)(2,1)S(1)}, bf16[256,256]{1,0:T(8,128)(2,1)S(1)}, u32[]{:S(2)}, u32[]{:S(2)}) collective-permute-start(bf16[256,256]{1,0:T(8,128)(2,1)S(1)} %shard_map.141.refs_0_), channel_id=1, source_target_pairs={{0,2},{2,0},{64,66},{66,64},{1,3},{3,1},{65,67},{67,65},{4,6},{6,4... | collective-permute-start | bytes 393224 | tf_op jit(solution)/shard_map/ppermute | solution.py:42
  276.5 10.7 %collective-permute-start.29 = (bf16[256,256]{1,0:T(8,128)(2,1)}, bf16[256,256]{1,0:T(8,128)(2,1)S(1)}, u32[]{:S(2)}, u32[]{:S(2)}) collective-permute-start(bf16[256,256]{1,0:T(8,128)(2,1)} %shard_map.142.refs_0_), channel_id=1, source_target_pairs={{0,64},{64,0},{1,65},{65,1},{2,66},{66,2},{3,67},{67,3},{4,68},{68... | collective-permute-start | bytes 393224 | tf_op jit(solution)/shard_map/ppermute | solution.py:715
  (15 other events, 33.0 us)

commit v5 on v4

--- a/solution.py
+++ b/solution.py
@@ -285,7 +285,8 @@
     for d in (1, 3):
         take(y_pair[d], 0, shard, (2, d, 0), (2, d, 1))
         take(z_pair[d], 0, shard, (d, 2, 0), (d, 2, 1))
-    slim, rest = wide // 2, shard - wide // 2
+    slim = 3 * wide // 8
+    rest = shard - slim
     for i, d in enumerate((1, 3)):
         for j, e in enumerate((1, 3)):
             take(y_pair[e], shard + i * slim, slim)
@@ -490,9 +491,21 @@
     out_ref[...] = hidden_gradient(scaled_ref, inner_ref, hidden_ref, scale_ref, incoming_ref)
 
 
-def low_kernel(where_ref, scaled_ref, inner_ref, hidden_ref, scale_ref, incoming_ref, top_ref, *rest):
-    grad = hidden_gradient(scaled_ref, inner_ref, hidden_ref, scale_ref, incoming_ref)
-    rest[-1][...] = jnp.where(where_ref[3] == 1, top_ref[...], grad)
+def low_kernel(
+    where_ref, scaled_ref, inner_ref, hidden_ref, scale_ref, incoming_ref, share_ref, other_ref, top_ref,
+    out_ref, bank_ref, sem,
+):
+    bank_ref[...] = share_ref[...].astype(F32) + other_ref[...].astype(F32)
+
+    @pl.when(where_ref[3] == 0)
+    def _():
+        out_ref[...] = hidden_gradient(scaled_ref, inner_ref, hidden_ref, scale_ref, incoming_ref)
+
+    @pl.when(where_ref[3] == 1)
+    def _():
+        copy = pltpu.make_async_copy(top_ref, out_ref, sem)
+        copy.start()
+        copy.wait()
 
 
 def finish_specs(rows, width, c):
@@ -518,18 +531,20 @@
     )(scaled, inner, hidden, scale, grad_top)
 
 
-def finish_low(where, scaled, inner, hidden, scale, incoming, top):
+def finish_low(where, scaled, inner, hidden, scale, incoming, share, other, top):
     rows, width = scaled.shape
     block = pl.BlockSpec((rows, width), lambda i: (0, 0))
+    bank = pl.BlockSpec(share.shape, lambda i: (0, 0))
     return pl.pallas_call(
         low_kernel,
         grid=(1,),
-        in_specs=[SMEM] + finish_specs(rows, width, 0) + [block, block],
-        out_specs=block,
-        out_shape=jax.ShapeDtypeStruct((rows, width), BF16),
+        in_specs=[SMEM] + finish_specs(rows, width, 0) + [block, bank, bank, HBM],
+        out_specs=[block, bank],
+        out_shape=[jax.ShapeDtypeStruct((rows, width), BF16), jax.ShapeDtypeStruct(share.shape, F32)],
+        scratch_shapes=[pltpu.SemaphoreType.DMA],
         compiler_params=pltpu.CompilerParams(vmem_limit_bytes=MEDIUM),
         cost_estimate=LIGHT,
-    )(where, scaled, inner, hidden, scale, incoming, top)
+    )(where, scaled, inner, hidden, scale, incoming, share, other, top)
 
 
 def grads_kernel(where_ref, hidden_ref, scale_ref, gain_ref, projected_ref, *refs):
@@ -655,7 +670,8 @@
 
     _, z_after, z_far_low, z_far_high, z_before = z_ring
     _, y_after, y_far_low, y_far_high, y_before = y_ring
-    slim, rest = half // 2, shard - half // 2
+    slim = 3 * half // 8
+    rest = shard - slim
     corner = join(where, 0, (z_far_low, z_far_high), ((0, half), (0, half)), y_far_high)
     corner = ring_move(corner, "y", 2, (0,))
 
@@ -668,15 +684,16 @@
         where, 0, (y_far_low, y_far_high, y_after, y_before),
         ((0, half), (0, half), (slim, rest), (slim, rest)), theirs,
     )
-    z_pair = (ring_move(along_z, "z", -1, (0,)), ring_move(along_z, "z", 1, (0,)))
+    z_pair = (ring_move(along_z, "z", -1), ring_move(along_z, "z", 1))
     own, to_after, to_far, to_before = add_mine(mine, got, other, corner)
     from_before = ring_move(to_after, "y", 1, (1,))
     from_far = ring_move(to_far, "y", 2, (1,))
     from_after = ring_move(to_before, "y", -1, (1,))
     along_y = join(
         where, 0, (z_far_low, z_far_high, z_after, z_before),
-        ((0, half), (0, half), (0, slim), (0, slim)), from_before, from_far, from_after,
-    )
+        ((0, half), (0, half), (0, slim), (0, slim)), theirs,
+    )
+    along_y = after(along_y, (from_before, from_far, from_after))
     y_pair = (ring_move(along_y, "y", -1, (0,)), ring_move(along_y, "y", 1, (0,)))
     w_pieces = (*z_ring, *y_ring[1:], corner, *y_pair, *z_pair)
 
@@ -693,8 +710,6 @@
     other = swap(theirs, "pair", (0,))
     scaled, inner = low_scaled(mine, got, other, low_mixed, a_local, norm_gain, hidden, scale)
     inner = lax.psum(inner, tensor)
-    result = finish_low(where, scaled, inner, hidden, scale, low_in, top_grad)
-
     grads = make_grads(
         where, hidden, scale, norm_gain, projected, ([first], [low_dz], [top_mixed], [low_mixed])
     )
@@ -713,7 +728,9 @@
     add_up = functools.partial(round_kernel, 1.0)
     share = small_call(add_up, half_shape, (share, pair_share))
     other_share = lax.ppermute(share, "section", [(0, 1), (1, 0)])
-    bank_grad = small_call(add_up, jax.ShapeDtypeStruct(bank_shape, F32), (share, other_share), inner)
+    result, bank_grad = finish_low(
+        where, scaled, inner, hidden, scale, low_in, share, other_share, top_grad
+    )
     return (result[None], bank_grad)
 
 

time: 295 us -> 295 us (level)
    ppermute x22, waiting for transfers between devices: 89.6 us -> 102 us  [ring_move(): lax.ppermute(block, ('section', axis), ring_route(distance, sections))]
    ppermute x1, waiting for transfers between devices: 40.8 us -> 30.1 us  [shards(): low_in = lax.ppermute(top_grad, 'section', [(1, 0)])]
    ppermute x22, starting transfers between devices: 33.5 us -> 30 us  [ring_move(): lax.ppermute(block, ('section', axis), ring_route(distance, sections))]
    unnamed x66 -> x70, local copies, waits for them, and re-layouts: 10.9 us -> 11.7 us
  transfers between devices with their start and end apart: 30 -> 30, of which waited for: 17 -> 18; matrix products, arithmetic and copies ran while one was open for 2% -> 2% of each run, Pallas kernels for 10% -> 8%
where the time goes in v5:
time: 295 us; the launch traced here: 293 us
  waiting for transfers between devices  142 us (48%)
  Pallas kernels  48.9 us (17%)
  starting transfers between devices  47.3 us (16%)
  blocking collectives  34.9 us (12%)
  local copies, waits for them, and re-layouts  13.8 us (5%)
  matrix products  4.12 us (1%)
    ppermute x22, waiting for transfers between devices, ring_move(): lax.ppermute(block, ('section', axis), ring_route(distance, sections))  102 us
    ppermute x1, waiting for transfers between devices, shards(): low_in = lax.ppermute(top_grad, 'section', [(1, 0)])  30.1 us
    ppermute x22, starting transfers between devices, ring_move(): lax.ppermute(block, ('section', axis), ring_route(distance, sections))  30 us
    pallas_call x1, Pallas kernels, low_product(): pl.pallas_call(in_order(functools.partial(low_product_kernel, copies), 3...  16.4 us
    ppermute x6, starting transfers between devices, swap(): return lax.ppermute(block, ('section', axis), pairs)  15.8 us
    unnamed x70, local copies, waits for them, and re-layouts  11.7 us
    psum x1, blocking collectives, shards(): lax.psum(jnp.concatenate([jnp.sum(hidden_f * hidden_f, axis=1)[None], jnp...  11 us
    psum x1, blocking collectives, shards(): lax.psum(inner, tensor)  10.2 us
  transfers between devices with their start and end apart: 30, of which 18 were waited for; matrix products, arithmetic and copies ran while one was open for 2% of the time, Pallas kernels for 8%

profile of v5, /device:TPU:1, one launch (start us, length us, event | category | flops | bytes accessed | tf_op | source)
XLA Modules:
  0.0 293.2 jit_solution(10758774477060282066)
XLA Ops:
  0.6 4.7 %collective-permute-start.3 = (bf16[512,2048]{1,0:T(8,128)(2,1)}, bf16[512,2048]{1,0:T(8,128)(2,1)S(1)}, u32[]{:S(2)}, u32[]{:S(2)}) collective-permute-start(bf16[512,2048]{1,0:T(8,128)(2,1)} %bitcast.35), channel_id=1, source_target_pairs={{0,48},{16,0},{32,16},{48,32},{64,112},{80,64},{96,80},{112,96},{1... | collective-permute-start | bytes 6291464 | tf_op jit(solution)/shard_map/ppermute | solution.py:37
  5.4 1.6 copy-done.10
  9.5 2.0 shard_map.122.refs_1_.refs_5_
  11.5 2.8 collective-permute-start
  15.4 2.1 fusion.4
  17.5 1.7 fusion
  19.3 11.0 %psum.28 = f32[9,256]{1,0:T(8,128)S(1)} all-reduce(f32[9,256]{1,0:T(8,128)S(1)} %pad_maximum_fusion.1), channel_id=1, replica_groups=mesh['section'=2,'z'=4,'y'=4,'pair'=2,'core'=2] {'pair','core'}, use_global_device_ids=true, to_apply=%region_2.0 | all-reduce | flops 2304 | bytes 18432 | tf_op jit(solution)/shard_map/psum | solution.py:652
  30.5 19.5 %collective-permute-done.3.refs_0_.refs_6_.refs_3_.refs_4_ = bf16[512,2048]{1,0:T(8,128)(2,1)S(1)} collective-permute-done((bf16[512,2048]{1,0:T(8,128)(2,1)}, bf16[512,2048]{1,0:T(8,128)(2,1)S(1)}, u32[]{:S(2)}, u32[]{:S(2)}) %collective-permute-start.3) | collective-permute-done | bytes 2097184 | tf_op jit(solution)/shard_map/ppermute | solution.py:37
  49.9 3.1 %collective-permute-done.4.refs_1_.refs_9_.refs_4_.refs_7_ = bf16[512,2048]{1,0:T(8,128)(2,1)} collective-permute-done((bf16[512,2048]{1,0:T(8,128)(2,1)}, bf16[512,2048]{1,0:T(8,128)(2,1)}, u32[]{:S(2)}, u32[]{:S(2)}) %collective-permute-start.4) | collective-permute-done | bytes 2097184 | tf_op jit(solution)/shard_map/ppermute | solution.py:37
  53.0 1.3 shard_map.124
  55.9 2.7 collective-permute-done.refs_0_.refs_2_.refs_3_.refs_8_
  58.6 3.1 %collective-permute-done.1.refs_1_.refs_4_.refs_11_ = bf16[512,2048]{1,0:T(8,128)(2,1)} collective-permute-done((bf16[512,2048]{1,0:T(8,128)(2,1)}, bf16[512,2048]{1,0:T(8,128)(2,1)}, u32[]{:S(2)}, u32[]{:S(2)}) %collective-permute-start.1) | collective-permute-done | bytes 2097184 | tf_op jit(solution)/shard_map/ppermute | solution.py:37
  61.7 1.6 shard_map.123
  63.4 2.7 collective-permute-start.2
  66.0 11.2 %collective-permute-done.5.refs_7_.refs_1_.refs_5_ = bf16[256,2048]{1,0:T(8,128)(2,1)S(1)} collective-permute-done((bf16[256,2048]{1,0:T(8,128)(2,1)S(1)}, bf16[256,2048]{1,0:T(8,128)(2,1)S(1)}, u32[]{:S(2)}, u32[]{:S(2)}) %collective-permute-start.5) | collective-permute-done | bytes 1048608 | tf_op jit(solution)/shard_map/ppermute | solution.py:37
  77.2 2.4 collective-permute-done.6.refs_8_.refs_2_.refs_6_
  79.6 7.5 %collective-permute-done.7.refs_10_.refs_3_.refs_2_ = bf16[256,2048]{1,0:T(8,128)(2,1)S(1)} collective-permute-done((bf16[256,2048]{1,0:T(8,128)(2,1)S(1)}, bf16[256,2048]{1,0:T(8,128)(2,1)S(1)}, u32[]{:S(2)}, u32[]{:S(2)}) %collective-permute-start.7) | collective-permute-done | bytes 1048608 | tf_op jit(solution)/shard_map/ppermute | solution.py:37
  88.8 4.7 %shard_map.133 = bf16[1344,2048]{1,0:T(8,128)(2,1)} custom-call(s32[4]{0:T(128)S(1)} %pad_add_fusion.where_ref.refs_0_, bf16[256,2048]{1,0:T(8,128)(2,1)S(1)} %collective-permute-done.2.refs_3_.refs_1_.refs_9_, bf16[256,2048]{1,0:T(8,128)(2,1)S(1)} %collective-permute-done.7.refs_10_.refs_3_.refs_2_, ...), custom_call_target="tpu_custom_call" | custom-call | bytes 1048576 | tf_op jit(solution)/shard_map/pallas_call | solution.py:136
  93.5 2.2 collective-permute-start.17
  96.5 3.1 %collective-permute-start.10 = (bf16[512,2048]{1,0:T(8,128)(2,1)S(1)}, bf16[512,2048]{1,0:T(8,128)(2,1)S(1)}, u32[]{:S(2)}, u32[]{:S(2)}) collective-permute-start(bf16[512,2048]{1,0:T(8,128)(2,1)S(1)} %shard_map.127), channel_id=1, source_target_pairs={{0,8},{4,12},{8,0},{12,4},{1,9},{5,13},{9,1},{13,5},{2,10},{6,14},... | collective-permute-start | bytes 6291464 | tf_op jit(solution)/shard_map/ppermute | solution.py:37
  100.3 43.1 %collective-permute-done.10.refs_3_.refs_12_ = bf16[512,2048]{1,0:T(8,128)(2,1)S(1)} collective-permute-done((bf16[512,2048]{1,0:T(8,128)(2,1)S(1)}, bf16[512,2048]{1,0:T(8,128)(2,1)S(1)}, u32[]{:S(2)}, u32[]{:S(2)}) %collective-permute-start.10) | collective-permute-done | bytes 2097184 | tf_op jit(solution)/shard_map/ppermute | solution.py:37
  147.1 3.0 %shard_map.132 = bf16[704,2048]{1,0:T(8,128)(2,1)} custom-call(s32[4]{0:T(128)S(1)} %pad_add_fusion.where_ref.refs_0_, bf16[256,2048]{1,0:T(8,128)(2,1)S(1)} %collective-permute-done.5.refs_7_.refs_1_.refs_5_, bf16[256,2048]{1,0:T(8,128)(2,1)S(1)} %collective-permute-done.6.refs_8_.refs_2_.refs_6_, bf16[512,2048]{1,0:T(8,128)(2,1)S(1)} %copy-done.4, ...), custom_call_target="tpu_custom_call" | custom-call | bytes 1048576 | tf_op jit(solution)/shard_map/pallas_call | solution.py:136
  150.2 4.1 %collective-permute-start.15 = (bf16[704,2048]{1,0:T(8,128)(2,1)}, bf16[704,2048]{1,0:T(8,128)(2,1)}, u32[]{:S(2)}, u32[]{:S(2)}) collective-permute-start(bf16[704,2048]{1,0:T(8,128)(2,1)} %shard_map.132), channel_id=1, source_target_pairs={{0,12},{4,0},{8,4},{12,8},{1,13},{5,1},{9,5},{13,9},{2,14},{6,2},{... | collective-permute-start | bytes 8650760 | tf_op jit(solution)/shard_map/ppermute | solution.py:37
  154.3 1.9 collective-permute-start.16
  156.3 2.7 shard_map.129
  159.0 10.2 %psum.29.inner_ref = f32[8,256]{1,0:T(8,128)S(1)} all-reduce(f32[8,256]{1,0:T(8,128)S(1)} %get-tuple-element.37), channel_id=1, replica_groups=mesh['section'=2,'z'=4,'y'=4,'pair'=2,'core'=2] {'pair','core'}, use_global_device_ids=true, to_apply=%region_3.0 | all-reduce | flops 2048 | bytes 16384 | tf_op jit(solution)/shard_map/psum | solution.py:702
  169.3 1.6 shard_map.130.top_ref
  170.9 1.4 collective-permute-start.14
  172.4 30.1 %collective-permute-done.14.refs_0_.incoming_ref = bf16[256,2048]{1,0:T(8,128)(2,1)} collective-permute-done((bf16[256,2048]{1,0:T(8,128)(2,1)}, bf16[256,2048]{1,0:T(8,128)(2,1)}, u32[]{:S(2)}, u32[]{:S(2)}) %collective-permute-start.14) | collective-permute-done | bytes 1048608 | tf_op jit(solution)/shard_map/ppermute | solution.py:703
  203.8 2.1 shard_map.131
  206.9 7.4 %psum.30.refs_17_.mixed_ref.refs_8_ = f32[4,256]{1,0:T(4,128)S(1)} all-reduce(f32[4,256]{1,0:T(4,128)S(1)} %get-tuple-element.40), channel_id=1, replica_groups=mesh['section'=2,'z'=4,'y'=4,'pair'=2,'core'=2] {'pair','core'}, use_global_device_ids=true, to_apply=%region_4.0 | all-reduce | flops 1024 | bytes 8192 | tf_op jit(solution)/shard_map/psum | solution.py:706
  214.3 2.3 collective-permute-done.16.refs_14_
  217.8 16.4 %shard_map.134 = (bf16[256,2048]{1,0:T(8,128)(2,1)S(1)}, bf16[256,2048]{1,0:T(8,128)(2,1)S(1)}, bf16[2,256,2048]{2,1,0:T(8,128)(2,1)}) custom-call(s32[4]{0:T(128)S(1)} %pad_add_fusion.where_ref.refs_0_, s32[32]{0:T(128)S(1)} %fusion.16.refs_1_, bf16[256,2048]{1,0:T(8,128)(2,1)S(1)} %copy-done.19, bf16[512,2048]{1,0:T(8,128)(2,1)} %bitcast.37, ...), custom_call_target="tpu_custom_call" | custom-call | flops 8589934592 | bytes 33554432 | tf_op jit(solution)/shard_map/pallas_call | solution.py:355
  234.3 8.0 %collective-permute-start.19 = (bf16[2,256,2048]{2,1,0:T(8,128)(2,1)}, bf16[2,256,2048]{2,1,0:T(8,128)(2,1)S(1)}, u32[]{:S(2)}, u32[]{:S(2)}) collective-permute-start(bf16[2,256,2048]{2,1,0:T(8,128)(2,1)} %get-tuple-element.42.refs_4_), channel_id=1, source_target_pairs={{0,1},{1,0},{2,3},{3,2},{4,5},{5,4},{6,7},{7,6},{8,9},{9,8},{10,11... | collective-permute-start | bytes 6291464 | tf_op jit(solution)/shard_map/ppermute | solution.py:42
  242.2 4.0 %collective-permute-done.19.got_ref = bf16[2,256,2048]{2,1,0:T(8,128)(2,1)S(1)} collective-permute-done((bf16[2,256,2048]{2,1,0:T(8,128)(2,1)}, bf16[2,256,2048]{2,1,0:T(8,128)(2,1)S(1)}, u32[]{:S(2)}, u32[]{:S(2)}) %collective-permute-start.19) | collective-permute-done | bytes 2097184 | tf_op jit(solution)/shard_map/ppermute | solution.py:42
  247.4 3.1 %collective-permute-start.20 = (bf16[256,2048]{1,0:T(8,128)(2,1)}, bf16[256,2048]{1,0:T(8,128)(2,1)}, u32[]{:S(2)}, u32[]{:S(2)}) collective-permute-start(bf16[256,2048]{1,0:T(8,128)(2,1)} %shard_map.135.refs_5_), channel_id=1, source_target_pairs={{0,2},{2,0},{1,3},{3,1},{4,6},{6,4},{5,7},{7,5},{8,10},{10,8},{9,1... | collective-permute-start | bytes 3145736 | tf_op jit(solution)/shard_map/ppermute | solution.py:42
  250.5 2.4 shard_map.137.refs_0_
  254.4 2.0 collective-permute-done.21.refs_1_
  257.7 1.5 collective-permute-done.23.refs_3_
  259.2 2.5 collective-permute-start.24
  263.9 2.6 collective-permute-done.25.refs_3_
  266.8 1.3 shard_map.139.refs_0_
  268.1 2.9 collective-permute-start.27
  272.6 4.4 %collective-permute-done.28.refs_1_ = bf16[256,256]{1,0:T(8,128)(2,1)S(1)} collective-permute-done((bf16[256,256]{1,0:T(8,128)(2,1)S(1)}, bf16[256,256]{1,0:T(8,128)(2,1)S(1)}, u32[]{:S(2)}, u32[]{:S(2)}) %collective-permute-start.28) | collective-permute-done | bytes 131104 | tf_op jit(solution)/shard_map/ppermute | solution.py:42
  277.2 3.4 %shard_map.136 = (bf16[256,2048]{1,0:T(8,128)(2,1)S(1)}, f32[8,256]{1,0:T(8,128)S(1)}) custom-call(bf16[256,2048]{1,0:T(8,128)(2,1)S(1)} %copy-done.24, bf16[2,256,2048]{2,1,0:T(8,128)(2,1)S(1)} %collective-permute-done.19.got_ref, bf16[256,2048]{1,0:T(8,128)(2,1)} %collective-permute-done.20.other_ref, f32[4,256]{1,0:T(4,128)S(1)} %psum.30.refs_17_.mixed_ref.refs_8_, ...), custom_call_target="tpu_custom_call" | custom-call | bytes 1048576 | tf_op jit(solution)/shard_map/pallas_call | solution.py:467
  281.6 6.3 %psum.31.inner_ref = f32[8,256]{1,0:T(8,128)S(1)} all-reduce(f32[8,256]{1,0:T(8,128)S(1)} %get-tuple-element.45), channel_id=1, replica_groups=mesh['section'=2,'z'=4,'y'=4,'pair'=2,'core'=2] {'pair','core'}, use_global_device_ids=true, to_apply=%region_5.6 | all-reduce | flops 2048 | bytes 16384 | tf_op jit(solution)/shard_map/psum | solution.py:712
  287.9 1.3 copy-done.22
  290.0 3.0 %shard_map.142 = (bf16[256,2048]{1,0:T(8,128)(2,1)}, f32[256,256]{1,0:T(8,128)}) custom-call(s32[4]{0:T(128)S(1)} %pad_add_fusion.where_ref.refs_0_, bf16[256,2048]{1,0:T(8,128)(2,1)S(1)} %copy-done.22, f32[8,256]{1,0:T(8,128)S(1)} %psum.31.inner_ref, bf16[256,2048]{1,0:T(8,128)(2,1)S(1)} %bitcast.34, f32[256,1]{1,0:T(8,128)S(1)} %copy.28.refs_2_.scale_ref, ...), custom_call_target="tpu_custom_call" | custom-call | bytes 1048576 | tf_op jit(solution)/shard_map/pallas_call | solution.py:538
  (132 shorter events, 25.9 us)
Async XLA Ops:
  0.6 14.1 %copy-start = (f32[256,256]{1,0:T(8,128)S(1)}, f32[256,256]{1,0:T(8,128)}, u32[]{:S(2)}) copy-start(f32[256,256]{1,0:T(8,128)} %param.15) | copy-start | bytes 786436
  0.6 49.3 %collective-permute-start.3 = (bf16[512,2048]{1,0:T(8,128)(2,1)}, bf16[512,2048]{1,0:T(8,128)(2,1)S(1)}, u32[]{:S(2)}, u32[]{:S(2)}) collective-permute-start(bf16[512,2048]{1,0:T(8,128)(2,1)} %bitcast.35), channel_id=1, source_target_pairs={{0,48},{16,0},{32,16},{48,32},{64,112},{80,64},{96,80},{112,96},{1... | collective-permute-start | bytes 6291464 | tf_op jit(solution)/shard_map/ppermute | solution.py:37
  5.3 47.7 %collective-permute-start.4 = (bf16[512,2048]{1,0:T(8,128)(2,1)}, bf16[512,2048]{1,0:T(8,128)(2,1)}, u32[]{:S(2)}, u32[]{:S(2)}) collective-permute-start(bf16[512,2048]{1,0:T(8,128)(2,1)} %bitcast.36), channel_id=1, source_target_pairs={{0,16},{16,32},{32,48},{48,0},{64,80},{80,96},{96,112},{112,64},{1... | collective-permute-start | bytes 6291464 | tf_op jit(solution)/shard_map/ppermute | solution.py:37
  9.5 4.9 %copy-start.30 = (s32[1,2,128,2]{2,3,1,0:T(2,128)S(1)}, s32[1,2,128,2]{2,3,1,0:T(2,128)}, u32[]{:S(2)}) copy-start(s32[1,2,128,2]{2,3,1,0:T(2,128)} %param.16) | copy-start | bytes 6148
  9.5 5.0 %copy-start.31 = (f32[1,2,128,2]{2,3,1,0:T(2,128)S(1)}, f32[1,2,128,2]{2,3,1,0:T(2,128)}, u32[]{:S(2)}) copy-start(f32[1,2,128,2]{2,3,1,0:T(2,128)} %param.17) | copy-start | bytes 6148
  9.5 5.7 %copy-start.2 = (bf16[1,256,2048]{2,1,0:T(8,128)(2,1)S(1)}, bf16[1,256,2048]{2,1,0:T(8,128)(2,1)}, u32[]{:S(2)}) copy-start(bf16[1,256,2048]{2,1,0:T(8,128)(2,1)} %param.11) | copy-start | bytes 3145732
  11.5 6.0 %copy-start.27 = (f32[1,2048]{1,0:T(1,128)S(1)}, f32[1,2048]{1,0:T(1,128)}, u32[]{:S(2)}) copy-start(f32[1,2048]{1,0:T(1,128)} %refs_3_.1) | copy-start | bytes 24580
  11.5 47.1 %collective-permute-start = (bf16[512,2048]{1,0:T(8,128)(2,1)}, bf16[512,2048]{1,0:T(8,128)(2,1)}, u32[]{:S(2)}, u32[]{:S(2)}) collective-permute-start(bf16[512,2048]{1,0:T(8,128)(2,1)} %shard_map.122.refs_1_.refs_5_), channel_id=1, source_target_pairs={{0,12},{4,0},{8,4},{12,8},{64,76},{68,64},{72,68},{76,72},{1,13},{... | collective-permute-start | bytes 6291464 | tf_op jit(solution)/shard_map/ppermute | solution.py:37
  14.3 47.4 %collective-permute-start.1 = (bf16[512,2048]{1,0:T(8,128)(2,1)}, bf16[512,2048]{1,0:T(8,128)(2,1)}, u32[]{:S(2)}, u32[]{:S(2)}) collective-permute-start(bf16[512,2048]{1,0:T(8,128)(2,1)} %shard_map.122.refs_1_.refs_5_), channel_id=1, source_target_pairs={{0,4},{4,8},{8,12},{12,0},{64,68},{68,72},{72,76},{76,64},{1,5},{5... | collective-permute-start | bytes 6291464 | tf_op jit(solution)/shard_map/ppermute | solution.py:37
  14.8 15.5 %copy-start.28 = (f32[2,4,8,256]{3,2,1,0:T(8,128)}, f32[2,4,8,256]{3,2,1,0:T(8,128)S(1)}, u32[]{:S(2)}) copy-start(f32[2,4,8,256]{3,2,1,0:T(8,128)S(1)} %select_reduce_fusion) | copy-start | bytes 196612
  54.3 22.9 %collective-permute-start.5 = (bf16[256,2048]{1,0:T(8,128)(2,1)S(1)}, bf16[256,2048]{1,0:T(8,128)(2,1)S(1)}, u32[]{:S(2)}, u32[]{:S(2)}) collective-permute-start(bf16[256,2048]{1,0:T(8,128)(2,1)S(1)} %get-tuple-element.26), channel_id=1, source_target_pairs={{0,48},{16,0},{32,16},{48,32},{64,112},{80,64},{96,80},{112,96},{1... | collective-permute-start | bytes 3145736 | tf_op jit(solution)/shard_map/ppermute | solution.py:37
  55.4 31.6 %copy-start.11 = (bf16[1,512,2048]{2,1,0:T(8,128)(2,1)S(1)}, bf16[1,512,2048]{2,1,0:T(8,128)(2,1)}, u32[]{:S(2)}) copy-start(bf16[1,512,2048]{2,1,0:T(8,128)(2,1)} %param.14) | copy-start | bytes 6291460
  55.4 24.1 %collective-permute-start.6 = (bf16[256,2048]{1,0:T(8,128)(2,1)S(1)}, bf16[256,2048]{1,0:T(8,128)(2,1)S(1)}, u32[]{:S(2)}, u32[]{:S(2)}) collective-permute-start(bf16[256,2048]{1,0:T(8,128)(2,1)S(1)} %get-tuple-element.27), channel_id=1, source_target_pairs={{0,16},{16,32},{32,48},{48,0},{64,80},{80,96},{96,112},{112,64},{1... | collective-permute-start | bytes 3145736 | tf_op jit(solution)/shard_map/ppermute | solution.py:37
  63.3 23.8 %collective-permute-start.7 = (bf16[256,2048]{1,0:T(8,128)(2,1)S(1)}, bf16[256,2048]{1,0:T(8,128)(2,1)S(1)}, u32[]{:S(2)}, u32[]{:S(2)}) collective-permute-start(bf16[256,2048]{1,0:T(8,128)(2,1)S(1)} %get-tuple-element.28), channel_id=1, source_target_pairs={{0,4},{4,8},{8,12},{12,0},{64,68},{68,72},{72,76},{76,64},{1,5},{5... | collective-permute-start | bytes 3145736 | tf_op jit(solution)/shard_map/ppermute | solution.py:37
  63.4 23.7 %collective-permute-start.2 = (bf16[256,2048]{1,0:T(8,128)(2,1)S(1)}, bf16[256,2048]{1,0:T(8,128)(2,1)S(1)}, u32[]{:S(2)}, u32[]{:S(2)}) collective-permute-start(bf16[256,2048]{1,0:T(8,128)(2,1)S(1)} %get-tuple-element.25), channel_id=1, source_target_pairs={{0,12},{4,0},{8,4},{12,8},{64,76},{68,64},{72,68},{76,72},{1,13},{... | collective-permute-start | bytes 3145736 | tf_op jit(solution)/shard_map/ppermute | solution.py:37
  77.2 69.9 %copy-start.5 = (bf16[256,2048]{1,0:T(8,128)(2,1)}, bf16[256,2048]{1,0:T(8,128)(2,1)S(1)}, u32[]{:S(2)}) copy-start(bf16[256,2048]{1,0:T(8,128)(2,1)S(1)} %collective-permute-done.5.refs_7_.refs_1_.refs_5_) | copy-start | bytes 3145732
  79.6 67.5 %copy-start.7 = (bf16[256,2048]{1,0:T(8,128)(2,1)}, bf16[256,2048]{1,0:T(8,128)(2,1)S(1)}, u32[]{:S(2)}) copy-start(bf16[256,2048]{1,0:T(8,128)(2,1)S(1)} %collective-permute-done.6.refs_8_.refs_2_.refs_6_) | copy-start | bytes 3145732
  87.1 8.6 %copy-start.9 = (bf16[256,2048]{1,0:T(8,128)(2,1)}, bf16[256,2048]{1,0:T(8,128)(2,1)S(1)}, u32[]{:S(2)}) copy-start(bf16[256,2048]{1,0:T(8,128)(2,1)S(1)} %collective-permute-done.7.refs_10_.refs_3_.refs_2_) | copy-start | bytes 3145732
  87.7 0.8 collective-permute-start.8
  93.5 123.1 %collective-permute-start.17 = (bf16[1344,2048]{1,0:T(8,128)(2,1)}, bf16[1344,2048]{1,0:T(8,128)(2,1)}, u32[]{:S(2)}, u32[]{:S(2)}) collective-permute-start(bf16[1344,2048]{1,0:T(8,128)(2,1)} %shard_map.133), channel_id=1, source_target_pairs={{0,48},{16,0},{32,16},{48,32},{64,112},{80,64},{96,80},{112,96},{1... | collective-permute-start | bytes 16515080 | tf_op jit(solution)/shard_map/ppermute | solution.py:37
  95.6 121.0 %collective-permute-start.18 = (bf16[1344,2048]{1,0:T(8,128)(2,1)}, bf16[1344,2048]{1,0:T(8,128)(2,1)}, u32[]{:S(2)}, u32[]{:S(2)}) collective-permute-start(bf16[1344,2048]{1,0:T(8,128)(2,1)} %shard_map.133), channel_id=1, source_target_pairs={{0,16},{16,32},{32,48},{48,0},{64,80},{80,96},{96,112},{112,64},{1... | collective-permute-start | bytes 16515080 | tf_op jit(solution)/shard_map/ppermute | solution.py:37
  96.5 46.9 %collective-permute-start.10 = (bf16[512,2048]{1,0:T(8,128)(2,1)S(1)}, bf16[512,2048]{1,0:T(8,128)(2,1)S(1)}, u32[]{:S(2)}, u32[]{:S(2)}) collective-permute-start(bf16[512,2048]{1,0:T(8,128)(2,1)S(1)} %shard_map.127), channel_id=1, source_target_pairs={{0,8},{4,12},{8,0},{12,4},{1,9},{5,13},{9,1},{13,5},{2,10},{6,14},... | collective-permute-start | bytes 6291464 | tf_op jit(solution)/shard_map/ppermute | solution.py:37
  99.6 43.8 %collective-permute-start.9 = (bf16[1024,512]{1,0:T(8,128)(2,1)S(1)}, bf16[1024,512]{1,0:T(8,128)(2,1)S(1)}, u32[]{:S(2)}, u32[]{:S(2)}) collective-permute-start(bf16[1024,512]{1,0:T(8,128)(2,1)S(1)} %shard_map.126.refs_5_), channel_id=1, source_target_pairs={{64,66},{66,64},{65,67},{67,65},{68,70},{70,68},{69,71},{71,69},{7... | collective-permute-start | bytes 3145736 | tf_op jit(solution)/shard_map/ppermute | solution.py:42
  144.7 5.4 %collective-permute-start.11 = (bf16[256,512]{1,0:T(8,128)(2,1)S(1)}, bf16[256,512]{1,0:T(8,128)(2,1)S(1)}, u32[]{:S(2)}, u32[]{:S(2)}) collective-permute-start(bf16[256,512]{1,0:T(8,128)(2,1)S(1)} %get-tuple-element.33), channel_id=1, source_target_pairs={{64,76},{68,64},{72,68},{76,72},{65,77},{69,65},{73,69},{77,73},{6... | collective-permute-start | bytes 786440 | tf_op jit(solution)/shard_map/ppermute | solution.py:37
  145.5 4.6 %collective-permute-start.12 = (bf16[256,512]{1,0:T(8,128)(2,1)S(1)}, bf16[256,512]{1,0:T(8,128)(2,1)S(1)}, u32[]{:S(2)}, u32[]{:S(2)}) collective-permute-start(bf16[256,512]{1,0:T(8,128)(2,1)S(1)} %get-tuple-element.34), channel_id=1, source_target_pairs={{64,72},{68,76},{72,64},{76,68},{65,73},{69,77},{73,65},{77,69},{6... | collective-permute-start | bytes 786440 | tf_op jit(solution)/shard_map/ppermute | solution.py:37
  146.2 3.9 %collective-permute-start.13 = (bf16[256,512]{1,0:T(8,128)(2,1)S(1)}, bf16[256,512]{1,0:T(8,128)(2,1)S(1)}, u32[]{:S(2)}, u32[]{:S(2)}) collective-permute-start(bf16[256,512]{1,0:T(8,128)(2,1)S(1)} %get-tuple-element.35), channel_id=1, source_target_pairs={{64,68},{68,72},{72,76},{76,64},{65,69},{69,73},{73,77},{77,65},{6... | collective-permute-start | bytes 786440 | tf_op jit(solution)/shard_map/ppermute | solution.py:37
  150.1 19.1 %copy-start.17 = (bf16[256,2048]{1,0:T(8,128)(2,1)S(1)}, bf16[256,2048]{1,0:T(8,128)(2,1)}, u32[]{:S(2)}) copy-start(bf16[256,2048]{1,0:T(8,128)(2,1)} %incoming_ref.3) | copy-start | bytes 3145732
  150.2 64.2 %collective-permute-start.15 = (bf16[704,2048]{1,0:T(8,128)(2,1)}, bf16[704,2048]{1,0:T(8,128)(2,1)}, u32[]{:S(2)}, u32[]{:S(2)}) collective-permute-start(bf16[704,2048]{1,0:T(8,128)(2,1)} %shard_map.132), channel_id=1, source_target_pairs={{0,12},{4,0},{8,4},{12,8},{1,13},{5,1},{9,5},{13,9},{2,14},{6,2},{... | collective-permute-start | bytes 8650760 | tf_op jit(solution)/shard_map/ppermute | solution.py:37
  154.3 62.3 %collective-permute-start.16 = (bf16[704,2048]{1,0:T(8,128)(2,1)}, bf16[704,2048]{1,0:T(8,128)(2,1)}, u32[]{:S(2)}, u32[]{:S(2)}) collective-permute-start(bf16[704,2048]{1,0:T(8,128)(2,1)} %shard_map.132), channel_id=1, source_target_pairs={{0,4},{4,8},{8,12},{12,0},{1,5},{5,9},{9,13},{13,1},{2,6},{6,10},{... | collective-permute-start | bytes 8650760 | tf_op jit(solution)/shard_map/ppermute | solution.py:37
  170.9 45.7 %copy-start.6 = (bf16[256,2048]{1,0:T(8,128)(2,1)S(1)}, bf16[256,2048]{1,0:T(8,128)(2,1)}, u32[]{:S(2)}) copy-start(bf16[256,2048]{1,0:T(8,128)(2,1)} %copy-done.5) | copy-start | bytes 3145732
  170.9 45.7 %copy-start.8 = (bf16[256,2048]{1,0:T(8,128)(2,1)S(1)}, bf16[256,2048]{1,0:T(8,128)(2,1)}, u32[]{:S(2)}) copy-start(bf16[256,2048]{1,0:T(8,128)(2,1)} %copy-done.7) | copy-start | bytes 3145732
  170.9 31.7 %collective-permute-start.14 = (bf16[256,2048]{1,0:T(8,128)(2,1)}, bf16[256,2048]{1,0:T(8,128)(2,1)}, u32[]{:S(2)}, u32[]{:S(2)}) collective-permute-start(bf16[256,2048]{1,0:T(8,128)(2,1)} %shard_map.130.top_ref), channel_id=1, source_target_pairs={{64,0},{65,1},{66,2},{67,3},{68,4},{69,5},{70,6},{71,7},{72,8},{73... | collective-permute-start | bytes 3145736 | tf_op jit(solution)/shard_map/ppermute | solution.py:703
  234.2 13.2 %copy-start.23 = (bf16[256,2048]{1,0:T(8,128)(2,1)}, bf16[256,2048]{1,0:T(8,128)(2,1)S(1)}, u32[]{:S(2)}) copy-start(bf16[256,2048]{1,0:T(8,128)(2,1)S(1)} %get-tuple-element.41.keep_ref) | copy-start | bytes 3145732
  234.3 11.9 %collective-permute-start.19 = (bf16[2,256,2048]{2,1,0:T(8,128)(2,1)}, bf16[2,256,2048]{2,1,0:T(8,128)(2,1)S(1)}, u32[]{:S(2)}, u32[]{:S(2)}) collective-permute-start(bf16[2,256,2048]{2,1,0:T(8,128)(2,1)} %get-tuple-element.42.refs_4_), channel_id=1, source_target_pairs={{0,1},{1,0},{2,3},{3,2},{4,5},{5,4},{6,7},{7,6},{8,9},{9,8},{10,11... | collective-permute-start | bytes 6291464 | tf_op jit(solution)/shard_map/ppermute | solution.py:42
  247.4 29.7 %collective-permute-start.20 = (bf16[256,2048]{1,0:T(8,128)(2,1)}, bf16[256,2048]{1,0:T(8,128)(2,1)}, u32[]{:S(2)}, u32[]{:S(2)}) collective-permute-start(bf16[256,2048]{1,0:T(8,128)(2,1)} %shard_map.135.refs_5_), channel_id=1, source_target_pairs={{0,2},{2,0},{1,3},{3,1},{4,6},{6,4},{5,7},{7,5},{8,10},{10,8},{9,1... | collective-permute-start | bytes 3145736 | tf_op jit(solution)/shard_map/ppermute | solution.py:42
  250.5 8.7 %copy-start.20 = (bf16[2,256,2048]{2,1,0:T(8,128)(2,1)S(1)}, bf16[2,256,2048]{2,1,0:T(8,128)(2,1)}, u32[]{:S(2)}) copy-start(bf16[2,256,2048]{2,1,0:T(8,128)(2,1)} %get-tuple-element.42.refs_4_) | copy-start | bytes 6291460
  252.9 9.4 %copy-start.29 = (f32[2,4,8,256]{3,2,1,0:T(8,128)S(1)}, f32[2,4,8,256]{3,2,1,0:T(8,128)}, u32[]{:S(2)}) copy-start(f32[2,4,8,256]{3,2,1,0:T(8,128)} %copy-done.28) | copy-start | bytes 196612
  252.9 3.6 %collective-permute-start.21 = (f32[8,2048]{1,0:T(8,128)S(1)}, f32[8,2048]{1,0:T(8,128)S(1)}, u32[]{:S(2)}, u32[]{:S(2)}) collective-permute-start(f32[8,2048]{1,0:T(8,128)S(1)} %shard_map.137.refs_0_), channel_id=1, source_target_pairs={{0,12},{4,0},{8,4},{12,8},{64,76},{68,64},{72,68},{76,72},{1,13},{... | collective-permute-start | bytes 196616 | tf_op jit(solution)/shard_map/ppermute | solution.py:37
  253.0 4.7 %collective-permute-start.22 = (f32[8,2048]{1,0:T(8,128)S(1)}, f32[8,2048]{1,0:T(8,128)S(1)}, u32[]{:S(2)}, u32[]{:S(2)}) collective-permute-start(f32[8,2048]{1,0:T(8,128)S(1)} %shard_map.137.refs_0_), channel_id=1, source_target_pairs={{0,8},{4,12},{8,0},{12,4},{64,72},{68,76},{72,64},{76,68},{1,9},{5... | collective-permute-start | bytes 196616 | tf_op jit(solution)/shard_map/ppermute | solution.py:37
  253.6 5.6 %collective-permute-start.23 = (f32[8,2048]{1,0:T(8,128)S(1)}, f32[8,2048]{1,0:T(8,128)S(1)}, u32[]{:S(2)}, u32[]{:S(2)}) collective-permute-start(f32[8,2048]{1,0:T(8,128)S(1)} %shard_map.137.refs_0_), channel_id=1, source_target_pairs={{0,4},{4,8},{8,12},{12,0},{64,68},{68,72},{72,76},{76,64},{1,5},{5... | collective-permute-start | bytes 196616 | tf_op jit(solution)/shard_map/ppermute | solution.py:37
  259.2 4.7 %collective-permute-start.24 = (f32[8,2048]{1,0:T(8,128)S(1)}, f32[8,2048]{1,0:T(8,128)S(1)}, u32[]{:S(2)}, u32[]{:S(2)}) collective-permute-start(f32[8,2048]{1,0:T(8,128)S(1)} %shard_map.138.refs_1_), channel_id=1, source_target_pairs={{0,48},{16,0},{32,16},{48,32},{64,112},{80,64},{96,80},{112,96},{1... | collective-permute-start | bytes 196616 | tf_op jit(solution)/shard_map/ppermute | solution.py:37
  261.7 4.8 %collective-permute-start.25 = (f32[8,2048]{1,0:T(8,128)S(1)}, f32[8,2048]{1,0:T(8,128)}, u32[]{:S(2)}, u32[]{:S(2)}) collective-permute-start(f32[8,2048]{1,0:T(8,128)S(1)} %shard_map.138.refs_1_), channel_id=1, source_target_pairs={{0,32},{16,48},{32,0},{48,16},{64,96},{80,112},{96,64},{112,80},{1... | collective-permute-start | bytes 196616 | tf_op jit(solution)/shard_map/ppermute | solution.py:37
  261.7 5.1 %collective-permute-start.26 = (f32[8,2048]{1,0:T(8,128)S(1)}, f32[8,2048]{1,0:T(8,128)}, u32[]{:S(2)}, u32[]{:S(2)}) collective-permute-start(f32[8,2048]{1,0:T(8,128)S(1)} %shard_map.138.refs_1_), channel_id=1, source_target_pairs={{0,16},{16,32},{32,48},{48,0},{64,80},{80,96},{96,112},{112,64},{1... | collective-permute-start | bytes 196616 | tf_op jit(solution)/shard_map/ppermute | solution.py:37
  263.9 13.3 %copy-start.24 = (bf16[256,2048]{1,0:T(8,128)(2,1)S(1)}, bf16[256,2048]{1,0:T(8,128)(2,1)}, u32[]{:S(2)}) copy-start(bf16[256,2048]{1,0:T(8,128)(2,1)} %copy-done.23) | copy-start | bytes 3145732
  268.1 4.1 %collective-permute-start.27 = (f32[256,256]{1,0:T(8,128)S(1)}, f32[256,256]{1,0:T(8,128)S(1)}, u32[]{:S(2)}, u32[]{:S(2)}) collective-permute-start(f32[256,256]{1,0:T(8,128)S(1)} %shard_map.139.refs_0_), channel_id=1, source_target_pairs={{0,1},{1,0},{64,65},{65,64},{2,3},{3,2},{66,67},{67,66},{4,5},{5,4... | collective-permute-start | bytes 786440 | tf_op jit(solution)/shard_map/ppermute | solution.py:42
  272.2 4.8 %collective-permute-start.28 = (bf16[256,256]{1,0:T(8,128)(2,1)S(1)}, bf16[256,256]{1,0:T(8,128)(2,1)S(1)}, u32[]{:S(2)}, u32[]{:S(2)}) collective-permute-start(bf16[256,256]{1,0:T(8,128)(2,1)S(1)} %shard_map.140.refs_0_), channel_id=1, source_target_pairs={{0,2},{2,0},{64,66},{66,64},{1,3},{3,1},{65,67},{67,65},{4,6},{6,4... | collective-permute-start | bytes 393224 | tf_op jit(solution)/shard_map/ppermute | solution.py:42
  277.0 10.8 %collective-permute-start.29 = (bf16[256,256]{1,0:T(8,128)(2,1)S(1)}, bf16[256,256]{1,0:T(8,128)(2,1)}, u32[]{:S(2)}, u32[]{:S(2)}) collective-permute-start(bf16[256,256]{1,0:T(8,128)(2,1)S(1)} %shard_map.141.share_ref), channel_id=1, source_target_pairs={{0,64},{64,0},{1,65},{65,1},{2,66},{66,2},{3,67},{67,3},{4,68},{68... | collective-permute-start | bytes 393224 | tf_op jit(solution)/shard_map/ppermute | solution.py:730
  287.8 5.2 %copy-start.1 = (f32[256,256]{1,0:T(8,128)S(1)}, f32[256,256]{1,0:T(8,128)}, u32[]{:S(2)}) copy-start(f32[256,256]{1,0:T(8,128)} %param.15) | copy-start | bytes 786436
  (17 other events, 34.8 us)

commit v6 on v5

--- a/solution.py
+++ b/solution.py
@@ -285,7 +285,7 @@
     for d in (1, 3):
         take(y_pair[d], 0, shard, (2, d, 0), (2, d, 1))
         take(z_pair[d], 0, shard, (d, 2, 0), (d, 2, 1))
-    slim = 3 * wide // 8
+    slim = 112
     rest = shard - slim
     for i, d in enumerate((1, 3)):
         for j, e in enumerate((1, 3)):
@@ -670,10 +670,10 @@
 
     _, z_after, z_far_low, z_far_high, z_before = z_ring
     _, y_after, y_far_low, y_far_high, y_before = y_ring
-    slim = 3 * half // 8
+    slim = 112
     rest = shard - slim
-    corner = join(where, 0, (z_far_low, z_far_high), ((0, half), (0, half)), y_far_high)
-    corner = ring_move(corner, "y", 2, (0,))
+    corner_parts = join(where, 0, (z_far_low, z_far_high), ((0, half), (0, half)), y_far_high)
+    corner = ring_move(corner_parts, "y", 2, (0,))
 
     dz_pieces = (y_ring[0], y_ring[1], y_ring[2], y_ring[4])
     mine, keep, send = top_product(where, tokens, dz_pieces, z_ring, y_far_high)
@@ -685,14 +685,14 @@
         ((0, half), (0, half), (slim, rest), (slim, rest)), theirs,
     )
     z_pair = (ring_move(along_z, "z", -1), ring_move(along_z, "z", 1))
-    own, to_after, to_far, to_before = add_mine(mine, got, other, corner)
+    along_y = join(
+        where, 0, (z_far_low, z_far_high, z_after, z_before),
+        ((0, half), (0, half), (0, slim), (0, slim)), theirs,
+    )
+    own, to_after, to_far, to_before = add_mine(mine, got, other, corner, along_y)
     from_before = ring_move(to_after, "y", 1, (1,))
     from_far = ring_move(to_far, "y", 2, (1,))
     from_after = ring_move(to_before, "y", -1, (1,))
-    along_y = join(
-        where, 0, (z_far_low, z_far_high, z_after, z_before),
-        ((0, half), (0, half), (0, slim), (0, slim)), theirs,
-    )
     along_y = after(along_y, (from_before, from_far, from_after))
     y_pair = (ring_move(along_y, "y", -1, (0,)), ring_move(along_y, "y", 1, (0,)))
     w_pieces = (*z_ring, *y_ring[1:], corner, *y_pair, *z_pair)

time: 295 us -> 292 us (0.990)
  starting transfers between devices: 47.3 us -> 43.7 us
    ppermute x1, waiting for transfers between devices: 30.1 us -> 37.4 us  [shards(): low_in = lax.ppermute(top_grad, 'section', [(1, 0)])]
    ppermute x22, waiting for transfers between devices: 102 us -> 95.8 us  [ring_move(): lax.ppermute(block, ('section', axis), ring_route(distance, sections))]
    unnamed x70 -> x68, local copies, waits for them, and re-layouts: 11.7 us -> 11.8 us
  transfers between devices with their start and end apart: 30 -> 30, of which waited for: 18 -> 20; matrix products, arithmetic and copies ran while one was open for 2% -> 2% of each run, Pallas kernels for 8% -> 10%
where the time goes in v6:
time: 292 us; the launch traced here: 290 us
  waiting for transfers between devices  143 us (49%)
  Pallas kernels  49.4 us (17%)
  starting transfers between devices  43.7 us (15%)
  blocking collectives  33.9 us (12%)
  local copies, waits for them, and re-layouts  13.8 us (5%)
  matrix products  4.13 us (1%)
    ppermute x22, waiting for transfers between devices, ring_move(): lax.ppermute(block, ('section', axis), ring_route(distance, sections))  95.8 us
    ppermute x1, waiting for transfers between devices, shards(): low_in = lax.ppermute(top_grad, 'section', [(1, 0)])  37.4 us
    ppermute x22, starting transfers between devices, ring_move(): lax.ppermute(block, ('section', axis), ring_route(distance, sections))  27.6 us
    pallas_call x1, Pallas kernels, low_product(): pl.pallas_call(in_order(functools.partial(low_product_kernel, copies), 3...  16.4 us
    ppermute x6, starting transfers between devices, swap(): return lax.ppermute(block, ('section', axis), pairs)  14.6 us
    unnamed x68, local copies, waits for them, and re-layouts  11.8 us
    psum x1, blocking collectives, shards(): lax.psum(jnp.concatenate([jnp.sum(hidden_f * hidden_f, axis=1)[None], jnp...  11 us
    psum x1, blocking collectives, shards(): lax.psum(inner, tensor)  9.64 us
  transfers between devices with their start and end apart: 30, of which 20 were waited for; matrix products, arithmetic and copies ran while one was open for 2% of the time, Pallas kernels for 10%

profile of v6, /device:TPU:1, one launch (start us, length us, event | category | flops | bytes accessed | tf_op | source)
XLA Modules:
  0.0 289.7 jit_solution(7089544603717055676)
XLA Ops:
  0.6 4.7 %collective-permute-start.3 = (bf16[512,2048]{1,0:T(8,128)(2,1)}, bf16[512,2048]{1,0:T(8,128)(2,1)}, u32[]{:S(2)}, u32[]{:S(2)}) collective-permute-start(bf16[512,2048]{1,0:T(8,128)(2,1)} %bitcast.35), channel_id=1, source_target_pairs={{0,48},{16,0},{32,16},{48,32},{64,112},{80,64},{96,80},{112,96},{1... | collective-permute-start | bytes 6291464 | tf_op jit(solution)/shard_map/ppermute | solution.py:37
  5.4 1.6 copy-done.9
  9.5 2.0 shard_map.122.refs_1_.refs_5_
  11.5 2.8 collective-permute-start
  15.4 2.1 fusion.4
  17.6 1.7 fusion
  19.3 11.0 %psum.28 = f32[9,256]{1,0:T(8,128)S(1)} all-reduce(f32[9,256]{1,0:T(8,128)S(1)} %pad_maximum_fusion.1), channel_id=1, replica_groups=mesh['section'=2,'z'=4,'y'=4,'pair'=2,'core'=2] {'pair','core'}, use_global_device_ids=true, to_apply=%region_2.0 | all-reduce | flops 2304 | bytes 18432 | tf_op jit(solution)/shard_map/psum | solution.py:652
  30.5 19.5 %collective-permute-done.3.refs_0_.refs_6_.refs_3_.refs_4_ = bf16[512,2048]{1,0:T(8,128)(2,1)} collective-permute-done((bf16[512,2048]{1,0:T(8,128)(2,1)}, bf16[512,2048]{1,0:T(8,128)(2,1)}, u32[]{:S(2)}, u32[]{:S(2)}) %collective-permute-start.3) | collective-permute-done | bytes 2097184 | tf_op jit(solution)/shard_map/ppermute | solution.py:37
  49.9 3.1 %collective-permute-done.4.refs_1_.refs_9_.refs_4_.refs_7_ = bf16[512,2048]{1,0:T(8,128)(2,1)} collective-permute-done((bf16[512,2048]{1,0:T(8,128)(2,1)}, bf16[512,2048]{1,0:T(8,128)(2,1)}, u32[]{:S(2)}, u32[]{:S(2)}) %collective-permute-start.4) | collective-permute-done | bytes 2097184 | tf_op jit(solution)/shard_map/ppermute | solution.py:37
  53.0 1.6 shard_map.124
  56.1 2.5 collective-permute-done.refs_0_.refs_2_.refs_3_.refs_8_
  58.6 3.1 %collective-permute-done.1.refs_1_.refs_4_.refs_11_ = bf16[512,2048]{1,0:T(8,128)(2,1)} collective-permute-done((bf16[512,2048]{1,0:T(8,128)(2,1)}, bf16[512,2048]{1,0:T(8,128)(2,1)}, u32[]{:S(2)}, u32[]{:S(2)}) %collective-permute-start.1) | collective-permute-done | bytes 2097184 | tf_op jit(solution)/shard_map/ppermute | solution.py:37
  61.7 1.3 shard_map.123
  64.6 12.8 %collective-permute-done.5.refs_7_.refs_1_.refs_5_ = bf16[256,2048]{1,0:T(8,128)(2,1)S(1)} collective-permute-done((bf16[256,2048]{1,0:T(8,128)(2,1)S(1)}, bf16[256,2048]{1,0:T(8,128)(2,1)S(1)}, u32[]{:S(2)}, u32[]{:S(2)}) %collective-permute-start.5) | collective-permute-done | bytes 1048608 | tf_op jit(solution)/shard_map/ppermute | solution.py:37
  77.4 1.6 collective-permute-done.6.refs_8_.refs_2_.refs_6_
  79.0 6.6 %collective-permute-done.2.refs_3_.refs_1_.refs_9_ = bf16[256,2048]{1,0:T(8,128)(2,1)S(1)} collective-permute-done((bf16[256,2048]{1,0:T(8,128)(2,1)S(1)}, bf16[256,2048]{1,0:T(8,128)(2,1)S(1)}, u32[]{:S(2)}, u32[]{:S(2)}) %collective-permute-start.2) | collective-permute-done | bytes 1048608 | tf_op jit(solution)/shard_map/ppermute | solution.py:37
  85.6 2.1 collective-permute-done.7.refs_10_.refs_3_.refs_2_
  90.1 1.9 collective-permute-start.10
  92.3 4.7 %shard_map.133 = bf16[1312,2048]{1,0:T(8,128)(2,1)} custom-call(s32[4]{0:T(128)S(1)} %pad_add_fusion.where_ref.refs_0_, bf16[256,2048]{1,0:T(8,128)(2,1)S(1)} %collective-permute-done.2.refs_3_.refs_1_.refs_9_, bf16[256,2048]{1,0:T(8,128)(2,1)S(1)} %collective-permute-done.7.refs_10_.refs_3_.refs_2_, ...), custom_call_target="tpu_custom_call" | custom-call | bytes 1048576 | tf_op jit(solution)/shard_map/pallas_call | solution.py:136
  97.0 2.1 collective-permute-start.17
  99.9 3.4 %shard_map.128.refs_4_ = bf16[736,2048]{1,0:T(8,128)(2,1)} custom-call(s32[4]{0:T(128)S(1)} %pad_add_fusion.where_ref.refs_0_, bf16[256,2048]{1,0:T(8,128)(2,1)S(1)} %collective-permute-done.5.refs_7_.refs_1_.refs_5_, bf16[256,2048]{1,0:T(8,128)(2,1)S(1)} %collective-permute-done.6.refs_8_.refs_2_.refs_6_, ...), custom_call_target="tpu_custom_call" | custom-call | bytes 1048576 | tf_op jit(solution)/shard_map/pallas_call | solution.py:136
  103.3 34.2 %collective-permute-done.10.refs_3_.refs_12_ = bf16[512,2048]{1,0:T(8,128)(2,1)S(1)} collective-permute-done((bf16[512,2048]{1,0:T(8,128)(2,1)S(1)}, bf16[512,2048]{1,0:T(8,128)(2,1)S(1)}, u32[]{:S(2)}, u32[]{:S(2)}) %collective-permute-start.10) | collective-permute-done | bytes 2097184 | tf_op jit(solution)/shard_map/ppermute | solution.py:37
  141.3 2.5 collective-permute-start.15
  143.8 2.8 collective-permute-start.16
  146.6 2.7 shard_map.130
  149.3 9.6 %psum.29.inner_ref = f32[8,256]{1,0:T(8,128)S(1)} all-reduce(f32[8,256]{1,0:T(8,128)S(1)} %get-tuple-element.37), channel_id=1, replica_groups=mesh['section'=2,'z'=4,'y'=4,'pair'=2,'core'=2] {'pair','core'}, use_global_device_ids=true, to_apply=%region_3.0 | all-reduce | flops 2048 | bytes 16384 | tf_op jit(solution)/shard_map/psum | solution.py:702
  159.0 1.6 shard_map.131.top_ref
  160.6 1.4 collective-permute-start.14
  162.2 37.4 %collective-permute-done.14.refs_0_.incoming_ref = bf16[256,2048]{1,0:T(8,128)(2,1)} collective-permute-done((bf16[256,2048]{1,0:T(8,128)(2,1)}, bf16[256,2048]{1,0:T(8,128)(2,1)}, u32[]{:S(2)}, u32[]{:S(2)}) %collective-permute-start.14) | collective-permute-done | bytes 1048608 | tf_op jit(solution)/shard_map/ppermute | solution.py:703
  200.8 2.1 shard_map.132
  203.9 7.1 %psum.30.refs_17_.mixed_ref.refs_8_ = f32[4,256]{1,0:T(4,128)S(1)} all-reduce(f32[4,256]{1,0:T(4,128)S(1)} %get-tuple-element.40), channel_id=1, replica_groups=mesh['section'=2,'z'=4,'y'=4,'pair'=2,'core'=2] {'pair','core'}, use_global_device_ids=true, to_apply=%region_4.0 | all-reduce | flops 1024 | bytes 8192 | tf_op jit(solution)/shard_map/psum | solution.py:706
  211.7 2.7 collective-permute-done.18.refs_16_
  215.6 16.4 %shard_map.134 = (bf16[256,2048]{1,0:T(8,128)(2,1)S(1)}, bf16[256,2048]{1,0:T(8,128)(2,1)S(1)}, bf16[2,256,2048]{2,1,0:T(8,128)(2,1)}) custom-call(s32[4]{0:T(128)S(1)} %pad_add_fusion.where_ref.refs_0_, s32[32]{0:T(128)S(1)} %fusion.16.refs_1_, bf16[256,2048]{1,0:T(8,128)(2,1)S(1)} %copy-done.18, bf16[512,2048]{1,0:T(8,128)(2,1)} %bitcast.37, ...), custom_call_target="tpu_custom_call" | custom-call | flops 8589934592 | bytes 33554432 | tf_op jit(solution)/shard_map/pallas_call | solution.py:355
  232.0 6.5 %collective-permute-start.19 = (bf16[2,256,2048]{2,1,0:T(8,128)(2,1)}, bf16[2,256,2048]{2,1,0:T(8,128)(2,1)S(1)}, u32[]{:S(2)}, u32[]{:S(2)}) collective-permute-start(bf16[2,256,2048]{2,1,0:T(8,128)(2,1)} %get-tuple-element.42.refs_4_), channel_id=1, source_target_pairs={{0,1},{1,0},{2,3},{3,2},{4,5},{5,4},{6,7},{7,6},{8,9},{9,8},{10,11... | collective-permute-start | bytes 6291464 | tf_op jit(solution)/shard_map/ppermute | solution.py:42
  238.5 4.0 %collective-permute-done.19.got_ref = bf16[2,256,2048]{2,1,0:T(8,128)(2,1)S(1)} collective-permute-done((bf16[2,256,2048]{2,1,0:T(8,128)(2,1)}, bf16[2,256,2048]{2,1,0:T(8,128)(2,1)S(1)}, u32[]{:S(2)}, u32[]{:S(2)}) %collective-permute-start.19) | collective-permute-done | bytes 2097184 | tf_op jit(solution)/shard_map/ppermute | solution.py:42
  243.7 3.1 %collective-permute-start.20 = (bf16[256,2048]{1,0:T(8,128)(2,1)}, bf16[256,2048]{1,0:T(8,128)(2,1)}, u32[]{:S(2)}, u32[]{:S(2)}) collective-permute-start(bf16[256,2048]{1,0:T(8,128)(2,1)} %shard_map.135.refs_5_), channel_id=1, source_target_pairs={{0,2},{2,0},{1,3},{3,1},{4,6},{6,4},{5,7},{7,5},{8,10},{10,8},{9,1... | collective-permute-start | bytes 3145736 | tf_op jit(solution)/shard_map/ppermute | solution.py:42
  246.8 2.4 shard_map.137.refs_0_
  249.2 1.5 collective-permute-start.21
  250.7 1.6 collective-permute-start.22
  253.1 2.3 collective-permute-done.22.refs_2_
  255.4 2.0 collective-permute-done.23.refs_3_
  260.9 1.3 collective-permute-done.25.refs_3_
  263.1 1.3 shard_map.139.refs_0_
  264.4 3.2 %collective-permute-start.27 = (f32[256,256]{1,0:T(8,128)S(1)}, f32[256,256]{1,0:T(8,128)S(1)}, u32[]{:S(2)}, u32[]{:S(2)}) collective-permute-start(f32[256,256]{1,0:T(8,128)S(1)} %shard_map.139.refs_0_), channel_id=1, source_target_pairs={{0,1},{1,0},{64,65},{65,64},{2,3},{3,2},{66,67},{67,66},{4,5},{5,4... | collective-permute-start | bytes 786440 | tf_op jit(solution)/shard_map/ppermute | solution.py:42
  269.0 4.5 %collective-permute-done.28.refs_1_ = bf16[256,256]{1,0:T(8,128)(2,1)S(1)} collective-permute-done((bf16[256,256]{1,0:T(8,128)(2,1)S(1)}, bf16[256,256]{1,0:T(8,128)(2,1)S(1)}, u32[]{:S(2)}, u32[]{:S(2)}) %collective-permute-start.28) | collective-permute-done | bytes 131104 | tf_op jit(solution)/shard_map/ppermute | solution.py:42
  273.7 3.4 %shard_map.136 = (bf16[256,2048]{1,0:T(8,128)(2,1)S(1)}, f32[8,256]{1,0:T(8,128)S(1)}) custom-call(bf16[256,2048]{1,0:T(8,128)(2,1)S(1)} %copy-done.23, bf16[2,256,2048]{2,1,0:T(8,128)(2,1)S(1)} %collective-permute-done.19.got_ref, bf16[256,2048]{1,0:T(8,128)(2,1)} %collective-permute-done.20.other_ref, f32[4,256]{1,0:T(4,128)S(1)} %psum.30.refs_17_.mixed_ref.refs_8_, ...), custom_call_target="tpu_custom_call" | custom-call | bytes 1048576 | tf_op jit(solution)/shard_map/pallas_call | solution.py:467
  278.1 6.3 %psum.31.inner_ref = f32[8,256]{1,0:T(8,128)S(1)} all-reduce(f32[8,256]{1,0:T(8,128)S(1)} %get-tuple-element.45), channel_id=1, replica_groups=mesh['section'=2,'z'=4,'y'=4,'pair'=2,'core'=2] {'pair','core'}, use_global_device_ids=true, to_apply=%region_5.6 | all-reduce | flops 2048 | bytes 16384 | tf_op jit(solution)/shard_map/psum | solution.py:712
  286.5 3.0 %shard_map.142 = (bf16[256,2048]{1,0:T(8,128)(2,1)}, f32[256,256]{1,0:T(8,128)}) custom-call(s32[4]{0:T(128)S(1)} %pad_add_fusion.where_ref.refs_0_, bf16[256,2048]{1,0:T(8,128)(2,1)S(1)} %copy-done.21, f32[8,256]{1,0:T(8,128)S(1)} %psum.31.inner_ref, bf16[256,2048]{1,0:T(8,128)(2,1)S(1)} %bitcast.34, f32[256,1]{1,0:T(8,128)S(1)} %copy.28.refs_2_.scale_ref, ...), custom_call_target="tpu_custom_call" | custom-call | bytes 1048576 | tf_op jit(solution)/shard_map/pallas_call | solution.py:538
  (130 shorter events, 29.2 us)
Async XLA Ops:
  0.6 14.1 %copy-start = (f32[256,256]{1,0:T(8,128)S(1)}, f32[256,256]{1,0:T(8,128)}, u32[]{:S(2)}) copy-start(f32[256,256]{1,0:T(8,128)} %param.15) | copy-start | bytes 786436
  0.6 49.3 %collective-permute-start.3 = (bf16[512,2048]{1,0:T(8,128)(2,1)}, bf16[512,2048]{1,0:T(8,128)(2,1)}, u32[]{:S(2)}, u32[]{:S(2)}) collective-permute-start(bf16[512,2048]{1,0:T(8,128)(2,1)} %bitcast.35), channel_id=1, source_target_pairs={{0,48},{16,0},{32,16},{48,32},{64,112},{80,64},{96,80},{112,96},{1... | collective-permute-start | bytes 6291464 | tf_op jit(solution)/shard_map/ppermute | solution.py:37
  5.3 47.7 %collective-permute-start.4 = (bf16[512,2048]{1,0:T(8,128)(2,1)}, bf16[512,2048]{1,0:T(8,128)(2,1)}, u32[]{:S(2)}, u32[]{:S(2)}) collective-permute-start(bf16[512,2048]{1,0:T(8,128)(2,1)} %bitcast.36), channel_id=1, source_target_pairs={{0,16},{16,32},{32,48},{48,0},{64,80},{80,96},{96,112},{112,64},{1... | collective-permute-start | bytes 6291464 | tf_op jit(solution)/shard_map/ppermute | solution.py:37
  9.5 5.0 %copy-start.30 = (f32[1,2,128,2]{2,3,1,0:T(2,128)S(1)}, f32[1,2,128,2]{2,3,1,0:T(2,128)}, u32[]{:S(2)}) copy-start(f32[1,2,128,2]{2,3,1,0:T(2,128)} %param.17) | copy-start | bytes 6148
  9.5 5.7 %copy-start.2 = (bf16[1,256,2048]{2,1,0:T(8,128)(2,1)S(1)}, bf16[1,256,2048]{2,1,0:T(8,128)(2,1)}, u32[]{:S(2)}) copy-start(bf16[1,256,2048]{2,1,0:T(8,128)(2,1)} %param.11) | copy-start | bytes 3145732
  11.5 6.0 %copy-start.26 = (f32[1,2048]{1,0:T(1,128)S(1)}, f32[1,2048]{1,0:T(1,128)}, u32[]{:S(2)}) copy-start(f32[1,2048]{1,0:T(1,128)} %refs_3_.1) | copy-start | bytes 24580
  11.5 47.1 %collective-permute-start = (bf16[512,2048]{1,0:T(8,128)(2,1)}, bf16[512,2048]{1,0:T(8,128)(2,1)S(1)}, u32[]{:S(2)}, u32[]{:S(2)}) collective-permute-start(bf16[512,2048]{1,0:T(8,128)(2,1)} %shard_map.122.refs_1_.refs_5_), channel_id=1, source_target_pairs={{0,12},{4,0},{8,4},{12,8},{64,76},{68,64},{72,68},{76,72},{1,13},{... | collective-permute-start | bytes 6291464 | tf_op jit(solution)/shard_map/ppermute | solution.py:37
  14.3 47.4 %collective-permute-start.1 = (bf16[512,2048]{1,0:T(8,128)(2,1)}, bf16[512,2048]{1,0:T(8,128)(2,1)}, u32[]{:S(2)}, u32[]{:S(2)}) collective-permute-start(bf16[512,2048]{1,0:T(8,128)(2,1)} %shard_map.122.refs_1_.refs_5_), channel_id=1, source_target_pairs={{0,4},{4,8},{8,12},{12,0},{64,68},{68,72},{72,76},{76,64},{1,5},{5... | collective-permute-start | bytes 6291464 | tf_op jit(solution)/shard_map/ppermute | solution.py:37
  14.8 15.5 %copy-start.27 = (f32[2,4,8,256]{3,2,1,0:T(8,128)}, f32[2,4,8,256]{3,2,1,0:T(8,128)S(1)}, u32[]{:S(2)}) copy-start(f32[2,4,8,256]{3,2,1,0:T(8,128)S(1)} %select_reduce_fusion) | copy-start | bytes 196612
  54.6 22.9 %collective-permute-start.5 = (bf16[256,2048]{1,0:T(8,128)(2,1)S(1)}, bf16[256,2048]{1,0:T(8,128)(2,1)S(1)}, u32[]{:S(2)}, u32[]{:S(2)}) collective-permute-start(bf16[256,2048]{1,0:T(8,128)(2,1)S(1)} %get-tuple-element.26), channel_id=1, source_target_pairs={{0,48},{16,0},{32,16},{48,32},{64,112},{80,64},{96,80},{112,96},{1... | collective-permute-start | bytes 3145736 | tf_op jit(solution)/shard_map/ppermute | solution.py:37
  55.0 32.8 %copy-start.10 = (bf16[1,512,2048]{2,1,0:T(8,128)(2,1)S(1)}, bf16[1,512,2048]{2,1,0:T(8,128)(2,1)}, u32[]{:S(2)}) copy-start(bf16[1,512,2048]{2,1,0:T(8,128)(2,1)} %param.14) | copy-start | bytes 6291460
  55.0 24.0 %collective-permute-start.6 = (bf16[256,2048]{1,0:T(8,128)(2,1)S(1)}, bf16[256,2048]{1,0:T(8,128)(2,1)S(1)}, u32[]{:S(2)}, u32[]{:S(2)}) collective-permute-start(bf16[256,2048]{1,0:T(8,128)(2,1)S(1)} %get-tuple-element.27), channel_id=1, source_target_pairs={{0,16},{16,32},{32,48},{48,0},{64,80},{80,96},{96,112},{112,64},{1... | collective-permute-start | bytes 3145736 | tf_op jit(solution)/shard_map/ppermute | solution.py:37
  58.6 33.6 %copy-start.3 = (bf16[512,2048]{1,0:T(8,128)(2,1)}, bf16[512,2048]{1,0:T(8,128)(2,1)S(1)}, u32[]{:S(2)}) copy-start(bf16[512,2048]{1,0:T(8,128)(2,1)S(1)} %collective-permute-done.refs_0_.refs_2_.refs_3_.refs_8_) | copy-start | bytes 6291460
  63.0 22.6 %collective-permute-start.2 = (bf16[256,2048]{1,0:T(8,128)(2,1)S(1)}, bf16[256,2048]{1,0:T(8,128)(2,1)S(1)}, u32[]{:S(2)}, u32[]{:S(2)}) collective-permute-start(bf16[256,2048]{1,0:T(8,128)(2,1)S(1)} %get-tuple-element.25), channel_id=1, source_target_pairs={{0,12},{4,0},{8,4},{12,8},{64,76},{68,64},{72,68},{76,72},{1,13},{... | collective-permute-start | bytes 3145736 | tf_op jit(solution)/shard_map/ppermute | solution.py:37
  64.0 23.7 %collective-permute-start.7 = (bf16[256,2048]{1,0:T(8,128)(2,1)S(1)}, bf16[256,2048]{1,0:T(8,128)(2,1)S(1)}, u32[]{:S(2)}, u32[]{:S(2)}) collective-permute-start(bf16[256,2048]{1,0:T(8,128)(2,1)S(1)} %get-tuple-element.28), channel_id=1, source_target_pairs={{0,4},{4,8},{8,12},{12,0},{64,68},{68,72},{72,76},{76,64},{1,5},{5... | collective-permute-start | bytes 3145736 | tf_op jit(solution)/shard_map/ppermute | solution.py:37
  77.4 22.4 %copy-start.5 = (bf16[256,2048]{1,0:T(8,128)(2,1)}, bf16[256,2048]{1,0:T(8,128)(2,1)S(1)}, u32[]{:S(2)}) copy-start(bf16[256,2048]{1,0:T(8,128)(2,1)S(1)} %collective-permute-done.5.refs_7_.refs_1_.refs_5_) | copy-start | bytes 3145732
  79.0 20.9 %copy-start.7 = (bf16[256,2048]{1,0:T(8,128)(2,1)}, bf16[256,2048]{1,0:T(8,128)(2,1)S(1)}, u32[]{:S(2)}) copy-start(bf16[256,2048]{1,0:T(8,128)(2,1)S(1)} %collective-permute-done.6.refs_8_.refs_2_.refs_6_) | copy-start | bytes 3145732
  85.6 6.6 %copy-start.12 = (bf16[256,2048]{1,0:T(8,128)(2,1)}, bf16[256,2048]{1,0:T(8,128)(2,1)S(1)}, u32[]{:S(2)}) copy-start(bf16[256,2048]{1,0:T(8,128)(2,1)S(1)} %collective-permute-done.2.refs_3_.refs_1_.refs_9_) | copy-start | bytes 3145732
  88.4 3.6 %collective-permute-start.8 = (bf16[2,1024,512]{2,1,0:T(8,128)(2,1)S(1)}, bf16[2,1024,512]{2,1,0:T(8,128)(2,1)S(1)}, u32[]{:S(2)}, u32[]{:S(2)}) collective-permute-start(bf16[2,1024,512]{2,1,0:T(8,128)(2,1)S(1)} %get-tuple-element.30), channel_id=1, source_target_pairs={{64,65},{65,64},{66,67},{67,66},{68,69},{69,68},{70,71},{71,70},{7... | collective-permute-start | bytes 6291464 | tf_op jit(solution)/shard_map/ppermute | solution.py:42
  90.1 47.5 %collective-permute-start.10 = (bf16[512,2048]{1,0:T(8,128)(2,1)S(1)}, bf16[512,2048]{1,0:T(8,128)(2,1)S(1)}, u32[]{:S(2)}, u32[]{:S(2)}) collective-permute-start(bf16[512,2048]{1,0:T(8,128)(2,1)S(1)} %shard_map.127), channel_id=1, source_target_pairs={{0,8},{4,12},{8,0},{12,4},{1,9},{5,13},{9,1},{13,5},{2,10},{6,14},... | collective-permute-start | bytes 6291464 | tf_op jit(solution)/shard_map/ppermute | solution.py:37
  97.0 114.7 %collective-permute-start.17 = (bf16[1312,2048]{1,0:T(8,128)(2,1)}, bf16[1312,2048]{1,0:T(8,128)(2,1)}, u32[]{:S(2)}, u32[]{:S(2)}) collective-permute-start(bf16[1312,2048]{1,0:T(8,128)(2,1)} %shard_map.133), channel_id=1, source_target_pairs={{0,48},{16,0},{32,16},{48,32},{64,112},{80,64},{96,80},{112,96},{1... | collective-permute-start | bytes 16121864 | tf_op jit(solution)/shard_map/ppermute | solution.py:37
  99.1 115.2 %collective-permute-start.18 = (bf16[1312,2048]{1,0:T(8,128)(2,1)}, bf16[1312,2048]{1,0:T(8,128)(2,1)}, u32[]{:S(2)}, u32[]{:S(2)}) collective-permute-start(bf16[1312,2048]{1,0:T(8,128)(2,1)} %shard_map.133), channel_id=1, source_target_pairs={{0,16},{16,32},{32,48},{48,0},{64,80},{80,96},{96,112},{112,64},{1... | collective-permute-start | bytes 16121864 | tf_op jit(solution)/shard_map/ppermute | solution.py:37
  99.1 38.4 %collective-permute-start.9 = (bf16[1024,512]{1,0:T(8,128)(2,1)S(1)}, bf16[1024,512]{1,0:T(8,128)(2,1)S(1)}, u32[]{:S(2)}, u32[]{:S(2)}) collective-permute-start(bf16[1024,512]{1,0:T(8,128)(2,1)S(1)} %shard_map.126.refs_5_), channel_id=1, source_target_pairs={{64,66},{66,64},{65,67},{67,65},{68,70},{70,68},{69,71},{71,69},{7... | collective-permute-start | bytes 3145736 | tf_op jit(solution)/shard_map/ppermute | solution.py:42
  138.9 20.1 %copy-start.16 = (bf16[256,2048]{1,0:T(8,128)(2,1)S(1)}, bf16[256,2048]{1,0:T(8,128)(2,1)}, u32[]{:S(2)}) copy-start(bf16[256,2048]{1,0:T(8,128)(2,1)} %incoming_ref.3) | copy-start | bytes 3145732
  138.9 2.4 collective-permute-start.11
  139.9 1.4 collective-permute-start.12
  140.6 0.7 collective-permute-start.13
  141.3 69.7 %collective-permute-start.15 = (bf16[736,2048]{1,0:T(8,128)(2,1)}, bf16[736,2048]{1,0:T(8,128)(2,1)}, u32[]{:S(2)}, u32[]{:S(2)}) collective-permute-start(bf16[736,2048]{1,0:T(8,128)(2,1)} %shard_map.128.refs_4_), channel_id=1, source_target_pairs={{0,12},{4,0},{8,4},{12,8},{1,13},{5,1},{9,5},{13,9},{2,14},{6,2},{... | collective-permute-start | bytes 9043976 | tf_op jit(solution)/shard_map/ppermute | solution.py:37
  143.8 67.2 %collective-permute-start.16 = (bf16[736,2048]{1,0:T(8,128)(2,1)}, bf16[736,2048]{1,0:T(8,128)(2,1)}, u32[]{:S(2)}, u32[]{:S(2)}) collective-permute-start(bf16[736,2048]{1,0:T(8,128)(2,1)} %shard_map.128.refs_4_), channel_id=1, source_target_pairs={{0,4},{4,8},{8,12},{12,0},{1,5},{5,9},{9,13},{13,1},{2,6},{6,10},{... | collective-permute-start | bytes 9043976 | tf_op jit(solution)/shard_map/ppermute | solution.py:37
  160.6 53.7 %copy-start.6 = (bf16[256,2048]{1,0:T(8,128)(2,1)S(1)}, bf16[256,2048]{1,0:T(8,128)(2,1)}, u32[]{:S(2)}) copy-start(bf16[256,2048]{1,0:T(8,128)(2,1)} %copy-done.5) | copy-start | bytes 3145732
  160.6 53.7 %copy-start.8 = (bf16[256,2048]{1,0:T(8,128)(2,1)S(1)}, bf16[256,2048]{1,0:T(8,128)(2,1)}, u32[]{:S(2)}) copy-start(bf16[256,2048]{1,0:T(8,128)(2,1)} %copy-done.7) | copy-start | bytes 3145732
  160.6 38.9 %collective-permute-start.14 = (bf16[256,2048]{1,0:T(8,128)(2,1)}, bf16[256,2048]{1,0:T(8,128)(2,1)}, u32[]{:S(2)}, u32[]{:S(2)}) collective-permute-start(bf16[256,2048]{1,0:T(8,128)(2,1)} %shard_map.131.top_ref), channel_id=1, source_target_pairs={{64,0},{65,1},{66,2},{67,3},{68,4},{69,5},{70,6},{71,7},{72,8},{73... | collective-permute-start | bytes 3145736 | tf_op jit(solution)/shard_map/ppermute | solution.py:703
  232.0 11.7 %copy-start.22 = (bf16[256,2048]{1,0:T(8,128)(2,1)}, bf16[256,2048]{1,0:T(8,128)(2,1)S(1)}, u32[]{:S(2)}) copy-start(bf16[256,2048]{1,0:T(8,128)(2,1)S(1)} %get-tuple-element.41.keep_ref) | copy-start | bytes 3145732
  232.0 10.5 %collective-permute-start.19 = (bf16[2,256,2048]{2,1,0:T(8,128)(2,1)}, bf16[2,256,2048]{2,1,0:T(8,128)(2,1)S(1)}, u32[]{:S(2)}, u32[]{:S(2)}) collective-permute-start(bf16[2,256,2048]{2,1,0:T(8,128)(2,1)} %get-tuple-element.42.refs_4_), channel_id=1, source_target_pairs={{0,1},{1,0},{2,3},{3,2},{4,5},{5,4},{6,7},{7,6},{8,9},{9,8},{10,11... | collective-permute-start | bytes 6291464 | tf_op jit(solution)/shard_map/ppermute | solution.py:42
  243.7 29.9 %collective-permute-start.20 = (bf16[256,2048]{1,0:T(8,128)(2,1)}, bf16[256,2048]{1,0:T(8,128)(2,1)}, u32[]{:S(2)}, u32[]{:S(2)}) collective-permute-start(bf16[256,2048]{1,0:T(8,128)(2,1)} %shard_map.135.refs_5_), channel_id=1, source_target_pairs={{0,2},{2,0},{1,3},{3,1},{4,6},{6,4},{5,7},{7,5},{8,10},{10,8},{9,1... | collective-permute-start | bytes 3145736 | tf_op jit(solution)/shard_map/ppermute | solution.py:42
  246.8 10.5 %copy-start.19 = (bf16[2,256,2048]{2,1,0:T(8,128)(2,1)S(1)}, bf16[2,256,2048]{2,1,0:T(8,128)(2,1)}, u32[]{:S(2)}) copy-start(bf16[2,256,2048]{2,1,0:T(8,128)(2,1)} %get-tuple-element.42.refs_4_) | copy-start | bytes 6291460
  249.2 9.7 %copy-start.28 = (f32[2,4,8,256]{3,2,1,0:T(8,128)S(1)}, f32[2,4,8,256]{3,2,1,0:T(8,128)}, u32[]{:S(2)}) copy-start(f32[2,4,8,256]{3,2,1,0:T(8,128)} %copy-done.27) | copy-start | bytes 196612
  249.2 3.9 %collective-permute-start.21 = (f32[8,2048]{1,0:T(8,128)S(1)}, f32[8,2048]{1,0:T(8,128)S(1)}, u32[]{:S(2)}, u32[]{:S(2)}) collective-permute-start(f32[8,2048]{1,0:T(8,128)S(1)} %shard_map.137.refs_0_), channel_id=1, source_target_pairs={{0,12},{4,0},{8,4},{12,8},{64,76},{68,64},{72,68},{76,72},{1,13},{... | collective-permute-start | bytes 196616 | tf_op jit(solution)/shard_map/ppermute | solution.py:37
  250.7 4.6 %collective-permute-start.22 = (f32[8,2048]{1,0:T(8,128)S(1)}, f32[8,2048]{1,0:T(8,128)S(1)}, u32[]{:S(2)}, u32[]{:S(2)}) collective-permute-start(f32[8,2048]{1,0:T(8,128)S(1)} %shard_map.137.refs_0_), channel_id=1, source_target_pairs={{0,8},{4,12},{8,0},{12,4},{64,72},{68,76},{72,64},{76,68},{1,9},{5... | collective-permute-start | bytes 196616 | tf_op jit(solution)/shard_map/ppermute | solution.py:37
  252.3 5.0 %collective-permute-start.23 = (f32[8,2048]{1,0:T(8,128)S(1)}, f32[8,2048]{1,0:T(8,128)S(1)}, u32[]{:S(2)}, u32[]{:S(2)}) collective-permute-start(f32[8,2048]{1,0:T(8,128)S(1)} %shard_map.137.refs_0_), channel_id=1, source_target_pairs={{0,4},{4,8},{8,12},{12,0},{64,68},{68,72},{72,76},{76,64},{1,5},{5... | collective-permute-start | bytes 196616 | tf_op jit(solution)/shard_map/ppermute | solution.py:37
  257.4 3.6 %collective-permute-start.24 = (f32[8,2048]{1,0:T(8,128)S(1)}, f32[8,2048]{1,0:T(8,128)S(1)}, u32[]{:S(2)}, u32[]{:S(2)}) collective-permute-start(f32[8,2048]{1,0:T(8,128)S(1)} %shard_map.138.refs_1_), channel_id=1, source_target_pairs={{0,48},{16,0},{32,16},{48,32},{64,112},{80,64},{96,80},{112,96},{1... | collective-permute-start | bytes 196616 | tf_op jit(solution)/shard_map/ppermute | solution.py:37
  257.4 4.8 %collective-permute-start.25 = (f32[8,2048]{1,0:T(8,128)S(1)}, f32[8,2048]{1,0:T(8,128)}, u32[]{:S(2)}, u32[]{:S(2)}) collective-permute-start(f32[8,2048]{1,0:T(8,128)S(1)} %shard_map.138.refs_1_), channel_id=1, source_target_pairs={{0,32},{16,48},{32,0},{48,16},{64,96},{80,112},{96,64},{112,80},{1... | collective-permute-start | bytes 196616 | tf_op jit(solution)/shard_map/ppermute | solution.py:37
  258.0 5.0 %collective-permute-start.26 = (f32[8,2048]{1,0:T(8,128)S(1)}, f32[8,2048]{1,0:T(8,128)}, u32[]{:S(2)}, u32[]{:S(2)}) collective-permute-start(f32[8,2048]{1,0:T(8,128)S(1)} %shard_map.138.refs_1_), channel_id=1, source_target_pairs={{0,16},{16,32},{32,48},{48,0},{64,80},{80,96},{96,112},{112,64},{1... | collective-permute-start | bytes 196616 | tf_op jit(solution)/shard_map/ppermute | solution.py:37
  260.4 13.2 %copy-start.23 = (bf16[256,2048]{1,0:T(8,128)(2,1)S(1)}, bf16[256,2048]{1,0:T(8,128)(2,1)}, u32[]{:S(2)}) copy-start(bf16[256,2048]{1,0:T(8,128)(2,1)} %copy-done.22) | copy-start | bytes 3145732
  264.4 4.3 %collective-permute-start.27 = (f32[256,256]{1,0:T(8,128)S(1)}, f32[256,256]{1,0:T(8,128)S(1)}, u32[]{:S(2)}, u32[]{:S(2)}) collective-permute-start(f32[256,256]{1,0:T(8,128)S(1)} %shard_map.139.refs_0_), channel_id=1, source_target_pairs={{0,1},{1,0},{64,65},{65,64},{2,3},{3,2},{66,67},{67,66},{4,5},{5,4... | collective-permute-start | bytes 786440 | tf_op jit(solution)/shard_map/ppermute | solution.py:42
  268.7 4.8 %collective-permute-start.28 = (bf16[256,256]{1,0:T(8,128)(2,1)S(1)}, bf16[256,256]{1,0:T(8,128)(2,1)S(1)}, u32[]{:S(2)}, u32[]{:S(2)}) collective-permute-start(bf16[256,256]{1,0:T(8,128)(2,1)S(1)} %shard_map.140.refs_0_), channel_id=1, source_target_pairs={{0,2},{2,0},{64,66},{66,64},{1,3},{3,1},{65,67},{67,65},{4,6},{6,4... | collective-permute-start | bytes 393224 | tf_op jit(solution)/shard_map/ppermute | solution.py:42
  273.5 10.8 %collective-permute-start.29 = (bf16[256,256]{1,0:T(8,128)(2,1)S(1)}, bf16[256,256]{1,0:T(8,128)(2,1)}, u32[]{:S(2)}, u32[]{:S(2)}) collective-permute-start(bf16[256,256]{1,0:T(8,128)(2,1)S(1)} %shard_map.141.share_ref), channel_id=1, source_target_pairs={{0,64},{64,0},{1,65},{65,1},{2,66},{66,2},{3,67},{67,3},{4,68},{68... | collective-permute-start | bytes 393224 | tf_op jit(solution)/shard_map/ppermute | solution.py:730
  284.3 5.2 %copy-start.1 = (f32[256,256]{1,0:T(8,128)S(1)}, f32[256,256]{1,0:T(8,128)}, u32[]{:S(2)}) copy-start(f32[256,256]{1,0:T(8,128)} %param.15) | copy-start | bytes 786436
  (16 other events, 34.3 us)

commit v7 on v6

--- a/solution.py
+++ b/solution.py
@@ -702,7 +702,9 @@
     top_grad = finish_top(scaled, lax.psum(inner, tensor), hidden, scale, grad_top, 0)
     low_in = lax.ppermute(top_grad, "section", [(1, 0)])
 
-    low_dz, part = make_dz(low_in, preact, b_both, 0)
+    flat = mixing.reshape(2, RANK, seg_local, bank_rows).transpose(2, 0, 1, 3)
+    flat = flat.reshape(2 * RANK * seg_local, bank_rows)
+    low_dz, part = make_dz(low_in, preact, b_both, 0, flat)
     low_mixed = lax.psum(part, tensor)
     mine, keep, send = low_product(where, z, y, place, low_dz, w_pieces, low_mixed)
     got = swap(send, "core", (0,))
@@ -716,8 +718,6 @@
     over_y = ring_moves(grads, "y")
     grads = small_call(ring_kernel, jax.ShapeDtypeStruct(grads.shape, F32), (grads, *over_y), send)
     over_z = ring_moves(grads, "z")
-    flat = mixing.reshape(2, RANK, seg_local, bank_rows).transpose(2, 0, 1, 3)
-    flat = flat.reshape(2 * RANK * seg_local, bank_rows)
     bank_shape = (bank_rows, SUB)
     share = small_call(bank_kernel, jax.ShapeDtypeStruct(bank_shape, F32), (flat, grads, *over_z), theirs)
     core_share = swap(share, "core")

time: 292 us -> 289 us (0.990)
  Pallas kernels: 49.4 us -> 46.2 us
    unnamed x68 -> x64, local copies, waits for them, and re-layouts: 11.8 us -> 11.8 us
  transfers between devices with their start and end apart: 30 -> 30, of which waited for: 20 -> 20; matrix products, arithmetic and copies ran while one was open for 2% -> 2% of each run, Pallas kernels for 10% -> 9%
where the time goes in v7:
time: 289 us; the launch traced here: 287 us
  waiting for transfers between devices  145 us (50%)
  Pallas kernels  46.2 us (16%)
  starting transfers between devices  43.7 us (15%)
  blocking collectives  33.6 us (12%)
  local copies, waits for them, and re-layouts  12.3 us (4%)
  matrix products  4.12 us (1%)
    ppermute x22, waiting for transfers between devices, ring_move(): lax.ppermute(block, ('section', axis), ring_route(distance, sections))  97.2 us
    ppermute x1, waiting for transfers between devices, shards(): low_in = lax.ppermute(top_grad, 'section', [(1, 0)])  37.3 us
    ppermute x22, starting transfers between devices, ring_move(): lax.ppermute(block, ('section', axis), ring_route(distance, sections))  27.6 us
    pallas_call x1, Pallas kernels, low_product(): pl.pallas_call(in_order(functools.partial(low_product_kernel, copies), 3...  16.4 us
    ppermute x6, starting transfers between devices, swap(): return lax.ppermute(block, ('section', axis), pairs)  14.6 us
    unnamed x64, local copies, waits for them, and re-layouts  11.8 us
    psum x1, blocking collectives, shards(): lax.psum(jnp.concatenate([jnp.sum(hidden_f * hidden_f, axis=1)[None], jnp...  11 us
    ppermute x6, waiting for transfers between devices, swap(): return lax.ppermute(block, ('section', axis), pairs)  10.2 us
  transfers between devices with their start and end apart: 30, of which 20 were waited for; matrix products, arithmetic and copies ran while one was open for 2% of the time, Pallas kernels for 9%

profile of v7, /device:TPU:1, one launch (start us, length us, event | category | flops | bytes accessed | tf_op | source)
XLA Modules:
  0.0 286.7 jit_solution(6978540013228919748)
XLA Ops:
  0.6 4.7 %collective-permute-start.3 = (bf16[512,2048]{1,0:T(8,128)(2,1)}, bf16[512,2048]{1,0:T(8,128)(2,1)}, u32[]{:S(2)}, u32[]{:S(2)}) collective-permute-start(bf16[512,2048]{1,0:T(8,128)(2,1)} %bitcast.35), channel_id=1, source_target_pairs={{0,48},{16,0},{32,16},{48,32},{64,112},{80,64},{96,80},{112,96},{1... | collective-permute-start | bytes 6291464 | tf_op jit(solution)/shard_map/ppermute | solution.py:37
  5.4 1.6 copy-done.9
  9.5 2.0 shard_map.122.refs_1_.refs_5_
  11.5 2.8 collective-permute-start
  15.4 2.1 fusion.4
  17.6 1.7 fusion
  19.3 11.0 %psum.28 = f32[9,256]{1,0:T(8,128)S(1)} all-reduce(f32[9,256]{1,0:T(8,128)S(1)} %pad_maximum_fusion.1), channel_id=1, replica_groups=mesh['section'=2,'z'=4,'y'=4,'pair'=2,'core'=2] {'pair','core'}, use_global_device_ids=true, to_apply=%region_2.0 | all-reduce | flops 2304 | bytes 18432 | tf_op jit(solution)/shard_map/psum | solution.py:652
  30.5 19.4 %collective-permute-done.3.refs_0_.refs_6_.refs_3_.refs_4_ = bf16[512,2048]{1,0:T(8,128)(2,1)} collective-permute-done((bf16[512,2048]{1,0:T(8,128)(2,1)}, bf16[512,2048]{1,0:T(8,128)(2,1)}, u32[]{:S(2)}, u32[]{:S(2)}) %collective-permute-start.3) | collective-permute-done | bytes 2097184 | tf_op jit(solution)/shard_map/ppermute | solution.py:37
  49.9 3.1 %collective-permute-done.4.refs_1_.refs_9_.refs_4_.refs_7_ = bf16[512,2048]{1,0:T(8,128)(2,1)} collective-permute-done((bf16[512,2048]{1,0:T(8,128)(2,1)}, bf16[512,2048]{1,0:T(8,128)(2,1)}, u32[]{:S(2)}, u32[]{:S(2)}) %collective-permute-start.4) | collective-permute-done | bytes 2097184 | tf_op jit(solution)/shard_map/ppermute | solution.py:37
  53.0 1.6 shard_map.124
  56.1 2.5 collective-permute-done.refs_0_.refs_2_.refs_3_.refs_8_
  58.6 3.1 %collective-permute-done.1.refs_1_.refs_4_.refs_11_ = bf16[512,2048]{1,0:T(8,128)(2,1)} collective-permute-done((bf16[512,2048]{1,0:T(8,128)(2,1)}, bf16[512,2048]{1,0:T(8,128)(2,1)}, u32[]{:S(2)}, u32[]{:S(2)}) %collective-permute-start.1) | collective-permute-done | bytes 2097184 | tf_op jit(solution)/shard_map/ppermute | solution.py:37
  61.7 1.3 shard_map.123
  64.6 12.8 %collective-permute-done.5.refs_7_.refs_1_.refs_5_ = bf16[256,2048]{1,0:T(8,128)(2,1)S(1)} collective-permute-done((bf16[256,2048]{1,0:T(8,128)(2,1)S(1)}, bf16[256,2048]{1,0:T(8,128)(2,1)S(1)}, u32[]{:S(2)}, u32[]{:S(2)}) %collective-permute-start.5) | collective-permute-done | bytes 1048608 | tf_op jit(solution)/shard_map/ppermute | solution.py:37
  77.4 1.6 collective-permute-done.6.refs_8_.refs_2_.refs_6_
  79.0 6.6 %collective-permute-done.2.refs_3_.refs_1_.refs_9_ = bf16[256,2048]{1,0:T(8,128)(2,1)S(1)} collective-permute-done((bf16[256,2048]{1,0:T(8,128)(2,1)S(1)}, bf16[256,2048]{1,0:T(8,128)(2,1)S(1)}, u32[]{:S(2)}, u32[]{:S(2)}) %collective-permute-start.2) | collective-permute-done | bytes 1048608 | tf_op jit(solution)/shard_map/ppermute | solution.py:37
  85.6 2.1 collective-permute-done.7.refs_10_.refs_3_.refs_2_
  90.1 1.9 collective-permute-start.10
  92.3 4.7 %shard_map.133 = bf16[1312,2048]{1,0:T(8,128)(2,1)} custom-call(s32[4]{0:T(128)S(1)} %pad_add_fusion.where_ref.refs_0_, bf16[256,2048]{1,0:T(8,128)(2,1)S(1)} %collective-permute-done.2.refs_3_.refs_1_.refs_9_, bf16[256,2048]{1,0:T(8,128)(2,1)S(1)} %collective-permute-done.7.refs_10_.refs_3_.refs_2_, ...), custom_call_target="tpu_custom_call" | custom-call | bytes 1048576 | tf_op jit(solution)/shard_map/pallas_call | solution.py:136
  97.0 2.1 collective-permute-start.17
  99.9 3.4 %shard_map.128.refs_4_ = bf16[736,2048]{1,0:T(8,128)(2,1)} custom-call(s32[4]{0:T(128)S(1)} %pad_add_fusion.where_ref.refs_0_, bf16[256,2048]{1,0:T(8,128)(2,1)S(1)} %collective-permute-done.5.refs_7_.refs_1_.refs_5_, bf16[256,2048]{1,0:T(8,128)(2,1)S(1)} %collective-permute-done.6.refs_8_.refs_2_.refs_6_, ...), custom_call_target="tpu_custom_call" | custom-call | bytes 1048576 | tf_op jit(solution)/shard_map/pallas_call | solution.py:136
  103.3 34.2 %collective-permute-done.10.refs_3_.refs_12_ = bf16[512,2048]{1,0:T(8,128)(2,1)S(1)} collective-permute-done((bf16[512,2048]{1,0:T(8,128)(2,1)S(1)}, bf16[512,2048]{1,0:T(8,128)(2,1)S(1)}, u32[]{:S(2)}, u32[]{:S(2)}) %collective-permute-start.10) | collective-permute-done | bytes 2097184 | tf_op jit(solution)/shard_map/ppermute | solution.py:37
  141.3 2.5 collective-permute-start.15
  143.8 2.8 collective-permute-start.16
  146.6 2.7 shard_map.130
  149.3 9.6 %psum.29.inner_ref = f32[8,256]{1,0:T(8,128)S(1)} all-reduce(f32[8,256]{1,0:T(8,128)S(1)} %get-tuple-element.37), channel_id=1, replica_groups=mesh['section'=2,'z'=4,'y'=4,'pair'=2,'core'=2] {'pair','core'}, use_global_device_ids=true, to_apply=%region_3.0 | all-reduce | flops 2048 | bytes 16384 | tf_op jit(solution)/shard_map/psum | solution.py:702
  159.0 1.6 shard_map.131.top_ref
  160.7 1.4 collective-permute-start.14
  162.3 37.3 %collective-permute-done.14.refs_0_.incoming_ref = bf16[256,2048]{1,0:T(8,128)(2,1)} collective-permute-done((bf16[256,2048]{1,0:T(8,128)(2,1)}, bf16[256,2048]{1,0:T(8,128)(2,1)}, u32[]{:S(2)}, u32[]{:S(2)}) %collective-permute-start.14) | collective-permute-done | bytes 1048608 | tf_op jit(solution)/shard_map/ppermute | solution.py:703
  200.8 2.1 shard_map.132
  203.9 7.1 %psum.30.refs_17_.mixed_ref.refs_8_ = f32[4,256]{1,0:T(4,128)S(1)} all-reduce(f32[4,256]{1,0:T(4,128)S(1)} %get-tuple-element.40), channel_id=1, replica_groups=mesh['section'=2,'z'=4,'y'=4,'pair'=2,'core'=2] {'pair','core'}, use_global_device_ids=true, to_apply=%region_4.0 | all-reduce | flops 1024 | bytes 8192 | tf_op jit(solution)/shard_map/psum | solution.py:708
  211.7 2.7 collective-permute-done.18.refs_16_
  215.6 16.4 %shard_map.134 = (bf16[256,2048]{1,0:T(8,128)(2,1)S(1)}, bf16[256,2048]{1,0:T(8,128)(2,1)S(1)}, bf16[2,256,2048]{2,1,0:T(8,128)(2,1)}) custom-call(s32[4]{0:T(128)S(1)} %pad_add_fusion.where_ref.refs_0_, s32[32]{0:T(128)S(1)} %fusion.16.refs_1_, bf16[256,2048]{1,0:T(8,128)(2,1)S(1)} %copy-done.18, bf16[512,2048]{1,0:T(8,128)(2,1)} %bitcast.37, ...), custom_call_target="tpu_custom_call" | custom-call | flops 8589934592 | bytes 33554432 | tf_op jit(solution)/shard_map/pallas_call | solution.py:355
  232.0 6.5 %collective-permute-start.19 = (bf16[2,256,2048]{2,1,0:T(8,128)(2,1)}, bf16[2,256,2048]{2,1,0:T(8,128)(2,1)S(1)}, u32[]{:S(2)}, u32[]{:S(2)}) collective-permute-start(bf16[2,256,2048]{2,1,0:T(8,128)(2,1)} %get-tuple-element.42.refs_4_), channel_id=1, source_target_pairs={{0,1},{1,0},{2,3},{3,2},{4,5},{5,4},{6,7},{7,6},{8,9},{9,8},{10,11... | collective-permute-start | bytes 6291464 | tf_op jit(solution)/shard_map/ppermute | solution.py:42
  238.5 4.0 %collective-permute-done.19.got_ref = bf16[2,256,2048]{2,1,0:T(8,128)(2,1)S(1)} collective-permute-done((bf16[2,256,2048]{2,1,0:T(8,128)(2,1)}, bf16[2,256,2048]{2,1,0:T(8,128)(2,1)S(1)}, u32[]{:S(2)}, u32[]{:S(2)}) %collective-permute-start.19) | collective-permute-done | bytes 2097184 | tf_op jit(solution)/shard_map/ppermute | solution.py:42
  242.7 3.1 %collective-permute-start.20 = (bf16[256,2048]{1,0:T(8,128)(2,1)S(1)}, bf16[256,2048]{1,0:T(8,128)(2,1)S(1)}, u32[]{:S(2)}, u32[]{:S(2)}) collective-permute-start(bf16[256,2048]{1,0:T(8,128)(2,1)S(1)} %shard_map.135.refs_5_), channel_id=1, source_target_pairs={{0,2},{2,0},{1,3},{3,1},{4,6},{6,4},{5,7},{7,5},{8,10},{10,8},{9,1... | collective-permute-start | bytes 3145736 | tf_op jit(solution)/shard_map/ppermute | solution.py:42
  245.8 2.3 shard_map.137.refs_0_
  248.2 1.5 collective-permute-start.21
  249.7 1.6 collective-permute-start.22
  252.0 2.3 collective-permute-done.22.refs_2_
  254.3 2.0 collective-permute-done.23.refs_3_
  257.8 1.9 collective-permute-done.24.refs_2_
  259.8 1.3 collective-permute-done.25.refs_3_
  262.3 3.2 %collective-permute-start.27 = (f32[256,256]{1,0:T(8,128)S(1)}, f32[256,256]{1,0:T(8,128)S(1)}, u32[]{:S(2)}, u32[]{:S(2)}) collective-permute-start(f32[256,256]{1,0:T(8,128)S(1)} %shard_map.139.refs_0_), channel_id=1, source_target_pairs={{0,1},{1,0},{64,65},{65,64},{2,3},{3,2},{66,67},{67,66},{4,5},{5,4... | collective-permute-start | bytes 786440 | tf_op jit(solution)/shard_map/ppermute | solution.py:42
  267.0 5.0 %collective-permute-done.28.refs_1_ = bf16[256,256]{1,0:T(8,128)(2,1)S(1)} collective-permute-done((bf16[256,256]{1,0:T(8,128)(2,1)S(1)}, bf16[256,256]{1,0:T(8,128)(2,1)S(1)}, u32[]{:S(2)}, u32[]{:S(2)}) %collective-permute-start.28) | collective-permute-done | bytes 131104 | tf_op jit(solution)/shard_map/ppermute | solution.py:42
  272.2 2.2 shard_map.136
  275.3 6.0 %psum.31.inner_ref = f32[8,256]{1,0:T(8,128)S(1)} all-reduce(f32[8,256]{1,0:T(8,128)S(1)} %get-tuple-element.45), channel_id=1, replica_groups=mesh['section'=2,'z'=4,'y'=4,'pair'=2,'core'=2] {'pair','core'}, use_global_device_ids=true, to_apply=%region_5.6 | all-reduce | flops 2048 | bytes 16384 | tf_op jit(solution)/shard_map/psum | solution.py:714
  283.5 3.0 %shard_map.142 = (bf16[256,2048]{1,0:T(8,128)(2,1)}, f32[256,256]{1,0:T(8,128)}) custom-call(s32[4]{0:T(128)S(1)} %pad_add_fusion.where_ref.refs_0_, bf16[256,2048]{1,0:T(8,128)(2,1)S(1)} %copy-done.21, f32[8,256]{1,0:T(8,128)S(1)} %psum.31.inner_ref, bf16[256,2048]{1,0:T(8,128)(2,1)S(1)} %bitcast.34, f32[256,1]{1,0:T(8,128)S(1)} %copy.28.refs_2_.scale_ref, ...), custom_call_target="tpu_custom_call" | custom-call | bytes 1048576 | tf_op jit(solution)/shard_map/pallas_call | solution.py:538
  (126 shorter events, 26.7 us)
Async XLA Ops:
  0.6 14.2 %copy-start = (f32[256,256]{1,0:T(8,128)S(1)}, f32[256,256]{1,0:T(8,128)}, u32[]{:S(2)}) copy-start(f32[256,256]{1,0:T(8,128)} %param.15) | copy-start | bytes 786436
  0.6 49.3 %collective-permute-start.3 = (bf16[512,2048]{1,0:T(8,128)(2,1)}, bf16[512,2048]{1,0:T(8,128)(2,1)}, u32[]{:S(2)}, u32[]{:S(2)}) collective-permute-start(bf16[512,2048]{1,0:T(8,128)(2,1)} %bitcast.35), channel_id=1, source_target_pairs={{0,48},{16,0},{32,16},{48,32},{64,112},{80,64},{96,80},{112,96},{1... | collective-permute-start | bytes 6291464 | tf_op jit(solution)/shard_map/ppermute | solution.py:37
  5.3 47.7 %collective-permute-start.4 = (bf16[512,2048]{1,0:T(8,128)(2,1)}, bf16[512,2048]{1,0:T(8,128)(2,1)}, u32[]{:S(2)}, u32[]{:S(2)}) collective-permute-start(bf16[512,2048]{1,0:T(8,128)(2,1)} %bitcast.36), channel_id=1, source_target_pairs={{0,16},{16,32},{32,48},{48,0},{64,80},{80,96},{96,112},{112,64},{1... | collective-permute-start | bytes 6291464 | tf_op jit(solution)/shard_map/ppermute | solution.py:37
  9.5 4.9 %copy-start.27 = (s32[1,2,128,2]{2,3,1,0:T(2,128)S(1)}, s32[1,2,128,2]{2,3,1,0:T(2,128)}, u32[]{:S(2)}) copy-start(s32[1,2,128,2]{2,3,1,0:T(2,128)} %param.16) | copy-start | bytes 6148
  9.5 5.0 %copy-start.28 = (f32[1,2,128,2]{2,3,1,0:T(2,128)S(1)}, f32[1,2,128,2]{2,3,1,0:T(2,128)}, u32[]{:S(2)}) copy-start(f32[1,2,128,2]{2,3,1,0:T(2,128)} %param.17) | copy-start | bytes 6148
  9.5 5.7 %copy-start.2 = (bf16[1,256,2048]{2,1,0:T(8,128)(2,1)S(1)}, bf16[1,256,2048]{2,1,0:T(8,128)(2,1)}, u32[]{:S(2)}) copy-start(bf16[1,256,2048]{2,1,0:T(8,128)(2,1)} %param.11) | copy-start | bytes 3145732
  11.5 6.0 %copy-start.24 = (f32[1,2048]{1,0:T(1,128)S(1)}, f32[1,2048]{1,0:T(1,128)}, u32[]{:S(2)}) copy-start(f32[1,2048]{1,0:T(1,128)} %refs_3_.1) | copy-start | bytes 24580
  11.5 47.1 %collective-permute-start = (bf16[512,2048]{1,0:T(8,128)(2,1)}, bf16[512,2048]{1,0:T(8,128)(2,1)S(1)}, u32[]{:S(2)}, u32[]{:S(2)}) collective-permute-start(bf16[512,2048]{1,0:T(8,128)(2,1)} %shard_map.122.refs_1_.refs_5_), channel_id=1, source_target_pairs={{0,12},{4,0},{8,4},{12,8},{64,76},{68,64},{72,68},{76,72},{1,13},{... | collective-permute-start | bytes 6291464 | tf_op jit(solution)/shard_map/ppermute | solution.py:37
  14.3 47.4 %collective-permute-start.1 = (bf16[512,2048]{1,0:T(8,128)(2,1)}, bf16[512,2048]{1,0:T(8,128)(2,1)}, u32[]{:S(2)}, u32[]{:S(2)}) collective-permute-start(bf16[512,2048]{1,0:T(8,128)(2,1)} %shard_map.122.refs_1_.refs_5_), channel_id=1, source_target_pairs={{0,4},{4,8},{8,12},{12,0},{64,68},{68,72},{72,76},{76,64},{1,5},{5... | collective-permute-start | bytes 6291464 | tf_op jit(solution)/shard_map/ppermute | solution.py:37
  14.8 15.5 %copy-start.25 = (f32[2,4,8,256]{3,2,1,0:T(8,128)}, f32[2,4,8,256]{3,2,1,0:T(8,128)S(1)}, u32[]{:S(2)}) copy-start(f32[2,4,8,256]{3,2,1,0:T(8,128)S(1)} %select_reduce_fusion) | copy-start | bytes 196612
  54.6 22.9 %collective-permute-start.5 = (bf16[256,2048]{1,0:T(8,128)(2,1)S(1)}, bf16[256,2048]{1,0:T(8,128)(2,1)S(1)}, u32[]{:S(2)}, u32[]{:S(2)}) collective-permute-start(bf16[256,2048]{1,0:T(8,128)(2,1)S(1)} %get-tuple-element.26), channel_id=1, source_target_pairs={{0,48},{16,0},{32,16},{48,32},{64,112},{80,64},{96,80},{112,96},{1... | collective-permute-start | bytes 3145736 | tf_op jit(solution)/shard_map/ppermute | solution.py:37
  55.0 32.8 %copy-start.10 = (bf16[1,512,2048]{2,1,0:T(8,128)(2,1)S(1)}, bf16[1,512,2048]{2,1,0:T(8,128)(2,1)}, u32[]{:S(2)}) copy-start(bf16[1,512,2048]{2,1,0:T(8,128)(2,1)} %param.14) | copy-start | bytes 6291460
  55.0 24.0 %collective-permute-start.6 = (bf16[256,2048]{1,0:T(8,128)(2,1)S(1)}, bf16[256,2048]{1,0:T(8,128)(2,1)S(1)}, u32[]{:S(2)}, u32[]{:S(2)}) collective-permute-start(bf16[256,2048]{1,0:T(8,128)(2,1)S(1)} %get-tuple-element.27), channel_id=1, source_target_pairs={{0,16},{16,32},{32,48},{48,0},{64,80},{80,96},{96,112},{112,64},{1... | collective-permute-start | bytes 3145736 | tf_op jit(solution)/shard_map/ppermute | solution.py:37
  58.6 33.6 %copy-start.3 = (bf16[512,2048]{1,0:T(8,128)(2,1)}, bf16[512,2048]{1,0:T(8,128)(2,1)S(1)}, u32[]{:S(2)}) copy-start(bf16[512,2048]{1,0:T(8,128)(2,1)S(1)} %collective-permute-done.refs_0_.refs_2_.refs_3_.refs_8_) | copy-start | bytes 6291460
  63.1 22.6 %collective-permute-start.2 = (bf16[256,2048]{1,0:T(8,128)(2,1)S(1)}, bf16[256,2048]{1,0:T(8,128)(2,1)S(1)}, u32[]{:S(2)}, u32[]{:S(2)}) collective-permute-start(bf16[256,2048]{1,0:T(8,128)(2,1)S(1)} %get-tuple-element.25), channel_id=1, source_target_pairs={{0,12},{4,0},{8,4},{12,8},{64,76},{68,64},{72,68},{76,72},{1,13},{... | collective-permute-start | bytes 3145736 | tf_op jit(solution)/shard_map/ppermute | solution.py:37
  64.0 23.7 %collective-permute-start.7 = (bf16[256,2048]{1,0:T(8,128)(2,1)S(1)}, bf16[256,2048]{1,0:T(8,128)(2,1)S(1)}, u32[]{:S(2)}, u32[]{:S(2)}) collective-permute-start(bf16[256,2048]{1,0:T(8,128)(2,1)S(1)} %get-tuple-element.28), channel_id=1, source_target_pairs={{0,4},{4,8},{8,12},{12,0},{64,68},{68,72},{72,76},{76,64},{1,5},{5... | collective-permute-start | bytes 3145736 | tf_op jit(solution)/shard_map/ppermute | solution.py:37
  77.4 22.4 %copy-start.5 = (bf16[256,2048]{1,0:T(8,128)(2,1)}, bf16[256,2048]{1,0:T(8,128)(2,1)S(1)}, u32[]{:S(2)}) copy-start(bf16[256,2048]{1,0:T(8,128)(2,1)S(1)} %collective-permute-done.5.refs_7_.refs_1_.refs_5_) | copy-start | bytes 3145732
  79.0 20.9 %copy-start.7 = (bf16[256,2048]{1,0:T(8,128)(2,1)}, bf16[256,2048]{1,0:T(8,128)(2,1)S(1)}, u32[]{:S(2)}) copy-start(bf16[256,2048]{1,0:T(8,128)(2,1)S(1)} %collective-permute-done.6.refs_8_.refs_2_.refs_6_) | copy-start | bytes 3145732
  85.6 6.6 %copy-start.12 = (bf16[256,2048]{1,0:T(8,128)(2,1)}, bf16[256,2048]{1,0:T(8,128)(2,1)S(1)}, u32[]{:S(2)}) copy-start(bf16[256,2048]{1,0:T(8,128)(2,1)S(1)} %collective-permute-done.2.refs_3_.refs_1_.refs_9_) | copy-start | bytes 3145732
  87.7 4.5 %copy-start.4 = (bf16[256,2048]{1,0:T(8,128)(2,1)}, bf16[256,2048]{1,0:T(8,128)(2,1)S(1)}, u32[]{:S(2)}) copy-start(bf16[256,2048]{1,0:T(8,128)(2,1)S(1)} %collective-permute-done.7.refs_10_.refs_3_.refs_2_) | copy-start | bytes 3145732
  88.4 3.6 %collective-permute-start.8 = (bf16[2,1024,512]{2,1,0:T(8,128)(2,1)S(1)}, bf16[2,1024,512]{2,1,0:T(8,128)(2,1)S(1)}, u32[]{:S(2)}, u32[]{:S(2)}) collective-permute-start(bf16[2,1024,512]{2,1,0:T(8,128)(2,1)S(1)} %get-tuple-element.30), channel_id=1, source_target_pairs={{64,65},{65,64},{66,67},{67,66},{68,69},{69,68},{70,71},{71,70},{7... | collective-permute-start | bytes 6291464 | tf_op jit(solution)/shard_map/ppermute | solution.py:42
  90.1 47.5 %collective-permute-start.10 = (bf16[512,2048]{1,0:T(8,128)(2,1)S(1)}, bf16[512,2048]{1,0:T(8,128)(2,1)S(1)}, u32[]{:S(2)}, u32[]{:S(2)}) collective-permute-start(bf16[512,2048]{1,0:T(8,128)(2,1)S(1)} %shard_map.127), channel_id=1, source_target_pairs={{0,8},{4,12},{8,0},{12,4},{1,9},{5,13},{9,1},{13,5},{2,10},{6,14},... | collective-permute-start | bytes 6291464 | tf_op jit(solution)/shard_map/ppermute | solution.py:37
  97.0 114.7 %collective-permute-start.17 = (bf16[1312,2048]{1,0:T(8,128)(2,1)}, bf16[1312,2048]{1,0:T(8,128)(2,1)}, u32[]{:S(2)}, u32[]{:S(2)}) collective-permute-start(bf16[1312,2048]{1,0:T(8,128)(2,1)} %shard_map.133), channel_id=1, source_target_pairs={{0,48},{16,0},{32,16},{48,32},{64,112},{80,64},{96,80},{112,96},{1... | collective-permute-start | bytes 16121864 | tf_op jit(solution)/shard_map/ppermute | solution.py:37
  99.1 115.2 %collective-permute-start.18 = (bf16[1312,2048]{1,0:T(8,128)(2,1)}, bf16[1312,2048]{1,0:T(8,128)(2,1)}, u32[]{:S(2)}, u32[]{:S(2)}) collective-permute-start(bf16[1312,2048]{1,0:T(8,128)(2,1)} %shard_map.133), channel_id=1, source_target_pairs={{0,16},{16,32},{32,48},{48,0},{64,80},{80,96},{96,112},{112,64},{1... | collective-permute-start | bytes 16121864 | tf_op jit(solution)/shard_map/ppermute | solution.py:37
  99.1 38.4 %collective-permute-start.9 = (bf16[1024,512]{1,0:T(8,128)(2,1)S(1)}, bf16[1024,512]{1,0:T(8,128)(2,1)S(1)}, u32[]{:S(2)}, u32[]{:S(2)}) collective-permute-start(bf16[1024,512]{1,0:T(8,128)(2,1)S(1)} %shard_map.126.refs_5_), channel_id=1, source_target_pairs={{64,66},{66,64},{65,67},{67,65},{68,70},{70,68},{69,71},{71,69},{7... | collective-permute-start | bytes 3145736 | tf_op jit(solution)/shard_map/ppermute | solution.py:42
  138.9 20.1 %copy-start.16 = (bf16[256,2048]{1,0:T(8,128)(2,1)S(1)}, bf16[256,2048]{1,0:T(8,128)(2,1)}, u32[]{:S(2)}) copy-start(bf16[256,2048]{1,0:T(8,128)(2,1)} %incoming_ref.3) | copy-start | bytes 3145732
  138.9 2.4 collective-permute-start.11
  139.9 1.4 collective-permute-start.12
  140.6 0.7 collective-permute-start.13
  141.3 69.7 %collective-permute-start.15 = (bf16[736,2048]{1,0:T(8,128)(2,1)}, bf16[736,2048]{1,0:T(8,128)(2,1)}, u32[]{:S(2)}, u32[]{:S(2)}) collective-permute-start(bf16[736,2048]{1,0:T(8,128)(2,1)} %shard_map.128.refs_4_), channel_id=1, source_target_pairs={{0,12},{4,0},{8,4},{12,8},{1,13},{5,1},{9,5},{13,9},{2,14},{6,2},{... | collective-permute-start | bytes 9043976 | tf_op jit(solution)/shard_map/ppermute | solution.py:37
  143.8 67.2 %collective-permute-start.16 = (bf16[736,2048]{1,0:T(8,128)(2,1)}, bf16[736,2048]{1,0:T(8,128)(2,1)}, u32[]{:S(2)}, u32[]{:S(2)}) collective-permute-start(bf16[736,2048]{1,0:T(8,128)(2,1)} %shard_map.128.refs_4_), channel_id=1, source_target_pairs={{0,4},{4,8},{8,12},{12,0},{1,5},{5,9},{9,13},{13,1},{2,6},{6,10},{... | collective-permute-start | bytes 9043976 | tf_op jit(solution)/shard_map/ppermute | solution.py:37
  159.0 3.2 %copy-start.29 = (s32[32]{0:T(128)S(1)}, s32[32]{0:T(128)}, u32[]{:S(2)}) copy-start(s32[32]{0:T(128)} %constant.100.clone) | copy-start | bytes 388
  160.7 53.7 %copy-start.6 = (bf16[256,2048]{1,0:T(8,128)(2,1)S(1)}, bf16[256,2048]{1,0:T(8,128)(2,1)}, u32[]{:S(2)}) copy-start(bf16[256,2048]{1,0:T(8,128)(2,1)} %copy-done.5) | copy-start | bytes 3145732
  160.7 53.7 %copy-start.8 = (bf16[256,2048]{1,0:T(8,128)(2,1)S(1)}, bf16[256,2048]{1,0:T(8,128)(2,1)}, u32[]{:S(2)}) copy-start(bf16[256,2048]{1,0:T(8,128)(2,1)} %copy-done.7) | copy-start | bytes 3145732
  160.7 39.0 %collective-permute-start.14 = (bf16[256,2048]{1,0:T(8,128)(2,1)}, bf16[256,2048]{1,0:T(8,128)(2,1)}, u32[]{:S(2)}, u32[]{:S(2)}) collective-permute-start(bf16[256,2048]{1,0:T(8,128)(2,1)} %shard_map.131.top_ref), channel_id=1, source_target_pairs={{64,0},{65,1},{66,2},{67,3},{68,4},{69,5},{70,6},{71,7},{72,8},{73... | collective-permute-start | bytes 3145736 | tf_op jit(solution)/shard_map/ppermute | solution.py:703
  232.0 10.5 %collective-permute-start.19 = (bf16[2,256,2048]{2,1,0:T(8,128)(2,1)}, bf16[2,256,2048]{2,1,0:T(8,128)(2,1)S(1)}, u32[]{:S(2)}, u32[]{:S(2)}) collective-permute-start(bf16[2,256,2048]{2,1,0:T(8,128)(2,1)} %get-tuple-element.42.refs_4_), channel_id=1, source_target_pairs={{0,1},{1,0},{2,3},{3,2},{4,5},{5,4},{6,7},{7,6},{8,9},{9,8},{10,11... | collective-permute-start | bytes 6291464 | tf_op jit(solution)/shard_map/ppermute | solution.py:42
  242.7 29.5 %collective-permute-start.20 = (bf16[256,2048]{1,0:T(8,128)(2,1)S(1)}, bf16[256,2048]{1,0:T(8,128)(2,1)S(1)}, u32[]{:S(2)}, u32[]{:S(2)}) collective-permute-start(bf16[256,2048]{1,0:T(8,128)(2,1)S(1)} %shard_map.135.refs_5_), channel_id=1, source_target_pairs={{0,2},{2,0},{1,3},{3,1},{4,6},{6,4},{5,7},{7,5},{8,10},{10,8},{9,1... | collective-permute-start | bytes 3145736 | tf_op jit(solution)/shard_map/ppermute | solution.py:42
  245.8 10.5 %copy-start.19 = (bf16[2,256,2048]{2,1,0:T(8,128)(2,1)S(1)}, bf16[2,256,2048]{2,1,0:T(8,128)(2,1)}, u32[]{:S(2)}) copy-start(bf16[2,256,2048]{2,1,0:T(8,128)(2,1)} %get-tuple-element.42.refs_4_) | copy-start | bytes 6291460
  248.2 3.9 %collective-permute-start.21 = (f32[8,2048]{1,0:T(8,128)S(1)}, f32[8,2048]{1,0:T(8,128)S(1)}, u32[]{:S(2)}, u32[]{:S(2)}) collective-permute-start(f32[8,2048]{1,0:T(8,128)S(1)} %shard_map.137.refs_0_), channel_id=1, source_target_pairs={{0,12},{4,0},{8,4},{12,8},{64,76},{68,64},{72,68},{76,72},{1,13},{... | collective-permute-start | bytes 196616 | tf_op jit(solution)/shard_map/ppermute | solution.py:37
  249.7 4.6 %collective-permute-start.22 = (f32[8,2048]{1,0:T(8,128)S(1)}, f32[8,2048]{1,0:T(8,128)S(1)}, u32[]{:S(2)}, u32[]{:S(2)}) collective-permute-start(f32[8,2048]{1,0:T(8,128)S(1)} %shard_map.137.refs_0_), channel_id=1, source_target_pairs={{0,8},{4,12},{8,0},{12,4},{64,72},{68,76},{72,64},{76,68},{1,9},{5... | collective-permute-start | bytes 196616 | tf_op jit(solution)/shard_map/ppermute | solution.py:37
  251.2 5.0 %collective-permute-start.23 = (f32[8,2048]{1,0:T(8,128)S(1)}, f32[8,2048]{1,0:T(8,128)S(1)}, u32[]{:S(2)}, u32[]{:S(2)}) collective-permute-start(f32[8,2048]{1,0:T(8,128)S(1)} %shard_map.137.refs_0_), channel_id=1, source_target_pairs={{0,4},{4,8},{8,12},{12,0},{64,68},{68,72},{72,76},{76,64},{1,5},{5... | collective-permute-start | bytes 196616 | tf_op jit(solution)/shard_map/ppermute | solution.py:37
  256.3 3.5 %collective-permute-start.24 = (f32[8,2048]{1,0:T(8,128)S(1)}, f32[8,2048]{1,0:T(8,128)S(1)}, u32[]{:S(2)}, u32[]{:S(2)}) collective-permute-start(f32[8,2048]{1,0:T(8,128)S(1)} %shard_map.138.refs_1_), channel_id=1, source_target_pairs={{0,48},{16,0},{32,16},{48,32},{64,112},{80,64},{96,80},{112,96},{1... | collective-permute-start | bytes 196616 | tf_op jit(solution)/shard_map/ppermute | solution.py:37
  256.4 4.7 %collective-permute-start.25 = (f32[8,2048]{1,0:T(8,128)S(1)}, f32[8,2048]{1,0:T(8,128)S(1)}, u32[]{:S(2)}, u32[]{:S(2)}) collective-permute-start(f32[8,2048]{1,0:T(8,128)S(1)} %shard_map.138.refs_1_), channel_id=1, source_target_pairs={{0,32},{16,48},{32,0},{48,16},{64,96},{80,112},{96,64},{112,80},{1... | collective-permute-start | bytes 196616 | tf_op jit(solution)/shard_map/ppermute | solution.py:37
  257.0 4.9 %collective-permute-start.26 = (f32[8,2048]{1,0:T(8,128)S(1)}, f32[8,2048]{1,0:T(8,128)S(1)}, u32[]{:S(2)}, u32[]{:S(2)}) collective-permute-start(f32[8,2048]{1,0:T(8,128)S(1)} %shard_map.138.refs_1_), channel_id=1, source_target_pairs={{0,16},{16,32},{32,48},{48,0},{64,80},{80,96},{96,112},{112,64},{1... | collective-permute-start | bytes 196616 | tf_op jit(solution)/shard_map/ppermute | solution.py:37
  262.3 4.3 %collective-permute-start.27 = (f32[256,256]{1,0:T(8,128)S(1)}, f32[256,256]{1,0:T(8,128)S(1)}, u32[]{:S(2)}, u32[]{:S(2)}) collective-permute-start(f32[256,256]{1,0:T(8,128)S(1)} %shard_map.139.refs_0_), channel_id=1, source_target_pairs={{0,1},{1,0},{64,65},{65,64},{2,3},{3,2},{66,67},{67,66},{4,5},{5,4... | collective-permute-start | bytes 786440 | tf_op jit(solution)/shard_map/ppermute | solution.py:42
  266.7 5.4 %collective-permute-start.28 = (bf16[256,256]{1,0:T(8,128)(2,1)S(1)}, bf16[256,256]{1,0:T(8,128)(2,1)S(1)}, u32[]{:S(2)}, u32[]{:S(2)}) collective-permute-start(bf16[256,256]{1,0:T(8,128)(2,1)S(1)} %shard_map.140.refs_0_), channel_id=1, source_target_pairs={{0,2},{2,0},{64,66},{66,64},{1,3},{3,1},{65,67},{67,65},{4,6},{6,4... | collective-permute-start | bytes 393224 | tf_op jit(solution)/shard_map/ppermute | solution.py:42
  272.1 9.2 %collective-permute-start.29 = (bf16[256,256]{1,0:T(8,128)(2,1)S(1)}, bf16[256,256]{1,0:T(8,128)(2,1)}, u32[]{:S(2)}, u32[]{:S(2)}) collective-permute-start(bf16[256,256]{1,0:T(8,128)(2,1)S(1)} %shard_map.141.share_ref), channel_id=1, source_target_pairs={{0,64},{64,0},{1,65},{65,1},{2,66},{66,2},{3,67},{67,3},{4,68},{68... | collective-permute-start | bytes 393224 | tf_op jit(solution)/shard_map/ppermute | solution.py:730
  281.3 5.2 %copy-start.1 = (f32[256,256]{1,0:T(8,128)S(1)}, f32[256,256]{1,0:T(8,128)}, u32[]{:S(2)}) copy-start(f32[256,256]{1,0:T(8,128)} %param.15) | copy-start | bytes 786436
  (14 other events, 23.8 us)

commit v8 on v7

--- a/solution.py
+++ b/solution.py
@@ -547,40 +547,44 @@
     )(where, scaled, inner, hidden, scale, incoming, share, other, top)
 
 
-def grads_kernel(where_ref, hidden_ref, scale_ref, gain_ref, projected_ref, *refs):
-    out_ref = refs[-1]
+def grads_kernel(
+    where_ref, hidden_ref, scale_ref, gain_ref, projected_ref, top_mixed, low_mixed, top_dz, low_dz,
+    out_ref, dz_ref, sem,
+):
     top = where_ref[3] == 1
-    count = (len(refs) - 2) // 3
-    total_a, total_b = 0.0, 0.0
-    for c in range(count):
-        low_dz, top_mixed, low_mixed = [refs[1 + k * count + c] for k in range(3)]
-        rows = pl.ds(c * low_dz.shape[0], low_dz.shape[0])
-        dz = jnp.where(top, refs[0][rows], low_dz[...])
-        mixed = jnp.where(top, top_mixed[...], low_mixed[...])
-        x = (hidden_ref[rows].astype(F32) * scale_ref[rows] * gain_ref[...]).astype(BF16)
-        projected = projected_ref[:, rows]
-
-        def both(left, right):
-            value = lax.dot_general(
-                two_halves(left), right, (((1,), (0,)), ((), ())), preferred_element_type=F32
-            )
-            return value[:RANK] + value[RANK:]
-
-        total_a = total_a + both(mixed, x)
-        total_b = total_b + both(projected, dz)
-    out_ref[...] = jnp.concatenate([total_a, total_b], axis=0)
-
-
-def make_grads(where, hidden, scale, gain, projected, lists, *earlier):
-    arrays = [array for arrays in lists for array in arrays]
-    return pl.pallas_call(
-        in_order(grads_kernel, 5 + len(arrays), len(earlier)),
-        in_specs=[SMEM] + [VMEM] * (4 + len(arrays)) + [ANY] * len(earlier),
+    rows = dz_ref.shape[0]
+
+    @pl.when(top)
+    def _():
+        pltpu.make_async_copy(top_dz.at[pl.ds(0, rows)], dz_ref, sem).start()
+
+    @pl.when(jnp.logical_not(top))
+    def _():
+        pltpu.make_async_copy(low_dz, dz_ref, sem).start()
+
+    def both(left, right):
+        value = lax.dot_general(
+            two_halves(left), right, (((1,), (0,)), ((), ())), preferred_element_type=F32
+        )
+        return value[:RANK] + value[RANK:]
+
+    mixed = jnp.where(top, top_mixed[...], low_mixed[...])
+    x = (hidden_ref[...].astype(F32) * scale_ref[...] * gain_ref[...]).astype(BF16)
+    out_ref[:RANK] = both(mixed, x)
+    pltpu.make_async_copy(low_dz, dz_ref, sem).wait()
+    out_ref[RANK:] = both(projected_ref[...], dz_ref[...])
+
+
+def make_grads(where, hidden, scale, gain, projected, top_mixed, low_mixed, top_dz, low_dz):
+    return pl.pallas_call(
+        grads_kernel,
+        in_specs=[SMEM] + [VMEM] * 6 + [HBM] * 2,
         out_specs=VMEM,
         out_shape=jax.ShapeDtypeStruct((2 * RANK, hidden.shape[1]), F32),
+        scratch_shapes=[pltpu.VMEM(low_dz.shape, BF16), pltpu.SemaphoreType.DMA],
         compiler_params=pltpu.CompilerParams(vmem_limit_bytes=MEDIUM),
         cost_estimate=LIGHT,
-    )(where, hidden, scale, gain, projected, *arrays, *earlier)
+    )(where, hidden, scale, gain, projected, top_mixed, low_mixed, top_dz, low_dz)
 
 
 def ring_total(value, moved):
@@ -712,9 +716,7 @@
     other = swap(theirs, "pair", (0,))
     scaled, inner = low_scaled(mine, got, other, low_mixed, a_local, norm_gain, hidden, scale)
     inner = lax.psum(inner, tensor)
-    grads = make_grads(
-        where, hidden, scale, norm_gain, projected, ([first], [low_dz], [top_mixed], [low_mixed])
-    )
+    grads = make_grads(where, hidden, scale, norm_gain, projected, top_mixed, low_mixed, first, low_dz)
     over_y = ring_moves(grads, "y")
     grads = small_call(ring_kernel, jax.ShapeDtypeStruct(grads.shape, F32), (grads, *over_y), send)
     over_z = ring_moves(grads, "z")

time: 289 us -> 289 us (level)
  no operation moved by 1% of the time
where the time goes in v8:
time: 289 us; the launch traced here: 287 us
  waiting for transfers between devices  145 us (50%)
  Pallas kernels  45.1 us (16%)
  starting transfers between devices  43.7 us (15%)
  blocking collectives  33.9 us (12%)
  local copies, waits for them, and re-layouts  12.3 us (4%)
  matrix products  4.12 us (1%)
    ppermute x22, waiting for transfers between devices, ring_move(): lax.ppermute(block, ('section', axis), ring_route(distance, sections))  97.2 us
    ppermute x1, waiting for transfers between devices, shards(): low_in = lax.ppermute(top_grad, 'section', [(1, 0)])  37.3 us
    ppermute x22, starting transfers between devices, ring_move(): lax.ppermute(block, ('section', axis), ring_route(distance, sections))  27.6 us
    pallas_call x1, Pallas kernels, low_product(): pl.pallas_call(in_order(functools.partial(low_product_kernel, copies), 3...  16.4 us
    ppermute x6, starting transfers between devices, swap(): return lax.ppermute(block, ('section', axis), pairs)  14.6 us
    unnamed x64, local copies, waits for them, and re-layouts  11.8 us
    psum x1, blocking collectives, shards(): lax.psum(jnp.concatenate([jnp.sum(hidden_f * hidden_f, axis=1)[None], jnp...  11 us
    ppermute x6, waiting for transfers between devices, swap(): return lax.ppermute(block, ('section', axis), pairs)  10.9 us
  transfers between devices with their start and end apart: 30, of which 20 were waited for; matrix products, arithmetic and copies ran while one was open for 2% of the time, Pallas kernels for 9%

profile of v8, /device:TPU:1, one launch (start us, length us, event | category | flops | bytes accessed | tf_op | source)
XLA Modules:
  0.0 286.7 jit_solution(4796042357394731150)
XLA Ops:
  0.6 4.7 %collective-permute-start.3 = (bf16[512,2048]{1,0:T(8,128)(2,1)}, bf16[512,2048]{1,0:T(8,128)(2,1)}, u32[]{:S(2)}, u32[]{:S(2)}) collective-permute-start(bf16[512,2048]{1,0:T(8,128)(2,1)} %bitcast.35), channel_id=1, source_target_pairs={{0,48},{16,0},{32,16},{48,32},{64,112},{80,64},{96,80},{112,96},{1... | collective-permute-start | bytes 6291464 | tf_op jit(solution)/shard_map/ppermute | solution.py:37
  5.4 1.6 copy-done.9
  9.5 2.0 shard_map.122.refs_1_.top_dz
  11.5 2.8 collective-permute-start
  15.4 2.1 fusion.4
  17.6 1.7 fusion
  19.3 11.0 %psum.28 = f32[9,256]{1,0:T(8,128)S(1)} all-reduce(f32[9,256]{1,0:T(8,128)S(1)} %pad_maximum_fusion.1), channel_id=1, replica_groups=mesh['section'=2,'z'=4,'y'=4,'pair'=2,'core'=2] {'pair','core'}, use_global_device_ids=true, to_apply=%region_2.0 | all-reduce | flops 2304 | bytes 18432 | tf_op jit(solution)/shard_map/psum | solution.py:656
  30.5 19.4 %collective-permute-done.3.refs_0_.refs_6_.refs_3_.refs_4_ = bf16[512,2048]{1,0:T(8,128)(2,1)} collective-permute-done((bf16[512,2048]{1,0:T(8,128)(2,1)}, bf16[512,2048]{1,0:T(8,128)(2,1)}, u32[]{:S(2)}, u32[]{:S(2)}) %collective-permute-start.3) | collective-permute-done | bytes 2097184 | tf_op jit(solution)/shard_map/ppermute | solution.py:37
  49.9 3.1 %collective-permute-done.4.refs_1_.refs_9_.refs_4_.refs_7_ = bf16[512,2048]{1,0:T(8,128)(2,1)} collective-permute-done((bf16[512,2048]{1,0:T(8,128)(2,1)}, bf16[512,2048]{1,0:T(8,128)(2,1)}, u32[]{:S(2)}, u32[]{:S(2)}) %collective-permute-start.4) | collective-permute-done | bytes 2097184 | tf_op jit(solution)/shard_map/ppermute | solution.py:37
  53.0 1.6 shard_map.124
  56.1 2.5 collective-permute-done.refs_0_.refs_2_.refs_3_.refs_8_
  58.6 3.1 %collective-permute-done.1.refs_1_.refs_4_.refs_11_ = bf16[512,2048]{1,0:T(8,128)(2,1)} collective-permute-done((bf16[512,2048]{1,0:T(8,128)(2,1)}, bf16[512,2048]{1,0:T(8,128)(2,1)}, u32[]{:S(2)}, u32[]{:S(2)}) %collective-permute-start.1) | collective-permute-done | bytes 2097184 | tf_op jit(solution)/shard_map/ppermute | solution.py:37
  61.7 1.3 shard_map.123
  64.6 12.8 %collective-permute-done.5.refs_7_.refs_1_.refs_5_ = bf16[256,2048]{1,0:T(8,128)(2,1)S(1)} collective-permute-done((bf16[256,2048]{1,0:T(8,128)(2,1)S(1)}, bf16[256,2048]{1,0:T(8,128)(2,1)S(1)}, u32[]{:S(2)}, u32[]{:S(2)}) %collective-permute-start.5) | collective-permute-done | bytes 1048608 | tf_op jit(solution)/shard_map/ppermute | solution.py:37
  77.4 1.6 collective-permute-done.6.refs_8_.refs_2_.refs_6_
  79.0 6.6 %collective-permute-done.2.refs_3_.refs_1_.refs_9_ = bf16[256,2048]{1,0:T(8,128)(2,1)S(1)} collective-permute-done((bf16[256,2048]{1,0:T(8,128)(2,1)S(1)}, bf16[256,2048]{1,0:T(8,128)(2,1)S(1)}, u32[]{:S(2)}, u32[]{:S(2)}) %collective-permute-start.2) | collective-permute-done | bytes 1048608 | tf_op jit(solution)/shard_map/ppermute | solution.py:37
  85.6 2.1 collective-permute-done.7.refs_10_.refs_3_.refs_2_
  90.1 1.9 collective-permute-start.10
  92.3 4.7 %shard_map.133 = bf16[1312,2048]{1,0:T(8,128)(2,1)} custom-call(s32[4]{0:T(128)S(1)} %pad_add_fusion.where_ref.refs_0_, bf16[256,2048]{1,0:T(8,128)(2,1)S(1)} %collective-permute-done.2.refs_3_.refs_1_.refs_9_, bf16[256,2048]{1,0:T(8,128)(2,1)S(1)} %collective-permute-done.7.refs_10_.refs_3_.refs_2_, ...), custom_call_target="tpu_custom_call" | custom-call | bytes 1048576 | tf_op jit(solution)/shard_map/pallas_call | solution.py:136
  97.0 2.1 collective-permute-start.17
  99.9 3.4 %shard_map.128.refs_4_ = bf16[736,2048]{1,0:T(8,128)(2,1)} custom-call(s32[4]{0:T(128)S(1)} %pad_add_fusion.where_ref.refs_0_, bf16[256,2048]{1,0:T(8,128)(2,1)S(1)} %collective-permute-done.5.refs_7_.refs_1_.refs_5_, bf16[256,2048]{1,0:T(8,128)(2,1)S(1)} %collective-permute-done.6.refs_8_.refs_2_.refs_6_, ...), custom_call_target="tpu_custom_call" | custom-call | bytes 1048576 | tf_op jit(solution)/shard_map/pallas_call | solution.py:136
  103.3 34.2 %collective-permute-done.10.refs_3_.refs_12_ = bf16[512,2048]{1,0:T(8,128)(2,1)S(1)} collective-permute-done((bf16[512,2048]{1,0:T(8,128)(2,1)S(1)}, bf16[512,2048]{1,0:T(8,128)(2,1)S(1)}, u32[]{:S(2)}, u32[]{:S(2)}) %collective-permute-start.10) | collective-permute-done | bytes 2097184 | tf_op jit(solution)/shard_map/ppermute | solution.py:37
  141.3 2.5 collective-permute-start.15
  143.8 2.8 collective-permute-start.16
  146.6 2.7 shard_map.130
  149.3 9.6 %psum.29.inner_ref = f32[8,256]{1,0:T(8,128)S(1)} all-reduce(f32[8,256]{1,0:T(8,128)S(1)} %get-tuple-element.37), channel_id=1, replica_groups=mesh['section'=2,'z'=4,'y'=4,'pair'=2,'core'=2] {'pair','core'}, use_global_device_ids=true, to_apply=%region_3.0 | all-reduce | flops 2048 | bytes 16384 | tf_op jit(solution)/shard_map/psum | solution.py:706
  159.0 1.6 shard_map.131.top_ref
  160.7 1.4 collective-permute-start.14
  162.3 37.3 %collective-permute-done.14.refs_0_.incoming_ref = bf16[256,2048]{1,0:T(8,128)(2,1)} collective-permute-done((bf16[256,2048]{1,0:T(8,128)(2,1)}, bf16[256,2048]{1,0:T(8,128)(2,1)}, u32[]{:S(2)}, u32[]{:S(2)}) %collective-permute-start.14) | collective-permute-done | bytes 1048608 | tf_op jit(solution)/shard_map/ppermute | solution.py:707
  200.8 2.1 shard_map.132
  203.9 7.1 %psum.30.refs_17_.mixed_ref.low_mixed = f32[4,256]{1,0:T(4,128)S(1)} all-reduce(f32[4,256]{1,0:T(4,128)S(1)} %get-tuple-element.40), channel_id=1, replica_groups=mesh['section'=2,'z'=4,'y'=4,'pair'=2,'core'=2] {'pair','core'}, use_global_device_ids=true, to_apply=%region_4.0 | all-reduce | flops 1024 | bytes 8192 | tf_op jit(solution)/shard_map/psum | solution.py:712
  211.7 2.7 collective-permute-done.18.refs_16_
  215.6 16.4 %shard_map.134 = (bf16[256,2048]{1,0:T(8,128)(2,1)S(1)}, bf16[256,2048]{1,0:T(8,128)(2,1)S(1)}, bf16[2,256,2048]{2,1,0:T(8,128)(2,1)}) custom-call(s32[4]{0:T(128)S(1)} %pad_add_fusion.where_ref.refs_0_, s32[32]{0:T(128)S(1)} %fusion.16.refs_1_, bf16[256,2048]{1,0:T(8,128)(2,1)S(1)} %copy-done.18, bf16[512,2048]{1,0:T(8,128)(2,1)} %bitcast.37, ...), custom_call_target="tpu_custom_call" | custom-call | flops 8589934592 | bytes 33554432 | tf_op jit(solution)/shard_map/pallas_call | solution.py:355
  232.0 6.5 %collective-permute-start.19 = (bf16[2,256,2048]{2,1,0:T(8,128)(2,1)}, bf16[2,256,2048]{2,1,0:T(8,128)(2,1)S(1)}, u32[]{:S(2)}, u32[]{:S(2)}) collective-permute-start(bf16[2,256,2048]{2,1,0:T(8,128)(2,1)} %get-tuple-element.42.refs_4_), channel_id=1, source_target_pairs={{0,1},{1,0},{2,3},{3,2},{4,5},{5,4},{6,7},{7,6},{8,9},{9,8},{10,11... | collective-permute-start | bytes 6291464 | tf_op jit(solution)/shard_map/ppermute | solution.py:42
  238.5 4.0 %collective-permute-done.19.got_ref = bf16[2,256,2048]{2,1,0:T(8,128)(2,1)S(1)} collective-permute-done((bf16[2,256,2048]{2,1,0:T(8,128)(2,1)}, bf16[2,256,2048]{2,1,0:T(8,128)(2,1)S(1)}, u32[]{:S(2)}, u32[]{:S(2)}) %collective-permute-start.19) | collective-permute-done | bytes 2097184 | tf_op jit(solution)/shard_map/ppermute | solution.py:42
  242.7 3.1 %collective-permute-start.20 = (bf16[256,2048]{1,0:T(8,128)(2,1)S(1)}, bf16[256,2048]{1,0:T(8,128)(2,1)S(1)}, u32[]{:S(2)}, u32[]{:S(2)}) collective-permute-start(bf16[256,2048]{1,0:T(8,128)(2,1)S(1)} %shard_map.135.refs_5_), channel_id=1, source_target_pairs={{0,2},{2,0},{1,3},{3,1},{4,6},{6,4},{5,7},{7,5},{8,10},{10,8},{9,1... | collective-permute-start | bytes 3145736 | tf_op jit(solution)/shard_map/ppermute | solution.py:42
  245.8 1.3 shard_map.137.refs_0_
  247.1 1.5 collective-permute-start.21
  248.7 1.6 collective-permute-start.22
  251.0 2.3 collective-permute-done.22.refs_2_
  253.3 2.0 collective-permute-done.23.refs_3_
  256.8 1.9 collective-permute-done.24.refs_2_
  258.8 1.3 collective-permute-done.25.refs_3_
  261.3 3.2 %collective-permute-start.27 = (f32[256,256]{1,0:T(8,128)S(1)}, f32[256,256]{1,0:T(8,128)S(1)}, u32[]{:S(2)}, u32[]{:S(2)}) collective-permute-start(f32[256,256]{1,0:T(8,128)S(1)} %shard_map.139.refs_0_), channel_id=1, source_target_pairs={{0,1},{1,0},{64,65},{65,64},{2,3},{3,2},{66,67},{67,66},{4,5},{5,4... | collective-permute-start | bytes 786440 | tf_op jit(solution)/shard_map/ppermute | solution.py:42
  266.0 5.8 %collective-permute-done.28.refs_1_ = bf16[256,256]{1,0:T(8,128)(2,1)S(1)} collective-permute-done((bf16[256,256]{1,0:T(8,128)(2,1)S(1)}, bf16[256,256]{1,0:T(8,128)(2,1)S(1)}, u32[]{:S(2)}, u32[]{:S(2)}) %collective-permute-start.28) | collective-permute-done | bytes 131104 | tf_op jit(solution)/shard_map/ppermute | solution.py:42
  271.9 2.2 shard_map.136
  275.0 6.3 %psum.31.inner_ref = f32[8,256]{1,0:T(8,128)S(1)} all-reduce(f32[8,256]{1,0:T(8,128)S(1)} %get-tuple-element.45), channel_id=1, replica_groups=mesh['section'=2,'z'=4,'y'=4,'pair'=2,'core'=2] {'pair','core'}, use_global_device_ids=true, to_apply=%region_5.6 | all-reduce | flops 2048 | bytes 16384 | tf_op jit(solution)/shard_map/psum | solution.py:718
  283.5 3.0 %shard_map.142 = (bf16[256,2048]{1,0:T(8,128)(2,1)}, f32[256,256]{1,0:T(8,128)}) custom-call(s32[4]{0:T(128)S(1)} %pad_add_fusion.where_ref.refs_0_, bf16[256,2048]{1,0:T(8,128)(2,1)S(1)} %copy-done.21, f32[8,256]{1,0:T(8,128)S(1)} %psum.31.inner_ref, bf16[256,2048]{1,0:T(8,128)(2,1)S(1)} %bitcast.34, f32[256,1]{1,0:T(8,128)S(1)} %copy.28.refs_2_.scale_ref, ...), custom_call_target="tpu_custom_call" | custom-call | bytes 1048576 | tf_op jit(solution)/shard_map/pallas_call | solution.py:538
  (126 shorter events, 26.7 us)
Async XLA Ops:
  0.6 14.2 %copy-start = (f32[256,256]{1,0:T(8,128)S(1)}, f32[256,256]{1,0:T(8,128)}, u32[]{:S(2)}) copy-start(f32[256,256]{1,0:T(8,128)} %param.15) | copy-start | bytes 786436
  0.6 49.3 %collective-permute-start.3 = (bf16[512,2048]{1,0:T(8,128)(2,1)}, bf16[512,2048]{1,0:T(8,128)(2,1)}, u32[]{:S(2)}, u32[]{:S(2)}) collective-permute-start(bf16[512,2048]{1,0:T(8,128)(2,1)} %bitcast.35), channel_id=1, source_target_pairs={{0,48},{16,0},{32,16},{48,32},{64,112},{80,64},{96,80},{112,96},{1... | collective-permute-start | bytes 6291464 | tf_op jit(solution)/shard_map/ppermute | solution.py:37
  5.3 47.7 %collective-permute-start.4 = (bf16[512,2048]{1,0:T(8,128)(2,1)}, bf16[512,2048]{1,0:T(8,128)(2,1)}, u32[]{:S(2)}, u32[]{:S(2)}) collective-permute-start(bf16[512,2048]{1,0:T(8,128)(2,1)} %bitcast.36), channel_id=1, source_target_pairs={{0,16},{16,32},{32,48},{48,0},{64,80},{80,96},{96,112},{112,64},{1... | collective-permute-start | bytes 6291464 | tf_op jit(solution)/shard_map/ppermute | solution.py:37
  9.5 4.9 %copy-start.27 = (s32[1,2,128,2]{2,3,1,0:T(2,128)S(1)}, s32[1,2,128,2]{2,3,1,0:T(2,128)}, u32[]{:S(2)}) copy-start(s32[1,2,128,2]{2,3,1,0:T(2,128)} %param.16) | copy-start | bytes 6148
  9.5 5.0 %copy-start.28 = (f32[1,2,128,2]{2,3,1,0:T(2,128)S(1)}, f32[1,2,128,2]{2,3,1,0:T(2,128)}, u32[]{:S(2)}) copy-start(f32[1,2,128,2]{2,3,1,0:T(2,128)} %param.17) | copy-start | bytes 6148
  9.5 5.7 %copy-start.2 = (bf16[1,256,2048]{2,1,0:T(8,128)(2,1)S(1)}, bf16[1,256,2048]{2,1,0:T(8,128)(2,1)}, u32[]{:S(2)}) copy-start(bf16[1,256,2048]{2,1,0:T(8,128)(2,1)} %param.11) | copy-start | bytes 3145732
  11.5 6.0 %copy-start.24 = (f32[1,2048]{1,0:T(1,128)S(1)}, f32[1,2048]{1,0:T(1,128)}, u32[]{:S(2)}) copy-start(f32[1,2048]{1,0:T(1,128)} %gain_ref.5) | copy-start | bytes 24580
  11.5 47.1 %collective-permute-start = (bf16[512,2048]{1,0:T(8,128)(2,1)}, bf16[512,2048]{1,0:T(8,128)(2,1)S(1)}, u32[]{:S(2)}, u32[]{:S(2)}) collective-permute-start(bf16[512,2048]{1,0:T(8,128)(2,1)} %shard_map.122.refs_1_.top_dz), channel_id=1, source_target_pairs={{0,12},{4,0},{8,4},{12,8},{64,76},{68,64},{72,68},{76,72},{1,13},{... | collective-permute-start | bytes 6291464 | tf_op jit(solution)/shard_map/ppermute | solution.py:37
  14.3 47.4 %collective-permute-start.1 = (bf16[512,2048]{1,0:T(8,128)(2,1)}, bf16[512,2048]{1,0:T(8,128)(2,1)}, u32[]{:S(2)}, u32[]{:S(2)}) collective-permute-start(bf16[512,2048]{1,0:T(8,128)(2,1)} %shard_map.122.refs_1_.top_dz), channel_id=1, source_target_pairs={{0,4},{4,8},{8,12},{12,0},{64,68},{68,72},{72,76},{76,64},{1,5},{5... | collective-permute-start | bytes 6291464 | tf_op jit(solution)/shard_map/ppermute | solution.py:37
  14.8 15.5 %copy-start.25 = (f32[2,4,8,256]{3,2,1,0:T(8,128)}, f32[2,4,8,256]{3,2,1,0:T(8,128)S(1)}, u32[]{:S(2)}) copy-start(f32[2,4,8,256]{3,2,1,0:T(8,128)S(1)} %select_reduce_fusion) | copy-start | bytes 196612
  54.6 22.9 %collective-permute-start.5 = (bf16[256,2048]{1,0:T(8,128)(2,1)S(1)}, bf16[256,2048]{1,0:T(8,128)(2,1)S(1)}, u32[]{:S(2)}, u32[]{:S(2)}) collective-permute-start(bf16[256,2048]{1,0:T(8,128)(2,1)S(1)} %get-tuple-element.26), channel_id=1, source_target_pairs={{0,48},{16,0},{32,16},{48,32},{64,112},{80,64},{96,80},{112,96},{1... | collective-permute-start | bytes 3145736 | tf_op jit(solution)/shard_map/ppermute | solution.py:37
  55.0 32.8 %copy-start.10 = (bf16[1,512,2048]{2,1,0:T(8,128)(2,1)S(1)}, bf16[1,512,2048]{2,1,0:T(8,128)(2,1)}, u32[]{:S(2)}) copy-start(bf16[1,512,2048]{2,1,0:T(8,128)(2,1)} %param.14) | copy-start | bytes 6291460
  55.0 24.0 %collective-permute-start.6 = (bf16[256,2048]{1,0:T(8,128)(2,1)S(1)}, bf16[256,2048]{1,0:T(8,128)(2,1)S(1)}, u32[]{:S(2)}, u32[]{:S(2)}) collective-permute-start(bf16[256,2048]{1,0:T(8,128)(2,1)S(1)} %get-tuple-element.27), channel_id=1, source_target_pairs={{0,16},{16,32},{32,48},{48,0},{64,80},{80,96},{96,112},{112,64},{1... | collective-permute-start | bytes 3145736 | tf_op jit(solution)/shard_map/ppermute | solution.py:37
  58.6 33.6 %copy-start.3 = (bf16[512,2048]{1,0:T(8,128)(2,1)}, bf16[512,2048]{1,0:T(8,128)(2,1)S(1)}, u32[]{:S(2)}) copy-start(bf16[512,2048]{1,0:T(8,128)(2,1)S(1)} %collective-permute-done.refs_0_.refs_2_.refs_3_.refs_8_) | copy-start | bytes 6291460
  63.1 22.6 %collective-permute-start.2 = (bf16[256,2048]{1,0:T(8,128)(2,1)S(1)}, bf16[256,2048]{1,0:T(8,128)(2,1)S(1)}, u32[]{:S(2)}, u32[]{:S(2)}) collective-permute-start(bf16[256,2048]{1,0:T(8,128)(2,1)S(1)} %get-tuple-element.25), channel_id=1, source_target_pairs={{0,12},{4,0},{8,4},{12,8},{64,76},{68,64},{72,68},{76,72},{1,13},{... | collective-permute-start | bytes 3145736 | tf_op jit(solution)/shard_map/ppermute | solution.py:37
  64.0 23.7 %collective-permute-start.7 = (bf16[256,2048]{1,0:T(8,128)(2,1)S(1)}, bf16[256,2048]{1,0:T(8,128)(2,1)S(1)}, u32[]{:S(2)}, u32[]{:S(2)}) collective-permute-start(bf16[256,2048]{1,0:T(8,128)(2,1)S(1)} %get-tuple-element.28), channel_id=1, source_target_pairs={{0,4},{4,8},{8,12},{12,0},{64,68},{68,72},{72,76},{76,64},{1,5},{5... | collective-permute-start | bytes 3145736 | tf_op jit(solution)/shard_map/ppermute | solution.py:37
  77.4 22.4 %copy-start.5 = (bf16[256,2048]{1,0:T(8,128)(2,1)}, bf16[256,2048]{1,0:T(8,128)(2,1)S(1)}, u32[]{:S(2)}) copy-start(bf16[256,2048]{1,0:T(8,128)(2,1)S(1)} %collective-permute-done.5.refs_7_.refs_1_.refs_5_) | copy-start | bytes 3145732
  79.0 20.9 %copy-start.7 = (bf16[256,2048]{1,0:T(8,128)(2,1)}, bf16[256,2048]{1,0:T(8,128)(2,1)S(1)}, u32[]{:S(2)}) copy-start(bf16[256,2048]{1,0:T(8,128)(2,1)S(1)} %collective-permute-done.6.refs_8_.refs_2_.refs_6_) | copy-start | bytes 3145732
  85.6 6.6 %copy-start.12 = (bf16[256,2048]{1,0:T(8,128)(2,1)}, bf16[256,2048]{1,0:T(8,128)(2,1)S(1)}, u32[]{:S(2)}) copy-start(bf16[256,2048]{1,0:T(8,128)(2,1)S(1)} %collective-permute-done.2.refs_3_.refs_1_.refs_9_) | copy-start | bytes 3145732
  87.7 4.5 %copy-start.4 = (bf16[256,2048]{1,0:T(8,128)(2,1)}, bf16[256,2048]{1,0:T(8,128)(2,1)S(1)}, u32[]{:S(2)}) copy-start(bf16[256,2048]{1,0:T(8,128)(2,1)S(1)} %collective-permute-done.7.refs_10_.refs_3_.refs_2_) | copy-start | bytes 3145732
  88.4 3.6 %collective-permute-start.8 = (bf16[2,1024,512]{2,1,0:T(8,128)(2,1)S(1)}, bf16[2,1024,512]{2,1,0:T(8,128)(2,1)S(1)}, u32[]{:S(2)}, u32[]{:S(2)}) collective-permute-start(bf16[2,1024,512]{2,1,0:T(8,128)(2,1)S(1)} %get-tuple-element.30), channel_id=1, source_target_pairs={{64,65},{65,64},{66,67},{67,66},{68,69},{69,68},{70,71},{71,70},{7... | collective-permute-start | bytes 6291464 | tf_op jit(solution)/shard_map/ppermute | solution.py:42
  90.1 47.5 %collective-permute-start.10 = (bf16[512,2048]{1,0:T(8,128)(2,1)S(1)}, bf16[512,2048]{1,0:T(8,128)(2,1)S(1)}, u32[]{:S(2)}, u32[]{:S(2)}) collective-permute-start(bf16[512,2048]{1,0:T(8,128)(2,1)S(1)} %shard_map.127), channel_id=1, source_target_pairs={{0,8},{4,12},{8,0},{12,4},{1,9},{5,13},{9,1},{13,5},{2,10},{6,14},... | collective-permute-start | bytes 6291464 | tf_op jit(solution)/shard_map/ppermute | solution.py:37
  97.0 114.7 %collective-permute-start.17 = (bf16[1312,2048]{1,0:T(8,128)(2,1)}, bf16[1312,2048]{1,0:T(8,128)(2,1)}, u32[]{:S(2)}, u32[]{:S(2)}) collective-permute-start(bf16[1312,2048]{1,0:T(8,128)(2,1)} %shard_map.133), channel_id=1, source_target_pairs={{0,48},{16,0},{32,16},{48,32},{64,112},{80,64},{96,80},{112,96},{1... | collective-permute-start | bytes 16121864 | tf_op jit(solution)/shard_map/ppermute | solution.py:37
  99.1 115.2 %collective-permute-start.18 = (bf16[1312,2048]{1,0:T(8,128)(2,1)}, bf16[1312,2048]{1,0:T(8,128)(2,1)}, u32[]{:S(2)}, u32[]{:S(2)}) collective-permute-start(bf16[1312,2048]{1,0:T(8,128)(2,1)} %shard_map.133), channel_id=1, source_target_pairs={{0,16},{16,32},{32,48},{48,0},{64,80},{80,96},{96,112},{112,64},{1... | collective-permute-start | bytes 16121864 | tf_op jit(solution)/shard_map/ppermute | solution.py:37
  99.1 38.4 %collective-permute-start.9 = (bf16[1024,512]{1,0:T(8,128)(2,1)S(1)}, bf16[1024,512]{1,0:T(8,128)(2,1)S(1)}, u32[]{:S(2)}, u32[]{:S(2)}) collective-permute-start(bf16[1024,512]{1,0:T(8,128)(2,1)S(1)} %shard_map.126.refs_5_), channel_id=1, source_target_pairs={{64,66},{66,64},{65,67},{67,65},{68,70},{70,68},{69,71},{71,69},{7... | collective-permute-start | bytes 3145736 | tf_op jit(solution)/shard_map/ppermute | solution.py:42
  138.9 20.1 %copy-start.16 = (bf16[256,2048]{1,0:T(8,128)(2,1)S(1)}, bf16[256,2048]{1,0:T(8,128)(2,1)}, u32[]{:S(2)}) copy-start(bf16[256,2048]{1,0:T(8,128)(2,1)} %incoming_ref.3) | copy-start | bytes 3145732
  138.9 2.4 collective-permute-start.11
  139.9 1.4 collective-permute-start.12
  140.6 0.7 collective-permute-start.13
  141.3 69.7 %collective-permute-start.15 = (bf16[736,2048]{1,0:T(8,128)(2,1)}, bf16[736,2048]{1,0:T(8,128)(2,1)}, u32[]{:S(2)}, u32[]{:S(2)}) collective-permute-start(bf16[736,2048]{1,0:T(8,128)(2,1)} %shard_map.128.refs_4_), channel_id=1, source_target_pairs={{0,12},{4,0},{8,4},{12,8},{1,13},{5,1},{9,5},{13,9},{2,14},{6,2},{... | collective-permute-start | bytes 9043976 | tf_op jit(solution)/shard_map/ppermute | solution.py:37
  143.8 67.2 %collective-permute-start.16 = (bf16[736,2048]{1,0:T(8,128)(2,1)}, bf16[736,2048]{1,0:T(8,128)(2,1)}, u32[]{:S(2)}, u32[]{:S(2)}) collective-permute-start(bf16[736,2048]{1,0:T(8,128)(2,1)} %shard_map.128.refs_4_), channel_id=1, source_target_pairs={{0,4},{4,8},{8,12},{12,0},{1,5},{5,9},{9,13},{13,1},{2,6},{6,10},{... | collective-permute-start | bytes 9043976 | tf_op jit(solution)/shard_map/ppermute | solution.py:37
  159.0 3.2 %copy-start.29 = (s32[32]{0:T(128)S(1)}, s32[32]{0:T(128)}, u32[]{:S(2)}) copy-start(s32[32]{0:T(128)} %constant.100.clone) | copy-start | bytes 388
  160.7 53.7 %copy-start.6 = (bf16[256,2048]{1,0:T(8,128)(2,1)S(1)}, bf16[256,2048]{1,0:T(8,128)(2,1)}, u32[]{:S(2)}) copy-start(bf16[256,2048]{1,0:T(8,128)(2,1)} %copy-done.5) | copy-start | bytes 3145732
  160.7 53.7 %copy-start.8 = (bf16[256,2048]{1,0:T(8,128)(2,1)S(1)}, bf16[256,2048]{1,0:T(8,128)(2,1)}, u32[]{:S(2)}) copy-start(bf16[256,2048]{1,0:T(8,128)(2,1)} %copy-done.7) | copy-start | bytes 3145732
  160.7 39.0 %collective-permute-start.14 = (bf16[256,2048]{1,0:T(8,128)(2,1)}, bf16[256,2048]{1,0:T(8,128)(2,1)}, u32[]{:S(2)}, u32[]{:S(2)}) collective-permute-start(bf16[256,2048]{1,0:T(8,128)(2,1)} %shard_map.131.top_ref), channel_id=1, source_target_pairs={{64,0},{65,1},{66,2},{67,3},{68,4},{69,5},{70,6},{71,7},{72,8},{73... | collective-permute-start | bytes 3145736 | tf_op jit(solution)/shard_map/ppermute | solution.py:707
  232.0 10.5 %collective-permute-start.19 = (bf16[2,256,2048]{2,1,0:T(8,128)(2,1)}, bf16[2,256,2048]{2,1,0:T(8,128)(2,1)S(1)}, u32[]{:S(2)}, u32[]{:S(2)}) collective-permute-start(bf16[2,256,2048]{2,1,0:T(8,128)(2,1)} %get-tuple-element.42.refs_4_), channel_id=1, source_target_pairs={{0,1},{1,0},{2,3},{3,2},{4,5},{5,4},{6,7},{7,6},{8,9},{9,8},{10,11... | collective-permute-start | bytes 6291464 | tf_op jit(solution)/shard_map/ppermute | solution.py:42
  242.7 29.2 %collective-permute-start.20 = (bf16[256,2048]{1,0:T(8,128)(2,1)S(1)}, bf16[256,2048]{1,0:T(8,128)(2,1)S(1)}, u32[]{:S(2)}, u32[]{:S(2)}) collective-permute-start(bf16[256,2048]{1,0:T(8,128)(2,1)S(1)} %shard_map.135.refs_5_), channel_id=1, source_target_pairs={{0,2},{2,0},{1,3},{3,1},{4,6},{6,4},{5,7},{7,5},{8,10},{10,8},{9,1... | collective-permute-start | bytes 3145736 | tf_op jit(solution)/shard_map/ppermute | solution.py:42
  245.8 9.5 %copy-start.19 = (bf16[2,256,2048]{2,1,0:T(8,128)(2,1)S(1)}, bf16[2,256,2048]{2,1,0:T(8,128)(2,1)}, u32[]{:S(2)}) copy-start(bf16[2,256,2048]{2,1,0:T(8,128)(2,1)} %get-tuple-element.42.refs_4_) | copy-start | bytes 6291460
  247.1 3.9 %collective-permute-start.21 = (f32[8,2048]{1,0:T(8,128)S(1)}, f32[8,2048]{1,0:T(8,128)S(1)}, u32[]{:S(2)}, u32[]{:S(2)}) collective-permute-start(f32[8,2048]{1,0:T(8,128)S(1)} %shard_map.137.refs_0_), channel_id=1, source_target_pairs={{0,12},{4,0},{8,4},{12,8},{64,76},{68,64},{72,68},{76,72},{1,13},{... | collective-permute-start | bytes 196616 | tf_op jit(solution)/shard_map/ppermute | solution.py:37
  248.7 4.6 %collective-permute-start.22 = (f32[8,2048]{1,0:T(8,128)S(1)}, f32[8,2048]{1,0:T(8,128)S(1)}, u32[]{:S(2)}, u32[]{:S(2)}) collective-permute-start(f32[8,2048]{1,0:T(8,128)S(1)} %shard_map.137.refs_0_), channel_id=1, source_target_pairs={{0,8},{4,12},{8,0},{12,4},{64,72},{68,76},{72,64},{76,68},{1,9},{5... | collective-permute-start | bytes 196616 | tf_op jit(solution)/shard_map/ppermute | solution.py:37
  250.2 5.0 %collective-permute-start.23 = (f32[8,2048]{1,0:T(8,128)S(1)}, f32[8,2048]{1,0:T(8,128)S(1)}, u32[]{:S(2)}, u32[]{:S(2)}) collective-permute-start(f32[8,2048]{1,0:T(8,128)S(1)} %shard_map.137.refs_0_), channel_id=1, source_target_pairs={{0,4},{4,8},{8,12},{12,0},{64,68},{68,72},{72,76},{76,64},{1,5},{5... | collective-permute-start | bytes 196616 | tf_op jit(solution)/shard_map/ppermute | solution.py:37
  255.3 3.5 %collective-permute-start.24 = (f32[8,2048]{1,0:T(8,128)S(1)}, f32[8,2048]{1,0:T(8,128)S(1)}, u32[]{:S(2)}, u32[]{:S(2)}) collective-permute-start(f32[8,2048]{1,0:T(8,128)S(1)} %shard_map.138.refs_1_), channel_id=1, source_target_pairs={{0,48},{16,0},{32,16},{48,32},{64,112},{80,64},{96,80},{112,96},{1... | collective-permute-start | bytes 196616 | tf_op jit(solution)/shard_map/ppermute | solution.py:37
  255.4 4.7 %collective-permute-start.25 = (f32[8,2048]{1,0:T(8,128)S(1)}, f32[8,2048]{1,0:T(8,128)S(1)}, u32[]{:S(2)}, u32[]{:S(2)}) collective-permute-start(f32[8,2048]{1,0:T(8,128)S(1)} %shard_map.138.refs_1_), channel_id=1, source_target_pairs={{0,32},{16,48},{32,0},{48,16},{64,96},{80,112},{96,64},{112,80},{1... | collective-permute-start | bytes 196616 | tf_op jit(solution)/shard_map/ppermute | solution.py:37
  256.0 4.9 %collective-permute-start.26 = (f32[8,2048]{1,0:T(8,128)S(1)}, f32[8,2048]{1,0:T(8,128)S(1)}, u32[]{:S(2)}, u32[]{:S(2)}) collective-permute-start(f32[8,2048]{1,0:T(8,128)S(1)} %shard_map.138.refs_1_), channel_id=1, source_target_pairs={{0,16},{16,32},{32,48},{48,0},{64,80},{80,96},{96,112},{112,64},{1... | collective-permute-start | bytes 196616 | tf_op jit(solution)/shard_map/ppermute | solution.py:37
  261.3 4.3 %collective-permute-start.27 = (f32[256,256]{1,0:T(8,128)S(1)}, f32[256,256]{1,0:T(8,128)S(1)}, u32[]{:S(2)}, u32[]{:S(2)}) collective-permute-start(f32[256,256]{1,0:T(8,128)S(1)} %shard_map.139.refs_0_), channel_id=1, source_target_pairs={{0,1},{1,0},{64,65},{65,64},{2,3},{3,2},{66,67},{67,66},{4,5},{5,4... | collective-permute-start | bytes 786440 | tf_op jit(solution)/shard_map/ppermute | solution.py:42
  265.7 6.1 %collective-permute-start.28 = (bf16[256,256]{1,0:T(8,128)(2,1)S(1)}, bf16[256,256]{1,0:T(8,128)(2,1)S(1)}, u32[]{:S(2)}, u32[]{:S(2)}) collective-permute-start(bf16[256,256]{1,0:T(8,128)(2,1)S(1)} %shard_map.140.refs_0_), channel_id=1, source_target_pairs={{0,2},{2,0},{64,66},{66,64},{1,3},{3,1},{65,67},{67,65},{4,6},{6,4... | collective-permute-start | bytes 393224 | tf_op jit(solution)/shard_map/ppermute | solution.py:42
  271.8 9.5 %collective-permute-start.29 = (bf16[256,256]{1,0:T(8,128)(2,1)S(1)}, bf16[256,256]{1,0:T(8,128)(2,1)}, u32[]{:S(2)}, u32[]{:S(2)}) collective-permute-start(bf16[256,256]{1,0:T(8,128)(2,1)S(1)} %shard_map.141.share_ref), channel_id=1, source_target_pairs={{0,64},{64,0},{1,65},{65,1},{2,66},{66,2},{3,67},{67,3},{4,68},{68... | collective-permute-start | bytes 393224 | tf_op jit(solution)/shard_map/ppermute | solution.py:732
  281.3 5.2 %copy-start.1 = (f32[256,256]{1,0:T(8,128)S(1)}, f32[256,256]{1,0:T(8,128)}, u32[]{:S(2)}) copy-start(f32[256,256]{1,0:T(8,128)} %param.15) | copy-start | bytes 786436
  (14 other events, 23.8 us)
